TPU v7x, 32 devices: a whole 2x2x4 slice. The times are simulated.
32 devices in a mesh: dp: 16 (over z, y, x), mp: 2 (over core).
Axes of the slice: x: 2, y: 2, z: 4, core: 2. Of those that a mesh axis runs over, the one named last changes fastest.
Arguments:
- inputs: bfloat16 [8192, 768], P('dp'), may hold values from -6 to 6
- norm_attn: float32 [768], replicated, may hold values from 0.1 to 1.9
- w_query: bfloat16 [768, 768], P(None, 'mp'), may hold values from -0.21875 to 0.21875
- w_key: bfloat16 [768, 768], P(None, 'mp'), may hold values from -0.21875 to 0.21875
- w_value: bfloat16 [768, 768], P(None, 'mp'), may hold values from -0.21875 to 0.21875
- w_out: bfloat16 [768, 768], P('mp'), may hold values from -1.25 to 1.25
- norm_mlp: float32 [768], replicated, may hold values from 0.1 to 1.9
- w_up: bfloat16 [768, 3072], P(None, 'mp'), may hold values from -0.21875 to 0.21875
- b_up: float32 [3072], P('mp'), may hold values from -3 to 3
- w_down: bfloat16 [3072, 768], P('mp'), may hold values from -0.109375 to 0.109375
- b_down: float32 [768], replicated, may hold values from -3 to 3
- cotangent: bfloat16 [8192, 768], P('dp'), may hold values from -6 to 6
- doc_lengths: int32 [16, 8], replicated, may hold values from 1 to 128, 256 in all within a row
- pad_counts: int32 [16], replicated, may hold values from 0 to 64
Outputs:
- output: bfloat16 [8192, 768], P('dp')
- grad_inputs: bfloat16 [8192, 768], P('dp')
- grad_norm_attn: float32 [768], replicated
- grad_query: float32 [768, 768], P(None, 'mp')
- grad_key: float32 [768, 768], P(None, 'mp')
- grad_value: float32 [768, 768], P(None, 'mp')
- grad_out: float32 [768, 768], P('mp')
- grad_norm_mlp: float32 [768], replicated
- grad_up: float32 [768, 3072], P(None, 'mp')
- grad_b_up: float32 [3072], P('mp')
- grad_down: float32 [3072, 768], P('mp')
- grad_b_down: float32 [768], replicated
Inputs may be any that keep to these rules, and one draw needn't show every extreme that they name: `doc_lengths`: row n lists the document lengths of sequence n in order; each row sums to 256 and its largest entry is 128. The last pad_counts[n] positions of sequence n are padding.
All inputs are finite; a program needn't handle non-finite values.
Results may differ from a plain program's by a relative error of at most 0.011.
Values sent between devices are 32-bit elements; how exact they have to be, the bound alone decides.
No kernel may reach another device: no remote copies, remote signals or barrier semaphores. Data moves between devices by JAX's collectives and lax.ppermute only.
A program may use at most 128 MiB of HBM per device.

v0:
```python
from functools import partial
import math

import jax
import jax.numpy as jnp
from jax import lax
from jax.sharding import PartitionSpec as P

HEAD = 64
BLOCK = 16
LEN = 256


norm_eps = 1e-05
rope_base = 10000.0
masked_score = -1e30


def matmul(left, right):
    return jnp.dot(left, right, preferred_element_type=jnp.float32)


def matmul_tn(left, right):
    return lax.dot_general(
        left, right, (((0,), (0,)), ((), ())), preferred_element_type=jnp.float32
    )


def matmul_nt(left, right):
    return lax.dot_general(
        left, right, (((1,), (1,)), ((), ())), preferred_element_type=jnp.float32
    )


def layer_norm(values, gain_row):
    centred = values - jnp.mean(values, axis=-1, keepdims=True)
    spread = jnp.mean(centred * centred, axis=-1, keepdims=True)
    return centred * lax.rsqrt(spread + norm_eps) * gain_row


def angles(places):
    half_head = HEAD // 2
    frequency = jnp.exp(
        jnp.arange(half_head, dtype=jnp.float32) * (-2.0 * math.log(rope_base) / HEAD)
    )
    turn_angle = places.astype(jnp.float32)[:, None] * frequency[None, :]
    return (jnp.cos(turn_angle), jnp.sin(turn_angle))


def rotate(values, cosine_rows, sine_rows):
    row_count = values.shape[0]
    half_head = HEAD // 2
    head_grid = values.reshape(row_count, -1, HEAD)
    first_half = head_grid[:, :, :half_head]
    second_half = head_grid[:, :, half_head:]
    cos_rows = cosine_rows[:, None, :]
    sin_rows = sine_rows[:, None, :]
    turned = jnp.concatenate(
        [
            first_half * cos_rows - second_half * sin_rows,
            second_half * cos_rows + first_half * sin_rows,
        ],
        axis=-1,
    )
    return turned.reshape(row_count, -1)


def row_facts(lengths, pad_count, places):
    doc_ends = jnp.cumsum(lengths)
    segment = jnp.sum((places[:, None] >= doc_ends[None, :]).astype(jnp.int32), axis=1)
    padded = places >= LEN - pad_count
    return (segment, padded)


def permitted(query_kind, query_place, query_segment, key_kind, key_place, key_segment, key_padded):
    query_block = (query_place // BLOCK)[:, None]
    key_block = (key_place // BLOCK)[None, :]
    query_copy = query_kind[:, None]
    key_copy = key_kind[None, :]
    noisy_rule = jnp.where(key_copy == 0, key_block == query_block, key_block < query_block)
    clean_rule = (key_copy == 1) & (key_block <= query_block)
    shaped = jnp.where(query_copy == 0, noisy_rule, clean_rule)
    same_doc = (query_segment[:, None] == key_segment[None, :]) & jnp.logical_not(
        key_padded[None, :]
    )
    itself = (query_place[:, None] == key_place[None, :]) & (query_copy == key_copy)
    return shaped & (same_doc | itself)


def merge_heads(stacked):
    return stacked.transpose(1, 0, 2).reshape(stacked.shape[1], -1)


def on_device(
    inputs,
    norm_attn,
    w_query,
    w_key,
    w_value,
    w_out,
    norm_mlp,
    w_up,
    b_up,
    w_down,
    b_down,
    cotangent,
    doc_lengths,
    pad_counts,
):
    row_count = inputs.shape[0]
    heads_dev = w_query.shape[1] // HEAD
    score_scale = HEAD ** (-0.5)
    sequence = lax.axis_index("dp")
    lengths = lax.dynamic_slice_in_dim(doc_lengths, sequence, 1, 0)[0]
    pad_count = lax.dynamic_slice_in_dim(pad_counts, sequence, 1, 0)[0]
    row_ids = jnp.arange(row_count, dtype=jnp.int32)
    row_kind = row_ids // LEN
    row_place = row_ids % LEN
    row_segment, row_padded = row_facts(lengths, pad_count, row_place)
    allowed = permitted(
        row_kind, row_place, row_segment, row_kind, row_place, row_segment, row_padded
    )
    cosine_rows, sine_rows = angles(row_place)

    def head_slice(values, head_index):
        return lax.dynamic_slice_in_dim(values, head_index * HEAD, HEAD, 1)

    def project(normed):
        queries = rotate(matmul(normed, w_query), cosine_rows, sine_rows).astype(jnp.bfloat16)
        key_rows = rotate(matmul(normed, w_key), cosine_rows, sine_rows).astype(jnp.bfloat16)
        value_rows = matmul(normed, w_value).astype(jnp.bfloat16)
        return (queries, key_rows, value_rows)

    def attend(queries, key_rows, value_rows):

        def one_head(head_index):
            query_head = head_slice(queries, head_index)
            key_head = head_slice(key_rows, head_index)
            value_head = head_slice(value_rows, head_index)
            scores = jnp.where(allowed, matmul_nt(query_head, key_head) * score_scale, masked_score)
            row_top = jnp.max(scores, axis=1, keepdims=True)
            weights = jnp.exp(scores - row_top)
            row_total = jnp.sum(weights, axis=1, keepdims=True)
            mixed_rows = matmul((weights / row_total).astype(jnp.bfloat16), value_head)
            return (mixed_rows, (row_top + jnp.log(row_total))[:, 0])

        mixed_rows, log_totals = lax.map(one_head, jnp.arange(heads_dev))
        return (merge_heads(mixed_rows).astype(jnp.bfloat16), log_totals)

    input_wide = inputs.astype(jnp.float32)
    normed = layer_norm(input_wide, norm_attn).astype(jnp.bfloat16)
    queries, key_rows, value_rows = project(normed)
    attended, log_totals = attend(queries, key_rows, value_rows)
    residual = input_wide + lax.psum(matmul(attended, w_out), "mp")
    normed_mlp = layer_norm(residual, norm_mlp).astype(jnp.bfloat16)
    up_rows = matmul(normed_mlp, w_up) + b_up
    activation = jax.nn.gelu(up_rows, approximate=True).astype(jnp.bfloat16)
    output = (residual + lax.psum(matmul(activation, w_down), "mp") + b_down).astype(jnp.bfloat16)
    input_wide, residual = lax.optimization_barrier((input_wide, residual))
    normed = layer_norm(input_wide, norm_attn).astype(jnp.bfloat16)
    queries, key_rows, value_rows = project(normed)
    attended, log_totals = attend(queries, key_rows, value_rows)
    normed_mlp = layer_norm(residual, norm_mlp).astype(jnp.bfloat16)
    up_rows = matmul(normed_mlp, w_up) + b_up
    activation = jax.nn.gelu(up_rows, approximate=True).astype(jnp.bfloat16)
    cot_wide = cotangent.astype(jnp.float32)
    grad_b_down = jnp.sum(cot_wide, axis=0)
    grad_down = matmul_tn(activation, cotangent)
    delta_act = matmul_nt(cotangent, w_down)
    gelu_back = jax.vjp(partial(jax.nn.gelu, approximate=True), up_rows)[1]
    delta_up = gelu_back(delta_act)[0].astype(jnp.bfloat16)
    grad_b_up = jnp.sum(delta_up.astype(jnp.float32), axis=0)
    grad_up = matmul_tn(normed_mlp, delta_up)
    delta_normed_mlp = lax.psum(matmul_nt(delta_up, w_up), "mp")
    delta_norm_part, grad_norm_mlp = jax.vjp(layer_norm, residual, norm_mlp)[1](delta_normed_mlp)
    delta_residual = cot_wide + delta_norm_part
    delta_branch = delta_residual.astype(jnp.bfloat16)
    grad_out = matmul_tn(attended, delta_branch)
    delta_attended = matmul_nt(delta_branch, w_out).astype(jnp.bfloat16)

    def head_back(head_index):
        query_head = head_slice(queries, head_index)
        key_head = head_slice(key_rows, head_index)
        value_head = head_slice(value_rows, head_index)
        delta_head = head_slice(delta_attended, head_index)
        scores = jnp.where(allowed, matmul_nt(query_head, key_head) * score_scale, masked_score)
        weights = jnp.exp(scores - log_totals[head_index][:, None])
        delta_weights = matmul_nt(delta_head, value_head)
        delta_scores = (
            weights * (delta_weights - jnp.sum(weights * delta_weights, axis=1, keepdims=True))
        ).astype(jnp.bfloat16)
        query_grad = matmul(delta_scores, key_head) * score_scale
        key_grad = matmul_tn(delta_scores, query_head) * score_scale
        value_grad = matmul_tn(weights.astype(jnp.bfloat16), delta_head)
        return (query_grad, key_grad, value_grad)

    query_grads, key_grads, value_grads = lax.map(head_back, jnp.arange(heads_dev))
    delta_query = rotate(merge_heads(query_grads), cosine_rows, -sine_rows).astype(jnp.bfloat16)
    delta_key = rotate(merge_heads(key_grads), cosine_rows, -sine_rows).astype(jnp.bfloat16)
    delta_value = merge_heads(value_grads).astype(jnp.bfloat16)
    grad_query = matmul_tn(normed, delta_query)
    grad_key = matmul_tn(normed, delta_key)
    grad_value = matmul_tn(normed, delta_value)
    delta_normed = lax.psum(
        matmul_nt(delta_query, w_query)
        + matmul_nt(delta_key, w_key)
        + matmul_nt(delta_value, w_value),
        "mp",
    )
    delta_input, grad_norm_attn = jax.vjp(layer_norm, input_wide, norm_attn)[1](delta_normed)
    grad_inputs = (delta_residual + delta_input).astype(jnp.bfloat16)
    (
        grad_norm_attn,
        grad_query,
        grad_key,
        grad_value,
        grad_out,
        grad_norm_mlp,
        grad_up,
        grad_b_up,
        grad_down,
        grad_b_down,
    ) = lax.psum(
        (
            grad_norm_attn,
            grad_query,
            grad_key,
            grad_value,
            grad_out,
            grad_norm_mlp,
            grad_up,
            grad_b_up,
            grad_down,
            grad_b_down,
        ),
        "dp",
    )
    return (
        output,
        grad_inputs,
        grad_norm_attn,
        grad_query,
        grad_key,
        grad_value,
        grad_out,
        grad_norm_mlp,
        grad_up,
        grad_b_up,
        grad_down,
        grad_b_down,
    )


def solution(mesh):
    return jax.shard_map(
        on_device,
        mesh=mesh,
        in_specs=(
            P("dp", None),
            P(),
            P(None, "mp"),
            P(None, "mp"),
            P(None, "mp"),
            P("mp", None),
            P(),
            P(None, "mp"),
            P("mp"),
            P("mp", None),
            P(),
            P("dp", None),
            P(),
            P(),
        ),
        out_specs=(
            P("dp", None),
            P("dp", None),
            P(),
            P(None, "mp"),
            P(None, "mp"),
            P(None, "mp"),
            P("mp", None),
            P(),
            P(None, "mp"),
            P("mp"),
            P("mp", None),
            P(),
        ),
        check_vma=False,
    )
```

profile of v0, /device:TPU:0, one launch (start us, length us, event | category | flops | bytes accessed | tf_op | source)
XLA Modules:
  0.0 699.3 jit_solution(3464507832857593635)
XLA Ops:
  22.3 27.6 %while.42 = (s32[]{:T(128)}, bf16[6,512,64]{1,2,0:T(8,128)(2,1)S(1)}, s32[6]{0:T(128)S(1)}, bf16[512,384]{0,1:T(8,128)(2,1)}, bf16[512,384]{0,1:T(8,128)(2,1)}, ...) while((s32[]{:T(128)}, ...), condition=%wide.region_7.8_spmd.clone.clone, body=%wide.region_4.7_spmd.clone.sunk.clone | while | flops 72612864 | bytes 3568847 | solution.py:147
  23.5 1.9 fusion.188
  28.1 1.9 fusion.188
  32.7 1.9 fusion.188
  37.3 1.9 fusion.188
  41.9 1.9 fusion.188
  46.5 1.9 fusion.188
  49.9 2.8 fusion.98
  54.4 4.7 fusion.99
  59.1 16.9 %all-reduce.8.cloned.1.call-done = f32[512,768]{1,0:T(8,128)} async-done(((f32[512,768]{1,0:T(8,128)}), f32[512,768]{1,0:T(8,128)}) %all-reduce.8.cloned.1.call-update) | async-done | bytes 1572880 | tf_op jit(solution)/shard_map/psum | solution.py:154
  76.0 3.3 fusion.94
  79.3 1.6 reduce_sum.193
  80.8 1.8 multiply_reduce_fusion.4
  85.1 1.4 fusion.102
  86.5 1.4 fusion.101
  87.9 1.6 reduce_sum.186
  89.5 1.8 multiply_reduce_fusion.6
  95.4 7.2 %convert_reduce_fusion = (f32[1536]{0:T(1024)}, bf16[512,1536]{1,0:T(8,128)(2,1)S(1)}, f32[512,1536]{1,0:T(8,128)}) fusion(f32[512,1536]{1,0:T(8,128)} %fusion.99, f32[1536]{0:T(1024)} %param.28, bf16[768,1536]{1,0:T(8,128)(2,1)S(1)} %copy-done, f32[512,768]{1,0:T(8,128)} %get-tuple-element.154, f32[512]{0:T(512)S(1)} %fusion.77, ...), kind=kOutput, calls=%fused_computation.77 | convolution fusion | flops 1227618816 | bytes 11815936 | tf_op jit(solution)/shard_map/dot_general | solution.py:20
  103.7 2.6 fusion.100
  107.3 40.1 %while.43 = (s32[]{:T(128)}, bf16[6,512,64]{1,2,0:T(8,128)(2,1)S(1)}, f32[6,512]{1,0:T(8,128)}, s32[6]{0:T(128)}, bf16[512,384]{1,0:T(8,128)(2,1)}, /*index=5*/b...) while((s32[]{:T(128)}, ...), condition=%wide.region_22.23_spmd.clone.clone, body=%wide.region_19.22_spmd.clone.sunk.clone | while | flops 72613376 | bytes 3710171 | solution.py:147
  109.1 2.0 fusion.192
  115.8 2.1 fusion.192
  122.5 2.1 fusion.192
  129.2 2.0 fusion.192
  135.8 2.0 fusion.192
  142.5 2.0 fusion.192
  148.0 1.7 multiply_reduce_fusion.7
  150.3 6.3 fusion.68
  156.7 3.2 multiply_reduce_fusion.1
  163.5 76.7 %while.44 = (s32[]{:T(128)}, f32[6,512,64]{1,2,0:T(8,128)}, f32[6,512,64]{1,2,0:T(8,128)}, bf16[6,512,64]{1,2,0:T(8,128)(2,1)S(1)}, s32[6]{0:T(128)S(1)}, /*inde...) while((s32[]{:T(128)}, f32[6,512,64]{1,2,0:T(8,128)}, ...), condition=%wide.region_25.26_spmd.clone.clone, body=%wide.region_23.25_spmd.clone.sunk.clone | while | flops 173604352 | bytes 9206045 | solution.py:197
  168.8 2.2 multiply_reduce_fusion.11
  172.5 1.9 fusion.205
  174.4 1.9 fusion.204
  181.6 2.2 multiply_reduce_fusion.11
  185.3 1.9 fusion.205
  187.2 1.9 fusion.204
  194.3 2.2 multiply_reduce_fusion.11
  198.1 1.9 fusion.205
  200.0 1.9 fusion.204
  207.1 2.2 multiply_reduce_fusion.11
  210.8 1.9 fusion.205
  212.8 1.9 fusion.204
  219.9 2.2 multiply_reduce_fusion.11
  223.6 1.9 fusion.205
  225.5 1.9 fusion.204
  232.7 2.2 multiply_reduce_fusion.11
  236.4 1.9 fusion.205
  238.3 1.9 fusion.204
  240.2 1.7 subtract_convert_fusion
  243.7 1.8 add_add_fusion.2
  246.2 5.3 fusion.88
  251.5 3.9 fusion.59
  255.4 1.6 fusion.105
  257.0 1.6 fusion.106
  258.6 1.6 fusion.107
  260.3 1.5 fusion.108
  261.8 8.3 %all-reduce.14.cloned.1.call-done = (f32[512,768]{1,0:T(8,128)}, f32[512,768]{1,0:T(8,128)}) async-done(((f32[512,768]{1,0:T(8,128)}, f32[512,768]{1,0:T(8,128)}), (f32[512,768]{1,0:T(8,128)}, f32[512,768]{1,0:T(8,128)})) %all-reduce.14.cloned.1.call-update) | async-done | bytes 3145744 | tf_op jit(solution)/shard_map/psum | solution.py:158
  270.1 2.6 multiply_reduce_fusion.2
  275.9 81.0 %all-reduce = (f32[768]{0:T(1024)}, f32[768]{0:T(1024)}, f32[1536]{0:T(1024)}, f32[768]{0:T(1024)}) all-reduce(f32[768]{0:T(1024)S(1)} %get-tuple-element.366, f32[768]{0:T(1024)S(1)} %copy-done.58, f32[1536]{0:T(1024)S(1)} %copy-done.60, f32[768]{0:T(1024)S(1)} %get-tuple-element.494), channel_id=1, replica_groups=mesh['dp'=16,'mp'=2] {'dp'}, use_global_device_ids=true, to_apply=%region_30.31 | all-reduce | flops 3840 | bytes 30720 | tf_op jit(solution)/shard_map/psum | solution.py:223
  356.9 2.5 add_convert_fusion.1
  359.3 321.4 %all-reduce.12.cloned.1.call-done = (f32[768,384]{1,0:T(8,128)}, f32[768,384]{1,0:T(8,128)}, f32[768,384]{1,0:T(8,128)}, f32[384,768]{1,0:T(8,128)}, f32[768,1536]{1,0:T(8,128)}, /*index=5*/f32[1536,768]{1,0:T(8,128)}) async-done(((f32[768,384]{1,0:T(8,128)}, f32[768,384]{1,0:T(8,128)}, f32[768,384]{1,0:T(8,128)}, f32[384,768]{1,0:T(8,128)}, f32[768,1536]{1,0:T(8,128)}, /*index=5*/f32[1536,768]{1,0:T(8,128)}), ...) | async-done | bytes 14155792 | tf_op jit(solution)/shard_map/psum | solution.py:223
  680.7 2.5 copy.85
  686.9 2.2 copy.89
  689.4 2.4 copy.90
  (275 shorter events, 101.0 us)
Async XLA Ops:
  7.2 88.2 %copy-start = (bf16[768,1536]{1,0:T(8,128)(2,1)S(1)}, bf16[768,1536]{1,0:T(8,128)(2,1)}, u32[]{:S(2)}) copy-start(bf16[768,1536]{1,0:T(8,128)(2,1)} %param.27) | copy-start | bytes 7077892
  7.2 8.0 %copy-start.7 = (bf16[512,768]{1,0:T(8,128)(2,1)S(1)}, bf16[512,768]{1,0:T(8,128)(2,1)}, u32[]{:S(2)}) copy-start(bf16[512,768]{1,0:T(8,128)(2,1)} %param.20) | copy-start | bytes 2359300
  7.2 8.3 %copy-start.48 = (f32[768]{0:T(1024)S(1)}, f32[768]{0:T(1024)}, u32[]{:S(2)}) copy-start(f32[768]{0:T(1024)} %param.21) | copy-start | bytes 9220
  7.2 68.7 %all-reduce.8.cloned.1.call-start = ((), (), s32[]{:S(2)}) async-start(), calls=%async_computation | async-start | bytes 3145728 | tf_op jit(solution)/shard_map/psum | solution.py:154
  9.0 7.9 %copy-start.8 = (bf16[6,512,64]{1,2,0:T(8,128)(2,1)}, bf16[6,512,64]{1,2,0:T(8,128)(2,1)S(1)}, u32[]{:S(2)}) copy-start(bf16[6,512,64]{1,2,0:T(8,128)(2,1)S(1)} %fusion.97) | copy-start | bytes 1179652
  12.5 3.0 copy-start.41
  15.6 1.4 copy-start.28
  21.0 1.3 copy-start.35
  21.0 1.3 copy-start.39
  21.0 1.3 copy-start.12
  52.7 103.9 %all-reduce.10.cloned.1.call-start = ((), (), s32[]{:S(2)}) async-start(), calls=%async_computation.1 | async-start | bytes 3145728 | tf_op jit(solution)/shard_map/psum | solution.py:174
  53.0 1.4 copy-start.19
  80.8 1.9 copy-start.3
  82.7 2.4 copy-start.52
  82.7 2.4 copy-start.50
  82.7 2.4 copy-start.29
  83.8 2.8 copy-start.26
  87.9 3.5 copy-start.36
  87.9 3.5 copy-start.40
  89.5 1.9 copy-start.17
  89.5 1.9 copy-start.18
  91.4 1.1 copy-start.54
  91.4 4.0 copy-start.45
  92.4 2.9 copy-start.44
  102.5 1.2 copy-start.31
  106.3 163.8 %all-reduce.14.cloned.1.call-start = ((), (), s32[]{:S(2)}) async-start(), calls=%async_computation.3 | async-start | bytes 6291456 | tf_op jit(solution)/shard_map/psum | solution.py:158
  147.3 9.3 %copy-start.10 = (bf16[6,512,64]{1,2,0:T(8,128)(2,1)}, bf16[6,512,64]{1,2,0:T(8,128)(2,1)S(1)}, u32[]{:S(2)}) copy-start(bf16[6,512,64]{1,2,0:T(8,128)(2,1)S(1)} %get-tuple-element.160) | copy-start | bytes 1179652
  148.0 1.7 copy-start.59
  150.3 6.3 copy-start.46
  156.6 3.3 copy-start.55
  156.6 3.3 copy-start.2
  156.6 3.2 copy-start.14
  159.9 1.1 copy-start.20
  160.5 1.2 copy-start.5
  160.6 1.2 copy-start.56
  161.0 1.1 copy-start.38
  162.2 1.3 copy-start.23
  162.2 1.3 copy-start.9
  163.5 76.7 %copy-start.37 = (f32[512,32]{0,1:T(8,128)S(1)}, f32[512,32]{0,1:T(8,128)}, u32[]{:S(2)}) copy-start(f32[512,32]{0,1:T(8,128)} %copy-done.35) | copy-start | bytes 196612
  240.2 1.7 copy-start.27
  242.5 1.1 copy-start.43
  245.5 435.2 %all-reduce.12.cloned.1.call-start = ((), (), s32[]{:S(2)}) async-start(), calls=%async_computation.2 | async-start | bytes 28311552 | tf_op jit(solution)/shard_map/psum | solution.py:223
  246.2 5.3 copy-start.21
  246.2 5.3 copy-start.62
  258.6 1.6 copy-start.11
  258.6 1.6 copy-start.24
  261.7 8.3 %copy-start.49 = (f32[768]{0:T(1024)S(1)}, f32[768]{0:T(1024)}, u32[]{:S(2)}) copy-start(f32[768]{0:T(1024)} %param.21) | copy-start | bytes 9220
  261.7 8.3 %copy-start.51 = (f32[512]{0:T(512)S(1)}, f32[512]{0:T(512)}, u32[]{:S(2)}) copy-start(f32[512]{0:T(512)} %copy-done.50) | copy-start | bytes 6148
  270.1 2.6 copy-start.53
  270.1 2.7 copy-start.4
  270.1 2.8 copy-start.15
  272.9 1.4 copy-start.6
  272.9 1.6 copy-start.22
  272.9 1.6 copy-start.57
  274.5 1.3 copy-start.58
  274.5 1.3 copy-start.60
  274.5 82.3 %copy-start.61 = (f32[768]{0:T(1024)S(1)}, f32[768]{0:T(1024)}, u32[]{:S(2)}) copy-start(f32[768]{0:T(1024)} %param.30) | copy-start | bytes 9220
  680.7 2.5 copy-start.34
  680.7 3.5 copy-start.33
  680.7 4.5 copy-start.32
  683.2 3.6 copy-start.16
  685.3 3.8 slice-start
  686.9 2.5 slice-start.1
  689.4 3.4 copy-start.1
  (5 other events, 4.9 us)
Sparse Core Ops, SparseCore 0:
  52.8 23.0 all-reduce.7
  106.4 21.5 all-reduce.9
  245.6 24.4 all-reduce.13
  278.6 402.0 all-reduce.11
where the time goes:
time: 702 us; the launch traced here: 699 us
  waiting for transfers between devices  347 us (49%)
  matrix products  140 us (20%)
  blocking collectives  81 us (12%)
  local copies, waits for them, and re-layouts  49.9 us (7%)
  other arithmetic  41.9 us (6%)
  loops' own time  23.4 us (3%)
  between operations  15.1 us (2%)
    psum x1, waiting for transfers between devices, on_device(): lax.psum((grad_norm_attn, grad_query, grad_key, grad_value, grad_out, gra...  321 us
    psum x1, blocking collectives, on_device(): lax.psum((grad_norm_attn, grad_query, grad_key, grad_value, grad_out, gra...  81 us
    dot_general x30, matrix products, matmul_nt(): lax.dot_general(left, right, (((1,), (1,)), ((), ())), preferred_element_...  56.6 us
    dot_general x27, matrix products, matmul(): return jnp.dot(left, right, preferred_element_type=jnp.float32)  49.2 us
    dot_general x18, matrix products, matmul_tn(): lax.dot_general(left, right, (((0,), (0,)), ((), ())), preferred_element_...  34.7 us
    unnamed x138, local copies, waits for them, and re-layouts  19.9 us
    psum x1, waiting for transfers between devices, on_device(): residual = input_wide + lax.psum(matmul(attended, w_out), 'mp')  16.9 us
    another operation x1, loops' own time, on_device(): lax.map(head_back, jnp.arange(heads_dev))  15.7 us
  transfers between devices with their start and end apart: 4, of which 3 were waited for; matrix products, arithmetic and copies ran while one was open for 11% of the time, Pallas kernels for 0%

commit v1 on v0

v1 whole, which is shorter than its diff:
```python
import math

import numpy as np

import jax
import jax.numpy as jnp
from jax import lax
from jax.experimental import pallas as pl
from jax.experimental.pallas import tpu as pltpu
from jax.sharding import PartitionSpec as P

HEAD = 64
BLOCK = 16
LEN = 256
HALF = 128
LANES = 128
GROUP = 16

norm_eps = 1e-05
rope_base = 10000.0
masked_score = -1e30
score_scale = HEAD ** (-0.5)
bf16 = jnp.bfloat16
f32 = jnp.float32

X, Y, Z1, Z2 = 1, 2, 4, 8
ORDERS_MLP = ((X, Y, Z1, Z2), (Y, X, Z1, Z2), (Z1, Z2, X, Y))
ORDERS_ATT = ((X, Y, Z1, Z2), (Y, X, Z1, Z2))

CASES = ((0, 0, 256, 0), (128, 256, 384, 128), (256, 640, 128, 128), (384, 768, 256, 128))
TILES = (
    (0, 0, 0, 0),
    (0, 1, 0, 0),
    (0, 1, 128, 0),
    (0, 1, 128, 128),
    (0, 0, 128, 128),
    (1, 1, 0, 0),
    (1, 1, 128, 0),
    (1, 1, 128, 128),
)
KEY_PLACE = (0, 3, 1, 2)


def mm(left, right):
    return jnp.dot(left, right, preferred_element_type=f32)


def tn(left, right):
    return lax.dot_general(left, right, (((0,), (0,)), ((), ())), preferred_element_type=f32)


def nt(left, right):
    return lax.dot_general(left, right, (((1,), (1,)), ((), ())), preferred_element_type=f32)


def rope_tables():
    half = HEAD // 2
    frequency = np.exp(np.arange(half) * (-2.0 * math.log(rope_base) / HEAD)).astype(np.float32)
    turn = (np.arange(LEN, dtype=np.float32)[:, None] * frequency[None, :]).astype(np.float32)
    cosine, sine = np.cos(turn.astype(np.float64)), np.sin(turn.astype(np.float64))
    cosine = np.tile(cosine, (1, LANES // half)).astype(np.float32)
    sine = np.tile(np.concatenate([-sine, sine], 1), (1, LANES // HEAD)).astype(np.float32)
    return cosine, sine


def swap_halves(values):
    lane = lax.broadcasted_iota(jnp.int32, values.shape, 1)
    return jnp.where(
        lane % HEAD < HEAD // 2, pltpu.roll(values, LANES - HEAD // 2, 1), pltpu.roll(values, HEAD // 2, 1)
    )


def head_mask(rows, which):
    lane = lax.broadcasted_iota(jnp.int32, (rows, LANES), 1)
    return (lane >= HEAD) if which else (lane < HEAD)


def layer_norm_rows(values, gain):
    centred = values - jnp.mean(values, axis=-1, keepdims=True)
    spread = jnp.mean(centred * centred, axis=-1, keepdims=True)
    return centred * lax.rsqrt(spread + norm_eps) * gain


def norm_back_rows(values, gain, delta):
    centred = values - jnp.mean(values, axis=-1, keepdims=True)
    spread = jnp.mean(centred * centred, axis=-1, keepdims=True)
    s = lax.rsqrt(spread + norm_eps)
    xhat = centred * s
    e = delta * gain
    back = s * (e - jnp.mean(e, axis=-1, keepdims=True) - xhat * jnp.mean(e * xhat, axis=-1, keepdims=True))
    return back, jnp.sum(delta * xhat, axis=0, keepdims=True)


def fill_bias(lengths_ref, pads_ref, bias_ref):
    sequence = lax.axis_index("dp")
    docs = lengths_ref.shape[1]
    ends, total = [], jnp.int32(0)
    for j in range(docs):
        total = total + lengths_ref[sequence, j]
        ends.append(total)
    first_pad = LEN - pads_ref[sequence]

    def segment(places):
        seg = jnp.zeros(places.shape, jnp.int32)
        for end in ends:
            seg = seg + (places >= end).astype(jnp.int32)
        return seg

    rows, cols, row_seg, col_seg = {}, {}, {}, {}
    for base in (0, HALF):
        rows[base] = lax.broadcasted_iota(jnp.int32, (HALF, LANES), 0) + base
        cols[base] = lax.broadcasted_iota(jnp.int32, (HALF, LANES), 1) + base
        row_seg[base] = segment(rows[base])
        col_seg[base] = segment(cols[base])
    for tile, (query_kind, key_kind, query_base, key_base) in enumerate(TILES):
        q, k = rows[query_base], cols[key_base]
        query_block, key_block = q // BLOCK, k // BLOCK
        same_doc = (row_seg[query_base] == col_seg[key_base]) & (k < first_pad)
        if query_kind == 0 and key_kind == 0:
            ok = (key_block == query_block) & (same_doc | (q == k))
        elif query_kind == 0:
            ok = (key_block < query_block) & same_doc
        else:
            ok = (key_block <= query_block) & (same_doc | (q == k))
        bias_ref[:, tile * LANES : (tile + 1) * LANES] = jnp.where(ok, 0.0, masked_score)


def attention_forward(
    lengths_ref, pads_ref, x_ref, gain_ref, wq_ref, wk_ref, wv_ref, wo_ref, cos_ref, sin_ref,
    normed_ref, q_ref, k_ref, v_ref, att_ref, prob_ref, part_ref, bias_ref,
):
    heads_cols = wq_ref.shape[1]
    pairs = heads_cols // LANES
    fill_bias(lengths_ref, pads_ref, bias_ref)

    @pl.loop(0, x_ref.shape[0] // 64)
    def _(i):
        rows = pl.ds(pl.multiple_of(i * 64, 64), 64)
        normed_ref[rows, :] = layer_norm_rows(x_ref[rows, :].astype(f32), gain_ref[...]).astype(bf16)

    for block in range(4):
        rows = slice(block * HALF, block * HALF + HALF)
        places = slice((block % 2) * HALF, (block % 2) * HALF + HALF)
        key_rows = slice(KEY_PLACE[block] * HALF, KEY_PLACE[block] * HALF + HALF)
        normed = normed_ref[rows, :]
        cosine, sine = cos_ref[places, :], sin_ref[places, :]
        query, key = mm(normed, wq_ref[...]), mm(normed, wk_ref[...])
        for t in range(pairs):
            cols = slice(t * LANES, (t + 1) * LANES)
            turned = query[:, cols] * cosine + swap_halves(query[:, cols]) * sine
            q_ref[rows, cols] = (turned.astype(bf16).astype(f32) * score_scale).astype(bf16)
            turned = key[:, cols] * cosine + swap_halves(key[:, cols]) * sine
            k_ref[key_rows, cols] = turned.astype(bf16)
        v_ref[key_rows, :] = mm(normed, wv_ref[...]).astype(bf16)

    for t in range(pairs):
        cols = slice(t * LANES, (t + 1) * LANES)
        key_pair, value_pair = k_ref[:, cols], v_ref[:, cols]
        mixed = [None] * 4
        for which in range(2):
            mask = head_mask(key_pair.shape[0], which)
            key_head = jnp.where(mask, key_pair, jnp.zeros_like(key_pair))
            value_head = jnp.where(mask, value_pair, jnp.zeros_like(value_pair))
            for case, (query_row, first, width, key_row) in enumerate(CASES):
                scores = nt(q_ref[query_row : query_row + HALF, cols], key_head[key_row : key_row + width])
                scores = scores + bias_ref[:, first : first + width]
                weights = jnp.exp(scores - jnp.max(scores, axis=1, keepdims=True))
                low = (weights * (1.0 / jnp.sum(weights, axis=1, keepdims=True))).astype(bf16)
                prob_ref[2 * t + which, :, first : first + width] = low
                part = mm(low, value_head[key_row : key_row + width])
                mixed[case] = part if mixed[case] is None else mixed[case] + part
        for case, (query_row, _, _, _) in enumerate(CASES):
            att_ref[query_row : query_row + HALF, cols] = mixed[case].astype(bf16)

    for block in range(2):
        rows = slice(block * 256, block * 256 + 256)
        part_ref[rows, :] = mm(att_ref[rows, :], wo_ref[...])


def pack(order, place):
    slot = 0
    for step, bit in enumerate(order):
        if place & (1 << (3 - step)):
            slot |= bit
    return slot


def mlp_kernel(
    x_ref, mine_ref, theirs_ref, gain_ref, wu_ref, bu_ref, wd_ref, cot_ref,
    residual_ref, normed_ref, act_ref, du_ref, gbu_ref, gbd_ref, *outs_and_scratch,
):
    *outs, gd_ref, gu_ref = outs_and_scratch
    row_count = x_ref.shape[0]
    units = wu_ref.shape[1]
    width = x_ref.shape[1]
    me = lax.axis_index("dp") % GROUP
    gbu_ref[...] = jnp.zeros_like(gbu_ref)
    gbd_ref[...] = jnp.zeros_like(gbd_ref)

    @pl.loop(0, row_count // 64)
    def _(i):
        rows = pl.ds(pl.multiple_of(i * 64, 64), 64)
        residual = x_ref[rows, :].astype(f32) + (mine_ref[rows, :] + theirs_ref[rows, :])
        residual_ref[rows, :] = residual
        normed_ref[rows, :] = layer_norm_rows(residual, gain_ref[...]).astype(bf16)
        gbd_ref[...] += jnp.sum(cot_ref[rows, :].astype(f32), axis=0, keepdims=True)

    c0 = math.sqrt(2.0 / math.pi)
    c1 = c0 * 0.044715

    @pl.loop(0, units // 256)
    def _(j):
        cols = pl.ds(pl.multiple_of(j * 256, 256), 256)
        for block in range(row_count // 256):
            rows = slice(block * 256, block * 256 + 256)
            u = mm(normed_ref[rows, :], wu_ref[:, cols]) + bu_ref[:, cols]
            delta = nt(cot_ref[rows, :], wd_ref[cols, :])
            square = u * u
            t = jnp.tanh(u * (c0 + c1 * square))
            half_up = 0.5 * (1.0 + t)
            act_ref[rows, cols] = (u * half_up).astype(bf16)
            slope = half_up + (0.5 * u) * (1.0 - t * t) * (c0 + (3.0 * c1) * square)
            low = (delta * slope).astype(bf16)
            du_ref[rows, cols] = low
            gbu_ref[:, cols] += jnp.sum(low.astype(f32), axis=0, keepdims=True)
        gd_ref[cols, :] = tn(act_ref[:, cols], cot_ref[...])
        gu_ref[:, cols] = tn(normed_ref[...], du_ref[:, cols])

    down_rows, up_rows = units // GROUP, width // GROUP
    part_cols = width // len(ORDERS_MLP)
    for p, order in enumerate(ORDERS_MLP):
        for place in range(GROUP):
            block = me ^ pack(order, place)
            out = outs[2 * p + (place >= 8)]
            spot = place % 8
            out[spot, 0:down_rows, :] = gd_ref[
                pl.ds(pl.multiple_of(block * down_rows, 8), down_rows), p * part_cols : (p + 1) * part_cols
            ]
            for half in range(units // width):
                start = half * width + p * part_cols
                at = down_rows + half * up_rows
                out[spot, at : at + up_rows, :] = gu_ref[
                    pl.ds(pl.multiple_of(block * up_rows, 8), up_rows), start : start + part_cols
                ]


def mlp_tail_kernel(act_ref, du_ref, wu_ref, wd_ref, delta_ref, out_ref):
    for block in range(act_ref.shape[0] // 256):
        rows = slice(block * 256, block * 256 + 256)
        delta_ref[rows, :] = nt(du_ref[rows, :], wu_ref[...])
    for block in range(act_ref.shape[0] // 256):
        rows = slice(block * 256, block * 256 + 256)
        out_ref[rows, :] = mm(act_ref[rows, :], wd_ref[...])


def attention_backward(
    mine_ref, theirs_ref, residual_ref, gain_ref, cot_ref, att_ref, wo_ref, q_ref, k_ref, v_ref, prob_ref,
    normed_ref, wq_ref, wk_ref, wv_ref, cos_ref, sin_ref,
    delta_ref, gnorm_ref, part_ref, *outs_and_scratch,
):
    *outs, branch_ref, datt_ref, dq_ref, dk_ref, dv_ref, dk_acc, dv_acc, go_ref, gq_ref, gk_ref, gv_ref = outs_and_scratch
    row_count = residual_ref.shape[0]
    heads_cols = wq_ref.shape[1]
    pairs = heads_cols // LANES
    me = lax.axis_index("dp") % GROUP
    gnorm_ref[...] = jnp.zeros_like(gnorm_ref)

    @pl.loop(0, row_count // 64)
    def _(i):
        rows = pl.ds(pl.multiple_of(i * 64, 64), 64)
        delta = mine_ref[rows, :] + theirs_ref[rows, :]
        back, gain_part = norm_back_rows(residual_ref[rows, :], gain_ref[...], delta)
        back = back + cot_ref[rows, :].astype(f32)
        delta_ref[rows, :] = back
        branch_ref[rows, :] = back.astype(bf16)
        gnorm_ref[...] += gain_part

    for block in range(2):
        rows = slice(block * 256, block * 256 + 256)
        datt_ref[rows, :] = nt(branch_ref[rows, :], wo_ref[...]).astype(bf16)
    go_ref[...] = tn(att_ref[...], branch_ref[...])

    for t in range(pairs):
        cols = slice(t * LANES, (t + 1) * LANES)
        key_pair, value_pair = k_ref[:, cols], v_ref[:, cols]
        dk_acc[...] = jnp.zeros_like(dk_acc)
        dv_acc[...] = jnp.zeros_like(dv_acc)
        query_grads = [None] * 4
        for which in range(2):
            mask = head_mask(key_pair.shape[0], which)
            key_head = jnp.where(mask, key_pair, jnp.zeros_like(key_pair))
            value_head = jnp.where(mask, value_pair, jnp.zeros_like(value_pair))
            small = head_mask(HALF, which)
            for case, (query_row, first, width, key_row) in enumerate(CASES):
                rows = slice(query_row, query_row + HALF)
                keys = slice(key_row, key_row + width)
                low = prob_ref[2 * t + which, :, first : first + width]
                wide = low.astype(f32)
                delta_head = datt_ref[rows, cols]
                g = nt(delta_head, value_head[keys])
                weighted = wide * g
                scores_back = (weighted - wide * jnp.sum(weighted, axis=1, keepdims=True)).astype(bf16)
                part = mm(scores_back, key_head[keys])
                query_grads[case] = part if query_grads[case] is None else query_grads[case] + part
                query = q_ref[rows, cols]
                query = jnp.where(small, query, jnp.zeros_like(query))
                delta_head = jnp.where(small, delta_head, jnp.zeros_like(delta_head))
                dk_acc[keys, :] += tn(scores_back, query)
                dv_acc[keys, :] += tn(low, delta_head)
        for block in range(4):
            rows = slice(block * HALF, block * HALF + HALF)
            places = slice((block % 2) * HALF, (block % 2) * HALF + HALF)
            key_rows = slice(KEY_PLACE[block] * HALF, KEY_PLACE[block] * HALF + HALF)
            cosine, sine = cos_ref[places, :], sin_ref[places, :]
            grad = query_grads[block] * score_scale
            dq_ref[rows, cols] = (grad * cosine - swap_halves(grad) * sine).astype(bf16)
            grad = dk_acc[key_rows, :]
            dk_ref[rows, cols] = (grad * cosine - swap_halves(grad) * sine).astype(bf16)
            dv_ref[rows, cols] = dv_acc[key_rows, :].astype(bf16)

    for block in range(2):
        rows = slice(block * 256, block * 256 + 256)
        part_ref[rows, :] = (
            nt(dq_ref[rows, :], wq_ref[...]) + nt(dk_ref[rows, :], wk_ref[...]) + nt(dv_ref[rows, :], wv_ref[...])
        )
    gq_ref[...] = tn(normed_ref[...], dq_ref[...])
    gk_ref[...] = tn(normed_ref[...], dk_ref[...])
    gv_ref[...] = tn(normed_ref[...], dv_ref[...])

    out_rows, in_rows = heads_cols // GROUP, normed_ref.shape[1] // GROUP
    half_rows = in_rows // 2
    for p, order in enumerate(ORDERS_ATT):
        for place in range(GROUP):
            block = me ^ pack(order, place)
            out = outs[2 * p + (place >= 8)]
            spot = place % 8
            out[spot, 0:out_rows, :] = go_ref[
                pl.ds(pl.multiple_of(block * out_rows, 8), out_rows), p * heads_cols : (p + 1) * heads_cols
            ]
            source = (gq_ref, gk_ref)[p]
            out[spot, out_rows : out_rows + in_rows, :] = source[pl.ds(pl.multiple_of(block * in_rows, 8), in_rows), :]
            out[spot, out_rows + in_rows : out_rows + in_rows + half_rows, :] = gv_ref[
                pl.ds(pl.multiple_of(block * in_rows + p * half_rows, 8), half_rows), :
            ]


def input_kernel(mine_ref, theirs_ref, x_ref, gain_ref, delta_ref, grad_ref, gnorm_ref):
    gnorm_ref[...] = jnp.zeros_like(gnorm_ref)

    @pl.loop(0, x_ref.shape[0] // 64)
    def _(i):
        rows = pl.ds(pl.multiple_of(i * 64, 64), 64)
        delta = mine_ref[rows, :] + theirs_ref[rows, :]
        back, gain_part = norm_back_rows(x_ref[rows, :].astype(f32), gain_ref[...], delta)
        grad_ref[rows, :] = (delta_ref[rows, :] + back).astype(bf16)
        gnorm_ref[...] += gain_part


def unpack_mlp_kernel(*refs):
    *ins, gd_ref, gu_ref = refs
    me = lax.axis_index("dp") % GROUP
    width = gd_ref.shape[1]
    units = gu_ref.shape[1]
    down_rows, up_rows = units // GROUP, width // GROUP
    part_cols = width // len(ORDERS_MLP)
    for p, order in enumerate(ORDERS_MLP):
        for place in range(GROUP):
            block = me ^ pack(order, place)
            source = ins[2 * p + (place >= 8)]
            spot = place % 8
            gd_ref[pl.ds(pl.multiple_of(block * down_rows, 8), down_rows), p * part_cols : (p + 1) * part_cols] = source[
                spot, 0:down_rows, :
            ]
            for half in range(units // width):
                start = half * width + p * part_cols
                at = down_rows + half * up_rows
                gu_ref[pl.ds(pl.multiple_of(block * up_rows, 8), up_rows), start : start + part_cols] = source[
                    spot, at : at + up_rows, :
                ]


def unpack_att_kernel(*refs):
    *ins, go_ref, gq_ref, gk_ref, gv_ref = refs
    me = lax.axis_index("dp") % GROUP
    heads_cols = gq_ref.shape[1]
    out_rows, in_rows = heads_cols // GROUP, gq_ref.shape[0] // GROUP
    half_rows = in_rows // 2
    for p, order in enumerate(ORDERS_ATT):
        for place in range(GROUP):
            block = me ^ pack(order, place)
            source = ins[2 * p + (place >= 8)]
            spot = place % 8
            go_ref[pl.ds(pl.multiple_of(block * out_rows, 8), out_rows), p * heads_cols : (p + 1) * heads_cols] = source[
                spot, 0:out_rows, :
            ]
            target = (gq_ref, gk_ref)[p]
            target[pl.ds(pl.multiple_of(block * in_rows, 8), in_rows), :] = source[spot, out_rows : out_rows + in_rows, :]
            gv_ref[pl.ds(pl.multiple_of(block * in_rows + p * half_rows, 8), half_rows), :] = source[
                spot, out_rows + in_rows : out_rows + in_rows + half_rows, :
            ]


VMEM = pl.BlockSpec(memory_space=pltpu.VMEM)
SMEM = pl.BlockSpec(memory_space=pltpu.SMEM)


def call(kernel, ins, outs, scratch=(), flops=0, limit=48, smem=0):
    shapes = [jax.ShapeDtypeStruct(shape, dtype) for shape, dtype in outs]
    moved = sum(math.prod(a.shape) * a.dtype.itemsize for a in list(ins) + shapes)
    return pl.pallas_call(
        kernel,
        out_shape=shapes,
        in_specs=[SMEM] * smem + [VMEM] * (len(ins) - smem),
        out_specs=[VMEM] * len(outs),
        scratch_shapes=[pltpu.VMEM(shape, dtype) for shape, dtype in scratch],
        compiler_params=pltpu.CompilerParams(vmem_limit_bytes=limit * 1024 * 1024),
        cost_estimate=pl.CostEstimate(flops=flops, bytes_accessed=moved, transcendentals=0),
    )(*ins)


def on_device(
    count,
    inputs, norm_attn, w_query, w_key, w_value, w_out, norm_mlp, w_up, b_up, w_down, b_down, cotangent,
    doc_lengths, pad_counts,
):
    rows, width = inputs.shape
    heads_cols = w_query.shape[1]
    units = w_up.shape[1]
    heads = heads_cols // HEAD
    cosine, sine = (jnp.asarray(t) for t in rope_tables())
    gain_attn, gain_mlp = norm_attn.reshape(1, -1), norm_mlp.reshape(1, -1)

    def swap(values):
        return lax.ppermute(values, "mp", [(0, 1), (1, 0)])

    def flip(values, bit):
        return lax.ppermute(values, "dp", [(i, i ^ bit) for i in range(count)])

    def across(values):
        if count == GROUP:
            return values
        groups = [[g * GROUP + j for g in range(count // GROUP)] for j in range(GROUP)]
        return lax.psum(values, "dp", axis_index_groups=groups)

    normed, q, k, v, attended, probs, part = call(
        attention_forward,
        [doc_lengths, pad_counts, inputs, gain_attn, w_query, w_key, w_value, w_out, cosine, sine],
        [
            ((rows, width), bf16),
            ((rows, heads_cols), bf16),
            ((rows, heads_cols), bf16),
            ((rows, heads_cols), bf16),
            ((rows, heads_cols), bf16),
            ((heads, HALF, 8 * LANES), bf16),
            ((rows, width), f32),
        ],
        [((HALF, 8 * LANES), f32)],
        flops=2 * rows * width * heads_cols * 4,
        smem=2,
    )
    part_other = swap(part)

    n_mlp = len(ORDERS_MLP)
    slot_rows = units // GROUP + (units // width) * (width // GROUP)
    portion = ((8, slot_rows, width // n_mlp), f32)
    residual, normed_mlp, act, du, grad_bu, grad_bd, *mlp_parts = call(
        mlp_kernel,
        [inputs, part, part_other, gain_mlp, w_up, b_up.reshape(1, -1), w_down, cotangent],
        [
            ((rows, width), f32),
            ((rows, width), bf16),
            ((rows, units), bf16),
            ((rows, units), bf16),
            ((1, units), f32),
            ((1, width), f32),
        ]
        + [portion] * (2 * n_mlp),
        [((units, width), f32), ((width, units), f32)],
        flops=2 * rows * width * units * 4,
        limit=56,
    )

    def scatter(keep, send, order):
        for step, bit in enumerate(order):
            got = flip(send, bit)
            if step == 3:
                return keep + got
            half = keep.shape[0] // 2
            send = keep[half:] + got[half:]
            keep = keep[:half] + got[:half]

    def gather(own, order):
        for step, bit in enumerate(reversed(order)):
            got = flip(own, bit)
            if step == 3:
                return own, got
            own = jnp.concatenate([own, got], 0)

    delta_part, out_part = call(
        mlp_tail_kernel,
        [act, du, w_up, w_down],
        [((rows, width), f32), ((rows, width), f32)],
        flops=2 * rows * width * units * 2,
    )
    delta_other, out_other = swap(delta_part), swap(out_part)

    n_att = len(ORDERS_ATT)
    slot_rows = heads_cols // GROUP + (width // GROUP) * 3 // 2
    portion = ((8, slot_rows, heads_cols), f32)
    delta_residual, grad_norm_mlp, normed_part, *att_parts = call(
        attention_backward,
        [
            delta_part, delta_other, residual, gain_mlp, cotangent, attended, w_out, q, k, v, probs,
            normed, w_query, w_key, w_value, cosine, sine,
        ],
        [((rows, width), f32), ((1, width), f32), ((rows, width), f32)] + [portion] * (2 * n_att),
        [
            ((rows, width), bf16),
            ((rows, heads_cols), bf16),
            ((rows, heads_cols), bf16),
            ((rows, heads_cols), bf16),
            ((rows, heads_cols), bf16),
            ((rows, LANES), f32),
            ((rows, LANES), f32),
            ((heads_cols, width), f32),
            ((width, heads_cols), f32),
            ((width, heads_cols), f32),
            ((width, heads_cols), f32),
        ],
        flops=2 * rows * width * heads_cols * 10,
    )
    normed_other = swap(normed_part)
    grad_inputs, grad_norm_attn = call(
        input_kernel,
        [normed_part, normed_other, inputs, gain_attn, delta_residual],
        [((rows, width), bf16), ((1, width), f32)],
    )
    output = (residual + (out_part + out_other) + b_down).astype(bf16)

    mlp_own = [across(scatter(mlp_parts[2 * p], mlp_parts[2 * p + 1], order)) for p, order in enumerate(ORDERS_MLP)]
    mlp_all = [a for own, order in zip(mlp_own, ORDERS_MLP) for a in gather(own, order)]
    att_own = [across(scatter(att_parts[2 * p], att_parts[2 * p + 1], order)) for p, order in enumerate(ORDERS_ATT)]
    att_all = [a for own, order in zip(att_own, ORDERS_ATT) for a in gather(own, order)]

    vectors = jnp.concatenate([grad_norm_attn, grad_norm_mlp, grad_bd, grad_bu], 1)
    for bit in (X, Y, Z1, Z2):
        vectors = vectors + flip(vectors, bit)
    vectors = across(vectors)[0]

    grad_down, grad_up = call(unpack_mlp_kernel, mlp_all, [((units, width), f32), ((width, units), f32)])
    grad_out, grad_query, grad_key, grad_value = call(
        unpack_att_kernel,
        att_all,
        [((heads_cols, width), f32), ((width, heads_cols), f32), ((width, heads_cols), f32), ((width, heads_cols), f32)],
    )
    return (
        output,
        grad_inputs,
        vectors[:width],
        grad_query,
        grad_key,
        grad_value,
        grad_out,
        vectors[width : 2 * width],
        grad_up,
        vectors[3 * width :],
        grad_down,
        vectors[2 * width : 3 * width],
    )


def solution(mesh):
    count = mesh.shape["dp"]

    def step(*args):
        return on_device(count, *args)

    return jax.shard_map(
        step,
        mesh=mesh,
        in_specs=(
            P("dp", None),
            P(),
            P(None, "mp"),
            P(None, "mp"),
            P(None, "mp"),
            P("mp", None),
            P(),
            P(None, "mp"),
            P("mp"),
            P("mp", None),
            P(),
            P("dp", None),
            P(),
            P(),
        ),
        out_specs=(
            P("dp", None),
            P("dp", None),
            P(),
            P(None, "mp"),
            P(None, "mp"),
            P(None, "mp"),
            P("mp", None),
            P(),
            P(None, "mp"),
            P("mp"),
            P("mp", None),
            P(),
        ),
        check_vma=False,
    )
```

time: 702 us -> 368 us (0.52)
  matrix products: 140 us -> 0 us
  waiting for transfers between devices: 347 us -> 224 us
  blocking collectives: 81 us -> 0 us
  Pallas kernels: 0 us -> 65.1 us
  starting transfers between devices: 0.82 us -> 52.5 us
  other arithmetic: 41.9 us -> 6.85 us
  local copies, waits for them, and re-layouts: 49.9 us -> 17.9 us
  loops' own time: 23.4 us -> 0 us
  between operations: 15.1 us -> 1.15 us
    psum x4 -> x0, waiting for transfers between devices: 347 us -> none  [the longest x1 321 us: on_device(): lax.psum((grad_norm_attn, grad_query, grad_key, grad_value, grad_out, gra...]
    ppermute x0 -> x48, waiting for transfers between devices: none -> 224 us  [the longest x44 222 us: flip(): return lax.ppermute(values, 'dp', [(i, i ^ bit) for i in range(count)])]
    dot_general x75 -> x0, matrix products: 140 us -> none  [the longest x30 56.6 us: matmul_nt(): lax.dot_general(left, right, (((1,), (1,)), ((), ())), preferred_element_...]
    psum x1 -> x0, blocking collectives: 81 us -> none  [on_device(): lax.psum((grad_norm_attn, grad_query, grad_key, grad_value, grad_out, gra...]
    pallas_call x0 -> x7, Pallas kernels: none -> 65.1 us  [call(): pl.pallas_call(kernel, out_shape=shapes, in_specs=[SMEM] * smem + [VMEM]...]
    ppermute x0 -> x48, starting transfers between devices: none -> 52.4 us  [the longest x44 51.6 us: flip(): return lax.ppermute(values, 'dp', [(i, i ^ bit) for i in range(count)])]
    reduce_sum x26 -> x0, other arithmetic: 25.6 us -> none  [the longest x6 9.03 us: layer_norm(): centred = values - jnp.mean(values, axis=-1, keepdims=True)]
    another operation x3 -> x0, loops' own time: 23.4 us -> none  [the longest x1 15.7 us: on_device(): lax.map(head_back, jnp.arange(heads_dev))]
  transfers between devices with their start and end apart: 4 -> 48, of which waited for: 3 -> 27; matrix products, arithmetic and copies ran while one was open for 11% -> 3% of each run, Pallas kernels for 0% -> 7%
where the time goes in v1:
time: 368 us
  waiting for transfers between devices  224 us (61%)
  Pallas kernels  65.1 us (18%)
  starting transfers between devices  52.5 us (14%)
  local copies, waits for them, and re-layouts  17.9 us (5%)
  other arithmetic  6.85 us (2%)
    ppermute x44, waiting for transfers between devices, flip(): return lax.ppermute(values, 'dp', [(i, i ^ bit) for i in range(count)])  222 us
    pallas_call x7, Pallas kernels, call(): pl.pallas_call(kernel, out_shape=shapes, in_specs=[SMEM] * smem + [VMEM]...  65.1 us
    ppermute x44, starting transfers between devices, flip(): return lax.ppermute(values, 'dp', [(i, i ^ bit) for i in range(count)])  51.6 us
    unnamed x80, local copies, waits for them, and re-layouts  14.8 us
  transfers between devices with their start and end apart: 48, of which 27 were waited for; matrix products, arithmetic and copies ran while one was open for 3% of the time, Pallas kernels for 7%

profile of v1, /device:TPU:0, one launch (start us, length us, event | category | flops | bytes accessed | tf_op | source)
XLA Modules:
  0.0 367.5 jit_solution(3858504568237956471)
XLA Ops:
  2.1 1.1 copy-done.3
  3.2 1.1 copy-done.6
  5.4 1.1 copy-done.10
  10.0 10.8 %shard_map.247 = (bf16[512,768]{1,0:T(8,128)(2,1)S(1)}, bf16[512,384]{1,0:T(8,128)(2,1)S(1)}, bf16[512,384]{1,0:T(8,128)(2,1)S(1)}, bf16[512,384]{1,0:T(8,128)(2...) custom-call(s32[16,8]{1,0:T(8,128)S(1)} %copy.28.lengths_ref, ...), custom_call_target="tpu_custom_call" | custom-call | flops 1207959552 | bytes 8916544 | tf_op jit(solution)/shard_map/pallas_call | solution.py:410
  22.4 2.1 collective-permute-done.theirs_ref
  24.4 1.2 copy-done.36
  25.6 19.4 %shard_map.248 = (f32[512,768]{1,0:T(8,128)}, bf16[512,768]{1,0:T(8,128)(2,1)}, bf16[512,1536]{1,0:T(8,128)(2,1)}, bf16[512,1536]{1,0:T(8,128)(2,1)}, f32[1,1536...) custom-call(bf16[512,768]{1,0:T(8,128)(2,1)} %x_ref.5, ...), custom_call_target="tpu_custom_call" | custom-call | flops 4831838208 | bytes 24397824 | tf_op jit(solution)/shard_map/pallas_call | solution.py:410
  45.1 1.4 copy-done.20
  46.5 5.6 %shard_map.249 = (f32[512,768]{1,0:T(8,128)S(1)}, f32[512,768]{1,0:T(8,128)S(1)}) custom-call(bf16[512,1536]{1,0:T(8,128)(2,1)S(1)} %copy-done.20, bf16[512,1536]{1,0:T(8,128)(2,1)} %get-tuple-element.50.du_ref, bf16[768,1536]{1,0:T(8,128)(2,1)} %wu_ref.3, bf16[1536,768]{1,0:T(8,128)(2,1)} %wd_ref.3), custom_call_target="tpu_custom_call" | custom-call | flops 2415919104 | bytes 11010048 | tf_op jit(solution)/shard_map/pallas_call | solution.py:410
  52.6 2.6 collective-permute-start.24
  55.3 1.5 collective-permute-start.32
  56.8 1.6 collective-permute-start.40
  58.4 1.2 copy-done.28
  59.6 16.5 %shard_map.250 = (f32[512,768]{1,0:T(8,128)}, f32[1,768]{1,0:T(1,128)S(1)}, f32[512,768]{1,0:T(8,128)}, f32[8,96,384]{2,1,0:T(8,128)}, f32[8,96,384]{2,1,0:T(8,1...) custom-call(f32[512,768]{1,0:T(8,128)} %copy-done.2, f32[512,768]{1,0:T(8,128)} %copy-done.28, ...), custom_call_target="tpu_custom_call" | custom-call | flops 3019898880 | bytes 19929088 | tf_op jit(solution)/shard_map/pallas_call | solution.py:410
  76.6 14.2 %collective-permute-done.24 = f32[8,192,256]{2,1,0:T(8,128)} collective-permute-done((f32[8,192,256]{2,1,0:T(8,128)}, f32[8,192,256]{2,1,0:T(8,128)}, u32[]{:S(2)}, u32[]{:S(2)}) %collective-permute-start.24) | collective-permute-done | bytes 1572896 | tf_op jit(solution)/shard_map/ppermute | solution.py:437
  90.8 1.7 slice_add_fusion.5
  92.5 2.1 collective-permute-start.25
  94.8 1.6 collective-permute-start.33
  96.6 2.7 collective-permute-start.41
  99.8 13.3 %collective-permute-done.25 = f32[4,192,256]{2,1,0:T(8,128)S(1)} collective-permute-done((f32[4,192,256]{2,1,0:T(8,128)S(1)}, f32[4,192,256]{2,1,0:T(8,128)S(1)}, u32[]{:S(2)}, u32[]{:S(2)}) %collective-permute-start.25) | collective-permute-done | bytes 786464 | tf_op jit(solution)/shard_map/ppermute | solution.py:437
  113.2 19.3 %collective-permute-done.33 = f32[4,192,256]{2,1,0:T(8,128)S(1)} collective-permute-done((f32[4,192,256]{2,1,0:T(8,128)S(1)}, f32[4,192,256]{2,1,0:T(8,128)S(1)}, u32[]{:S(2)}, u32[]{:S(2)}) %collective-permute-start.33) | collective-permute-done | bytes 786464 | tf_op jit(solution)/shard_map/ppermute | solution.py:437
  132.6 1.9 collective-permute-start.26
  135.1 1.7 collective-permute-done.16
  136.8 1.5 collective-permute-start.42
  138.4 6.2 %collective-permute-done.26 = f32[2,192,256]{2,1,0:T(8,128)S(1)} collective-permute-done((f32[2,192,256]{2,1,0:T(8,128)S(1)}, f32[2,192,256]{2,1,0:T(8,128)S(1)}, u32[]{:S(2)}, u32[]{:S(2)}) %collective-permute-start.26) | collective-permute-done | bytes 393248 | tf_op jit(solution)/shard_map/ppermute | solution.py:437
  144.6 1.8 collective-permute-start.9
  146.4 6.3 %collective-permute-done.34 = f32[2,192,256]{2,1,0:T(8,128)S(1)} collective-permute-done((f32[2,192,256]{2,1,0:T(8,128)S(1)}, f32[2,192,256]{2,1,0:T(8,128)S(1)}, u32[]{:S(2)}, u32[]{:S(2)}) %collective-permute-start.34) | collective-permute-done | bytes 393248 | tf_op jit(solution)/shard_map/ppermute | solution.py:437
  152.8 1.7 collective-permute-start.17
  154.5 2.7 collective-permute-start.27
  157.2 8.7 %collective-permute-done.27 = f32[1,192,256]{2,1,0:T(8,128)S(1)} collective-permute-done((f32[1,192,256]{2,1,0:T(8,128)S(1)}, f32[1,192,256]{2,1,0:T(8,128)S(1)}, u32[]{:S(2)}, u32[]{:S(2)}) %collective-permute-start.27) | collective-permute-done | bytes 196640 | tf_op jit(solution)/shard_map/ppermute | solution.py:437
  165.9 10.8 %collective-permute-done.35 = f32[1,192,256]{2,1,0:T(8,128)S(1)} collective-permute-done((f32[1,192,256]{2,1,0:T(8,128)S(1)}, f32[1,192,256]{2,1,0:T(8,128)S(1)}, u32[]{:S(2)}, u32[]{:S(2)}) %collective-permute-start.35) | collective-permute-done | bytes 196640 | tf_op jit(solution)/shard_map/ppermute | solution.py:437
  176.8 1.5 collective-permute-start.43
  178.3 4.1 %collective-permute-done.43 = f32[1,192,256]{2,1,0:T(8,128)S(1)} collective-permute-done((f32[1,192,256]{2,1,0:T(8,128)S(1)}, f32[1,192,256]{2,1,0:T(8,128)S(1)}, u32[]{:S(2)}, u32[]{:S(2)}) %collective-permute-start.43) | collective-permute-done | bytes 196640 | tf_op jit(solution)/shard_map/ppermute | solution.py:437
  182.5 3.0 collective-permute-start.36
  185.5 3.5 shard_map.251
  189.0 8.5 %collective-permute-done.28 = f32[1,192,256]{2,1,0:T(8,128)S(1)} collective-permute-done((f32[1,192,256]{2,1,0:T(8,128)S(1)}, f32[1,192,256]{2,1,0:T(8,128)S(1)}, u32[]{:S(2)}, u32[]{:S(2)}) %collective-permute-start.28) | collective-permute-done | bytes 196640 | tf_op jit(solution)/shard_map/ppermute | solution.py:437
  197.5 1.5 collective-permute-start.44
  200.0 3.2 collective-permute-done.44
  203.4 1.9 collective-permute-start.37
  206.0 9.2 %collective-permute-done.29 = f32[2,192,256]{2,1,0:T(8,128)S(1)} collective-permute-done((f32[2,192,256]{2,1,0:T(8,128)S(1)}, f32[2,192,256]{2,1,0:T(8,128)S(1)}, u32[]{:S(2)}, u32[]{:S(2)}) %collective-permute-start.29) | collective-permute-done | bytes 393248 | tf_op jit(solution)/shard_map/ppermute | solution.py:437
  215.3 11.9 %collective-permute-done.10 = f32[2,96,384]{2,1,0:T(8,128)S(1)} collective-permute-done((f32[2,96,384]{2,1,0:T(8,128)S(1)}, f32[2,96,384]{2,1,0:T(8,128)S(1)}, u32[]{:S(2)}, u32[]{:S(2)}) %collective-permute-start.10) | collective-permute-done | bytes 294944 | tf_op jit(solution)/shard_map/ppermute | solution.py:437
  227.2 1.5 collective-permute-start.5
  228.8 1.6 collective-permute-done.18
  230.4 3.4 collective-permute-start.11
  233.8 5.2 %collective-permute-done.11 = f32[1,96,384]{2,1,0:T(8,128)S(1)} collective-permute-done((f32[1,96,384]{2,1,0:T(8,128)S(1)}, f32[1,96,384]{2,1,0:T(8,128)S(1)}, u32[]{:S(2)}, u32[]{:S(2)}) %collective-permute-start.11) | collective-permute-done | bytes 147488 | tf_op jit(solution)/shard_map/ppermute | solution.py:437
  240.0 7.5 %collective-permute-done.19 = f32[1,96,384]{2,1,0:T(8,128)S(1)} collective-permute-done((f32[1,96,384]{2,1,0:T(8,128)S(1)}, f32[1,96,384]{2,1,0:T(8,128)S(1)}, u32[]{:S(2)}, u32[]{:S(2)}) %collective-permute-start.19) | collective-permute-done | bytes 147488 | tf_op jit(solution)/shard_map/ppermute | solution.py:437
  247.4 9.9 %collective-permute-done.12 = f32[1,96,384]{2,1,0:T(8,128)S(1)} collective-permute-done((f32[1,96,384]{2,1,0:T(8,128)S(1)}, f32[1,96,384]{2,1,0:T(8,128)S(1)}, u32[]{:S(2)}, u32[]{:S(2)}) %collective-permute-start.12) | collective-permute-done | bytes 147488 | tf_op jit(solution)/shard_map/ppermute | solution.py:437
  257.3 1.6 collective-permute-start.30
  259.0 2.2 collective-permute-start.13
  262.0 5.3 %collective-permute-done.20 = f32[1,96,384]{2,1,0:T(8,128)S(1)} collective-permute-done((f32[1,96,384]{2,1,0:T(8,128)S(1)}, f32[1,96,384]{2,1,0:T(8,128)S(1)}, u32[]{:S(2)}, u32[]{:S(2)}) %collective-permute-start.20) | collective-permute-done | bytes 147488 | tf_op jit(solution)/shard_map/ppermute | solution.py:437
  267.3 7.0 %collective-permute-done.13 = f32[2,96,384]{2,1,0:T(8,128)S(1)} collective-permute-done((f32[2,96,384]{2,1,0:T(8,128)S(1)}, f32[2,96,384]{2,1,0:T(8,128)S(1)}, u32[]{:S(2)}, u32[]{:S(2)}) %collective-permute-start.13) | collective-permute-done | bytes 294944 | tf_op jit(solution)/shard_map/ppermute | solution.py:437
  274.3 16.9 %collective-permute-done.21 = f32[2,96,384]{2,1,0:T(8,128)S(1)} collective-permute-done((f32[2,96,384]{2,1,0:T(8,128)S(1)}, f32[2,96,384]{2,1,0:T(8,128)S(1)}, u32[]{:S(2)}, u32[]{:S(2)}) %collective-permute-start.21) | collective-permute-done | bytes 294944 | tf_op jit(solution)/shard_map/ppermute | solution.py:437
  292.4 2.5 collective-permute-start.6
  295.1 4.8 %collective-permute-done.46 = f32[4,192,256]{2,1,0:T(8,128)S(1)} collective-permute-done((f32[4,192,256]{2,1,0:T(8,128)S(1)}, f32[4,192,256]{2,1,0:T(8,128)S(1)}, u32[]{:S(2)}, u32[]{:S(2)}) %collective-permute-start.46) | collective-permute-done | bytes 786464 | tf_op jit(solution)/shard_map/ppermute | solution.py:437
  301.2 6.3 %collective-permute-done.14 = f32[4,96,384]{2,1,0:T(8,128)S(1)} collective-permute-done((f32[4,96,384]{2,1,0:T(8,128)S(1)}, f32[4,96,384]{2,1,0:T(8,128)S(1)}, u32[]{:S(2)}, u32[]{:S(2)}) %collective-permute-start.14) | collective-permute-done | bytes 589856 | tf_op jit(solution)/shard_map/ppermute | solution.py:437
  307.5 2.5 collective-permute-start.47
  310.1 1.4 collective-permute-start.7
  312.2 28.4 %collective-permute-done.7 = f32[1,3840]{1,0:T(1,128)S(1)} collective-permute-done((f32[1,3840]{1,0:T(1,128)S(1)}, f32[1,3840]{1,0:T(1,128)S(1)}, u32[]{:S(2)}, u32[]{:S(2)}) %collective-permute-start.7) | collective-permute-done | bytes 15392 | tf_op jit(solution)/shard_map/ppermute | solution.py:437
  341.1 2.7 add_convert_fusion
  345.1 1.1 copy-done.23
  346.3 1.2 copy-done.24
  347.4 6.7 %shard_map.253 = (f32[1536,768]{1,0:T(8,128)}, f32[768,1536]{1,0:T(8,128)}) custom-call(f32[8,192,256]{2,1,0:T(8,128)S(1)} %pad_maximum_fusion.refs_0_, f32[8,192,256]{2,1,0:T(8,128)S(1)} %collective-permute-done.31.refs_1_, f32[8,192,256]{2,1,0:T(8,128)S(1)} %pad_maximum_fusion.1.refs_2_, f32[8,192,256]{2,1,0:T(8,128)} %copy-done.23, ...), custom_call_target="tpu_custom_call" | custom-call | bytes 18874368 | tf_op jit(solution)/shard_map/pallas_call | solution.py:410
  354.1 10.9 %collective-permute-done.15.refs_1_ = f32[8,96,384]{2,1,0:T(8,128)S(1)} collective-permute-done((f32[8,96,384]{2,1,0:T(8,128)S(1)}, f32[8,96,384]{2,1,0:T(8,128)S(1)}, u32[]{:S(2)}, u32[]{:S(2)}) %collective-permute-start.15) | collective-permute-done | bytes 1179680 | tf_op jit(solution)/shard_map/ppermute | solution.py:437
  365.0 2.5 shard_map.252
  (165 shorter events, 19.6 us)
Async XLA Ops:
  9.9 11.2 %copy-start.34 = (f32[768]{0:T(1024)S(1)}, f32[768]{0:T(1024)}, u32[]{:S(2)}) copy-start(f32[768]{0:T(1024)} %param.22) | copy-start | bytes 9220
  10.0 11.8 %copy-start.31 = (f32[1536]{0:T(1024)S(1)}, f32[1536]{0:T(1024)}, u32[]{:S(2)}) copy-start(f32[1536]{0:T(1024)} %param.24) | copy-start | bytes 18436
  20.7 3.7 %collective-permute-start = (f32[512,768]{1,0:T(8,128)}, f32[512,768]{1,0:T(8,128)S(1)}, u32[]{:S(2)}, u32[]{:S(2)}) collective-permute-start(f32[512,768]{1,0:T(8,128)} %get-tuple-element.47.mine_ref), channel_id=1, source_target_pairs={{0,1},{1,0},{2,3},{3,2},{4,5},{5,4},{6,7},{7,6},{8,9},{9,8},{10,11... | collective-permute-start | bytes 4718600 | tf_op jit(solution)/shard_map/ppermute | solution.py:434
  46.5 13.1 %copy-start.5 = (bf16[512,768]{1,0:T(8,128)(2,1)S(1)}, bf16[512,768]{1,0:T(8,128)(2,1)}, u32[]{:S(2)}) copy-start(bf16[512,768]{1,0:T(8,128)(2,1)} %cot_ref.3) | copy-start | bytes 2359300
  46.5 13.1 %copy-start.7 = (bf16[768,384]{1,0:T(8,128)(2,1)S(1)}, bf16[768,384]{1,0:T(8,128)(2,1)}, u32[]{:S(2)}) copy-start(bf16[768,384]{1,0:T(8,128)(2,1)} %wq_ref.3) | copy-start | bytes 1769476
  46.5 13.1 %copy-start.9 = (bf16[768,384]{1,0:T(8,128)(2,1)S(1)}, bf16[768,384]{1,0:T(8,128)(2,1)}, u32[]{:S(2)}) copy-start(bf16[768,384]{1,0:T(8,128)(2,1)} %wk_ref.3) | copy-start | bytes 1769476
  46.5 13.1 %copy-start.11 = (bf16[768,384]{1,0:T(8,128)(2,1)S(1)}, bf16[768,384]{1,0:T(8,128)(2,1)}, u32[]{:S(2)}) copy-start(bf16[768,384]{1,0:T(8,128)(2,1)} %wv_ref.3) | copy-start | bytes 1769476
  46.5 13.1 %copy-start.13 = (bf16[384,768]{1,0:T(8,128)(2,1)S(1)}, bf16[384,768]{1,0:T(8,128)(2,1)}, u32[]{:S(2)}) copy-start(bf16[384,768]{1,0:T(8,128)(2,1)} %wo_ref.3) | copy-start | bytes 1769476
  46.5 13.1 %copy-start.15 = (f32[256,128]{1,0:T(8,128)S(1)}, f32[256,128]{1,0:T(8,128)}, u32[]{:S(2)}) copy-start(f32[256,128]{1,0:T(8,128)} %constant.5.clone.sin_ref) | copy-start | bytes 393220
  46.5 13.1 %copy-start.17 = (f32[256,128]{1,0:T(8,128)S(1)}, f32[256,128]{1,0:T(8,128)}, u32[]{:S(2)}) copy-start(f32[256,128]{1,0:T(8,128)} %constant.4.clone.cos_ref) | copy-start | bytes 393220
  46.5 13.1 %copy-start.18 = (f32[1,768]{1,0:T(1,128)S(1)}, f32[1,768]{1,0:T(1,128)}, u32[]{:S(2)}) copy-start(f32[1,768]{1,0:T(1,128)} %reshape.39.gain_ref) | copy-start | bytes 9220
  52.2 6.2 %collective-permute-start.2 = (f32[512,768]{1,0:T(8,128)S(1)}, f32[512,768]{1,0:T(8,128)S(1)}, u32[]{:S(2)}, u32[]{:S(2)}) collective-permute-start(f32[512,768]{1,0:T(8,128)S(1)} %get-tuple-element.52.mine_ref), channel_id=1, source_target_pairs={{0,1},{1,0},{2,3},{3,2},{4,5},{5,4},{6,7},{7,6},{8,9},{9,8},{10,11... | collective-permute-start | bytes 4718600 | tf_op jit(solution)/shard_map/ppermute | solution.py:434
  52.6 38.2 %collective-permute-start.24 = (f32[8,192,256]{2,1,0:T(8,128)}, f32[8,192,256]{2,1,0:T(8,128)}, u32[]{:S(2)}, u32[]{:S(2)}) collective-permute-start(f32[8,192,256]{2,1,0:T(8,128)} %get-tuple-element.75), channel_id=1, source_target_pairs={{0,2},{2,0},{4,6},{6,4},{8,10},{10,8},{12,14},{14,12},{16,18},{18,... | collective-permute-start | bytes 4718600 | tf_op jit(solution)/shard_map/ppermute | solution.py:437
  55.3 39.3 %collective-permute-start.32 = (f32[8,192,256]{2,1,0:T(8,128)}, f32[8,192,256]{2,1,0:T(8,128)S(1)}, u32[]{:S(2)}, u32[]{:S(2)}) collective-permute-start(f32[8,192,256]{2,1,0:T(8,128)} %get-tuple-element.77), channel_id=1, source_target_pairs={{0,4},{2,6},{4,0},{6,2},{8,12},{10,14},{12,8},{14,10},{16,20},{18,... | collective-permute-start | bytes 4718600 | tf_op jit(solution)/shard_map/ppermute | solution.py:437
  56.8 39.6 %collective-permute-start.40 = (f32[8,192,256]{2,1,0:T(8,128)}, f32[8,192,256]{2,1,0:T(8,128)S(1)}, u32[]{:S(2)}, u32[]{:S(2)}) collective-permute-start(f32[8,192,256]{2,1,0:T(8,128)} %get-tuple-element.79), channel_id=1, source_target_pairs={{0,8},{2,10},{4,12},{6,14},{8,0},{10,2},{12,4},{14,6},{16,24},{18,... | collective-permute-start | bytes 4718600 | tf_op jit(solution)/shard_map/ppermute | solution.py:437
  59.6 31.2 %copy-start.27 = (f32[8,192,256]{2,1,0:T(8,128)S(1)}, f32[8,192,256]{2,1,0:T(8,128)}, u32[]{:S(2)}) copy-start(f32[8,192,256]{2,1,0:T(8,128)} %get-tuple-element.74) | copy-start | bytes 4718596
  76.1 58.6 %collective-permute-start.8 = (f32[8,96,384]{2,1,0:T(8,128)}, f32[8,96,384]{2,1,0:T(8,128)S(1)}, u32[]{:S(2)}, u32[]{:S(2)}) collective-permute-start(f32[8,96,384]{2,1,0:T(8,128)} %get-tuple-element.67), channel_id=1, source_target_pairs={{0,2},{2,0},{4,6},{6,4},{8,10},{10,8},{12,14},{14,12},{16,18},{18,... | collective-permute-start | bytes 3538952 | tf_op jit(solution)/shard_map/ppermute | solution.py:437
  92.5 20.5 %collective-permute-start.25 = (f32[4,192,256]{2,1,0:T(8,128)S(1)}, f32[4,192,256]{2,1,0:T(8,128)S(1)}, u32[]{:S(2)}, u32[]{:S(2)}) collective-permute-start(f32[4,192,256]{2,1,0:T(8,128)S(1)} %get-tuple-element.90), channel_id=1, source_target_pairs={{0,4},{2,6},{4,0},{6,2},{8,12},{10,14},{12,8},{14,10},{16,20},{18,... | collective-permute-start | bytes 2359304 | tf_op jit(solution)/shard_map/ppermute | solution.py:437
  94.8 37.7 %collective-permute-start.33 = (f32[4,192,256]{2,1,0:T(8,128)S(1)}, f32[4,192,256]{2,1,0:T(8,128)S(1)}, u32[]{:S(2)}, u32[]{:S(2)}) collective-permute-start(f32[4,192,256]{2,1,0:T(8,128)S(1)} %get-tuple-element.88), channel_id=1, source_target_pairs={{0,2},{2,0},{4,6},{6,4},{8,10},{10,8},{12,14},{14,12},{16,18},{18,... | collective-permute-start | bytes 2359304 | tf_op jit(solution)/shard_map/ppermute | solution.py:437
  96.6 35.9 %copy-start.1 = (f32[512,768]{1,0:T(8,128)S(1)}, f32[512,768]{1,0:T(8,128)}, u32[]{:S(2)}) copy-start(f32[512,768]{1,0:T(8,128)} %get-tuple-element.59.mine_ref) | copy-start | bytes 4718596
  96.6 36.0 %collective-permute-start.41 = (f32[4,192,256]{2,1,0:T(8,128)S(1)}, f32[4,192,256]{2,1,0:T(8,128)S(1)}, u32[]{:S(2)}, u32[]{:S(2)}) collective-permute-start(f32[4,192,256]{2,1,0:T(8,128)S(1)} %get-tuple-element.86), channel_id=1, source_target_pairs={{0,16},{2,18},{4,20},{6,22},{8,24},{10,26},{12,28},{14,30},{16,0},... | collective-permute-start | bytes 2359304 | tf_op jit(solution)/shard_map/ppermute | solution.py:437
  99.3 37.5 %collective-permute-start.16 = (f32[8,96,384]{2,1,0:T(8,128)S(1)}, f32[8,96,384]{2,1,0:T(8,128)S(1)}, u32[]{:S(2)}, u32[]{:S(2)}) collective-permute-start(f32[8,96,384]{2,1,0:T(8,128)S(1)} %copy-done.37), channel_id=1, source_target_pairs={{0,4},{2,6},{4,0},{6,2},{8,12},{10,14},{12,8},{14,10},{16,20},{18,... | collective-permute-start | bytes 3538952 | tf_op jit(solution)/shard_map/ppermute | solution.py:437
  113.0 198.6 %collective-permute-start.1 = (f32[512,768]{1,0:T(8,128)S(1)}, f32[512,768]{1,0:T(8,128)}, u32[]{:S(2)}, u32[]{:S(2)}) collective-permute-start(f32[512,768]{1,0:T(8,128)S(1)} %get-tuple-element.51), channel_id=1, source_target_pairs={{0,1},{1,0},{2,3},{3,2},{4,5},{5,4},{6,7},{7,6},{8,9},{9,8},{10,11... | collective-permute-start | bytes 4718600 | tf_op jit(solution)/shard_map/ppermute | solution.py:434
  132.5 50.0 %collective-permute-start.3 = (f32[512,768]{1,0:T(8,128)S(1)}, f32[512,768]{1,0:T(8,128)S(1)}, u32[]{:S(2)}, u32[]{:S(2)}) collective-permute-start(f32[512,768]{1,0:T(8,128)S(1)} %copy-done.1), channel_id=1, source_target_pairs={{0,1},{1,0},{2,3},{3,2},{4,5},{5,4},{6,7},{7,6},{8,9},{9,8},{10,11... | collective-permute-start | bytes 4718600 | tf_op jit(solution)/shard_map/ppermute | solution.py:434
  132.6 12.0 %collective-permute-start.26 = (f32[2,192,256]{2,1,0:T(8,128)S(1)}, f32[2,192,256]{2,1,0:T(8,128)S(1)}, u32[]{:S(2)}, u32[]{:S(2)}) collective-permute-start(f32[2,192,256]{2,1,0:T(8,128)S(1)} %get-tuple-element.100), channel_id=1, source_target_pairs={{0,8},{2,10},{4,12},{6,14},{8,0},{10,2},{12,4},{14,6},{16,24},{18,... | collective-permute-start | bytes 1179656 | tf_op jit(solution)/shard_map/ppermute | solution.py:437
  134.7 18.1 %collective-permute-start.34 = (f32[2,192,256]{2,1,0:T(8,128)S(1)}, f32[2,192,256]{2,1,0:T(8,128)S(1)}, u32[]{:S(2)}, u32[]{:S(2)}) collective-permute-start(f32[2,192,256]{2,1,0:T(8,128)S(1)} %get-tuple-element.98), channel_id=1, source_target_pairs={{0,8},{2,10},{4,12},{6,14},{8,0},{10,2},{12,4},{14,6},{16,24},{18,... | collective-permute-start | bytes 1179656 | tf_op jit(solution)/shard_map/ppermute | solution.py:437
  136.8 17.7 %collective-permute-start.42 = (f32[2,192,256]{2,1,0:T(8,128)S(1)}, f32[2,192,256]{2,1,0:T(8,128)S(1)}, u32[]{:S(2)}, u32[]{:S(2)}) collective-permute-start(f32[2,192,256]{2,1,0:T(8,128)S(1)} %get-tuple-element.96), channel_id=1, source_target_pairs={{0,2},{2,0},{4,6},{6,4},{8,10},{10,8},{12,14},{14,12},{16,18},{18,... | collective-permute-start | bytes 1179656 | tf_op jit(solution)/shard_map/ppermute | solution.py:437
  144.6 60.7 %collective-permute-start.9 = (f32[4,96,384]{2,1,0:T(8,128)S(1)}, f32[4,96,384]{2,1,0:T(8,128)S(1)}, u32[]{:S(2)}, u32[]{:S(2)}) collective-permute-start(f32[4,96,384]{2,1,0:T(8,128)S(1)} %get-tuple-element.94), channel_id=1, source_target_pairs={{0,4},{2,6},{4,0},{6,2},{8,12},{10,14},{12,8},{14,10},{16,20},{18,... | collective-permute-start | bytes 1769480 | tf_op jit(solution)/shard_map/ppermute | solution.py:437
  152.8 53.0 %collective-permute-start.17 = (f32[4,96,384]{2,1,0:T(8,128)S(1)}, f32[4,96,384]{2,1,0:T(8,128)S(1)}, u32[]{:S(2)}, u32[]{:S(2)}) collective-permute-start(f32[4,96,384]{2,1,0:T(8,128)S(1)} %get-tuple-element.92), channel_id=1, source_target_pairs={{0,2},{2,0},{4,6},{6,4},{8,10},{10,8},{12,14},{14,12},{16,18},{18,... | collective-permute-start | bytes 1769480 | tf_op jit(solution)/shard_map/ppermute | solution.py:437
  154.4 31.0 %copy-start = (f32[512,768]{1,0:T(8,128)S(1)}, f32[512,768]{1,0:T(8,128)}, u32[]{:S(2)}) copy-start(f32[512,768]{1,0:T(8,128)} %get-tuple-element.60.delta_ref) | copy-start | bytes 4718596
  154.4 31.0 %copy-start.4 = (bf16[512,768]{1,0:T(8,128)(2,1)S(1)}, bf16[512,768]{1,0:T(8,128)(2,1)}, u32[]{:S(2)}) copy-start(bf16[512,768]{1,0:T(8,128)(2,1)} %x_ref.5) | copy-start | bytes 2359300
  154.5 11.4 %collective-permute-start.27 = (f32[1,192,256]{2,1,0:T(8,128)S(1)}, f32[1,192,256]{2,1,0:T(8,128)S(1)}, u32[]{:S(2)}, u32[]{:S(2)}) collective-permute-start(f32[1,192,256]{2,1,0:T(8,128)S(1)} %slice_add_fusion.24), channel_id=1, source_target_pairs={{0,16},{2,18},{4,20},{6,22},{8,24},{10,26},{12,28},{14,30},{16,0},... | collective-permute-start | bytes 589832 | tf_op jit(solution)/shard_map/ppermute | solution.py:437
  165.9 10.9 %collective-permute-start.35 = (f32[1,192,256]{2,1,0:T(8,128)S(1)}, f32[1,192,256]{2,1,0:T(8,128)S(1)}, u32[]{:S(2)}, u32[]{:S(2)}) collective-permute-start(f32[1,192,256]{2,1,0:T(8,128)S(1)} %slice_add_fusion.22), channel_id=1, source_target_pairs={{0,16},{2,18},{4,20},{6,22},{8,24},{10,26},{12,28},{14,30},{16,0},... | collective-permute-start | bytes 589832 | tf_op jit(solution)/shard_map/ppermute | solution.py:437
  176.8 5.7 %collective-permute-start.43 = (f32[1,192,256]{2,1,0:T(8,128)S(1)}, f32[1,192,256]{2,1,0:T(8,128)S(1)}, u32[]{:S(2)}, u32[]{:S(2)}) collective-permute-start(f32[1,192,256]{2,1,0:T(8,128)S(1)} %slice_add_fusion.20), channel_id=1, source_target_pairs={{0,4},{2,6},{4,0},{6,2},{8,12},{10,14},{12,8},{14,10},{16,20},{18,... | collective-permute-start | bytes 589832 | tf_op jit(solution)/shard_map/ppermute | solution.py:437
  182.4 15.1 %collective-permute-start.28 = (f32[1,192,256]{2,1,0:T(8,128)S(1)}, f32[1,192,256]{2,1,0:T(8,128)S(1)}, u32[]{:S(2)}, u32[]{:S(2)}) collective-permute-start(f32[1,192,256]{2,1,0:T(8,128)S(1)} %fusion.2), channel_id=1, source_target_pairs={{0,16},{2,18},{4,20},{6,22},{8,24},{10,26},{12,28},{14,30},{16,0},... | collective-permute-start | bytes 589832 | tf_op jit(solution)/shard_map/ppermute | solution.py:437
  182.5 17.2 %collective-permute-start.36 = (f32[1,192,256]{2,1,0:T(8,128)S(1)}, f32[1,192,256]{2,1,0:T(8,128)S(1)}, u32[]{:S(2)}, u32[]{:S(2)}) collective-permute-start(f32[1,192,256]{2,1,0:T(8,128)S(1)} %fusion.1), channel_id=1, source_target_pairs={{0,16},{2,18},{4,20},{6,22},{8,24},{10,26},{12,28},{14,30},{16,0},... | collective-permute-start | bytes 589832 | tf_op jit(solution)/shard_map/ppermute | solution.py:437
  197.5 5.7 %collective-permute-start.44 = (f32[1,192,256]{2,1,0:T(8,128)S(1)}, f32[1,192,256]{2,1,0:T(8,128)S(1)}, u32[]{:S(2)}, u32[]{:S(2)}) collective-permute-start(f32[1,192,256]{2,1,0:T(8,128)S(1)} %fusion), channel_id=1, source_target_pairs={{0,4},{2,6},{4,0},{6,2},{8,12},{10,14},{12,8},{14,10},{16,20},{18,... | collective-permute-start | bytes 589832 | tf_op jit(solution)/shard_map/ppermute | solution.py:437
  199.6 3.7 %collective-permute-start.4 = (f32[1,3840]{1,0:T(1,128)S(1)}, f32[1,3840]{1,0:T(1,128)S(1)}, u32[]{:S(2)}, u32[]{:S(2)}) collective-permute-start(f32[1,3840]{1,0:T(1,128)S(1)} %constant_dynamic-update-slice_fusion), channel_id=1, source_target_pairs={{0,2},{2,0},{4,6},{6,4},{8,10},{10,8},{12,14},{14,12},{16,18},{18,... | collective-permute-start | bytes 46088 | tf_op jit(solution)/shard_map/ppermute | solution.py:437
  203.2 12.1 %collective-permute-start.29 = (f32[2,192,256]{2,1,0:T(8,128)S(1)}, f32[2,192,256]{2,1,0:T(8,128)S(1)}, u32[]{:S(2)}, u32[]{:S(2)}) collective-permute-start(f32[2,192,256]{2,1,0:T(8,128)S(1)} %pad_maximum_fusion.10), channel_id=1, source_target_pairs={{0,8},{2,10},{4,12},{6,14},{8,0},{10,2},{12,4},{14,6},{16,24},{18,... | collective-permute-start | bytes 1179656 | tf_op jit(solution)/shard_map/ppermute | solution.py:437
  203.4 55.7 %collective-permute-start.37 = (f32[2,192,256]{2,1,0:T(8,128)S(1)}, f32[2,192,256]{2,1,0:T(8,128)S(1)}, u32[]{:S(2)}, u32[]{:S(2)}) collective-permute-start(f32[2,192,256]{2,1,0:T(8,128)S(1)} %pad_maximum_fusion.11), channel_id=1, source_target_pairs={{0,8},{2,10},{4,12},{6,14},{8,0},{10,2},{12,4},{14,6},{16,24},{18,... | collective-permute-start | bytes 1179656 | tf_op jit(solution)/shard_map/ppermute | solution.py:437
  205.3 56.0 %collective-permute-start.45 = (f32[2,192,256]{2,1,0:T(8,128)S(1)}, f32[2,192,256]{2,1,0:T(8,128)S(1)}, u32[]{:S(2)}, u32[]{:S(2)}) collective-permute-start(f32[2,192,256]{2,1,0:T(8,128)S(1)} %pad_maximum_fusion.12), channel_id=1, source_target_pairs={{0,2},{2,0},{4,6},{6,4},{8,10},{10,8},{12,14},{14,12},{16,18},{18,... | collective-permute-start | bytes 1179656 | tf_op jit(solution)/shard_map/ppermute | solution.py:437
  205.7 21.5 %collective-permute-start.10 = (f32[2,96,384]{2,1,0:T(8,128)S(1)}, f32[2,96,384]{2,1,0:T(8,128)S(1)}, u32[]{:S(2)}, u32[]{:S(2)}) collective-permute-start(f32[2,96,384]{2,1,0:T(8,128)S(1)} %get-tuple-element.104), channel_id=1, source_target_pairs={{0,8},{2,10},{4,12},{6,14},{8,0},{10,2},{12,4},{14,6},{16,24},{18,... | collective-permute-start | bytes 884744 | tf_op jit(solution)/shard_map/ppermute | solution.py:437
  215.2 15.2 %collective-permute-start.18 = (f32[2,96,384]{2,1,0:T(8,128)S(1)}, f32[2,96,384]{2,1,0:T(8,128)S(1)}, u32[]{:S(2)}, u32[]{:S(2)}) collective-permute-start(f32[2,96,384]{2,1,0:T(8,128)S(1)} %get-tuple-element.102), channel_id=1, source_target_pairs={{0,8},{2,10},{4,12},{6,14},{8,0},{10,2},{12,4},{14,6},{16,24},{18,... | collective-permute-start | bytes 884744 | tf_op jit(solution)/shard_map/ppermute | solution.py:437
  227.2 31.7 %collective-permute-start.5 = (f32[1,3840]{1,0:T(1,128)S(1)}, f32[1,3840]{1,0:T(1,128)S(1)}, u32[]{:S(2)}, u32[]{:S(2)}) collective-permute-start(f32[1,3840]{1,0:T(1,128)S(1)} %add.135), channel_id=1, source_target_pairs={{0,4},{2,6},{4,0},{6,2},{8,12},{10,14},{12,8},{14,10},{16,20},{18,... | collective-permute-start | bytes 46088 | tf_op jit(solution)/shard_map/ppermute | solution.py:437
  230.4 8.6 %collective-permute-start.11 = (f32[1,96,384]{2,1,0:T(8,128)S(1)}, f32[1,96,384]{2,1,0:T(8,128)S(1)}, u32[]{:S(2)}, u32[]{:S(2)}) collective-permute-start(f32[1,96,384]{2,1,0:T(8,128)S(1)} %slice_add_fusion.28), channel_id=1, source_target_pairs={{0,16},{2,18},{4,20},{6,22},{8,24},{10,26},{12,28},{14,30},{16,0},... | collective-permute-start | bytes 442376 | tf_op jit(solution)/shard_map/ppermute | solution.py:437
  239.0 8.4 %collective-permute-start.19 = (f32[1,96,384]{2,1,0:T(8,128)S(1)}, f32[1,96,384]{2,1,0:T(8,128)S(1)}, u32[]{:S(2)}, u32[]{:S(2)}) collective-permute-start(f32[1,96,384]{2,1,0:T(8,128)S(1)} %slice_add_fusion.26), channel_id=1, source_target_pairs={{0,16},{2,18},{4,20},{6,22},{8,24},{10,26},{12,28},{14,30},{16,0},... | collective-permute-start | bytes 442376 | tf_op jit(solution)/shard_map/ppermute | solution.py:437
  247.4 9.9 %collective-permute-start.12 = (f32[1,96,384]{2,1,0:T(8,128)S(1)}, f32[1,96,384]{2,1,0:T(8,128)S(1)}, u32[]{:S(2)}, u32[]{:S(2)}) collective-permute-start(f32[1,96,384]{2,1,0:T(8,128)S(1)} %fusion.4), channel_id=1, source_target_pairs={{0,16},{2,18},{4,20},{6,22},{8,24},{10,26},{12,28},{14,30},{16,0},... | collective-permute-start | bytes 442376 | tf_op jit(solution)/shard_map/ppermute | solution.py:437
  257.3 34.4 %collective-permute-start.30 = (f32[4,192,256]{2,1,0:T(8,128)S(1)}, f32[4,192,256]{2,1,0:T(8,128)S(1)}, u32[]{:S(2)}, u32[]{:S(2)}) collective-permute-start(f32[4,192,256]{2,1,0:T(8,128)S(1)} %pad_maximum_fusion.5), channel_id=1, source_target_pairs={{0,4},{2,6},{4,0},{6,2},{8,12},{10,14},{12,8},{14,10},{16,20},{18,... | collective-permute-start | bytes 2359304 | tf_op jit(solution)/shard_map/ppermute | solution.py:437
  258.9 8.3 %collective-permute-start.20 = (f32[1,96,384]{2,1,0:T(8,128)S(1)}, f32[1,96,384]{2,1,0:T(8,128)S(1)}, u32[]{:S(2)}, u32[]{:S(2)}) collective-permute-start(f32[1,96,384]{2,1,0:T(8,128)S(1)} %fusion.3), channel_id=1, source_target_pairs={{0,16},{2,18},{4,20},{6,22},{8,24},{10,26},{12,28},{14,30},{16,0},... | collective-permute-start | bytes 442376 | tf_op jit(solution)/shard_map/ppermute | solution.py:437
  259.0 15.2 %collective-permute-start.13 = (f32[2,96,384]{2,1,0:T(8,128)S(1)}, f32[2,96,384]{2,1,0:T(8,128)S(1)}, u32[]{:S(2)}, u32[]{:S(2)}) collective-permute-start(f32[2,96,384]{2,1,0:T(8,128)S(1)} %pad_maximum_fusion.13), channel_id=1, source_target_pairs={{0,8},{2,10},{4,12},{6,14},{8,0},{10,2},{12,4},{14,6},{16,24},{18,... | collective-permute-start | bytes 884744 | tf_op jit(solution)/shard_map/ppermute | solution.py:437
  261.3 31.0 %collective-permute-start.38 = (f32[4,192,256]{2,1,0:T(8,128)S(1)}, f32[4,192,256]{2,1,0:T(8,128)S(1)}, u32[]{:S(2)}, u32[]{:S(2)}) collective-permute-start(f32[4,192,256]{2,1,0:T(8,128)S(1)} %pad_maximum_fusion.6), channel_id=1, source_target_pairs={{0,2},{2,0},{4,6},{6,4},{8,10},{10,8},{12,14},{14,12},{16,18},{18,... | collective-permute-start | bytes 2359304 | tf_op jit(solution)/shard_map/ppermute | solution.py:437
  267.3 32.6 %collective-permute-start.46 = (f32[4,192,256]{2,1,0:T(8,128)S(1)}, f32[4,192,256]{2,1,0:T(8,128)S(1)}, u32[]{:S(2)}, u32[]{:S(2)}) collective-permute-start(f32[4,192,256]{2,1,0:T(8,128)S(1)} %pad_maximum_fusion.7), channel_id=1, source_target_pairs={{0,16},{2,18},{4,20},{6,22},{8,24},{10,26},{12,28},{14,30},{16,0},... | collective-permute-start | bytes 2359304 | tf_op jit(solution)/shard_map/ppermute | solution.py:437
  274.3 16.9 %collective-permute-start.21 = (f32[2,96,384]{2,1,0:T(8,128)S(1)}, f32[2,96,384]{2,1,0:T(8,128)S(1)}, u32[]{:S(2)}, u32[]{:S(2)}) collective-permute-start(f32[2,96,384]{2,1,0:T(8,128)S(1)} %pad_maximum_fusion.14), channel_id=1, source_target_pairs={{0,8},{2,10},{4,12},{6,14},{8,0},{10,2},{12,4},{14,6},{16,24},{18,... | collective-permute-start | bytes 884744 | tf_op jit(solution)/shard_map/ppermute | solution.py:437
  291.2 16.3 %collective-permute-start.14 = (f32[4,96,384]{2,1,0:T(8,128)S(1)}, f32[4,96,384]{2,1,0:T(8,128)S(1)}, u32[]{:S(2)}, u32[]{:S(2)}) collective-permute-start(f32[4,96,384]{2,1,0:T(8,128)S(1)} %pad_maximum_fusion.8), channel_id=1, source_target_pairs={{0,4},{2,6},{4,0},{6,2},{8,12},{10,14},{12,8},{14,10},{16,20},{18,... | collective-permute-start | bytes 1769480 | tf_op jit(solution)/shard_map/ppermute | solution.py:437
  291.7 18.4 %collective-permute-start.22 = (f32[4,96,384]{2,1,0:T(8,128)S(1)}, f32[4,96,384]{2,1,0:T(8,128)S(1)}, u32[]{:S(2)}, u32[]{:S(2)}) collective-permute-start(f32[4,96,384]{2,1,0:T(8,128)S(1)} %pad_maximum_fusion.9), channel_id=1, source_target_pairs={{0,2},{2,0},{4,6},{6,4},{8,10},{10,8},{12,14},{14,12},{16,18},{18,... | collective-permute-start | bytes 1769480 | tf_op jit(solution)/shard_map/ppermute | solution.py:437
  292.4 8.2 %collective-permute-start.6 = (f32[1,3840]{1,0:T(1,128)S(1)}, f32[1,3840]{1,0:T(1,128)S(1)}, u32[]{:S(2)}, u32[]{:S(2)}) collective-permute-start(f32[1,3840]{1,0:T(1,128)S(1)} %add.136), channel_id=1, source_target_pairs={{0,8},{2,10},{4,12},{6,14},{8,0},{10,2},{12,4},{14,6},{16,24},{18,... | collective-permute-start | bytes 46088 | tf_op jit(solution)/shard_map/ppermute | solution.py:437
  299.9 45.2 %collective-permute-start.31 = (f32[8,192,256]{2,1,0:T(8,128)S(1)}, f32[8,192,256]{2,1,0:T(8,128)S(1)}, u32[]{:S(2)}, u32[]{:S(2)}) collective-permute-start(f32[8,192,256]{2,1,0:T(8,128)S(1)} %pad_maximum_fusion.refs_0_), channel_id=1, source_target_pairs={{0,2},{2,0},{4,6},{6,4},{8,10},{10,8},{12,14},{14,12},{16,18},{18,... | collective-permute-start | bytes 4718600 | tf_op jit(solution)/shard_map/ppermute | solution.py:437
  300.6 44.6 %collective-permute-start.39 = (f32[8,192,256]{2,1,0:T(8,128)S(1)}, f32[8,192,256]{2,1,0:T(8,128)S(1)}, u32[]{:S(2)}, u32[]{:S(2)}) collective-permute-start(f32[8,192,256]{2,1,0:T(8,128)S(1)} %pad_maximum_fusion.1.refs_2_), channel_id=1, source_target_pairs={{0,4},{2,6},{4,0},{6,2},{8,12},{10,14},{12,8},{14,10},{16,20},{18,... | collective-permute-start | bytes 4718600 | tf_op jit(solution)/shard_map/ppermute | solution.py:437
  307.5 37.6 %collective-permute-start.47 = (f32[8,192,256]{2,1,0:T(8,128)S(1)}, f32[8,192,256]{2,1,0:T(8,128)S(1)}, u32[]{:S(2)}, u32[]{:S(2)}) collective-permute-start(f32[8,192,256]{2,1,0:T(8,128)S(1)} %pad_maximum_fusion.2.refs_4_), channel_id=1, source_target_pairs={{0,8},{2,10},{4,12},{6,14},{8,0},{10,2},{12,4},{14,6},{16,24},{18,... | collective-permute-start | bytes 4718600 | tf_op jit(solution)/shard_map/ppermute | solution.py:437
  310.1 31.0 %copy-start.22 = (f32[512,768]{1,0:T(8,128)S(1)}, f32[512,768]{1,0:T(8,128)}, u32[]{:S(2)}) copy-start(f32[512,768]{1,0:T(8,128)} %get-tuple-element.48.residual_ref) | copy-start | bytes 4718596
  310.1 31.0 %copy-start.33 = (f32[768]{0:T(1024)S(1)}, f32[768]{0:T(1024)}, u32[]{:S(2)}) copy-start(f32[768]{0:T(1024)} %param.26) | copy-start | bytes 9220
  310.1 30.5 %collective-permute-start.7 = (f32[1,3840]{1,0:T(1,128)S(1)}, f32[1,3840]{1,0:T(1,128)S(1)}, u32[]{:S(2)}, u32[]{:S(2)}) collective-permute-start(f32[1,3840]{1,0:T(1,128)S(1)} %add.137), channel_id=1, source_target_pairs={{0,16},{2,18},{4,20},{6,22},{8,24},{10,26},{12,28},{14,30},{16,0},... | collective-permute-start | bytes 46088 | tf_op jit(solution)/shard_map/ppermute | solution.py:437
  311.6 53.4 %collective-permute-start.15 = (f32[8,96,384]{2,1,0:T(8,128)S(1)}, f32[8,96,384]{2,1,0:T(8,128)S(1)}, u32[]{:S(2)}, u32[]{:S(2)}) collective-permute-start(f32[8,96,384]{2,1,0:T(8,128)S(1)} %pad_maximum_fusion.3.refs_0_), channel_id=1, source_target_pairs={{0,2},{2,0},{4,6},{6,4},{8,10},{10,8},{12,14},{14,12},{16,18},{18,... | collective-permute-start | bytes 3538952 | tf_op jit(solution)/shard_map/ppermute | solution.py:437
  340.6 24.4 %collective-permute-start.23 = (f32[8,96,384]{2,1,0:T(8,128)S(1)}, f32[8,96,384]{2,1,0:T(8,128)S(1)}, u32[]{:S(2)}, u32[]{:S(2)}) collective-permute-start(f32[8,96,384]{2,1,0:T(8,128)S(1)} %pad_maximum_fusion.4.refs_2_), channel_id=1, source_target_pairs={{0,4},{2,6},{4,0},{6,2},{8,12},{10,14},{12,8},{14,10},{16,20},{18,... | collective-permute-start | bytes 3538952 | tf_op jit(solution)/shard_map/ppermute | solution.py:437
  (22 other events, 53.5 us)

commit v2 on v1

v2 whole, which is shorter than its diff:
```python
from functools import partial
import math

import numpy as np

import jax
import jax.numpy as jnp
from jax import lax
from jax.experimental import pallas as pl
from jax.experimental.pallas import tpu as pltpu
from jax.sharding import PartitionSpec as P

HEAD = 64
BLOCK = 16
LEN = 256
HALF = 128
LANES = 128
PLANE = 4
STACK = 4
GROUP = PLANE * STACK

norm_eps = 1e-05
rope_base = 10000.0
masked_score = -1e30
score_scale = HEAD ** (-0.5)
bf16 = jnp.bfloat16
f32 = jnp.float32

X, Y, Z1, Z2 = 1, 2, 4, 8
FIRST, SECOND = (X, Y), (Y, X)
Z_SLOTS = (0, 2, 1, 3)

ORDER = "dPcuTdcKcdudIuacbdudabudbudbcacbuabuabcabacdacuba"

CASES = ((0, 0, 256, 0), (128, 256, 384, 128), (256, 640, 128, 128), (384, 768, 256, 128))
TILES = (
    (0, 0, 0, 0),
    (0, 1, 0, 0),
    (0, 1, 128, 0),
    (0, 1, 128, 128),
    (0, 0, 128, 128),
    (1, 1, 0, 0),
    (1, 1, 128, 0),
    (1, 1, 128, 128),
)
KEY_PLACE = (0, 3, 1, 2)


def mm(left, right):
    return jnp.dot(left, right, preferred_element_type=f32)


def tn(left, right):
    return lax.dot_general(left, right, (((0,), (0,)), ((), ())), preferred_element_type=f32)


def nt(left, right):
    return lax.dot_general(left, right, (((1,), (1,)), ((), ())), preferred_element_type=f32)


def rope_tables():
    half = HEAD // 2
    frequency = np.exp(np.arange(half) * (-2.0 * math.log(rope_base) / HEAD)).astype(np.float32)
    turn = (np.arange(LEN, dtype=np.float32)[:, None] * frequency[None, :]).astype(np.float32)
    cosine, sine = np.cos(turn.astype(np.float64)), np.sin(turn.astype(np.float64))
    cosine = np.tile(cosine, (1, LANES // half)).astype(np.float32)
    sine = np.tile(np.concatenate([-sine, sine], 1), (1, LANES // HEAD)).astype(np.float32)
    return cosine, sine


def swap_halves(values):
    lane = lax.broadcasted_iota(jnp.int32, values.shape, 1)
    return jnp.where(
        lane % HEAD < HEAD // 2, pltpu.roll(values, LANES - HEAD // 2, 1), pltpu.roll(values, HEAD // 2, 1)
    )


def head_mask(rows, which):
    lane = lax.broadcasted_iota(jnp.int32, (rows, LANES), 1)
    return (lane >= HEAD) if which else (lane < HEAD)


def layer_norm_rows(values, gain):
    centred = values - jnp.mean(values, axis=-1, keepdims=True)
    spread = jnp.mean(centred * centred, axis=-1, keepdims=True)
    return centred * lax.rsqrt(spread + norm_eps) * gain


def scaled_rows(values):
    centred = values - jnp.mean(values, axis=-1, keepdims=True)
    return centred * lax.rsqrt(jnp.mean(centred * centred, axis=-1, keepdims=True) + norm_eps)


def norm_back_rows(values, gain, delta):
    centred = values - jnp.mean(values, axis=-1, keepdims=True)
    spread = jnp.mean(centred * centred, axis=-1, keepdims=True)
    s = lax.rsqrt(spread + norm_eps)
    xhat = centred * s
    e = delta * gain
    back = s * (e - jnp.mean(e, axis=-1, keepdims=True) - xhat * jnp.mean(e * xhat, axis=-1, keepdims=True))
    return back, jnp.sum(delta * xhat, axis=0, keepdims=True)


def fill_bias(lengths_ref, pads_ref, bias_ref):
    sequence = lax.axis_index("dp")
    docs = lengths_ref.shape[1]
    ends, total = [], jnp.int32(0)
    for j in range(docs):
        total = total + lengths_ref[sequence, j]
        ends.append(total)
    first_pad = LEN - pads_ref[sequence]

    def segment(places):
        seg = jnp.zeros(places.shape, jnp.int32)
        for end in ends:
            seg = seg + (places >= end).astype(jnp.int32)
        return seg

    rows, cols, row_seg, col_seg = {}, {}, {}, {}
    for base in (0, HALF):
        rows[base] = lax.broadcasted_iota(jnp.int32, (HALF, LANES), 0) + base
        cols[base] = lax.broadcasted_iota(jnp.int32, (HALF, LANES), 1) + base
        row_seg[base] = segment(rows[base])
        col_seg[base] = segment(cols[base])
    for tile, (query_kind, key_kind, query_base, key_base) in enumerate(TILES):
        q, k = rows[query_base], cols[key_base]
        query_block, key_block = q // BLOCK, k // BLOCK
        same_doc = (row_seg[query_base] == col_seg[key_base]) & (k < first_pad)
        if query_kind == 0 and key_kind == 0:
            ok = (key_block == query_block) & (same_doc | (q == k))
        elif query_kind == 0:
            ok = (key_block < query_block) & same_doc
        else:
            ok = (key_block <= query_block) & (same_doc | (q == k))
        bias_ref[:, tile * LANES : (tile + 1) * LANES] = jnp.where(ok, 0.0, masked_score)


def fetch(pairs, sems):
    copies = [pltpu.make_async_copy(source, target, sems.at[i]) for i, (source, target) in enumerate(pairs)]
    for copy in copies:
        copy.start()
    return copies


def attention_forward(
    lengths_ref, pads_ref, gain_ref, x_in, wq_in, wk_in, wv_in, cos_in, sin_in, wo_in,
    normed_ref, q_ref, k_ref, v_ref, att_ref, prob_ref, part_ref,
    bias_ref, x_ref, wq_ref, wk_ref, wv_ref, cos_ref, sin_ref, wo_ref, sems,
):
    copies = fetch(
        (
            (x_in, x_ref), (wq_in, wq_ref), (wk_in, wk_ref), (wv_in, wv_ref),
            (cos_in, cos_ref), (sin_in, sin_ref), (wo_in, wo_ref),
        ),
        sems,
    )
    heads_cols = wq_ref.shape[1]
    pairs = heads_cols // LANES
    fill_bias(lengths_ref, pads_ref, bias_ref)
    copies[0].wait()

    @pl.loop(0, x_ref.shape[0] // 64)
    def _(i):
        rows = pl.ds(pl.multiple_of(i * 64, 64), 64)
        normed_ref[rows, :] = layer_norm_rows(x_ref[rows, :].astype(f32), gain_ref[...]).astype(bf16)

    for copy in copies[1:6]:
        copy.wait()
    for block in range(4):
        rows = slice(block * HALF, block * HALF + HALF)
        places = slice((block % 2) * HALF, (block % 2) * HALF + HALF)
        key_rows = slice(KEY_PLACE[block] * HALF, KEY_PLACE[block] * HALF + HALF)
        normed = normed_ref[rows, :]
        cosine, sine = cos_ref[places, :], sin_ref[places, :]
        query, key = mm(normed, wq_ref[...]), mm(normed, wk_ref[...])
        for t in range(pairs):
            cols = slice(t * LANES, (t + 1) * LANES)
            turned = query[:, cols] * cosine + swap_halves(query[:, cols]) * sine
            q_ref[rows, cols] = (turned.astype(bf16).astype(f32) * score_scale).astype(bf16)
            turned = key[:, cols] * cosine + swap_halves(key[:, cols]) * sine
            k_ref[key_rows, cols] = turned.astype(bf16)
        v_ref[key_rows, :] = mm(normed, wv_ref[...]).astype(bf16)

    for t in range(pairs):
        cols = slice(t * LANES, (t + 1) * LANES)
        key_pair, value_pair = k_ref[:, cols], v_ref[:, cols]
        mixed = [None] * 4
        for which in range(2):
            mask = head_mask(key_pair.shape[0], which)
            key_head = jnp.where(mask, key_pair, jnp.zeros_like(key_pair))
            value_head = jnp.where(mask, value_pair, jnp.zeros_like(value_pair))
            for case, (query_row, first, width, key_row) in enumerate(CASES):
                scores = nt(q_ref[query_row : query_row + HALF, cols], key_head[key_row : key_row + width])
                scores = scores + bias_ref[:, first : first + width]
                weights = jnp.exp(scores - jnp.max(scores, axis=1, keepdims=True))
                low = (weights * (1.0 / jnp.sum(weights, axis=1, keepdims=True))).astype(bf16)
                prob_ref[2 * t + which, :, first : first + width] = low
                part = mm(low, value_head[key_row : key_row + width])
                mixed[case] = part if mixed[case] is None else mixed[case] + part
        for case, (query_row, _, _, _) in enumerate(CASES):
            att_ref[query_row : query_row + HALF, cols] = mixed[case].astype(bf16)

    copies[6].wait()
    for block in range(2):
        rows = slice(block * 256, block * 256 + 256)
        part_ref[rows, :] = mm(att_ref[rows, :], wo_ref[...])


def fourths(start, part):
    return pl.ds(pl.multiple_of(start * part, 8), part)


def z_place(me, block):
    relative = (me // PLANE) ^ block
    return (relative % 2) * 2 + relative // 2


def quarter_at(place):
    core = lax.axis_index("mp") % 2
    slot = (place // 2) * (X + core) + (place % 2) * (Y - core)
    return lax.axis_index("dp") % PLANE ^ slot


def place_quarter(outs, place, value):
    me = lax.axis_index("dp") % GROUP
    part = value.shape[0] // STACK
    for block in range(STACK):
        outs[place // 2][place % 2, z_place(me, block)] = value[block * part : (block + 1) * part]


def place_quarter_z_first(outs, place, value):
    me = lax.axis_index("dp") % GROUP
    part = value.shape[0] // STACK
    for block in range(STACK):
        z = z_place(me, block)
        for sent in range(2):

            @pl.when(z // 2 == sent)
            def _(out=outs[sent], z=z, piece=value[block * part : (block + 1) * part]):
                out[z % 2, place] = piece


def mlp_kernel(
    gain_ref, bu_ref, mine_ref, theirs_ref, x_in, wu_in, wd_in, cot_in,
    residual_ref, normed_ref, act_ref, du_ref, gbu_ref, gbd_ref, *outs_and_scratch,
):
    *outs, x_ref, wu_ref, wd_ref, cot_ref, sems = outs_and_scratch
    copies = fetch(((x_in, x_ref), (cot_in, cot_ref), (wu_in, wu_ref), (wd_in, wd_ref)), sems)
    row_count = x_ref.shape[0]
    units = wu_ref.shape[1]
    gbu_ref[...] = jnp.zeros_like(gbu_ref)
    gbd_ref[...] = jnp.zeros_like(gbd_ref)
    copies[0].wait()
    copies[1].wait()

    @pl.loop(0, row_count // 64)
    def _(i):
        rows = pl.ds(pl.multiple_of(i * 64, 64), 64)
        residual = x_ref[rows, :].astype(f32) + (mine_ref[rows, :] + theirs_ref[rows, :])
        residual_ref[rows, :] = residual
        normed_ref[rows, :] = layer_norm_rows(residual, gain_ref[...]).astype(bf16)
        gbd_ref[...] += jnp.sum(cot_ref[rows, :].astype(f32), axis=0, keepdims=True)

    copies[2].wait()
    copies[3].wait()
    c0 = math.sqrt(2.0 / math.pi)
    c1 = c0 * 0.044715

    @pl.loop(0, units // 256)
    def _(j):
        cols = pl.ds(pl.multiple_of(j * 256, 256), 256)
        for block in range(row_count // 256):
            rows = slice(block * 256, block * 256 + 256)
            u = mm(normed_ref[rows, :], wu_ref[:, cols]) + bu_ref[:, cols]
            delta = nt(cot_ref[rows, :], wd_ref[cols, :])
            square = u * u
            t = jnp.tanh(u * (c0 + c1 * square))
            half_up = 0.5 * (1.0 + t)
            act_ref[rows, cols] = (u * half_up).astype(bf16)
            slope = half_up + (0.5 * u) * (1.0 - t * t) * (c0 + (3.0 * c1) * square)
            low = (delta * slope).astype(bf16)
            du_ref[rows, cols] = low
            gbu_ref[:, cols] += jnp.sum(low.astype(f32), axis=0, keepdims=True)

    quarter = units // PLANE
    cut = cot_ref.shape[1] * 2 // 3
    for place in range(PLANE):
        cols = pl.ds(pl.multiple_of(quarter_at(place) * quarter, LANES), quarter)
        grad = tn(act_ref[:, cols], cot_ref[...])
        place_quarter(outs[:2], place, grad[:, :cut])
        place_quarter_z_first(outs[2:], place, grad[:, cut:])


def up_kernel(normed_ref, du_ref, *outs):
    quarter = du_ref.shape[1] // PLANE
    for place in range(PLANE):
        cols = pl.ds(pl.multiple_of(quarter_at(place) * quarter, LANES), quarter)
        place_quarter(outs, place, tn(normed_ref[...], du_ref[:, cols]))


def tail_kernel(act_ref, du_ref, wu_ref, wd_ref, out_ref):
    for block in range(act_ref.shape[0] // 256):
        rows = slice(block * 256, block * 256 + 256)
        out_ref[0, rows, :] = nt(du_ref[rows, :], wu_ref[...])
        out_ref[1, rows, :] = mm(act_ref[rows, :], wd_ref[...])


def attention_backward(
    mine_ref, theirs_ref, residual_ref, gain_ref, cot_ref, att_ref, wo_ref, q_ref, k_ref, v_ref, prob_ref,
    normed_ref, wq_ref, wk_ref, wv_ref, cos_ref, sin_ref, x_ref, bd_ref, gbd_ref, gbu_ref,
    output_ref, delta_ref, vec_ref, part_ref, *outs_and_scratch,
):
    *outs, branch_ref, datt_ref, dq_ref, dk_ref, dv_ref, dk_acc, dv_acc, grads_ref, gnorm_ref = outs_and_scratch
    row_count = residual_ref.shape[0]
    heads_cols = wq_ref.shape[1]
    pairs = heads_cols // LANES
    gnorm_ref[...] = jnp.zeros_like(gnorm_ref)

    @pl.loop(0, row_count // 64)
    def _(i):
        rows = pl.ds(pl.multiple_of(i * 64, 64), 64)
        delta = mine_ref[0, rows, :] + theirs_ref[0, rows, :]
        residual = residual_ref[rows, :]
        output_ref[rows, :] = (residual + (mine_ref[1, rows, :] + theirs_ref[1, rows, :]) + bd_ref[...]).astype(bf16)
        back, gain_part = norm_back_rows(residual, gain_ref[...], delta)
        back = back + cot_ref[rows, :].astype(f32)
        delta_ref[rows, :] = back
        branch_ref[rows, :] = back.astype(bf16)
        gnorm_ref[0:1, :] += gain_part

    for block in range(2):
        rows = slice(block * 256, block * 256 + 256)
        datt_ref[rows, :] = nt(branch_ref[rows, :], wo_ref[...]).astype(bf16)
    half = heads_cols
    grad = tn(att_ref[...], branch_ref[...])
    grads_ref[0, 0], grads_ref[0, 1] = grad[:, :half], grad[:, half:]

    for t in range(pairs):
        cols = slice(t * LANES, (t + 1) * LANES)
        key_pair, value_pair = k_ref[:, cols], v_ref[:, cols]
        dk_acc[...] = jnp.zeros_like(dk_acc)
        dv_acc[...] = jnp.zeros_like(dv_acc)
        query_grads = [None] * 4
        for which in range(2):
            mask = head_mask(key_pair.shape[0], which)
            key_head = jnp.where(mask, key_pair, jnp.zeros_like(key_pair))
            value_head = jnp.where(mask, value_pair, jnp.zeros_like(value_pair))
            small = head_mask(HALF, which)
            for case, (query_row, first, width, key_row) in enumerate(CASES):
                rows = slice(query_row, query_row + HALF)
                keys = slice(key_row, key_row + width)
                low = prob_ref[2 * t + which, :, first : first + width]
                wide = low.astype(f32)
                delta_head = datt_ref[rows, cols]
                g = nt(delta_head, value_head[keys])
                weighted = wide * g
                scores_back = (weighted - wide * jnp.sum(weighted, axis=1, keepdims=True)).astype(bf16)
                part = mm(scores_back, key_head[keys])
                query_grads[case] = part if query_grads[case] is None else query_grads[case] + part
                query = q_ref[rows, cols]
                query = jnp.where(small, query, jnp.zeros_like(query))
                delta_head = jnp.where(small, delta_head, jnp.zeros_like(delta_head))
                dk_acc[keys, :] += tn(scores_back, query)
                dv_acc[keys, :] += tn(low, delta_head)
        for block in range(4):
            rows = slice(block * HALF, block * HALF + HALF)
            places = slice((block % 2) * HALF, (block % 2) * HALF + HALF)
            key_rows = slice(KEY_PLACE[block] * HALF, KEY_PLACE[block] * HALF + HALF)
            cosine, sine = cos_ref[places, :], sin_ref[places, :]
            grad = query_grads[block] * score_scale
            dq_ref[rows, cols] = (grad * cosine - swap_halves(grad) * sine).astype(bf16)
            grad = dk_acc[key_rows, :]
            dk_ref[rows, cols] = (grad * cosine - swap_halves(grad) * sine).astype(bf16)
            dv_ref[rows, cols] = dv_acc[key_rows, :].astype(bf16)

    for block in range(2):
        rows = slice(block * 256, block * 256 + 256)
        part_ref[rows, :] = (
            nt(dq_ref[rows, :], wq_ref[...]) + nt(dk_ref[rows, :], wk_ref[...]) + nt(dv_ref[rows, :], wv_ref[...])
        )

    @pl.loop(0, row_count // 64)
    def _(i):
        rows = pl.ds(pl.multiple_of(i * 64, 64), 64)
        gnorm_ref[1:2, :] += jnp.sum(part_ref[rows, :] * scaled_rows(x_ref[rows, :].astype(f32)), axis=0, keepdims=True)

    vec_ref[...] = jnp.zeros_like(vec_ref)
    row = 0
    once = jnp.where(lax.axis_index("mp") == 0, 1.0, 0.0)
    for values in (gnorm_ref[1:2, :], gnorm_ref[0:1, :] * once, gbd_ref[...] * once, gbu_ref[...]):
        for first in range(0, values.shape[1], half):
            vec_ref[row : row + 1, :] = values[:, first : first + half]
            row += 1

    for matrix, grad_rows in ((1, dq_ref), (2, dk_ref), (3, dv_ref)):
        grad = tn(normed_ref[...], grad_rows[...])
        grads_ref[matrix, 0], grads_ref[matrix, 1] = grad[:half], grad[half:]
    for place in range(PLANE):
        quarter = quarter_at(place)
        place_quarter(outs[:2], place, grads_ref[quarter, 0])
        place_quarter(outs[2:], place, grads_ref[quarter, 1])


def input_kernel(mine_ref, theirs_ref, x_ref, gain_ref, delta_ref, grad_ref):
    @pl.loop(0, x_ref.shape[0] // 64)
    def _(i):
        rows = pl.ds(pl.multiple_of(i * 64, 64), 64)
        delta = mine_ref[rows, :] + theirs_ref[rows, :]
        back, _ = norm_back_rows(x_ref[rows, :].astype(f32), gain_ref[...], delta)
        grad_ref[rows, :] = (delta_ref[rows, :] + back).astype(bf16)


def each_block(own_ref, got_ref, put, z_first=False):
    me = lax.axis_index("dp") % GROUP
    for place in range(PLANE):
        for z in range(STACK):
            first, second = (z, place) if z_first else (place, z)
            value = (got_ref if first // 2 else own_ref)[first % 2, second]
            put(quarter_at(place), me // PLANE ^ Z_SLOTS[z], value)


def unpack_down(own_ref, got_ref, z_own_ref, z_got_ref, out_ref):
    cut = own_ref.shape[-1]

    def put(quarter, fourth, value):
        cols = slice(0, cut) if value.shape[1] == cut else slice(cut, None)
        out_ref[fourths(quarter * STACK + fourth, value.shape[0]), cols] = value

    each_block(own_ref, got_ref, put)
    each_block(z_own_ref, z_got_ref, put, True)


def unpack_up(own_ref, got_ref, out_ref):
    def put(quarter, fourth, value):
        part, cols = value.shape
        out_ref[fourths(fourth, part), pl.ds(pl.multiple_of(quarter * cols, LANES), cols)] = value

    each_block(own_ref, got_ref, put)


def unpack_attention(own_a, got_a, own_b, got_b, *outs):
    grads_ref = outs[4]
    for portion, (own_ref, got_ref) in enumerate(((own_a, got_a), (own_b, got_b))):

        def put(quarter, fourth, value, portion=portion):
            grads_ref[quarter, portion, fourths(fourth, value.shape[0])] = value

        each_block(own_ref, got_ref, put)
    finish_att(outs)


def finish_att(outs):
    *outs, grads_ref, sems = outs
    half = grads_ref.shape[-1]
    copies = []
    for matrix, out in enumerate(outs):
        for portion in range(2):
            place = pl.ds(portion * half, half)
            target = out.at[place, :] if matrix else out.at[:, place]
            copies.append((grads_ref.at[matrix, portion], target))
    for copy in fetch(copies, sems):
        copy.wait()


VMEM = pl.BlockSpec(memory_space=pltpu.VMEM)
SMEM = pl.BlockSpec(memory_space=pltpu.SMEM)
HBM = pl.BlockSpec(memory_space=pltpu.HBM)


def call(kernel, outs, scalars=(), held=(), loose=(), scratch=(), flops=0, limit=40, out_space=VMEM):
    ins = [*scalars, *held, *loose]
    shapes = [jax.ShapeDtypeStruct(shape, dtype) for shape, dtype in outs]
    moved = sum(math.prod(a.shape) * a.dtype.itemsize for a in ins + shapes)
    return pl.pallas_call(
        kernel,
        name=getattr(kernel, "__name__", "unpack_kernel"),
        out_shape=shapes,
        in_specs=[SMEM] * len(scalars) + [VMEM] * len(held) + [HBM] * len(loose),
        out_specs=[out_space] * len(outs),
        scratch_shapes=[s if not isinstance(s, tuple) else pltpu.VMEM(*s) for s in scratch],
        compiler_params=pltpu.CompilerParams(vmem_limit_bytes=limit * 1024 * 1024),
        cost_estimate=pl.CostEstimate(flops=flops, bytes_accessed=moved, transcendentals=0),
    )(*ins)


def on_device(
    count,
    inputs, norm_attn, w_query, w_key, w_value, w_out, norm_mlp, w_up, b_up, w_down, b_down, cotangent,
    doc_lengths, pad_counts,
):
    rows, width = inputs.shape
    heads_cols = w_query.shape[1]
    units = w_up.shape[1]
    heads = heads_cols // HEAD
    cosine, sine = (jnp.asarray(t) for t in rope_tables())
    gain_attn, gain_mlp = norm_attn.reshape(1, -1), norm_mlp.reshape(1, -1)

    def swap(values):
        return lax.ppermute(values, "mp", [(0, 1), (1, 0)])

    def flip(values, bits, name):
        pairs = [(2 * i + core, 2 * (i ^ bits[core]) + core) for i in range(count) for core in range(2)]
        with jax.named_scope(name):
            return lax.ppermute(values, ("dp", "mp"), pairs)

    def sems(n):
        return pltpu.SemaphoreType.DMA((n,))

    half = heads_cols

    def portions(*shape):
        return [((2, STACK) + shape, f32)] * 2

    last = []

    def turn(*values):
        if not last:
            return values
        values, _ = lax.optimization_barrier((values, last.pop()))
        return values

    def did(value):
        last[:] = [value]
        return value

    def over_groups(values):
        if count == GROUP:
            return values
        groups = [[k * GROUP + j for k in range(count // GROUP)] for j in range(GROUP)]
        return lax.psum(values, "dp", axis_index_groups=groups)

    def chain(name, parts, result, z_first=False, vec=None):
        keep, send = parts
        plane, stack = [(FIRST, "first"), (SECOND, "second")], [((Z1, Z1), "z1"), ((Z2, Z2), "z2")]
        steps = stack + plane if z_first else plane + stack

        def join(values):
            return values if vec is None else jnp.concatenate([values.reshape(-1, values.shape[-1]), vec], 0)

        def part_of(got, like, vec):
            if vec is None:
                return got, None
            return got[: -vec.shape[0]].reshape(like.shape), vec + got[-vec.shape[0] :]

        for step, (bits, label) in enumerate(steps):
            if step:
                keep, got, vec = turn(keep, got, vec)
                got, vec = part_of(got, keep, vec)
                cut = keep.shape[0] // 2
                send, keep = keep[cut:] + got[cut:], keep[:cut] + got[:cut]
                if step == 1:
                    keep, send = keep[0], send[0]
                send = did(join(send))
            else:
                send = join(send)
            got = flip(send, bits, f"{name}_sum_{label}")
            yield
        keep, got, vec = turn(keep, got, vec)
        got, vec = part_of(got, keep, vec)
        own = over_groups(did(keep + got))
        if vec is not None:
            result.append(over_groups(vec))
        for step, (bits, label) in enumerate(reversed(steps)):
            got = flip(own, bits, f"{name}_gather_{label}")
            yield
            own, got = turn(own, got)
            if step < 3:
                own = did(jnp.stack([own, got]) if step == 2 else jnp.concatenate([own, got], 0))
        result.extend((own, got))
        yield

    normed, q, k, v, attended, probs, branch = call(
        attention_forward,
        [
            ((rows, width), bf16),
            ((rows, heads_cols), bf16),
            ((rows, heads_cols), bf16),
            ((rows, heads_cols), bf16),
            ((rows, heads_cols), bf16),
            ((heads, HALF, 8 * LANES), bf16),
            ((rows, width), f32),
        ],
        scalars=[doc_lengths, pad_counts],
        held=[gain_attn],
        loose=[inputs, w_query, w_key, w_value, cosine, sine, w_out],
        scratch=[
            ((HALF, 8 * LANES), f32),
            ((rows, width), bf16),
            ((width, heads_cols), bf16),
            ((width, heads_cols), bf16),
            ((width, heads_cols), bf16),
            (cosine.shape, f32),
            (sine.shape, f32),
            ((heads_cols, width), bf16),
            sems(7),
        ],
        flops=2 * rows * width * heads_cols * 4,
    )
    branch_other = swap(branch)

    residual, normed_mlp, act, du, grad_bu, grad_bd, *down_parts = call(
        mlp_kernel,
        [
            ((rows, width), f32),
            ((rows, width), bf16),
            ((rows, units), bf16),
            ((rows, units), bf16),
            ((1, units), f32),
            ((1, width), f32),
        ]
        + portions(units // GROUP, width * 2 // 3)
        + portions(units // GROUP, width // 3),
        held=[gain_mlp, b_up.reshape(1, -1), branch, branch_other],
        loose=[inputs, w_up, w_down, cotangent],
        scratch=[
            ((rows, width), bf16),
            ((width, units), bf16),
            ((units, width), bf16),
            ((rows, width), bf16),
            sems(4),
        ],
        flops=2 * rows * width * units * 3,
    )
    made, grads = {key: [] for key in "dcuab"}, {}
    chains = {"d": chain("down", down_parts[:2], made["d"]), "c": chain("down_stack", down_parts[2:], made["c"], True)}
    state = {}

    def tail():
        operands = turn(act, du)
        (state["shares"],) = call(
            tail_kernel, [((2, rows, width), f32)], held=[*operands, w_up, w_down], flops=2 * rows * width * units * 2
        )
        state["shares_other"] = swap(did(state["shares"]))

    def grad_up_parts():
        operands = turn(normed_mlp, du)
        parts = call(
            up_kernel,
            portions(width // STACK, units // PLANE),
            held=operands,
            flops=2 * rows * width * units,
        )
        did(parts[0])
        chains["u"] = chain("up", parts, made["u"])

    def backward():
        (shares_other,) = turn(state["shares_other"])
        state["output"], state["delta_residual"], vec, state["normed_part"], *parts = call(
            attention_backward,
            [((rows, width), bf16), ((rows, width), f32), ((16, half), f32), ((rows, width), f32)]
            + portions(half // STACK, half) * 2,
            held=[
                state["shares"], shares_other, residual, gain_mlp, cotangent, attended, w_out, q, k, v, probs,
                normed, w_query, w_key, w_value, cosine, sine, inputs, b_down.reshape(1, -1), grad_bd, grad_bu,
            ],
            scratch=[
                ((rows, width), bf16),
                ((rows, heads_cols), bf16),
                ((rows, heads_cols), bf16),
                ((rows, heads_cols), bf16),
                ((rows, heads_cols), bf16),
                ((rows, LANES), f32),
                ((rows, LANES), f32),
                ((PLANE, 2, half, half), f32),
                ((8, width), f32),
            ],
            flops=2 * rows * width * heads_cols * 10,
        )
        did(vec)
        state["normed_other"] = swap(state["normed_part"])
        chains["a"] = chain("attention", parts[:2], made["a"], vec=vec)
        chains["b"] = chain("attention_rest", parts[2:], made["b"])

    def input_back():
        (normed_other,) = turn(state["normed_other"])
        (state["grad_inputs"],) = call(
            input_kernel,
            [((rows, width), bf16)],
            held=[state["normed_part"], normed_other, inputs, gain_attn, state["delta_residual"]],
        )
        did(state["grad_inputs"])

    def unpack():
        if "down" not in grads and len(made["d"]) == len(made["c"]) == 2:
            grads["down"] = call(unpack_down, [((units, width), f32)], held=made["d"] + made["c"])
            did(grads["down"][0])
        if "up" not in grads and len(made["u"]) == 2:
            grads["up"] = call(unpack_up, [((width, units), f32)], held=made["u"])
            did(grads["up"][0])
        if "attention" not in grads and len(made["a"]) == 3 and len(made["b"]) == 2:
            grads["attention"] = call(
                unpack_attention,
                [((heads_cols, width), f32)] + [((width, heads_cols), f32)] * 3,
                held=made["a"][1:] + made["b"],
                scratch=[((PLANE, 2, half, half), f32), sems(8)],
                out_space=HBM,
            )

    did(grad_bd)
    pieces = {"T": tail, "P": grad_up_parts, "K": backward, "I": input_back}
    for key in ORDER:
        if key in pieces:
            pieces[key]()
        else:
            next(chains[key])
            unpack()
    assert len(grads) == 3

    vec = made["a"][0]
    n = width // half
    shared = (vec[: 3 * n] + swap(vec[: 3 * n])).reshape(3, width)
    grad_bu = vec[3 * n :].reshape(-1)[:units]
    (grad_down,), (grad_up,) = grads["down"], grads["up"]
    grad_out, grad_query, grad_key, grad_value = grads["attention"]
    output, grad_inputs = state["output"], state["grad_inputs"]
    return (
        output,
        grad_inputs,
        shared[0],
        grad_query,
        grad_key,
        grad_value,
        grad_out,
        shared[1],
        grad_up,
        grad_bu,
        grad_down,
        shared[2],
    )


def solution(mesh):
    count = mesh.shape["dp"]

    def step(*args):
        return on_device(count, *args)

    return jax.shard_map(
        step,
        mesh=mesh,
        in_specs=(
            P("dp", None),
            P(),
            P(None, "mp"),
            P(None, "mp"),
            P(None, "mp"),
            P("mp", None),
            P(),
            P(None, "mp"),
            P("mp"),
            P("mp", None),
            P(),
            P("dp", None),
            P(),
            P(),
        ),
        out_specs=(
            P("dp", None),
            P("dp", None),
            P(),
            P(None, "mp"),
            P(None, "mp"),
            P(None, "mp"),
            P("mp", None),
            P(),
            P(None, "mp"),
            P("mp"),
            P("mp", None),
            P(),
        ),
        check_vma=False,
    )
```

time: 368 us -> 331 us (0.90)
  waiting for transfers between devices: 224 us -> 154 us
  starting transfers between devices: 52.5 us -> 78.9 us
  local copies, waits for them, and re-layouts: 17.9 us -> 23.7 us
    ppermute x44 -> x40, waiting for transfers between devices: 222 us -> 151 us  [flip(): return lax.ppermute(values, ('dp', 'mp'), pairs)]
    ppermute x44 -> x40, starting transfers between devices: 51.6 us -> 77.9 us  [flip(): return lax.ppermute(values, ('dp', 'mp'), pairs)]
    unnamed x80 -> x93, local copies, waits for them, and re-layouts: 14.8 us -> 20.3 us
    pallas_call x7 -> x9, Pallas kernels: 65.1 us -> 63.5 us  [call(): pl.pallas_call(kernel, name=getattr(kernel, '__name__', 'unpack_kernel'),...]
  transfers between devices with their start and end apart: 48 -> 44, of which waited for: 27 -> 28; matrix products, arithmetic and copies ran while one was open for 3% -> 3% of each run, Pallas kernels for 7% -> 9%
where the time goes in v2:
time: 331 us; the launch traced here: 330 us
  waiting for transfers between devices  154 us (47%)
  starting transfers between devices  78.9 us (24%)
  Pallas kernels  63.5 us (19%)
  local copies, waits for them, and re-layouts  23.7 us (7%)
  other arithmetic  8.38 us (3%)
    ppermute x40, waiting for transfers between devices, flip(): return lax.ppermute(values, ('dp', 'mp'), pairs)  151 us
    ppermute x40, starting transfers between devices, flip(): return lax.ppermute(values, ('dp', 'mp'), pairs)  77.9 us
    pallas_call x9, Pallas kernels, call(): pl.pallas_call(kernel, name=getattr(kernel, '__name__', 'unpack_kernel'),...  63.5 us
    unnamed x93, local copies, waits for them, and re-layouts  20.3 us
  transfers between devices with their start and end apart: 44, of which 28 were waited for; matrix products, arithmetic and copies ran while one was open for 3% of the time, Pallas kernels for 9%

profile of v2, /device:TPU:0, one launch (start us, length us, event | category | flops | bytes accessed | tf_op | source)
XLA Modules:
  0.0 330.4 jit_solution(9624863513173556163)
XLA Ops:
  10.0 10.7 %attention_forward.1 = (bf16[512,768]{1,0:T(8,128)(2,1)S(1)}, bf16[512,384]{1,0:T(8,128)(2,1)S(1)}, bf16[512,384]{1,0:T(8,128)(2,1)S(1)}, bf16[512,384]{1,0:T(8,...) custom-call(s32[16,8]{1,0:T(8,128)S(1)} %copy.28.lengths_ref, ...), custom_call_target="tpu_custom_call" | custom-call | flops 1207959552 | bytes 8916544 | tf_op jit(solution)/shard_map/attention_forward/pallas_call | solution.py:474
  20.7 1.2 copy-done.5
  25.5 3.0 collective-permute-done.theirs_ref
  28.5 1.1 copy-done.40
  29.6 11.6 %mlp_kernel.1 = (f32[512,768]{1,0:T(8,128)S(1)}, bf16[512,768]{1,0:T(8,128)(2,1)S(1)}, bf16[512,1536]{1,0:T(8,128)(2,1)S(1)}, bf16[512,1536]{1,0:T(8,128)(2,1)S(...) custom-call(f32[1,768]{1,0:T(1,128)S(1)} %reshape.66.gain_ref, ...), custom_call_target="tpu_custom_call" | custom-call | flops 3623878656 | bytes 19679232 | tf_op jit(solution)/shard_map/mlp_kernel/pallas_call | solution.py:474
  41.3 1.2 copy-done.6
  43.6 3.2 up_kernel.1
  46.8 1.4 copy-done.10
  48.2 2.6 tail_kernel.1.mine_ref
  51.3 2.6 collective-permute-start.3
  54.0 2.1 collective-permute-start.2
  56.0 16.3 %collective-permute-done.3 = f32[2,4,96,512]{3,2,1,0:T(8,128)S(1)} collective-permute-done((f32[2,4,96,512]{3,2,1,0:T(8,128)S(1)}, f32[2,4,96,512]{3,2,1,0:T(8,128)S(1)}, u32[]{:S(2)}, u32[]{:S(2)}) %collective-permute-start.3) | collective-permute-done | bytes 1572896 | tf_op jit(solution)/shard_map/down_sum_first/ppermute | solution.py:504
  72.4 1.2 add_bitcast_fusion.2
  73.6 2.1 collective-permute-start.5
  75.8 2.7 collective-permute-start.6
  78.5 1.7 copy-done.34
  80.2 18.2 %attention_backward.1 = (bf16[512,768]{1,0:T(8,128)(2,1)}, f32[512,768]{1,0:T(8,128)S(1)}, f32[16,384]{1,0:T(8,128)S(1)}, f32[512,768]{1,0:T(8,128)S(1)}, f32[2,...) custom-call(f32[2,512,768]{2,1,0:T(8,128)} %copy-done, ...), custom_call_target="tpu_custom_call" | custom-call | flops 3019898880 | bytes 24681472 | tf_op jit(solution)/shard_map/attention_backward/pallas_call | solution.py:474
  99.8 6.3 %collective-permute-done.8 = f32[2,4,192,384]{3,2,1,0:T(8,128)S(1)} collective-permute-done((f32[2,4,192,384]{3,2,1,0:T(8,128)}, f32[2,4,192,384]{3,2,1,0:T(8,128)S(1)}, u32[]{:S(2)}, u32[]{:S(2)}) %collective-permute-start.8) | collective-permute-done | bytes 2359328 | tf_op jit(solution)/shard_map/up_sum_first/ppermute | solution.py:504
  106.4 2.1 collective-permute-start.12
  108.5 1.6 collective-permute-start.7
  110.1 1.5 collective-permute-start.9
  111.7 7.0 %collective-permute-done.7 = f32[2,96,512]{2,1,0:T(8,128)S(1)} collective-permute-done((f32[2,96,512]{2,1,0:T(8,128)S(1)}, f32[2,96,512]{2,1,0:T(8,128)S(1)}, u32[]{:S(2)}, u32[]{:S(2)}) %collective-permute-start.7) | collective-permute-done | bytes 393248 | tf_op jit(solution)/shard_map/down_sum_z1/ppermute | solution.py:504
  118.8 3.5 %input_kernel.1 = bf16[512,768]{1,0:T(8,128)(2,1)} custom-call(f32[512,768]{1,0:T(8,128)S(1)} %get-tuple-element.157.mine_ref, f32[512,768]{1,0:T(8,128)S(1)} %collective-permute-done.4.theirs_ref, bf16[512,768]{1,0:T(8,128)(2,1)S(1)} %copy-done.2, f32[1,768]{1,0:T(1,128)S(1)} %reshape.68.gain_ref, f32[512,768]{1,0:T(8,128)S(1)} %get-tuple-element.169.delta_ref), custom_call_target="tpu_custom_call" | custom-call | bytes 6294528 | tf_op jit(solution)/shard_map/input_kernel/pallas_call | solution.py:474
  122.2 11.4 %collective-permute-done.12 = f32[4,192,384]{2,1,0:T(8,128)S(1)} collective-permute-done((f32[4,192,384]{2,1,0:T(8,128)S(1)}, f32[4,192,384]{2,1,0:T(8,128)S(1)}, u32[]{:S(2)}, u32[]{:S(2)}) %collective-permute-start.12) | collective-permute-done | bytes 1179680 | tf_op jit(solution)/shard_map/up_sum_second/ppermute | solution.py:504
  133.8 3.7 %collective-permute-start.14 = (f32[2,192,384]{2,1,0:T(8,128)S(1)}, f32[2,192,384]{2,1,0:T(8,128)S(1)}, u32[]{:S(2)}, u32[]{:S(2)}) collective-permute-start(f32[2,192,384]{2,1,0:T(8,128)S(1)} %get-tuple-element.253), channel_id=1, source_target_pairs={{0,8},{1,9},{2,10},{3,11},{4,12},{5,13},{6,14},{7,15},{8,0},{9,1},... | collective-permute-start | bytes 1769480 | tf_op jit(solution)/shard_map/up_sum_z1/ppermute | solution.py:504
  137.5 1.2 collective-permute-start.11
  139.6 2.6 collective-permute-start.10
  143.2 8.9 %collective-permute-done.10 = f32[1,96,512]{2,1,0:T(8,128)S(1)} collective-permute-done((f32[1,96,512]{2,1,0:T(8,128)S(1)}, f32[1,96,512]{2,1,0:T(8,128)S(1)}, u32[]{:S(2)}, u32[]{:S(2)}) %collective-permute-start.10) | collective-permute-done | bytes 196640 | tf_op jit(solution)/shard_map/down_sum_z2/ppermute | solution.py:504
  152.1 3.5 %collective-permute-start.13 = (f32[1,96,512]{2,1,0:T(8,128)S(1)}, f32[1,96,512]{2,1,0:T(8,128)S(1)}, u32[]{:S(2)}, u32[]{:S(2)}) collective-permute-start(f32[1,96,512]{2,1,0:T(8,128)S(1)} %add.134), channel_id=1, source_target_pairs={{0,16},{1,17},{2,18},{3,19},{4,20},{5,21},{6,22},{7,23},{8,24},{9,... | collective-permute-start | bytes 589832 | tf_op jit(solution)/shard_map/down_gather_z2/ppermute | solution.py:504
  155.8 11.1 %collective-permute-done.13 = f32[1,96,512]{2,1,0:T(8,128)S(1)} collective-permute-done((f32[1,96,512]{2,1,0:T(8,128)S(1)}, f32[1,96,512]{2,1,0:T(8,128)S(1)}, u32[]{:S(2)}, u32[]{:S(2)}) %collective-permute-start.13) | collective-permute-done | bytes 196640 | tf_op jit(solution)/shard_map/down_gather_z2/ppermute | solution.py:504
  167.5 3.0 collective-permute-start.18
  171.4 6.1 %collective-permute-done.19 = f32[2,96,512]{2,1,0:T(8,128)S(1)} collective-permute-done((f32[2,96,512]{2,1,0:T(8,128)S(1)}, f32[2,96,512]{2,1,0:T(8,128)S(1)}, u32[]{:S(2)}, u32[]{:S(2)}) %collective-permute-start.19) | collective-permute-done | bytes 393248 | tf_op jit(solution)/shard_map/down_gather_z1/ppermute | solution.py:504
  177.5 6.4 %collective-permute-start.22 = (f32[4,96,512]{2,1,0:T(8,128)S(1)}, f32[4,96,512]{2,1,0:T(8,128)S(1)}, u32[]{:S(2)}, u32[]{:S(2)}) collective-permute-start(f32[4,96,512]{2,1,0:T(8,128)S(1)} %constant_dynamic-update-slice_fusion.2), channel_id=1, source_target_pairs={{0,4},{1,3},{2,6},{3,1},{4,0},{5,7},{6,2},{7,5},{8,12},{9,11},{10,... | collective-permute-start | bytes 2359304 | tf_op jit(solution)/shard_map/down_gather_second/ppermute | solution.py:504
  184.1 1.9 collective-permute-start.15
  186.0 2.4 collective-permute-start.21
  188.4 6.0 %collective-permute-done.23 = f32[1,192,384]{2,1,0:T(8,128)S(1)} collective-permute-done((f32[1,192,384]{2,1,0:T(8,128)S(1)}, f32[1,192,384]{2,1,0:T(8,128)S(1)}, u32[]{:S(2)}, u32[]{:S(2)}) %collective-permute-start.23) | collective-permute-done | bytes 294944 | tf_op jit(solution)/shard_map/up_gather_z2/ppermute | solution.py:504
  194.5 2.1 collective-permute-start.25
  196.5 1.3 pad_maximum_fusion.1.own_ref
  197.9 3.5 %collective-permute-start.26 = (f32[1,96,384]{2,1,0:T(8,128)S(1)}, f32[1,96,384]{2,1,0:T(8,128)S(1)}, u32[]{:S(2)}, u32[]{:S(2)}) collective-permute-start(f32[1,96,384]{2,1,0:T(8,128)S(1)} %get-tuple-element.275), channel_id=1, source_target_pairs={{0,16},{1,17},{2,18},{3,19},{4,20},{5,21},{6,22},{7,23},{8,24},{9,... | collective-permute-start | bytes 442376 | tf_op jit(solution)/shard_map/attention_rest_sum_z2/ppermute | solution.py:504
  201.4 2.6 collective-permute-start.27
  204.2 2.4 collective-permute-done.27
  206.6 2.3 collective-permute-done.26
  209.1 9.8 %collective-permute-start.29 = (f32[4,192,384]{2,1,0:T(8,128)S(1)}, f32[4,192,384]{2,1,0:T(8,128)S(1)}, u32[]{:S(2)}, u32[]{:S(2)}) collective-permute-start(f32[4,192,384]{2,1,0:T(8,128)S(1)} %constant_dynamic-update-slice_fusion.8), channel_id=1, source_target_pairs={{0,4},{1,3},{2,6},{3,1},{4,0},{5,7},{6,2},{7,5},{8,12},{9,11},{10,... | collective-permute-start | bytes 3538952 | tf_op jit(solution)/shard_map/up_gather_second/ppermute | solution.py:504
  219.4 1.2 collective-permute-start.33
  220.6 1.7 collective-permute-start.30
  222.3 6.9 %collective-permute-done.24 = f32[208,384]{1,0:T(8,128)S(1)} collective-permute-done((f32[208,384]{1,0:T(8,128)S(1)}, f32[208,384]{1,0:T(8,128)S(1)}, u32[]{:S(2)}, u32[]{:S(2)}) %collective-permute-start.24) | collective-permute-done | bytes 319520 | tf_op jit(solution)/shard_map/attention_sum_z1/ppermute | solution.py:504
  229.3 1.3 collective-permute-start.28
  231.5 2.2 collective-permute-start.34
  233.7 1.4 collective-permute-done.29
  235.3 4.6 %collective-permute-done.28 = f32[112,384]{1,0:T(8,128)S(1)} collective-permute-done((f32[112,384]{1,0:T(8,128)S(1)}, f32[112,384]{1,0:T(8,128)S(1)}, u32[]{:S(2)}, u32[]{:S(2)}) %collective-permute-start.28) | collective-permute-done | bytes 172064 | tf_op jit(solution)/shard_map/attention_sum_z2/ppermute | solution.py:504
  241.2 2.8 collective-permute-start.36
  244.0 3.6 %collective-permute-done.32 = f32[1,96,384]{2,1,0:T(8,128)S(1)} collective-permute-done((f32[1,96,384]{2,1,0:T(8,128)S(1)}, f32[1,96,384]{2,1,0:T(8,128)S(1)}, u32[]{:S(2)}, u32[]{:S(2)}) %collective-permute-start.32) | collective-permute-done | bytes 147488 | tf_op jit(solution)/shard_map/attention_gather_z2/ppermute | solution.py:504
  249.1 3.6 %collective-permute-done.36 = f32[4,96,384]{2,1,0:T(8,128)S(1)} collective-permute-done((f32[4,96,384]{2,1,0:T(8,128)S(1)}, f32[4,96,384]{2,1,0:T(8,128)S(1)}, u32[]{:S(2)}, u32[]{:S(2)}) %collective-permute-start.36) | collective-permute-done | bytes 589856 | tf_op jit(solution)/shard_map/attention_rest_gather_second/ppermute | solution.py:504
  252.8 1.7 collective-permute-done.35
  254.5 4.4 %collective-permute-start.37 = (f32[4,96,384]{2,1,0:T(8,128)S(1)}, f32[4,96,384]{2,1,0:T(8,128)S(1)}, u32[]{:S(2)}, u32[]{:S(2)}) collective-permute-start(f32[4,96,384]{2,1,0:T(8,128)S(1)} %constant_dynamic-update-slice_fusion.18), channel_id=1, source_target_pairs={{0,4},{1,3},{2,6},{3,1},{4,0},{5,7},{6,2},{7,5},{8,12},{9,11},{10,... | collective-permute-start | bytes 1769480 | tf_op jit(solution)/shard_map/attention_gather_second/ppermute | solution.py:504
  260.6 1.3 collective-permute-start.39
  261.9 11.3 %collective-permute-done.37 = f32[4,96,384]{2,1,0:T(8,128)S(1)} collective-permute-done((f32[4,96,384]{2,1,0:T(8,128)S(1)}, f32[4,96,384]{2,1,0:T(8,128)S(1)}, u32[]{:S(2)}, u32[]{:S(2)}) %collective-permute-start.37) | collective-permute-done | bytes 589856 | tf_op jit(solution)/shard_map/attention_gather_second/ppermute | solution.py:504
  275.3 3.7 %collective-permute-done.42 = f32[4,96,256]{2,1,0:T(8,128)S(1)} collective-permute-done((f32[4,96,256]{2,1,0:T(8,128)S(1)}, f32[4,96,256]{2,1,0:T(8,128)S(1)}, u32[]{:S(2)}, u32[]{:S(2)}) %collective-permute-start.42) | collective-permute-done | bytes 393248 | tf_op jit(solution)/shard_map/down_stack_gather_z2/ppermute | solution.py:504
  283.9 16.4 %collective-permute-done.41.got_ref = f32[2,4,96,512]{3,2,1,0:T(8,128)} collective-permute-done((f32[2,4,96,512]{3,2,1,0:T(8,128)}, f32[2,4,96,512]{3,2,1,0:T(8,128)}, u32[]{:S(2)}, u32[]{:S(2)}) %collective-permute-start.41) | collective-permute-done | bytes 1572896 | tf_op jit(solution)/shard_map/down_gather_first/ppermute | solution.py:504
  300.8 4.8 %unpack_down.1 = f32[1536,768]{1,0:T(8,128)} custom-call(f32[2,4,96,512]{3,2,1,0:T(8,128)} %pad_maximum_fusion.1.own_ref, f32[2,4,96,512]{3,2,1,0:T(8,128)} %collective-permute-done.41.got_ref, f32[2,4,96,256]{3,2,1,0:T(8,128)} %pad_maximum_fusion.5.z_own_ref, f32[2,4,96,256]{3,2,1,0:T(8,128)} %collective-permute-done.43.z_got_ref), custom_call_target="tpu_custom_call" | custom-call | bytes 9437184 | tf_op jit(solution)/shard_map/unpack_down/pallas_call | solution.py:474
  305.6 4.2 %unpack_up.1 = f32[768,1536]{1,0:T(8,128)} custom-call(f32[2,4,192,384]{3,2,1,0:T(8,128)S(1)} %pad_maximum_fusion.own_ref, f32[2,4,192,384]{3,2,1,0:T(8,128)} %collective-permute-done.40.got_ref), custom_call_target="tpu_custom_call" | custom-call | bytes 9437184 | tf_op jit(solution)/shard_map/unpack_up/pallas_call | solution.py:474
  309.8 3.1 collective-permute-done.39.got_b
  313.0 12.6 %collective-permute-done.38.got_a = f32[2,4,96,384]{3,2,1,0:T(8,128)} collective-permute-done((f32[2,4,96,384]{3,2,1,0:T(8,128)}, f32[2,4,96,384]{3,2,1,0:T(8,128)}, u32[]{:S(2)}, u32[]{:S(2)}) %collective-permute-start.38) | collective-permute-done | bytes 1179680 | tf_op jit(solution)/shard_map/attention_gather_first/ppermute | solution.py:504
  325.6 4.6 %unpack_attention.1 = (f32[384,768]{1,0:T(8,128)}, f32[768,384]{1,0:T(8,128)}, f32[768,384]{1,0:T(8,128)}, f32[768,384]{1,0:T(8,128)}) custom-call(f32[2,4,96,384]{3,2,1,0:T(8,128)} %pad_maximum_fusion.4.own_a, f32[2,4,96,384]{3,2,1,0:T(8,128)} %collective-permute-done.38.got_a, f32[2,4,96,384]{3,2,1,0:T(8,128)S(1)} %pad_maximum_fusion.3.own_b, ...), custom_call_target="tpu_custom_call" | custom-call | bytes 9437184 | tf_op jit(solution)/shard_map/unpack_attention/pallas_call | solution.py:474
  (183 shorter events, 34.6 us)
Async XLA Ops:
  9.9 15.5 %copy-start.38 = (f32[768]{0:T(1024)S(1)}, f32[768]{0:T(1024)}, u32[]{:S(2)}) copy-start(f32[768]{0:T(1024)} %param.22) | copy-start | bytes 9220
  10.0 15.5 %copy-start.37 = (f32[1536]{0:T(1024)S(1)}, f32[1536]{0:T(1024)}, u32[]{:S(2)}) copy-start(f32[1536]{0:T(1024)} %param.24) | copy-start | bytes 18436
  10.0 19.7 %copy-start.2 = (bf16[512,768]{1,0:T(8,128)(2,1)S(1)}, bf16[512,768]{1,0:T(8,128)(2,1)}, u32[]{:S(2)}) copy-start(bf16[512,768]{1,0:T(8,128)(2,1)} %x_ref.3) | copy-start | bytes 2359300
  10.0 19.7 %copy-start.11 = (bf16[512,768]{1,0:T(8,128)(2,1)S(1)}, bf16[512,768]{1,0:T(8,128)(2,1)}, u32[]{:S(2)}) copy-start(bf16[512,768]{1,0:T(8,128)(2,1)} %cot_ref.1) | copy-start | bytes 2359300
  25.0 3.5 %collective-permute-start = (f32[512,768]{1,0:T(8,128)S(1)}, f32[512,768]{1,0:T(8,128)S(1)}, u32[]{:S(2)}, u32[]{:S(2)}) collective-permute-start(f32[512,768]{1,0:T(8,128)S(1)} %get-tuple-element.129.mine_ref), channel_id=1, source_target_pairs={{0,1},{1,0},{2,3},{3,2},{4,5},{5,4},{6,7},{7,6},{8,9},{9,8},{10,11... | collective-permute-start | bytes 4718600 | tf_op jit(solution)/shard_map/ppermute | solution.py:499
  29.6 17.2 %copy-start.4 = (bf16[1536,768]{1,0:T(8,128)(2,1)S(1)}, bf16[1536,768]{1,0:T(8,128)(2,1)}, u32[]{:S(2)}) copy-start(bf16[1536,768]{1,0:T(8,128)(2,1)} %wd_ref.1) | copy-start | bytes 7077892
  43.6 3.2 copy-start.3
  43.6 3.2 copy-start.8
  50.9 22.7 %copy-start = (f32[2,512,768]{2,1,0:T(8,128)}, f32[2,512,768]{2,1,0:T(8,128)S(1)}, u32[]{:S(2)}) copy-start(f32[2,512,768]{2,1,0:T(8,128)S(1)} %tail_kernel.1.mine_ref) | copy-start | bytes 9437188
  50.9 27.6 %collective-permute-start.1 = (f32[2,512,768]{2,1,0:T(8,128)S(1)}, f32[2,512,768]{2,1,0:T(8,128)S(1)}, u32[]{:S(2)}, u32[]{:S(2)}) collective-permute-start(f32[2,512,768]{2,1,0:T(8,128)S(1)} %tail_kernel.1.mine_ref), channel_id=1, source_target_pairs={{0,1},{1,0},{2,3},{3,2},{4,5},{5,4},{6,7},{7,6},{8,9},{9,8},{10,11... | collective-permute-start | bytes 9437192 | tf_op jit(solution)/shard_map/ppermute | solution.py:499
  51.3 21.0 %collective-permute-start.3 = (f32[2,4,96,512]{3,2,1,0:T(8,128)S(1)}, f32[2,4,96,512]{3,2,1,0:T(8,128)S(1)}, u32[]{:S(2)}, u32[]{:S(2)}) collective-permute-start(f32[2,4,96,512]{3,2,1,0:T(8,128)S(1)} %get-tuple-element.142), channel_id=1, source_target_pairs={{0,2},{1,5},{2,0},{3,7},{4,6},{5,1},{6,4},{7,3},{8,10},{9,13},{10,... | collective-permute-start | bytes 4718600 | tf_op jit(solution)/shard_map/down_sum_first/ppermute | solution.py:504
  53.9 52.1 %collective-permute-start.8 = (f32[2,4,192,384]{3,2,1,0:T(8,128)}, f32[2,4,192,384]{3,2,1,0:T(8,128)S(1)}, u32[]{:S(2)}, u32[]{:S(2)}) collective-permute-start(f32[2,4,192,384]{3,2,1,0:T(8,128)} %get-tuple-element.163), channel_id=1, source_target_pairs={{0,2},{1,5},{2,0},{3,7},{4,6},{5,1},{6,4},{7,3},{8,10},{9,13},{10,... | collective-permute-start | bytes 7077896 | tf_op jit(solution)/shard_map/up_sum_first/ppermute | solution.py:504
  54.0 21.7 %collective-permute-start.2 = (f32[2,4,96,256]{3,2,1,0:T(8,128)S(1)}, f32[2,4,96,256]{3,2,1,0:T(8,128)S(1)}, u32[]{:S(2)}, u32[]{:S(2)}) collective-permute-start(f32[2,4,96,256]{3,2,1,0:T(8,128)S(1)} %get-tuple-element.140), channel_id=1, source_target_pairs={{0,8},{1,9},{2,10},{3,11},{4,12},{5,13},{6,14},{7,15},{8,0},{9,1},... | collective-permute-start | bytes 2359304 | tf_op jit(solution)/shard_map/down_stack_sum_z1/ppermute | solution.py:504
  72.3 7.8 %copy-start.18 = (bf16[768,384]{1,0:T(8,128)(2,1)S(1)}, bf16[768,384]{1,0:T(8,128)(2,1)}, u32[]{:S(2)}) copy-start(bf16[768,384]{1,0:T(8,128)(2,1)} %wk_ref.1) | copy-start | bytes 1769476
  72.3 7.8 %copy-start.20 = (bf16[768,384]{1,0:T(8,128)(2,1)S(1)}, bf16[768,384]{1,0:T(8,128)(2,1)}, u32[]{:S(2)}) copy-start(bf16[768,384]{1,0:T(8,128)(2,1)} %wv_ref.1) | copy-start | bytes 1769476
  72.3 7.8 %copy-start.22 = (bf16[384,768]{1,0:T(8,128)(2,1)S(1)}, bf16[384,768]{1,0:T(8,128)(2,1)}, u32[]{:S(2)}) copy-start(bf16[384,768]{1,0:T(8,128)(2,1)} %wo_ref.1) | copy-start | bytes 1769476
  72.3 7.8 %copy-start.24 = (bf16[512,384]{1,0:T(8,128)(2,1)S(1)}, bf16[512,384]{1,0:T(8,128)(2,1)}, u32[]{:S(2)}) copy-start(bf16[512,384]{1,0:T(8,128)(2,1)} %copy-done.23) | copy-start | bytes 1179652
  72.3 7.8 %copy-start.26 = (bf16[512,384]{1,0:T(8,128)(2,1)S(1)}, bf16[512,384]{1,0:T(8,128)(2,1)}, u32[]{:S(2)}) copy-start(bf16[512,384]{1,0:T(8,128)(2,1)} %copy-done.25) | copy-start | bytes 1179652
  72.3 7.8 %copy-start.28 = (bf16[512,384]{1,0:T(8,128)(2,1)S(1)}, bf16[512,384]{1,0:T(8,128)(2,1)}, u32[]{:S(2)}) copy-start(bf16[512,384]{1,0:T(8,128)(2,1)} %copy-done.27) | copy-start | bytes 1179652
  72.4 7.8 %copy-start.32 = (f32[256,128]{1,0:T(8,128)S(1)}, f32[256,128]{1,0:T(8,128)}, u32[]{:S(2)}) copy-start(f32[256,128]{1,0:T(8,128)} %constant.4.clone.cos_in.cos_ref) | copy-start | bytes 393220
  73.6 25.9 %collective-permute-start.5 = (f32[4,96,512]{2,1,0:T(8,128)}, f32[4,96,512]{2,1,0:T(8,128)S(1)}, u32[]{:S(2)}, u32[]{:S(2)}) collective-permute-start(f32[4,96,512]{2,1,0:T(8,128)} %get-tuple-element.249), channel_id=1, source_target_pairs={{0,4},{1,3},{2,6},{3,1},{4,0},{5,7},{6,2},{7,5},{8,12},{9,11},{10,... | collective-permute-start | bytes 2359304 | tf_op jit(solution)/shard_map/down_sum_second/ppermute | solution.py:504
  75.7 4.5 %copy-start.12 = (bf16[512,768]{1,0:T(8,128)(2,1)S(1)}, bf16[512,768]{1,0:T(8,128)(2,1)}, u32[]{:S(2)}) copy-start(bf16[512,768]{1,0:T(8,128)(2,1)} %cot_ref.1) | copy-start | bytes 2359300
  75.7 4.5 %copy-start.14 = (bf16[512,768]{1,0:T(8,128)(2,1)S(1)}, bf16[512,768]{1,0:T(8,128)(2,1)}, u32[]{:S(2)}) copy-start(bf16[512,768]{1,0:T(8,128)(2,1)} %copy-done.13) | copy-start | bytes 2359300
  75.7 4.5 %copy-start.16 = (bf16[768,384]{1,0:T(8,128)(2,1)S(1)}, bf16[768,384]{1,0:T(8,128)(2,1)}, u32[]{:S(2)}) copy-start(bf16[768,384]{1,0:T(8,128)(2,1)} %wq_ref.1) | copy-start | bytes 1769476
  75.7 4.5 %copy-start.30 = (f32[256,128]{1,0:T(8,128)S(1)}, f32[256,128]{1,0:T(8,128)}, u32[]{:S(2)}) copy-start(f32[256,128]{1,0:T(8,128)} %constant.5.clone.sin_in.sin_ref) | copy-start | bytes 393220
  75.8 22.6 %collective-permute-start.6 = (f32[4,96,256]{2,1,0:T(8,128)S(1)}, f32[4,96,256]{2,1,0:T(8,128)}, u32[]{:S(2)}, u32[]{:S(2)}) collective-permute-start(f32[4,96,256]{2,1,0:T(8,128)S(1)} %get-tuple-element.257), channel_id=1, source_target_pairs={{0,16},{1,17},{2,18},{3,19},{4,20},{5,21},{6,22},{7,23},{8,24},{9,... | collective-permute-start | bytes 1179656 | tf_op jit(solution)/shard_map/down_stack_sum_z2/ppermute | solution.py:504
  99.5 19.2 %collective-permute-start.4 = (f32[512,768]{1,0:T(8,128)S(1)}, f32[512,768]{1,0:T(8,128)S(1)}, u32[]{:S(2)}, u32[]{:S(2)}) collective-permute-start(f32[512,768]{1,0:T(8,128)S(1)} %get-tuple-element.157.mine_ref), channel_id=1, source_target_pairs={{0,1},{1,0},{2,3},{3,2},{4,5},{5,4},{6,7},{7,6},{8,9},{9,8},{10,11... | collective-permute-start | bytes 4718600 | tf_op jit(solution)/shard_map/ppermute | solution.py:499
  106.4 27.3 %collective-permute-start.12 = (f32[4,192,384]{2,1,0:T(8,128)S(1)}, f32[4,192,384]{2,1,0:T(8,128)S(1)}, u32[]{:S(2)}, u32[]{:S(2)}) collective-permute-start(f32[4,192,384]{2,1,0:T(8,128)S(1)} %get-tuple-element.247), channel_id=1, source_target_pairs={{0,4},{1,3},{2,6},{3,1},{4,0},{5,7},{6,2},{7,5},{8,12},{9,11},{10,... | collective-permute-start | bytes 3538952 | tf_op jit(solution)/shard_map/up_sum_second/ppermute | solution.py:504
  108.5 10.2 %collective-permute-start.7 = (f32[2,96,512]{2,1,0:T(8,128)S(1)}, f32[2,96,512]{2,1,0:T(8,128)S(1)}, u32[]{:S(2)}, u32[]{:S(2)}) collective-permute-start(f32[2,96,512]{2,1,0:T(8,128)S(1)} %get-tuple-element.254), channel_id=1, source_target_pairs={{0,8},{1,9},{2,10},{3,11},{4,12},{5,13},{6,14},{7,15},{8,0},{9,1},... | collective-permute-start | bytes 1179656 | tf_op jit(solution)/shard_map/down_sum_z1/ppermute | solution.py:504
  110.1 56.9 %collective-permute-start.9 = (f32[784,384]{1,0:T(8,128)S(1)}, f32[784,384]{1,0:T(8,128)S(1)}, u32[]{:S(2)}, u32[]{:S(2)}) collective-permute-start(f32[784,384]{1,0:T(8,128)S(1)} %pad_maximum_fusion.2), channel_id=1, source_target_pairs={{0,2},{1,5},{2,0},{3,7},{4,6},{5,1},{6,4},{7,3},{8,10},{9,13},{10,... | collective-permute-start | bytes 3612680 | tf_op jit(solution)/shard_map/attention_sum_first/ppermute | solution.py:504
  133.8 21.8 %collective-permute-start.14 = (f32[2,192,384]{2,1,0:T(8,128)S(1)}, f32[2,192,384]{2,1,0:T(8,128)S(1)}, u32[]{:S(2)}, u32[]{:S(2)}) collective-permute-start(f32[2,192,384]{2,1,0:T(8,128)S(1)} %get-tuple-element.253), channel_id=1, source_target_pairs={{0,8},{1,9},{2,10},{3,11},{4,12},{5,13},{6,14},{7,15},{8,0},{9,1},... | collective-permute-start | bytes 1769480 | tf_op jit(solution)/shard_map/up_sum_z1/ppermute | solution.py:504
  137.5 5.7 %collective-permute-start.11 = (f32[2,96,256]{2,1,0:T(8,128)S(1)}, f32[2,96,256]{2,1,0:T(8,128)S(1)}, u32[]{:S(2)}, u32[]{:S(2)}) collective-permute-start(f32[2,96,256]{2,1,0:T(8,128)S(1)} %get-tuple-element.267), channel_id=1, source_target_pairs={{0,2},{1,5},{2,0},{3,7},{4,6},{5,1},{6,4},{7,3},{8,10},{9,13},{10,... | collective-permute-start | bytes 589832 | tf_op jit(solution)/shard_map/down_stack_sum_first/ppermute | solution.py:504
  138.8 28.6 %collective-permute-start.17 = (f32[2,4,96,384]{3,2,1,0:T(8,128)S(1)}, f32[2,4,96,384]{3,2,1,0:T(8,128)S(1)}, u32[]{:S(2)}, u32[]{:S(2)}) collective-permute-start(f32[2,4,96,384]{3,2,1,0:T(8,128)S(1)} %get-tuple-element.186), channel_id=1, source_target_pairs={{0,2},{1,5},{2,0},{3,7},{4,6},{5,1},{6,4},{7,3},{8,10},{9,13},{10,... | collective-permute-start | bytes 3538952 | tf_op jit(solution)/shard_map/attention_rest_sum_first/ppermute | solution.py:504
  139.6 12.5 %collective-permute-start.10 = (f32[1,96,512]{2,1,0:T(8,128)S(1)}, f32[1,96,512]{2,1,0:T(8,128)S(1)}, u32[]{:S(2)}, u32[]{:S(2)}) collective-permute-start(f32[1,96,512]{2,1,0:T(8,128)S(1)} %get-tuple-element.269), channel_id=1, source_target_pairs={{0,16},{1,17},{2,18},{3,19},{4,20},{5,21},{6,22},{7,23},{8,24},{9,... | collective-permute-start | bytes 589832 | tf_op jit(solution)/shard_map/down_sum_z2/ppermute | solution.py:504
  152.1 14.8 %collective-permute-start.13 = (f32[1,96,512]{2,1,0:T(8,128)S(1)}, f32[1,96,512]{2,1,0:T(8,128)S(1)}, u32[]{:S(2)}, u32[]{:S(2)}) collective-permute-start(f32[1,96,512]{2,1,0:T(8,128)S(1)} %add.134), channel_id=1, source_target_pairs={{0,16},{1,17},{2,18},{3,19},{4,20},{5,21},{6,22},{7,23},{8,24},{9,... | collective-permute-start | bytes 589832 | tf_op jit(solution)/shard_map/down_gather_z2/ppermute | solution.py:504
  155.7 15.6 %collective-permute-start.20 = (f32[1,192,384]{2,1,0:T(8,128)S(1)}, f32[1,192,384]{2,1,0:T(8,128)S(1)}, u32[]{:S(2)}, u32[]{:S(2)}) collective-permute-start(f32[1,192,384]{2,1,0:T(8,128)S(1)} %get-tuple-element.263), channel_id=1, source_target_pairs={{0,16},{1,17},{2,18},{3,19},{4,20},{5,21},{6,22},{7,23},{8,24},{9,... | collective-permute-start | bytes 884744 | tf_op jit(solution)/shard_map/up_sum_z2/ppermute | solution.py:504
  166.9 10.5 %collective-permute-start.19 = (f32[2,96,512]{2,1,0:T(8,128)S(1)}, f32[2,96,512]{2,1,0:T(8,128)S(1)}, u32[]{:S(2)}, u32[]{:S(2)}) collective-permute-start(f32[2,96,512]{2,1,0:T(8,128)S(1)} %constant_dynamic-update-slice_fusion), channel_id=1, source_target_pairs={{0,8},{1,9},{2,10},{3,11},{4,12},{5,13},{6,14},{7,15},{8,0},{9,1},... | collective-permute-start | bytes 1179656 | tf_op jit(solution)/shard_map/down_gather_z1/ppermute | solution.py:504
  167.5 18.4 %collective-permute-start.18 = (f32[4,96,384]{2,1,0:T(8,128)S(1)}, f32[4,96,384]{2,1,0:T(8,128)S(1)}, u32[]{:S(2)}, u32[]{:S(2)}) collective-permute-start(f32[4,96,384]{2,1,0:T(8,128)S(1)} %get-tuple-element.250), channel_id=1, source_target_pairs={{0,4},{1,3},{2,6},{3,1},{4,0},{5,7},{6,2},{7,5},{8,12},{9,11},{10,... | collective-permute-start | bytes 1769480 | tf_op jit(solution)/shard_map/attention_rest_sum_second/ppermute | solution.py:504
  177.5 19.0 %collective-permute-start.22 = (f32[4,96,512]{2,1,0:T(8,128)S(1)}, f32[4,96,512]{2,1,0:T(8,128)S(1)}, u32[]{:S(2)}, u32[]{:S(2)}) collective-permute-start(f32[4,96,512]{2,1,0:T(8,128)S(1)} %constant_dynamic-update-slice_fusion.2), channel_id=1, source_target_pairs={{0,4},{1,3},{2,6},{3,1},{4,0},{5,7},{6,2},{7,5},{8,12},{9,11},{10,... | collective-permute-start | bytes 2359304 | tf_op jit(solution)/shard_map/down_gather_second/ppermute | solution.py:504
  183.9 10.5 %collective-permute-start.23 = (f32[1,192,384]{2,1,0:T(8,128)S(1)}, f32[1,192,384]{2,1,0:T(8,128)S(1)}, u32[]{:S(2)}, u32[]{:S(2)}) collective-permute-start(f32[1,192,384]{2,1,0:T(8,128)S(1)} %add.144), channel_id=1, source_target_pairs={{0,16},{1,17},{2,18},{3,19},{4,20},{5,21},{6,22},{7,23},{8,24},{9,... | collective-permute-start | bytes 884744 | tf_op jit(solution)/shard_map/up_gather_z2/ppermute | solution.py:504
  183.9 17.5 %collective-permute-start.16 = (f32[1,96,256]{2,1,0:T(8,128)S(1)}, f32[1,96,256]{2,1,0:T(8,128)S(1)}, u32[]{:S(2)}, u32[]{:S(2)}) collective-permute-start(f32[1,96,256]{2,1,0:T(8,128)S(1)} %get-tuple-element.279), channel_id=1, source_target_pairs={{0,4},{1,3},{2,6},{3,1},{4,0},{5,7},{6,2},{7,5},{8,12},{9,11},{10,... | collective-permute-start | bytes 294920 | tf_op jit(solution)/shard_map/down_stack_sum_second/ppermute | solution.py:504
  184.1 19.9 %collective-permute-start.15 = (f32[400,384]{1,0:T(8,128)S(1)}, f32[400,384]{1,0:T(8,128)S(1)}, u32[]{:S(2)}, u32[]{:S(2)}) collective-permute-start(f32[400,384]{1,0:T(8,128)S(1)} %pad_maximum_fusion.6), channel_id=1, source_target_pairs={{0,4},{1,3},{2,6},{3,1},{4,0},{5,7},{6,2},{7,5},{8,12},{9,11},{10,... | collective-permute-start | bytes 1843208 | tf_op jit(solution)/shard_map/attention_sum_second/ppermute | solution.py:504
  186.0 11.8 %collective-permute-start.21 = (f32[2,96,384]{2,1,0:T(8,128)S(1)}, f32[2,96,384]{2,1,0:T(8,128)S(1)}, u32[]{:S(2)}, u32[]{:S(2)}) collective-permute-start(f32[2,96,384]{2,1,0:T(8,128)S(1)} %get-tuple-element.260), channel_id=1, source_target_pairs={{0,8},{1,9},{2,10},{3,11},{4,12},{5,13},{6,14},{7,15},{8,0},{9,1},... | collective-permute-start | bytes 884744 | tf_op jit(solution)/shard_map/attention_rest_sum_z1/ppermute | solution.py:504
  194.5 14.5 %collective-permute-start.25 = (f32[2,192,384]{2,1,0:T(8,128)S(1)}, f32[2,192,384]{2,1,0:T(8,128)S(1)}, u32[]{:S(2)}, u32[]{:S(2)}) collective-permute-start(f32[2,192,384]{2,1,0:T(8,128)S(1)} %constant_dynamic-update-slice_fusion.4), channel_id=1, source_target_pairs={{0,8},{1,9},{2,10},{3,11},{4,12},{5,13},{6,14},{7,15},{8,0},{9,1},... | collective-permute-start | bytes 1769480 | tf_op jit(solution)/shard_map/up_gather_z1/ppermute | solution.py:504
  197.9 11.1 %collective-permute-start.26 = (f32[1,96,384]{2,1,0:T(8,128)S(1)}, f32[1,96,384]{2,1,0:T(8,128)S(1)}, u32[]{:S(2)}, u32[]{:S(2)}) collective-permute-start(f32[1,96,384]{2,1,0:T(8,128)S(1)} %get-tuple-element.275), channel_id=1, source_target_pairs={{0,16},{1,17},{2,18},{3,19},{4,20},{5,21},{6,22},{7,23},{8,24},{9,... | collective-permute-start | bytes 442376 | tf_op jit(solution)/shard_map/attention_rest_sum_z2/ppermute | solution.py:504
  201.4 5.2 %collective-permute-start.27 = (f32[1,96,256]{2,1,0:T(8,128)S(1)}, f32[1,96,256]{2,1,0:T(8,128)S(1)}, u32[]{:S(2)}, u32[]{:S(2)}) collective-permute-start(f32[1,96,256]{2,1,0:T(8,128)S(1)} %add.148), channel_id=1, source_target_pairs={{0,4},{1,3},{2,6},{3,1},{4,0},{5,7},{6,2},{7,5},{8,12},{9,11},{10,... | collective-permute-start | bytes 294920 | tf_op jit(solution)/shard_map/down_stack_gather_second/ppermute | solution.py:504
  209.1 26.0 %collective-permute-start.29 = (f32[4,192,384]{2,1,0:T(8,128)S(1)}, f32[4,192,384]{2,1,0:T(8,128)S(1)}, u32[]{:S(2)}, u32[]{:S(2)}) collective-permute-start(f32[4,192,384]{2,1,0:T(8,128)S(1)} %constant_dynamic-update-slice_fusion.8), channel_id=1, source_target_pairs={{0,4},{1,3},{2,6},{3,1},{4,0},{5,7},{6,2},{7,5},{8,12},{9,11},{10,... | collective-permute-start | bytes 3538952 | tf_op jit(solution)/shard_map/up_gather_second/ppermute | solution.py:504
  218.8 10.4 %collective-permute-start.24 = (f32[208,384]{1,0:T(8,128)S(1)}, f32[208,384]{1,0:T(8,128)S(1)}, u32[]{:S(2)}, u32[]{:S(2)}) collective-permute-start(f32[208,384]{1,0:T(8,128)S(1)} %pad_maximum_fusion.7), channel_id=1, source_target_pairs={{0,8},{1,9},{2,10},{3,11},{4,12},{5,13},{6,14},{7,15},{8,0},{9,1},... | collective-permute-start | bytes 958472 | tf_op jit(solution)/shard_map/attention_sum_z1/ppermute | solution.py:504
  219.4 24.5 %collective-permute-start.33 = (f32[2,96,256]{2,1,0:T(8,128)S(1)}, f32[2,96,256]{2,1,0:T(8,128)S(1)}, u32[]{:S(2)}, u32[]{:S(2)}) collective-permute-start(f32[2,96,256]{2,1,0:T(8,128)S(1)} %constant_dynamic-update-slice_fusion.6), channel_id=1, source_target_pairs={{0,2},{1,5},{2,0},{3,7},{4,6},{5,1},{6,4},{7,3},{8,10},{9,13},{10,... | collective-permute-start | bytes 589832 | tf_op jit(solution)/shard_map/down_stack_gather_first/ppermute | solution.py:504
  220.6 10.9 %collective-permute-start.30 = (f32[1,96,384]{2,1,0:T(8,128)S(1)}, f32[1,96,384]{2,1,0:T(8,128)S(1)}, u32[]{:S(2)}, u32[]{:S(2)}) collective-permute-start(f32[1,96,384]{2,1,0:T(8,128)S(1)} %add.153), channel_id=1, source_target_pairs={{0,16},{1,17},{2,18},{3,19},{4,20},{5,21},{6,22},{7,23},{8,24},{9,... | collective-permute-start | bytes 442376 | tf_op jit(solution)/shard_map/attention_rest_gather_z2/ppermute | solution.py:504
  229.3 10.6 %collective-permute-start.28 = (f32[112,384]{1,0:T(8,128)S(1)}, f32[112,384]{1,0:T(8,128)S(1)}, u32[]{:S(2)}, u32[]{:S(2)}) collective-permute-start(f32[112,384]{1,0:T(8,128)S(1)} %pad_maximum_fusion.8), channel_id=1, source_target_pairs={{0,16},{1,17},{2,18},{3,19},{4,20},{5,21},{6,22},{7,23},{8,24},{9,... | collective-permute-start | bytes 516104 | tf_op jit(solution)/shard_map/attention_sum_z2/ppermute | solution.py:504
  231.5 9.6 %collective-permute-start.34 = (f32[2,96,384]{2,1,0:T(8,128)S(1)}, f32[2,96,384]{2,1,0:T(8,128)S(1)}, u32[]{:S(2)}, u32[]{:S(2)}) collective-permute-start(f32[2,96,384]{2,1,0:T(8,128)S(1)} %constant_dynamic-update-slice_fusion.10), channel_id=1, source_target_pairs={{0,8},{1,9},{2,10},{3,11},{4,12},{5,13},{6,14},{7,15},{8,0},{9,1},... | collective-permute-start | bytes 884744 | tf_op jit(solution)/shard_map/attention_rest_gather_z1/ppermute | solution.py:504
  239.9 7.7 %collective-permute-start.32 = (f32[1,96,384]{2,1,0:T(8,128)S(1)}, f32[1,96,384]{2,1,0:T(8,128)S(1)}, u32[]{:S(2)}, u32[]{:S(2)}) collective-permute-start(f32[1,96,384]{2,1,0:T(8,128)S(1)} %bitcast_add_fusion), channel_id=1, source_target_pairs={{0,16},{1,17},{2,18},{3,19},{4,20},{5,21},{6,22},{7,23},{8,24},{9,... | collective-permute-start | bytes 442376 | tf_op jit(solution)/shard_map/attention_gather_z2/ppermute | solution.py:504
  241.2 11.5 %collective-permute-start.36 = (f32[4,96,384]{2,1,0:T(8,128)S(1)}, f32[4,96,384]{2,1,0:T(8,128)S(1)}, u32[]{:S(2)}, u32[]{:S(2)}) collective-permute-start(f32[4,96,384]{2,1,0:T(8,128)S(1)} %constant_dynamic-update-slice_fusion.12), channel_id=1, source_target_pairs={{0,4},{1,3},{2,6},{3,1},{4,0},{5,7},{6,2},{7,5},{8,12},{9,11},{10,... | collective-permute-start | bytes 1769480 | tf_op jit(solution)/shard_map/attention_rest_gather_second/ppermute | solution.py:504
  247.6 6.8 %collective-permute-start.35 = (f32[2,96,384]{2,1,0:T(8,128)S(1)}, f32[2,96,384]{2,1,0:T(8,128)S(1)}, u32[]{:S(2)}, u32[]{:S(2)}) collective-permute-start(f32[2,96,384]{2,1,0:T(8,128)S(1)} %constant_dynamic-update-slice_fusion.16), channel_id=1, source_target_pairs={{0,8},{1,9},{2,10},{3,11},{4,12},{5,13},{6,14},{7,15},{8,0},{9,1},... | collective-permute-start | bytes 884744 | tf_op jit(solution)/shard_map/attention_gather_z1/ppermute | solution.py:504
  248.2 57.4 %collective-permute-start.40 = (f32[2,4,192,384]{3,2,1,0:T(8,128)S(1)}, f32[2,4,192,384]{3,2,1,0:T(8,128)}, u32[]{:S(2)}, u32[]{:S(2)}) collective-permute-start(f32[2,4,192,384]{3,2,1,0:T(8,128)S(1)} %pad_maximum_fusion.own_ref), channel_id=1, source_target_pairs={{0,2},{1,5},{2,0},{3,7},{4,6},{5,1},{6,4},{7,3},{8,10},{9,13},{10,... | collective-permute-start | bytes 7077896 | tf_op jit(solution)/shard_map/up_gather_first/ppermute | solution.py:504
  254.5 18.7 %collective-permute-start.37 = (f32[4,96,384]{2,1,0:T(8,128)S(1)}, f32[4,96,384]{2,1,0:T(8,128)S(1)}, u32[]{:S(2)}, u32[]{:S(2)}) collective-permute-start(f32[4,96,384]{2,1,0:T(8,128)S(1)} %constant_dynamic-update-slice_fusion.18), channel_id=1, source_target_pairs={{0,4},{1,3},{2,6},{3,1},{4,0},{5,7},{6,2},{7,5},{8,12},{9,11},{10,... | collective-permute-start | bytes 1769480 | tf_op jit(solution)/shard_map/attention_gather_second/ppermute | solution.py:504
  258.9 41.4 %collective-permute-start.41 = (f32[2,4,96,512]{3,2,1,0:T(8,128)}, f32[2,4,96,512]{3,2,1,0:T(8,128)}, u32[]{:S(2)}, u32[]{:S(2)}) collective-permute-start(f32[2,4,96,512]{3,2,1,0:T(8,128)} %pad_maximum_fusion.1.own_ref), channel_id=1, source_target_pairs={{0,2},{1,5},{2,0},{3,7},{4,6},{5,1},{6,4},{7,3},{8,10},{9,13},{10,... | collective-permute-start | bytes 4718600 | tf_op jit(solution)/shard_map/down_gather_first/ppermute | solution.py:504
  259.9 19.1 %collective-permute-start.42 = (f32[4,96,256]{2,1,0:T(8,128)S(1)}, f32[4,96,256]{2,1,0:T(8,128)S(1)}, u32[]{:S(2)}, u32[]{:S(2)}) collective-permute-start(f32[4,96,256]{2,1,0:T(8,128)S(1)} %constant_dynamic-update-slice_fusion.14), channel_id=1, source_target_pairs={{0,16},{1,17},{2,18},{3,19},{4,20},{5,21},{6,22},{7,23},{8,24},{9,... | collective-permute-start | bytes 1179656 | tf_op jit(solution)/shard_map/down_stack_gather_z2/ppermute | solution.py:504
  260.6 52.4 %collective-permute-start.39 = (f32[2,4,96,384]{3,2,1,0:T(8,128)S(1)}, f32[2,4,96,384]{3,2,1,0:T(8,128)}, u32[]{:S(2)}, u32[]{:S(2)}) collective-permute-start(f32[2,4,96,384]{3,2,1,0:T(8,128)S(1)} %pad_maximum_fusion.3.own_b), channel_id=1, source_target_pairs={{0,2},{1,5},{2,0},{3,7},{4,6},{5,1},{6,4},{7,3},{8,10},{9,13},{10,... | collective-permute-start | bytes 3538952 | tf_op jit(solution)/shard_map/attention_rest_gather_first/ppermute | solution.py:504
  274.3 51.3 %collective-permute-start.38 = (f32[2,4,96,384]{3,2,1,0:T(8,128)}, f32[2,4,96,384]{3,2,1,0:T(8,128)}, u32[]{:S(2)}, u32[]{:S(2)}) collective-permute-start(f32[2,4,96,384]{3,2,1,0:T(8,128)} %pad_maximum_fusion.4.own_a), channel_id=1, source_target_pairs={{0,2},{1,5},{2,0},{3,7},{4,6},{5,1},{6,4},{7,3},{8,10},{9,13},{10,... | collective-permute-start | bytes 3538952 | tf_op jit(solution)/shard_map/attention_gather_first/ppermute | solution.py:504
  275.3 5.5 %copy-start.35 = (f32[16,384]{1,0:T(8,128)}, f32[16,384]{1,0:T(8,128)S(1)}, u32[]{:S(2)}) copy-start(f32[16,384]{1,0:T(8,128)S(1)} %slice_add_fusion.19) | copy-start | bytes 73732
  279.0 1.2 collective-permute-start.31
  280.8 20.0 %collective-permute-start.43 = (f32[2,4,96,256]{3,2,1,0:T(8,128)}, f32[2,4,96,256]{3,2,1,0:T(8,128)}, u32[]{:S(2)}, u32[]{:S(2)}) collective-permute-start(f32[2,4,96,256]{3,2,1,0:T(8,128)} %pad_maximum_fusion.5.z_own_ref), channel_id=1, source_target_pairs={{0,8},{1,9},{2,10},{3,11},{4,12},{5,13},{6,14},{7,15},{8,0},{9,1},... | collective-permute-start | bytes 2359304 | tf_op jit(solution)/shard_map/down_stack_gather_z1/ppermute | solution.py:504
  (21 other events, 25.3 us)

commit v3 on v2

--- a/solution.py
+++ b/solution.py
@@ -30,7 +30,7 @@
 FIRST, SECOND = (X, Y), (Y, X)
 Z_SLOTS = (0, 2, 1, 3)
 
-ORDER = "dPcuTdcKcdudIuacbdudabudbudbcacbuabuabcabacdacuba"
+ORDER = "dcudcKcdudIuacbdudabudbudbcacbuabuabcabacdacuba"
 
 CASES = ((0, 0, 256, 0), (128, 256, 384, 128), (256, 640, 128, 128), (384, 768, 256, 128))
 TILES = (
@@ -142,29 +142,49 @@
     return copies
 
 
+class Sender:
+    def __init__(self, sems):
+        self.sems, self.copies = sems, []
+
+    def send(self, source, target):
+        self.copies.append(pltpu.make_async_copy(source, target, self.sems.at[len(self.copies)]))
+        self.copies[-1].start()
+
+    def finish(self):
+        for copy in self.copies:
+            copy.wait()
+
+
 def attention_forward(
-    lengths_ref, pads_ref, gain_ref, x_in, wq_in, wk_in, wv_in, cos_in, sin_in, wo_in,
-    normed_ref, q_ref, k_ref, v_ref, att_ref, prob_ref, part_ref,
-    bias_ref, x_ref, wq_ref, wk_ref, wv_ref, cos_ref, sin_ref, wo_ref, sems,
+    lengths_in, pads_in, gain_in, x_in, wq_in, wk_in, wv_in, cos_in, sin_in, wo_in,
+    normed_out, q_out, k_out, v_out, att_out, prob_out, part_out,
+    bias_ref, lengths_ref, pads_ref, gain_ref, x_ref, wq_ref, wk_ref, wv_ref, cos_ref, sin_ref, wo_ref,
+    normed_ref, q_ref, k_ref, v_ref, att_ref, prob_ref, part_ref, sems, out_sems,
 ):
+    first = fetch(((lengths_in, lengths_ref), (pads_in, pads_ref), (x_in, x_ref), (gain_in, gain_ref)), sems.at[:4])
     copies = fetch(
         (
-            (x_in, x_ref), (wq_in, wq_ref), (wk_in, wk_ref), (wv_in, wv_ref),
-            (cos_in, cos_ref), (sin_in, sin_ref), (wo_in, wo_ref),
+            (wq_in, wq_ref), (wk_in, wk_ref), (wv_in, wv_ref), (cos_in, cos_ref), (sin_in, sin_ref), (wo_in, wo_ref),
         ),
-        sems,
+        sems.at[4:],
     )
+    sender = Sender(out_sems)
+    first[0].wait()
+    first[1].wait()
     heads_cols = wq_ref.shape[1]
     pairs = heads_cols // LANES
     fill_bias(lengths_ref, pads_ref, bias_ref)
-    copies[0].wait()
+    first[2].wait()
+    first[3].wait()
+    gain = gain_ref[...].reshape(1, -1)
 
     @pl.loop(0, x_ref.shape[0] // 64)
     def _(i):
         rows = pl.ds(pl.multiple_of(i * 64, 64), 64)
-        normed_ref[rows, :] = layer_norm_rows(x_ref[rows, :].astype(f32), gain_ref[...]).astype(bf16)
-
-    for copy in copies[1:6]:
+        normed_ref[rows, :] = layer_norm_rows(x_ref[rows, :].astype(f32), gain).astype(bf16)
+
+    sender.send(normed_ref, normed_out)
+    for copy in copies[:5]:
         copy.wait()
     for block in range(4):
         rows = slice(block * HALF, block * HALF + HALF)
@@ -180,6 +200,8 @@
             turned = key[:, cols] * cosine + swap_halves(key[:, cols]) * sine
             k_ref[key_rows, cols] = turned.astype(bf16)
         v_ref[key_rows, :] = mm(normed, wv_ref[...]).astype(bf16)
+    for source, target in ((q_ref, q_out), (k_ref, k_out), (v_ref, v_out)):
+        sender.send(source, target)
 
     for t in range(pairs):
         cols = slice(t * LANES, (t + 1) * LANES)
@@ -199,11 +221,15 @@
                 mixed[case] = part if mixed[case] is None else mixed[case] + part
         for case, (query_row, _, _, _) in enumerate(CASES):
             att_ref[query_row : query_row + HALF, cols] = mixed[case].astype(bf16)
-
-    copies[6].wait()
+        sender.send(prob_ref.at[2 * t : 2 * t + 2], prob_out.at[2 * t : 2 * t + 2])
+
+    sender.send(att_ref, att_out)
+    copies[5].wait()
     for block in range(2):
         rows = slice(block * 256, block * 256 + 256)
         part_ref[rows, :] = mm(att_ref[rows, :], wo_ref[...])
+        sender.send(part_ref.at[rows, :], part_out.at[rows, :])
+    sender.finish()
 
 
 def fourths(start, part):
@@ -241,28 +267,38 @@
 
 
 def mlp_kernel(
-    gain_ref, bu_ref, mine_ref, theirs_ref, x_in, wu_in, wd_in, cot_in,
-    residual_ref, normed_ref, act_ref, du_ref, gbu_ref, gbd_ref, *outs_and_scratch,
+    gain_in, bu_in, x_in, mine_in, theirs_in, cot_in, wu_in, wd_in,
+    residual_out, gbu_ref, gbd_ref, d_kept, d_sent, c_kept, c_sent, u_kept, u_sent, shares_out,
+    gain_ref, bu_ref, x_ref, mine_ref, theirs_ref, cot_ref, wu_ref, wd_ref,
+    residual_ref, normed_ref, act_ref, du_ref, d_kept_ref, d_sent_ref, c_kept_ref, c_sent_ref, u_kept_ref, u_sent_ref, shares_ref,
+    sems, out_sems,
 ):
-    *outs, x_ref, wu_ref, wd_ref, cot_ref, sems = outs_and_scratch
-    copies = fetch(((x_in, x_ref), (cot_in, cot_ref), (wu_in, wu_ref), (wd_in, wd_ref)), sems)
     row_count = x_ref.shape[0]
     units = wu_ref.shape[1]
+    halves = (slice(0, row_count // 2), slice(row_count // 2, row_count))
+    pairs = [(gain_in, gain_ref), (bu_in, bu_ref)]
+    for rows in halves:
+        pairs += [(a.at[rows, :], b.at[rows, :]) for a, b in ((x_in, x_ref), (mine_in, mine_ref), (theirs_in, theirs_ref))]
+    copies = fetch(pairs + [(cot_in, cot_ref), (wu_in, wu_ref), (wd_in, wd_ref)], sems)
+    sender = Sender(out_sems)
     gbu_ref[...] = jnp.zeros_like(gbu_ref)
     gbd_ref[...] = jnp.zeros_like(gbd_ref)
     copies[0].wait()
-    copies[1].wait()
-
-    @pl.loop(0, row_count // 64)
-    def _(i):
-        rows = pl.ds(pl.multiple_of(i * 64, 64), 64)
-        residual = x_ref[rows, :].astype(f32) + (mine_ref[rows, :] + theirs_ref[rows, :])
-        residual_ref[rows, :] = residual
-        normed_ref[rows, :] = layer_norm_rows(residual, gain_ref[...]).astype(bf16)
-        gbd_ref[...] += jnp.sum(cot_ref[rows, :].astype(f32), axis=0, keepdims=True)
-
-    copies[2].wait()
-    copies[3].wait()
+    gain = gain_ref[...].reshape(1, -1)
+    for half in range(2):
+        for copy in copies[2 + 3 * half : 5 + 3 * half]:
+            copy.wait()
+
+        @pl.loop(0, row_count // 128)
+        def _(i, half=half):
+            rows = pl.ds(pl.multiple_of(half * (row_count // 2) + i * 64, 64), 64)
+            residual = x_ref[rows, :].astype(f32) + (mine_ref[rows, :] + theirs_ref[rows, :])
+            residual_ref[rows, :] = residual
+            normed_ref[rows, :] = layer_norm_rows(residual, gain).astype(bf16)
+
+    sender.send(residual_ref, residual_out)
+    for copy in (copies[1], *copies[8:]):
+        copy.wait()
     c0 = math.sqrt(2.0 / math.pi)
     c1 = c0 * 0.044715
 
@@ -271,7 +307,7 @@
         cols = pl.ds(pl.multiple_of(j * 256, 256), 256)
         for block in range(row_count // 256):
             rows = slice(block * 256, block * 256 + 256)
-            u = mm(normed_ref[rows, :], wu_ref[:, cols]) + bu_ref[:, cols]
+            u = mm(normed_ref[rows, :], wu_ref[:, cols]) + bu_ref[cols].reshape(1, -1)
             delta = nt(cot_ref[rows, :], wd_ref[cols, :])
             square = u * u
             t = jnp.tanh(u * (c0 + c1 * square))
@@ -284,25 +320,36 @@
 
     quarter = units // PLANE
     cut = cot_ref.shape[1] * 2 // 3
+    quarters = {}
     for place in range(PLANE):
-        cols = pl.ds(pl.multiple_of(quarter_at(place) * quarter, LANES), quarter)
-        grad = tn(act_ref[:, cols], cot_ref[...])
-        place_quarter(outs[:2], place, grad[:, :cut])
-        place_quarter_z_first(outs[2:], place, grad[:, cut:])
-
-
-def up_kernel(normed_ref, du_ref, *outs):
-    quarter = du_ref.shape[1] // PLANE
-    for place in range(PLANE):
-        cols = pl.ds(pl.multiple_of(quarter_at(place) * quarter, LANES), quarter)
-        place_quarter(outs, place, tn(normed_ref[...], du_ref[:, cols]))
-
-
-def tail_kernel(act_ref, du_ref, wu_ref, wd_ref, out_ref):
-    for block in range(act_ref.shape[0] // 256):
-        rows = slice(block * 256, block * 256 + 256)
-        out_ref[0, rows, :] = nt(du_ref[rows, :], wu_ref[...])
-        out_ref[1, rows, :] = mm(act_ref[rows, :], wd_ref[...])
+        quarters[place] = pl.ds(pl.multiple_of(quarter_at(place) * quarter, LANES), quarter)
+    for place in (2, 3, 0, 1):
+        grad = tn(act_ref[:, quarters[place]], cot_ref[...])
+        place_quarter((d_kept_ref, d_sent_ref), place, grad[:, :cut])
+        place_quarter_z_first((c_kept_ref, c_sent_ref), place, grad[:, cut:])
+        if place == 3:
+            sender.send(d_sent_ref, d_sent)
+    for source, target in ((c_sent_ref, c_sent), (d_kept_ref, d_kept), (c_kept_ref, c_kept)):
+        sender.send(source, target)
+    for place in (2, 3, 0, 1):
+        place_quarter((u_kept_ref, u_sent_ref), place, tn(normed_ref[...], du_ref[:, quarters[place]]))
+        if place == 3:
+            sender.send(u_sent_ref, u_sent)
+    sender.send(u_kept_ref, u_kept)
+    for share in range(2):
+        for rows in halves:
+            if share == 0:
+                shares_ref[share, rows, :] = nt(du_ref[rows, :], wu_ref[...])
+            else:
+                shares_ref[share, rows, :] = mm(act_ref[rows, :], wd_ref[...])
+        sender.send(shares_ref.at[share], shares_out.at[share])
+
+    @pl.loop(0, row_count // 64)
+    def _(i):
+        rows = pl.ds(pl.multiple_of(i * 64, 64), 64)
+        gbd_ref[...] += jnp.sum(cot_ref[rows, :].astype(f32), axis=0, keepdims=True)
+
+    sender.finish()
 
 
 def attention_backward(
@@ -463,20 +510,20 @@
 
 
 VMEM = pl.BlockSpec(memory_space=pltpu.VMEM)
-SMEM = pl.BlockSpec(memory_space=pltpu.SMEM)
 HBM = pl.BlockSpec(memory_space=pltpu.HBM)
 
 
-def call(kernel, outs, scalars=(), held=(), loose=(), scratch=(), flops=0, limit=40, out_space=VMEM):
-    ins = [*scalars, *held, *loose]
+def call(kernel, outs, held=(), loose=(), scratch=(), flops=0, limit=40, loose_outs=None):
+    ins = [*held, *loose]
     shapes = [jax.ShapeDtypeStruct(shape, dtype) for shape, dtype in outs]
     moved = sum(math.prod(a.shape) * a.dtype.itemsize for a in ins + shapes)
+    out_specs = [HBM if loose_outs and i in loose_outs else VMEM for i in range(len(outs))]
     return pl.pallas_call(
         kernel,
-        name=getattr(kernel, "__name__", "unpack_kernel"),
+        name=kernel.__name__,
         out_shape=shapes,
-        in_specs=[SMEM] * len(scalars) + [VMEM] * len(held) + [HBM] * len(loose),
-        out_specs=[out_space] * len(outs),
+        in_specs=[VMEM] * len(held) + [HBM] * len(loose),
+        out_specs=out_specs,
         scratch_shapes=[s if not isinstance(s, tuple) else pltpu.VMEM(*s) for s in scratch],
         compiler_params=pltpu.CompilerParams(vmem_limit_bytes=limit * 1024 * 1024),
         cost_estimate=pl.CostEstimate(flops=flops, bytes_accessed=moved, transcendentals=0),
@@ -569,79 +616,71 @@
         result.extend((own, got))
         yield
 
+    scores = (heads, HALF, 8 * LANES)
+    rows_of = {"width": ((rows, width), bf16), "heads": ((rows, heads_cols), bf16), "sum": ((rows, width), f32)}
+    outs = [rows_of["width"]] + [rows_of["heads"]] * 4 + [(scores, bf16), rows_of["sum"]]
     normed, q, k, v, attended, probs, branch = call(
         attention_forward,
-        [
-            ((rows, width), bf16),
-            ((rows, heads_cols), bf16),
-            ((rows, heads_cols), bf16),
-            ((rows, heads_cols), bf16),
-            ((rows, heads_cols), bf16),
-            ((heads, HALF, 8 * LANES), bf16),
-            ((rows, width), f32),
-        ],
-        scalars=[doc_lengths, pad_counts],
-        held=[gain_attn],
-        loose=[inputs, w_query, w_key, w_value, cosine, sine, w_out],
+        outs,
+        loose=[doc_lengths, pad_counts, norm_attn, inputs, w_query, w_key, w_value, cosine, sine, w_out],
         scratch=[
-            ((HALF, 8 * LANES), f32),
-            ((rows, width), bf16),
-            ((width, heads_cols), bf16),
-            ((width, heads_cols), bf16),
-            ((width, heads_cols), bf16),
+            (scores[1:], f32),
+            pltpu.SMEM(doc_lengths.shape, jnp.int32),
+            pltpu.SMEM(pad_counts.shape, jnp.int32),
+            (norm_attn.shape, f32),
+            rows_of["width"],
+            *[((width, heads_cols), bf16)] * 3,
             (cosine.shape, f32),
             (sine.shape, f32),
             ((heads_cols, width), bf16),
-            sems(7),
+            *outs,
+            sems(10),
+            sems(10),
         ],
         flops=2 * rows * width * heads_cols * 4,
+        limit=62,
+        loose_outs=range(7),
     )
     branch_other = swap(branch)
 
-    residual, normed_mlp, act, du, grad_bu, grad_bd, *down_parts = call(
+    big = [
+        *portions(units // GROUP, width * 2 // 3),
+        *portions(units // GROUP, width // 3),
+        *portions(width // STACK, units // PLANE),
+        ((2, rows, width), f32),
+    ]
+    residual, grad_bu, grad_bd, *parts, shares = call(
         mlp_kernel,
-        [
-            ((rows, width), f32),
-            ((rows, width), bf16),
+        [rows_of["sum"], ((1, units), f32), ((1, width), f32), *big],
+        loose=[norm_mlp, b_up, inputs, branch, branch_other, cotangent, w_up, w_down],
+        scratch=[
+            (norm_mlp.shape, f32),
+            (b_up.shape, f32),
+            rows_of["width"],
+            rows_of["sum"],
+            rows_of["sum"],
+            rows_of["width"],
+            ((width, units), bf16),
+            ((units, width), bf16),
+            rows_of["sum"],
+            rows_of["width"],
             ((rows, units), bf16),
             ((rows, units), bf16),
-            ((1, units), f32),
-            ((1, width), f32),
-        ]
-        + portions(units // GROUP, width * 2 // 3)
-        + portions(units // GROUP, width // 3),
-        held=[gain_mlp, b_up.reshape(1, -1), branch, branch_other],
-        loose=[inputs, w_up, w_down, cotangent],
-        scratch=[
-            ((rows, width), bf16),
-            ((width, units), bf16),
-            ((units, width), bf16),
-            ((rows, width), bf16),
-            sems(4),
+            *big,
+            sems(11),
+            sems(9),
         ],
-        flops=2 * rows * width * units * 3,
+        flops=2 * rows * width * units * 6,
+        limit=62,
+        loose_outs=(0, *range(3, 10)),
     )
     made, grads = {key: [] for key in "dcuab"}, {}
-    chains = {"d": chain("down", down_parts[:2], made["d"]), "c": chain("down_stack", down_parts[2:], made["c"], True)}
-    state = {}
-
-    def tail():
-        operands = turn(act, du)
-        (state["shares"],) = call(
-            tail_kernel, [((2, rows, width), f32)], held=[*operands, w_up, w_down], flops=2 * rows * width * units * 2
-        )
-        state["shares_other"] = swap(did(state["shares"]))
-
-    def grad_up_parts():
-        operands = turn(normed_mlp, du)
-        parts = call(
-            up_kernel,
-            portions(width // STACK, units // PLANE),
-            held=operands,
-            flops=2 * rows * width * units,
-        )
-        did(parts[0])
-        chains["u"] = chain("up", parts, made["u"])
+    chains = {
+        "d": chain("down", parts[:2], made["d"]),
+        "c": chain("down_stack", parts[2:4], made["c"], True),
+        "u": chain("up", parts[4:], made["u"]),
+    }
+    state = {"shares_other": swap(shares)}
 
     def backward():
         (shares_other,) = turn(state["shares_other"])
@@ -650,7 +689,7 @@
             [((rows, width), bf16), ((rows, width), f32), ((16, half), f32), ((rows, width), f32)]
             + portions(half // STACK, half) * 2,
             held=[
-                state["shares"], shares_other, residual, gain_mlp, cotangent, attended, w_out, q, k, v, probs,
+                shares, shares_other, residual, gain_mlp, cotangent, attended, w_out, q, k, v, probs,
                 normed, w_query, w_key, w_value, cosine, sine, inputs, b_down.reshape(1, -1), grad_bd, grad_bu,
             ],
             scratch=[
@@ -693,11 +732,11 @@
                 [((heads_cols, width), f32)] + [((width, heads_cols), f32)] * 3,
                 held=made["a"][1:] + made["b"],
                 scratch=[((PLANE, 2, half, half), f32), sems(8)],
-                out_space=HBM,
+                loose_outs=range(4),
             )
 
     did(grad_bd)
-    pieces = {"T": tail, "P": grad_up_parts, "K": backward, "I": input_back}
+    pieces = {"K": backward, "I": input_back}
     for key in ORDER:
         if key in pieces:
             pieces[key]()

time: 331 us -> 316 us (0.955)
  local copies, waits for them, and re-layouts: 23.7 us -> 7.8 us
    unnamed x93 -> x57, local copies, waits for them, and re-layouts: 20.3 us -> 5.04 us
    pallas_call x9 -> x7, Pallas kernels: 63.5 us -> 63.9 us  [call(): pl.pallas_call(kernel, name=kernel.__name__, out_shape=shapes, in_specs=[...]
  transfers between devices with their start and end apart: 44 -> 44, of which waited for: 28 -> 29; matrix products, arithmetic and copies ran while one was open for 3% -> 4% of each run, Pallas kernels for 9% -> 10%
where the time goes in v3:
time: 316 us; the launch traced here: 315 us
  waiting for transfers between devices  154 us (49%)
  starting transfers between devices  78.7 us (25%)
  Pallas kernels  63.9 us (20%)
  other arithmetic  9.3 us (3%)
  local copies, waits for them, and re-layouts  7.8 us (2%)
    ppermute x40, waiting for transfers between devices, flip(): return lax.ppermute(values, ('dp', 'mp'), pairs)  151 us
    ppermute x40, starting transfers between devices, flip(): return lax.ppermute(values, ('dp', 'mp'), pairs)  77.7 us
    pallas_call x7, Pallas kernels, call(): pl.pallas_call(kernel, name=kernel.__name__, out_shape=shapes, in_specs=[...  63.9 us
  transfers between devices with their start and end apart: 44, of which 29 were waited for; matrix products, arithmetic and copies ran while one was open for 4% of the time, Pallas kernels for 10%

profile of v3, /device:TPU:0, one launch (start us, length us, event | category | flops | bytes accessed | tf_op | source)
XLA Modules:
  0.0 315.4 jit_solution(7853465501394769028)
XLA Ops:
  0.6 1.4 copy.28.lengths_in
  2.0 11.3 %attention_forward.1 = (bf16[512,768]{1,0:T(8,128)(2,1)}, bf16[512,384]{1,0:T(8,128)(2,1)}, bf16[512,384]{1,0:T(8,128)(2,1)}, bf16[512,384]{1,0:T(8,128)(2,1)}, ...) custom-call(s32[16,8]{1,0:T(8,128)} %copy.28.lengths_in, s32[16]{0:T(128)} %pads_in.1, ...), custom_call_target="tpu_custom_call" | custom-call | flops 1207959552 | bytes 8916544 | tf_op jit(solution)/shard_map/attention_forward/pallas_call | solution.py:521
  13.8 3.2 %collective-permute-done.theirs_in = f32[512,768]{1,0:T(8,128)S(1)} collective-permute-done((f32[512,768]{1,0:T(8,128)}, f32[512,768]{1,0:T(8,128)S(1)}, u32[]{:S(2)}, u32[]{:S(2)}) %collective-permute-start) | collective-permute-done | bytes 1572896 | tf_op jit(solution)/shard_map/ppermute | solution.py:546
  17.0 1.1 copy-done.22
  18.2 17.4 %mlp_kernel.1 = (f32[512,768]{1,0:T(8,128)}, f32[1,1536]{1,0:T(1,128)}, f32[1,768]{1,0:T(1,128)}, f32[2,4,96,512]{3,2,1,0:T(8,128)}, f32[2,4,96,512]{3,2,1,0:T(8...) custom-call(f32[768]{0:T(1024)} %gain_in.3, ...), custom_call_target="tpu_custom_call" | custom-call | flops 7247757312 | bytes 23611392 | tf_op jit(solution)/shard_map/mlp_kernel/pallas_call | solution.py:521
  36.0 2.6 collective-permute-start.3
  38.6 2.1 collective-permute-start.2
  40.7 16.5 %collective-permute-done.3 = f32[2,4,96,512]{3,2,1,0:T(8,128)S(1)} collective-permute-done((f32[2,4,96,512]{3,2,1,0:T(8,128)}, f32[2,4,96,512]{3,2,1,0:T(8,128)S(1)}, u32[]{:S(2)}, u32[]{:S(2)}) %collective-permute-start.3) | collective-permute-done | bytes 1572896 | tf_op jit(solution)/shard_map/down_sum_first/ppermute | solution.py:551
  57.3 1.9 add_bitcast_fusion.2
  59.2 2.1 collective-permute-start.5
  61.3 1.4 add_bitcast_fusion.7
  62.7 2.7 collective-permute-start.6
  65.4 1.7 copy-done.15
  67.2 18.2 %attention_backward.1 = (bf16[512,768]{1,0:T(8,128)(2,1)}, f32[512,768]{1,0:T(8,128)S(1)}, f32[16,384]{1,0:T(8,128)S(1)}, f32[512,768]{1,0:T(8,128)S(1)}, f32[2,...) custom-call(f32[2,512,768]{2,1,0:T(8,128)} %get-tuple-element.124.mi, ...), custom_call_target="tpu_custom_call" | custom-call | flops 3019898880 | bytes 24681472 | tf_op jit(solution)/shard_map/attention_backward/pallas_call | solution.py:521
  85.7 5.2 %collective-permute-done.8 = f32[2,4,192,384]{3,2,1,0:T(8,128)S(1)} collective-permute-done((f32[2,4,192,384]{3,2,1,0:T(8,128)}, f32[2,4,192,384]{3,2,1,0:T(8,128)S(1)}, u32[]{:S(2)}, u32[]{:S(2)}) %collective-permute-start.8) | collective-permute-done | bytes 2359328 | tf_op jit(solution)/shard_map/up_sum_first/ppermute | solution.py:551
  91.3 2.1 collective-permute-start.12
  93.4 1.6 collective-permute-start.7
  95.0 1.6 collective-permute-start.9
  96.6 7.0 %collective-permute-done.7 = f32[2,96,512]{2,1,0:T(8,128)S(1)} collective-permute-done((f32[2,96,512]{2,1,0:T(8,128)S(1)}, f32[2,96,512]{2,1,0:T(8,128)S(1)}, u32[]{:S(2)}, u32[]{:S(2)}) %collective-permute-start.7) | collective-permute-done | bytes 393248 | tf_op jit(solution)/shard_map/down_sum_z1/ppermute | solution.py:551
  103.7 3.5 %input_kernel.1 = bf16[512,768]{1,0:T(8,128)(2,1)} custom-call(f32[512,768]{1,0:T(8,128)S(1)} %get-tuple-element.144.mine_ref, f32[512,768]{1,0:T(8,128)S(1)} %collective-permute-done.4.theirs_ref, bf16[512,768]{1,0:T(8,128)(2,1)S(1)} %copy-done, f32[1,768]{1,0:T(1,128)S(1)} %reshape.65.gain_ref, f32[512,768]{1,0:T(8,128)S(1)} %get-tuple-element.157.delta_ref), custom_call_target="tpu_custom_call" | custom-call | bytes 6294528 | tf_op jit(solution)/shard_map/input_kernel/pallas_call | solution.py:521
  107.1 11.3 %collective-permute-done.12 = f32[4,192,384]{2,1,0:T(8,128)S(1)} collective-permute-done((f32[4,192,384]{2,1,0:T(8,128)S(1)}, f32[4,192,384]{2,1,0:T(8,128)S(1)}, u32[]{:S(2)}, u32[]{:S(2)}) %collective-permute-start.12) | collective-permute-done | bytes 1179680 | tf_op jit(solution)/shard_map/up_sum_second/ppermute | solution.py:551
  118.6 3.7 %collective-permute-start.14 = (f32[2,192,384]{2,1,0:T(8,128)S(1)}, f32[2,192,384]{2,1,0:T(8,128)S(1)}, u32[]{:S(2)}, u32[]{:S(2)}) collective-permute-start(f32[2,192,384]{2,1,0:T(8,128)S(1)} %get-tuple-element.241), channel_id=1, source_target_pairs={{0,8},{1,9},{2,10},{3,11},{4,12},{5,13},{6,14},{7,15},{8,0},{9,1},... | collective-permute-start | bytes 1769480 | tf_op jit(solution)/shard_map/up_sum_z1/ppermute | solution.py:551
  122.4 1.3 collective-permute-start.11
  124.4 2.6 collective-permute-start.10
  128.1 8.9 %collective-permute-done.10 = f32[1,96,512]{2,1,0:T(8,128)S(1)} collective-permute-done((f32[1,96,512]{2,1,0:T(8,128)S(1)}, f32[1,96,512]{2,1,0:T(8,128)S(1)}, u32[]{:S(2)}, u32[]{:S(2)}) %collective-permute-start.10) | collective-permute-done | bytes 196640 | tf_op jit(solution)/shard_map/down_sum_z2/ppermute | solution.py:551
  137.0 3.5 %collective-permute-start.13 = (f32[1,96,512]{2,1,0:T(8,128)S(1)}, f32[1,96,512]{2,1,0:T(8,128)S(1)}, u32[]{:S(2)}, u32[]{:S(2)}) collective-permute-start(f32[1,96,512]{2,1,0:T(8,128)S(1)} %add.134), channel_id=1, source_target_pairs={{0,16},{1,17},{2,18},{3,19},{4,20},{5,21},{6,22},{7,23},{8,24},{9,... | collective-permute-start | bytes 589832 | tf_op jit(solution)/shard_map/down_gather_z2/ppermute | solution.py:551
  140.7 11.3 %collective-permute-done.13 = f32[1,96,512]{2,1,0:T(8,128)S(1)} collective-permute-done((f32[1,96,512]{2,1,0:T(8,128)S(1)}, f32[1,96,512]{2,1,0:T(8,128)S(1)}, u32[]{:S(2)}, u32[]{:S(2)}) %collective-permute-start.13) | collective-permute-done | bytes 196640 | tf_op jit(solution)/shard_map/down_gather_z2/ppermute | solution.py:551
  152.6 2.8 collective-permute-start.18
  156.3 6.1 %collective-permute-done.19 = f32[2,96,512]{2,1,0:T(8,128)S(1)} collective-permute-done((f32[2,96,512]{2,1,0:T(8,128)S(1)}, f32[2,96,512]{2,1,0:T(8,128)S(1)}, u32[]{:S(2)}, u32[]{:S(2)}) %collective-permute-start.19) | collective-permute-done | bytes 393248 | tf_op jit(solution)/shard_map/down_gather_z1/ppermute | solution.py:551
  162.5 6.4 %collective-permute-start.22 = (f32[4,96,512]{2,1,0:T(8,128)S(1)}, f32[4,96,512]{2,1,0:T(8,128)S(1)}, u32[]{:S(2)}, u32[]{:S(2)}) collective-permute-start(f32[4,96,512]{2,1,0:T(8,128)S(1)} %constant_dynamic-update-slice_fusion.2), channel_id=1, source_target_pairs={{0,4},{1,3},{2,6},{3,1},{4,0},{5,7},{6,2},{7,5},{8,12},{9,11},{10,... | collective-permute-start | bytes 2359304 | tf_op jit(solution)/shard_map/down_gather_second/ppermute | solution.py:551
  169.0 1.9 collective-permute-start.15
  170.9 2.4 collective-permute-start.21
  173.3 6.4 %collective-permute-done.23 = f32[1,192,384]{2,1,0:T(8,128)S(1)} collective-permute-done((f32[1,192,384]{2,1,0:T(8,128)S(1)}, f32[1,192,384]{2,1,0:T(8,128)S(1)}, u32[]{:S(2)}, u32[]{:S(2)}) %collective-permute-start.23) | collective-permute-done | bytes 294944 | tf_op jit(solution)/shard_map/up_gather_z2/ppermute | solution.py:551
  179.7 1.7 collective-permute-start.25
  181.4 1.3 pad_maximum_fusion.1.own_ref
  182.8 3.5 %collective-permute-start.26 = (f32[1,96,384]{2,1,0:T(8,128)S(1)}, f32[1,96,384]{2,1,0:T(8,128)S(1)}, u32[]{:S(2)}, u32[]{:S(2)}) collective-permute-start(f32[1,96,384]{2,1,0:T(8,128)S(1)} %get-tuple-element.263), channel_id=1, source_target_pairs={{0,16},{1,17},{2,18},{3,19},{4,20},{5,21},{6,22},{7,23},{8,24},{9,... | collective-permute-start | bytes 442376 | tf_op jit(solution)/shard_map/attention_rest_sum_z2/ppermute | solution.py:551
  186.3 2.7 collective-permute-start.27
  189.1 2.4 collective-permute-done.27
  191.6 2.2 collective-permute-done.26
  194.0 9.8 %collective-permute-start.29 = (f32[4,192,384]{2,1,0:T(8,128)S(1)}, f32[4,192,384]{2,1,0:T(8,128)S(1)}, u32[]{:S(2)}, u32[]{:S(2)}) collective-permute-start(f32[4,192,384]{2,1,0:T(8,128)S(1)} %constant_dynamic-update-slice_fusion.8), channel_id=1, source_target_pairs={{0,4},{1,3},{2,6},{3,1},{4,0},{5,7},{6,2},{7,5},{8,12},{9,11},{10,... | collective-permute-start | bytes 3538952 | tf_op jit(solution)/shard_map/up_gather_second/ppermute | solution.py:551
  204.4 1.2 collective-permute-start.33
  205.6 1.7 collective-permute-start.30
  207.3 6.8 %collective-permute-done.24 = f32[208,384]{1,0:T(8,128)S(1)} collective-permute-done((f32[208,384]{1,0:T(8,128)S(1)}, f32[208,384]{1,0:T(8,128)S(1)}, u32[]{:S(2)}, u32[]{:S(2)}) %collective-permute-start.24) | collective-permute-done | bytes 319520 | tf_op jit(solution)/shard_map/attention_sum_z1/ppermute | solution.py:551
  214.2 1.4 collective-permute-start.28
  216.4 2.2 collective-permute-start.34
  218.7 1.4 collective-permute-done.29
  220.2 4.6 %collective-permute-done.28 = f32[112,384]{1,0:T(8,128)S(1)} collective-permute-done((f32[112,384]{1,0:T(8,128)S(1)}, f32[112,384]{1,0:T(8,128)S(1)}, u32[]{:S(2)}, u32[]{:S(2)}) %collective-permute-start.28) | collective-permute-done | bytes 172064 | tf_op jit(solution)/shard_map/attention_sum_z2/ppermute | solution.py:551
  226.1 2.7 collective-permute-start.36
  228.9 3.6 %collective-permute-done.32 = f32[1,96,384]{2,1,0:T(8,128)S(1)} collective-permute-done((f32[1,96,384]{2,1,0:T(8,128)S(1)}, f32[1,96,384]{2,1,0:T(8,128)S(1)}, u32[]{:S(2)}, u32[]{:S(2)}) %collective-permute-start.32) | collective-permute-done | bytes 147488 | tf_op jit(solution)/shard_map/attention_gather_z2/ppermute | solution.py:551
  233.9 3.6 %collective-permute-done.36 = f32[4,96,384]{2,1,0:T(8,128)S(1)} collective-permute-done((f32[4,96,384]{2,1,0:T(8,128)S(1)}, f32[4,96,384]{2,1,0:T(8,128)S(1)}, u32[]{:S(2)}, u32[]{:S(2)}) %collective-permute-start.36) | collective-permute-done | bytes 589856 | tf_op jit(solution)/shard_map/attention_rest_gather_second/ppermute | solution.py:551
  237.7 1.7 collective-permute-done.35
  239.4 4.4 %collective-permute-start.37 = (f32[4,96,384]{2,1,0:T(8,128)S(1)}, f32[4,96,384]{2,1,0:T(8,128)S(1)}, u32[]{:S(2)}, u32[]{:S(2)}) collective-permute-start(f32[4,96,384]{2,1,0:T(8,128)S(1)} %constant_dynamic-update-slice_fusion.18), channel_id=1, source_target_pairs={{0,4},{1,3},{2,6},{3,1},{4,0},{5,7},{6,2},{7,5},{8,12},{9,11},{10,... | collective-permute-start | bytes 1769480 | tf_op jit(solution)/shard_map/attention_gather_second/ppermute | solution.py:551
  243.8 1.1 collective-permute-start.41
  245.5 1.2 collective-permute-start.39
  246.7 11.3 %collective-permute-done.37 = f32[4,96,384]{2,1,0:T(8,128)S(1)} collective-permute-done((f32[4,96,384]{2,1,0:T(8,128)S(1)}, f32[4,96,384]{2,1,0:T(8,128)S(1)}, u32[]{:S(2)}, u32[]{:S(2)}) %collective-permute-start.37) | collective-permute-done | bytes 589856 | tf_op jit(solution)/shard_map/attention_gather_second/ppermute | solution.py:551
  258.1 1.1 pad_maximum_fusion.4.own_a
  259.2 1.1 collective-permute-start.38
  260.3 3.7 %collective-permute-done.42 = f32[4,96,256]{2,1,0:T(8,128)S(1)} collective-permute-done((f32[4,96,256]{2,1,0:T(8,128)S(1)}, f32[4,96,256]{2,1,0:T(8,128)S(1)}, u32[]{:S(2)}, u32[]{:S(2)}) %collective-permute-start.42) | collective-permute-done | bytes 393248 | tf_op jit(solution)/shard_map/down_stack_gather_z2/ppermute | solution.py:551
  268.9 16.5 %collective-permute-done.41.got_ref = f32[2,4,96,512]{3,2,1,0:T(8,128)} collective-permute-done((f32[2,4,96,512]{3,2,1,0:T(8,128)}, f32[2,4,96,512]{3,2,1,0:T(8,128)}, u32[]{:S(2)}, u32[]{:S(2)}) %collective-permute-start.41) | collective-permute-done | bytes 1572896 | tf_op jit(solution)/shard_map/down_gather_first/ppermute | solution.py:551
  285.8 4.8 %unpack_down.1 = f32[1536,768]{1,0:T(8,128)} custom-call(f32[2,4,96,512]{3,2,1,0:T(8,128)} %pad_maximum_fusion.1.own_ref, f32[2,4,96,512]{3,2,1,0:T(8,128)} %collective-permute-done.41.got_ref, f32[2,4,96,256]{3,2,1,0:T(8,128)} %pad_maximum_fusion.5.z_own_ref, f32[2,4,96,256]{3,2,1,0:T(8,128)} %collective-permute-done.43.z_got_ref), custom_call_target="tpu_custom_call" | custom-call | bytes 9437184 | tf_op jit(solution)/shard_map/unpack_down/pallas_call | solution.py:521
  290.6 4.2 %unpack_up.1 = f32[768,1536]{1,0:T(8,128)} custom-call(f32[2,4,192,384]{3,2,1,0:T(8,128)S(1)} %pad_maximum_fusion.own_ref, f32[2,4,192,384]{3,2,1,0:T(8,128)} %collective-permute-done.40.got_ref), custom_call_target="tpu_custom_call" | custom-call | bytes 9437184 | tf_op jit(solution)/shard_map/unpack_up/pallas_call | solution.py:521
  294.8 3.2 %collective-permute-done.39.got_b = f32[2,4,96,384]{3,2,1,0:T(8,128)} collective-permute-done((f32[2,4,96,384]{3,2,1,0:T(8,128)S(1)}, f32[2,4,96,384]{3,2,1,0:T(8,128)}, u32[]{:S(2)}, u32[]{:S(2)}) %collective-permute-start.39) | collective-permute-done | bytes 1179680 | tf_op jit(solution)/shard_map/attention_rest_gather_first/ppermute | solution.py:551
  298.0 12.6 %collective-permute-done.38.got_a = f32[2,4,96,384]{3,2,1,0:T(8,128)} collective-permute-done((f32[2,4,96,384]{3,2,1,0:T(8,128)}, f32[2,4,96,384]{3,2,1,0:T(8,128)}, u32[]{:S(2)}, u32[]{:S(2)}) %collective-permute-start.38) | collective-permute-done | bytes 1179680 | tf_op jit(solution)/shard_map/attention_gather_first/ppermute | solution.py:551
  310.7 4.6 %unpack_attention.1 = (f32[384,768]{1,0:T(8,128)}, f32[768,384]{1,0:T(8,128)}, f32[768,384]{1,0:T(8,128)}, f32[768,384]{1,0:T(8,128)}) custom-call(f32[2,4,96,384]{3,2,1,0:T(8,128)} %pad_maximum_fusion.4.own_a, f32[2,4,96,384]{3,2,1,0:T(8,128)} %collective-permute-done.38.got_a, f32[2,4,96,384]{3,2,1,0:T(8,128)S(1)} %pad_maximum_fusion.3.own_b, ...), custom_call_target="tpu_custom_call" | custom-call | bytes 9437184 | tf_op jit(solution)/shard_map/unpack_attention/pallas_call | solution.py:521
  (144 shorter events, 16.6 us)
Async XLA Ops:
  13.3 3.8 %collective-permute-start = (f32[512,768]{1,0:T(8,128)}, f32[512,768]{1,0:T(8,128)S(1)}, u32[]{:S(2)}, u32[]{:S(2)}) collective-permute-start(f32[512,768]{1,0:T(8,128)} %get-tuple-element.123.mine_in), channel_id=1, source_target_pairs={{0,1},{1,0},{2,3},{3,2},{4,5},{5,4},{6,7},{7,6},{8,9},{9,8},{10,11... | collective-permute-start | bytes 4718600 | tf_op jit(solution)/shard_map/ppermute | solution.py:546
  35.6 29.8 %collective-permute-start.1 = (f32[2,512,768]{2,1,0:T(8,128)}, f32[2,512,768]{2,1,0:T(8,128)S(1)}, u32[]{:S(2)}, u32[]{:S(2)}) collective-permute-start(f32[2,512,768]{2,1,0:T(8,128)} %get-tuple-element.124.mine_ref), channel_id=1, source_target_pairs={{0,1},{1,0},{2,3},{3,2},{4,5},{5,4},{6,7},{7,6},{8,9},{9,8},{10,11... | collective-permute-start | bytes 9437192 | tf_op jit(solution)/shard_map/ppermute | solution.py:546
  36.0 21.2 %collective-permute-start.3 = (f32[2,4,96,512]{3,2,1,0:T(8,128)}, f32[2,4,96,512]{3,2,1,0:T(8,128)S(1)}, u32[]{:S(2)}, u32[]{:S(2)}) collective-permute-start(f32[2,4,96,512]{3,2,1,0:T(8,128)} %get-tuple-element.128), channel_id=1, source_target_pairs={{0,2},{1,5},{2,0},{3,7},{4,6},{5,1},{6,4},{7,3},{8,10},{9,13},{10,... | collective-permute-start | bytes 4718600 | tf_op jit(solution)/shard_map/down_sum_first/ppermute | solution.py:551
  38.6 52.3 %collective-permute-start.8 = (f32[2,4,192,384]{3,2,1,0:T(8,128)}, f32[2,4,192,384]{3,2,1,0:T(8,128)S(1)}, u32[]{:S(2)}, u32[]{:S(2)}) collective-permute-start(f32[2,4,192,384]{3,2,1,0:T(8,128)} %get-tuple-element.151), channel_id=1, source_target_pairs={{0,2},{1,5},{2,0},{3,7},{4,6},{5,1},{6,4},{7,3},{8,10},{9,13},{10,... | collective-permute-start | bytes 7077896 | tf_op jit(solution)/shard_map/up_sum_first/ppermute | solution.py:551
  38.6 22.7 %collective-permute-start.2 = (f32[2,4,96,256]{3,2,1,0:T(8,128)}, f32[2,4,96,256]{3,2,1,0:T(8,128)S(1)}, u32[]{:S(2)}, u32[]{:S(2)}) collective-permute-start(f32[2,4,96,256]{3,2,1,0:T(8,128)} %get-tuple-element.126), channel_id=1, source_target_pairs={{0,8},{1,9},{2,10},{3,11},{4,12},{5,13},{6,14},{7,15},{8,0},{9,1},... | collective-permute-start | bytes 2359304 | tf_op jit(solution)/shard_map/down_stack_sum_z1/ppermute | solution.py:551
  57.2 8.2 %copy-start.19 = (f32[768]{0:T(1024)S(1)}, f32[768]{0:T(1024)}, u32[]{:S(2)}) copy-start(f32[768]{0:T(1024)} %gain_in.3) | copy-start | bytes 9220
  57.2 8.2 %copy-start.20 = (f32[768]{0:T(1024)S(1)}, f32[768]{0:T(1024)}, u32[]{:S(2)}) copy-start(f32[768]{0:T(1024)} %param.26) | copy-start | bytes 9220
  57.2 9.9 %copy-start.3 = (bf16[768,384]{1,0:T(8,128)(2,1)S(1)}, bf16[768,384]{1,0:T(8,128)(2,1)}, u32[]{:S(2)}) copy-start(bf16[768,384]{1,0:T(8,128)(2,1)} %wq_ref.1) | copy-start | bytes 1769476
  57.2 9.9 %copy-start.4 = (bf16[768,384]{1,0:T(8,128)(2,1)S(1)}, bf16[768,384]{1,0:T(8,128)(2,1)}, u32[]{:S(2)}) copy-start(bf16[768,384]{1,0:T(8,128)(2,1)} %wk_ref.1) | copy-start | bytes 1769476
  57.2 9.9 %copy-start.5 = (bf16[768,384]{1,0:T(8,128)(2,1)S(1)}, bf16[768,384]{1,0:T(8,128)(2,1)}, u32[]{:S(2)}) copy-start(bf16[768,384]{1,0:T(8,128)(2,1)} %wv_ref.1) | copy-start | bytes 1769476
  57.2 9.8 %copy-start.6 = (bf16[384,768]{1,0:T(8,128)(2,1)S(1)}, bf16[384,768]{1,0:T(8,128)(2,1)}, u32[]{:S(2)}) copy-start(bf16[384,768]{1,0:T(8,128)(2,1)} %wo_ref.1) | copy-start | bytes 1769476
  57.3 9.8 %copy-start.7 = (bf16[512,384]{1,0:T(8,128)(2,1)S(1)}, bf16[512,384]{1,0:T(8,128)(2,1)}, u32[]{:S(2)}) copy-start(bf16[512,384]{1,0:T(8,128)(2,1)} %get-tuple-element.137.q_ref) | copy-start | bytes 1179652
  57.3 9.8 %copy-start.8 = (bf16[512,384]{1,0:T(8,128)(2,1)S(1)}, bf16[512,384]{1,0:T(8,128)(2,1)}, u32[]{:S(2)}) copy-start(bf16[512,384]{1,0:T(8,128)(2,1)} %get-tuple-element.138.k_ref) | copy-start | bytes 1179652
  57.3 9.8 %copy-start.9 = (bf16[512,384]{1,0:T(8,128)(2,1)S(1)}, bf16[512,384]{1,0:T(8,128)(2,1)}, u32[]{:S(2)}) copy-start(bf16[512,384]{1,0:T(8,128)(2,1)} %get-tuple-element.139.v_ref) | copy-start | bytes 1179652
  57.3 9.8 %copy-start.10 = (bf16[512,384]{1,0:T(8,128)(2,1)S(1)}, bf16[512,384]{1,0:T(8,128)(2,1)}, u32[]{:S(2)}) copy-start(bf16[512,384]{1,0:T(8,128)(2,1)} %get-tuple-element.136.att_ref) | copy-start | bytes 1179652
  57.3 9.8 %copy-start.11 = (f32[256,128]{1,0:T(8,128)S(1)}, f32[256,128]{1,0:T(8,128)}, u32[]{:S(2)}) copy-start(f32[256,128]{1,0:T(8,128)} %constant.4.clone.cos_in.cos_ref) | copy-start | bytes 393220
  57.3 9.8 %copy-start.12 = (f32[256,128]{1,0:T(8,128)S(1)}, f32[256,128]{1,0:T(8,128)}, u32[]{:S(2)}) copy-start(f32[256,128]{1,0:T(8,128)} %constant.5.clone.sin_in.sin_ref) | copy-start | bytes 393220
  59.2 26.3 %collective-permute-start.5 = (f32[4,96,512]{2,1,0:T(8,128)S(1)}, f32[4,96,512]{2,1,0:T(8,128)S(1)}, u32[]{:S(2)}, u32[]{:S(2)}) collective-permute-start(f32[4,96,512]{2,1,0:T(8,128)S(1)} %get-tuple-element.237), channel_id=1, source_target_pairs={{0,4},{1,3},{2,6},{3,1},{4,0},{5,7},{6,2},{7,5},{8,12},{9,11},{10,... | collective-permute-start | bytes 2359304 | tf_op jit(solution)/shard_map/down_sum_second/ppermute | solution.py:551
  61.3 5.8 %copy-start = (bf16[512,768]{1,0:T(8,128)(2,1)S(1)}, bf16[512,768]{1,0:T(8,128)(2,1)}, u32[]{:S(2)}) copy-start(bf16[512,768]{1,0:T(8,128)(2,1)} %x_ref.3) | copy-start | bytes 2359300
  61.3 5.9 %copy-start.1 = (bf16[512,768]{1,0:T(8,128)(2,1)S(1)}, bf16[512,768]{1,0:T(8,128)(2,1)}, u32[]{:S(2)}) copy-start(bf16[512,768]{1,0:T(8,128)(2,1)} %cot_ref.1) | copy-start | bytes 2359300
  61.3 5.9 %copy-start.2 = (bf16[512,768]{1,0:T(8,128)(2,1)S(1)}, bf16[512,768]{1,0:T(8,128)(2,1)}, u32[]{:S(2)}) copy-start(bf16[512,768]{1,0:T(8,128)(2,1)} %get-tuple-element.141.normed_ref) | copy-start | bytes 2359300
  61.3 5.9 %copy-start.13 = (f32[1,1536]{1,0:T(1,128)S(1)}, f32[1,1536]{1,0:T(1,128)}, u32[]{:S(2)}) copy-start(f32[1,1536]{1,0:T(1,128)} %get-tuple-element.142.gbu_ref) | copy-start | bytes 18436
  61.3 5.9 %copy-start.14 = (f32[1,768]{1,0:T(1,128)S(1)}, f32[1,768]{1,0:T(1,128)}, u32[]{:S(2)}) copy-start(f32[1,768]{1,0:T(1,128)} %get-tuple-element.129.gbd_ref) | copy-start | bytes 9220
  62.7 22.7 %collective-permute-start.6 = (f32[4,96,256]{2,1,0:T(8,128)S(1)}, f32[4,96,256]{2,1,0:T(8,128)S(1)}, u32[]{:S(2)}, u32[]{:S(2)}) collective-permute-start(f32[4,96,256]{2,1,0:T(8,128)S(1)} %get-tuple-element.245), channel_id=1, source_target_pairs={{0,16},{1,17},{2,18},{3,19},{4,20},{5,21},{6,22},{7,23},{8,24},{9,... | collective-permute-start | bytes 1179656 | tf_op jit(solution)/shard_map/down_stack_sum_z2/ppermute | solution.py:551
  85.5 5.4 %copy-start.16 = (f32[2,4,192,384]{3,2,1,0:T(8,128)S(1)}, f32[2,4,192,384]{3,2,1,0:T(8,128)}, u32[]{:S(2)}) copy-start(f32[2,4,192,384]{3,2,1,0:T(8,128)} %get-tuple-element.152) | copy-start | bytes 7077892
  85.5 18.2 %collective-permute-start.4 = (f32[512,768]{1,0:T(8,128)S(1)}, f32[512,768]{1,0:T(8,128)S(1)}, u32[]{:S(2)}, u32[]{:S(2)}) collective-permute-start(f32[512,768]{1,0:T(8,128)S(1)} %get-tuple-element.144.mine_ref), channel_id=1, source_target_pairs={{0,1},{1,0},{2,3},{3,2},{4,5},{5,4},{6,7},{7,6},{8,9},{9,8},{10,11... | collective-permute-start | bytes 4718600 | tf_op jit(solution)/shard_map/ppermute | solution.py:546
  90.9 4.0 %copy-start.21 = (f32[768]{0:T(1024)S(1)}, f32[768]{0:T(1024)}, u32[]{:S(2)}) copy-start(f32[768]{0:T(1024)} %gain_in.2) | copy-start | bytes 9220
  91.3 27.2 %collective-permute-start.12 = (f32[4,192,384]{2,1,0:T(8,128)S(1)}, f32[4,192,384]{2,1,0:T(8,128)S(1)}, u32[]{:S(2)}, u32[]{:S(2)}) collective-permute-start(f32[4,192,384]{2,1,0:T(8,128)S(1)} %get-tuple-element.235), channel_id=1, source_target_pairs={{0,4},{1,3},{2,6},{3,1},{4,0},{5,7},{6,2},{7,5},{8,12},{9,11},{10,... | collective-permute-start | bytes 3538952 | tf_op jit(solution)/shard_map/up_sum_second/ppermute | solution.py:551
  93.4 10.2 %collective-permute-start.7 = (f32[2,96,512]{2,1,0:T(8,128)S(1)}, f32[2,96,512]{2,1,0:T(8,128)S(1)}, u32[]{:S(2)}, u32[]{:S(2)}) collective-permute-start(f32[2,96,512]{2,1,0:T(8,128)S(1)} %get-tuple-element.242), channel_id=1, source_target_pairs={{0,8},{1,9},{2,10},{3,11},{4,12},{5,13},{6,14},{7,15},{8,0},{9,1},... | collective-permute-start | bytes 1179656 | tf_op jit(solution)/shard_map/down_sum_z1/ppermute | solution.py:551
  95.0 57.1 %collective-permute-start.9 = (f32[784,384]{1,0:T(8,128)S(1)}, f32[784,384]{1,0:T(8,128)S(1)}, u32[]{:S(2)}, u32[]{:S(2)}) collective-permute-start(f32[784,384]{1,0:T(8,128)S(1)} %pad_maximum_fusion.2), channel_id=1, source_target_pairs={{0,2},{1,5},{2,0},{3,7},{4,6},{5,1},{6,4},{7,3},{8,10},{9,13},{10,... | collective-permute-start | bytes 3612680 | tf_op jit(solution)/shard_map/attention_sum_first/ppermute | solution.py:551
  118.6 21.9 %collective-permute-start.14 = (f32[2,192,384]{2,1,0:T(8,128)S(1)}, f32[2,192,384]{2,1,0:T(8,128)S(1)}, u32[]{:S(2)}, u32[]{:S(2)}) collective-permute-start(f32[2,192,384]{2,1,0:T(8,128)S(1)} %get-tuple-element.241), channel_id=1, source_target_pairs={{0,8},{1,9},{2,10},{3,11},{4,12},{5,13},{6,14},{7,15},{8,0},{9,1},... | collective-permute-start | bytes 1769480 | tf_op jit(solution)/shard_map/up_sum_z1/ppermute | solution.py:551
  122.4 5.7 %collective-permute-start.11 = (f32[2,96,256]{2,1,0:T(8,128)S(1)}, f32[2,96,256]{2,1,0:T(8,128)S(1)}, u32[]{:S(2)}, u32[]{:S(2)}) collective-permute-start(f32[2,96,256]{2,1,0:T(8,128)S(1)} %get-tuple-element.255), channel_id=1, source_target_pairs={{0,2},{1,5},{2,0},{3,7},{4,6},{5,1},{6,4},{7,3},{8,10},{9,13},{10,... | collective-permute-start | bytes 589832 | tf_op jit(solution)/shard_map/down_stack_sum_first/ppermute | solution.py:551
  123.7 28.7 %collective-permute-start.17 = (f32[2,4,96,384]{3,2,1,0:T(8,128)S(1)}, f32[2,4,96,384]{3,2,1,0:T(8,128)S(1)}, u32[]{:S(2)}, u32[]{:S(2)}) collective-permute-start(f32[2,4,96,384]{3,2,1,0:T(8,128)S(1)} %get-tuple-element.174), channel_id=1, source_target_pairs={{0,2},{1,5},{2,0},{3,7},{4,6},{5,1},{6,4},{7,3},{8,10},{9,13},{10,... | collective-permute-start | bytes 3538952 | tf_op jit(solution)/shard_map/attention_rest_sum_first/ppermute | solution.py:551
  124.4 12.5 %collective-permute-start.10 = (f32[1,96,512]{2,1,0:T(8,128)S(1)}, f32[1,96,512]{2,1,0:T(8,128)S(1)}, u32[]{:S(2)}, u32[]{:S(2)}) collective-permute-start(f32[1,96,512]{2,1,0:T(8,128)S(1)} %get-tuple-element.257), channel_id=1, source_target_pairs={{0,16},{1,17},{2,18},{3,19},{4,20},{5,21},{6,22},{7,23},{8,24},{9,... | collective-permute-start | bytes 589832 | tf_op jit(solution)/shard_map/down_sum_z2/ppermute | solution.py:551
  137.0 15.0 %collective-permute-start.13 = (f32[1,96,512]{2,1,0:T(8,128)S(1)}, f32[1,96,512]{2,1,0:T(8,128)S(1)}, u32[]{:S(2)}, u32[]{:S(2)}) collective-permute-start(f32[1,96,512]{2,1,0:T(8,128)S(1)} %add.134), channel_id=1, source_target_pairs={{0,16},{1,17},{2,18},{3,19},{4,20},{5,21},{6,22},{7,23},{8,24},{9,... | collective-permute-start | bytes 589832 | tf_op jit(solution)/shard_map/down_gather_z2/ppermute | solution.py:551
  140.6 15.7 %collective-permute-start.20 = (f32[1,192,384]{2,1,0:T(8,128)S(1)}, f32[1,192,384]{2,1,0:T(8,128)S(1)}, u32[]{:S(2)}, u32[]{:S(2)}) collective-permute-start(f32[1,192,384]{2,1,0:T(8,128)S(1)} %get-tuple-element.251), channel_id=1, source_target_pairs={{0,16},{1,17},{2,18},{3,19},{4,20},{5,21},{6,22},{7,23},{8,24},{9,... | collective-permute-start | bytes 884744 | tf_op jit(solution)/shard_map/up_sum_z2/ppermute | solution.py:551
  152.0 10.4 %collective-permute-start.19 = (f32[2,96,512]{2,1,0:T(8,128)S(1)}, f32[2,96,512]{2,1,0:T(8,128)S(1)}, u32[]{:S(2)}, u32[]{:S(2)}) collective-permute-start(f32[2,96,512]{2,1,0:T(8,128)S(1)} %constant_dynamic-update-slice_fusion), channel_id=1, source_target_pairs={{0,8},{1,9},{2,10},{3,11},{4,12},{5,13},{6,14},{7,15},{8,0},{9,1},... | collective-permute-start | bytes 1179656 | tf_op jit(solution)/shard_map/down_gather_z1/ppermute | solution.py:551
  152.6 18.2 %collective-permute-start.18 = (f32[4,96,384]{2,1,0:T(8,128)S(1)}, f32[4,96,384]{2,1,0:T(8,128)S(1)}, u32[]{:S(2)}, u32[]{:S(2)}) collective-permute-start(f32[4,96,384]{2,1,0:T(8,128)S(1)} %get-tuple-element.238), channel_id=1, source_target_pairs={{0,4},{1,3},{2,6},{3,1},{4,0},{5,7},{6,2},{7,5},{8,12},{9,11},{10,... | collective-permute-start | bytes 1769480 | tf_op jit(solution)/shard_map/attention_rest_sum_second/ppermute | solution.py:551
  162.5 19.0 %collective-permute-start.22 = (f32[4,96,512]{2,1,0:T(8,128)S(1)}, f32[4,96,512]{2,1,0:T(8,128)S(1)}, u32[]{:S(2)}, u32[]{:S(2)}) collective-permute-start(f32[4,96,512]{2,1,0:T(8,128)S(1)} %constant_dynamic-update-slice_fusion.2), channel_id=1, source_target_pairs={{0,4},{1,3},{2,6},{3,1},{4,0},{5,7},{6,2},{7,5},{8,12},{9,11},{10,... | collective-permute-start | bytes 2359304 | tf_op jit(solution)/shard_map/down_gather_second/ppermute | solution.py:551
  168.8 10.8 %collective-permute-start.23 = (f32[1,192,384]{2,1,0:T(8,128)S(1)}, f32[1,192,384]{2,1,0:T(8,128)S(1)}, u32[]{:S(2)}, u32[]{:S(2)}) collective-permute-start(f32[1,192,384]{2,1,0:T(8,128)S(1)} %add.144), channel_id=1, source_target_pairs={{0,16},{1,17},{2,18},{3,19},{4,20},{5,21},{6,22},{7,23},{8,24},{9,... | collective-permute-start | bytes 884744 | tf_op jit(solution)/shard_map/up_gather_z2/ppermute | solution.py:551
  168.8 17.4 %collective-permute-start.16 = (f32[1,96,256]{2,1,0:T(8,128)S(1)}, f32[1,96,256]{2,1,0:T(8,128)S(1)}, u32[]{:S(2)}, u32[]{:S(2)}) collective-permute-start(f32[1,96,256]{2,1,0:T(8,128)S(1)} %get-tuple-element.267), channel_id=1, source_target_pairs={{0,4},{1,3},{2,6},{3,1},{4,0},{5,7},{6,2},{7,5},{8,12},{9,11},{10,... | collective-permute-start | bytes 294920 | tf_op jit(solution)/shard_map/down_stack_sum_second/ppermute | solution.py:551
  169.0 20.0 %collective-permute-start.15 = (f32[400,384]{1,0:T(8,128)S(1)}, f32[400,384]{1,0:T(8,128)S(1)}, u32[]{:S(2)}, u32[]{:S(2)}) collective-permute-start(f32[400,384]{1,0:T(8,128)S(1)} %pad_maximum_fusion.6), channel_id=1, source_target_pairs={{0,4},{1,3},{2,6},{3,1},{4,0},{5,7},{6,2},{7,5},{8,12},{9,11},{10,... | collective-permute-start | bytes 1843208 | tf_op jit(solution)/shard_map/attention_sum_second/ppermute | solution.py:551
  170.9 11.8 %collective-permute-start.21 = (f32[2,96,384]{2,1,0:T(8,128)S(1)}, f32[2,96,384]{2,1,0:T(8,128)S(1)}, u32[]{:S(2)}, u32[]{:S(2)}) collective-permute-start(f32[2,96,384]{2,1,0:T(8,128)S(1)} %get-tuple-element.248), channel_id=1, source_target_pairs={{0,8},{1,9},{2,10},{3,11},{4,12},{5,13},{6,14},{7,15},{8,0},{9,1},... | collective-permute-start | bytes 884744 | tf_op jit(solution)/shard_map/attention_rest_sum_z1/ppermute | solution.py:551
  179.7 14.2 %collective-permute-start.25 = (f32[2,192,384]{2,1,0:T(8,128)S(1)}, f32[2,192,384]{2,1,0:T(8,128)S(1)}, u32[]{:S(2)}, u32[]{:S(2)}) collective-permute-start(f32[2,192,384]{2,1,0:T(8,128)S(1)} %constant_dynamic-update-slice_fusion.4), channel_id=1, source_target_pairs={{0,8},{1,9},{2,10},{3,11},{4,12},{5,13},{6,14},{7,15},{8,0},{9,1},... | collective-permute-start | bytes 1769480 | tf_op jit(solution)/shard_map/up_gather_z1/ppermute | solution.py:551
  182.8 11.1 %collective-permute-start.26 = (f32[1,96,384]{2,1,0:T(8,128)S(1)}, f32[1,96,384]{2,1,0:T(8,128)S(1)}, u32[]{:S(2)}, u32[]{:S(2)}) collective-permute-start(f32[1,96,384]{2,1,0:T(8,128)S(1)} %get-tuple-element.263), channel_id=1, source_target_pairs={{0,16},{1,17},{2,18},{3,19},{4,20},{5,21},{6,22},{7,23},{8,24},{9,... | collective-permute-start | bytes 442376 | tf_op jit(solution)/shard_map/attention_rest_sum_z2/ppermute | solution.py:551
  186.3 5.3 %collective-permute-start.27 = (f32[1,96,256]{2,1,0:T(8,128)S(1)}, f32[1,96,256]{2,1,0:T(8,128)S(1)}, u32[]{:S(2)}, u32[]{:S(2)}) collective-permute-start(f32[1,96,256]{2,1,0:T(8,128)S(1)} %add.148), channel_id=1, source_target_pairs={{0,4},{1,3},{2,6},{3,1},{4,0},{5,7},{6,2},{7,5},{8,12},{9,11},{10,... | collective-permute-start | bytes 294920 | tf_op jit(solution)/shard_map/down_stack_gather_second/ppermute | solution.py:551
  194.0 26.0 %collective-permute-start.29 = (f32[4,192,384]{2,1,0:T(8,128)S(1)}, f32[4,192,384]{2,1,0:T(8,128)S(1)}, u32[]{:S(2)}, u32[]{:S(2)}) collective-permute-start(f32[4,192,384]{2,1,0:T(8,128)S(1)} %constant_dynamic-update-slice_fusion.8), channel_id=1, source_target_pairs={{0,4},{1,3},{2,6},{3,1},{4,0},{5,7},{6,2},{7,5},{8,12},{9,11},{10,... | collective-permute-start | bytes 3538952 | tf_op jit(solution)/shard_map/up_gather_second/ppermute | solution.py:551
  203.8 10.3 %collective-permute-start.24 = (f32[208,384]{1,0:T(8,128)S(1)}, f32[208,384]{1,0:T(8,128)S(1)}, u32[]{:S(2)}, u32[]{:S(2)}) collective-permute-start(f32[208,384]{1,0:T(8,128)S(1)} %pad_maximum_fusion.7), channel_id=1, source_target_pairs={{0,8},{1,9},{2,10},{3,11},{4,12},{5,13},{6,14},{7,15},{8,0},{9,1},... | collective-permute-start | bytes 958472 | tf_op jit(solution)/shard_map/attention_sum_z1/ppermute | solution.py:551
  204.4 24.4 %collective-permute-start.33 = (f32[2,96,256]{2,1,0:T(8,128)S(1)}, f32[2,96,256]{2,1,0:T(8,128)S(1)}, u32[]{:S(2)}, u32[]{:S(2)}) collective-permute-start(f32[2,96,256]{2,1,0:T(8,128)S(1)} %constant_dynamic-update-slice_fusion.6), channel_id=1, source_target_pairs={{0,2},{1,5},{2,0},{3,7},{4,6},{5,1},{6,4},{7,3},{8,10},{9,13},{10,... | collective-permute-start | bytes 589832 | tf_op jit(solution)/shard_map/down_stack_gather_first/ppermute | solution.py:551
  205.6 10.8 %collective-permute-start.30 = (f32[1,96,384]{2,1,0:T(8,128)S(1)}, f32[1,96,384]{2,1,0:T(8,128)S(1)}, u32[]{:S(2)}, u32[]{:S(2)}) collective-permute-start(f32[1,96,384]{2,1,0:T(8,128)S(1)} %add.153), channel_id=1, source_target_pairs={{0,16},{1,17},{2,18},{3,19},{4,20},{5,21},{6,22},{7,23},{8,24},{9,... | collective-permute-start | bytes 442376 | tf_op jit(solution)/shard_map/attention_rest_gather_z2/ppermute | solution.py:551
  214.2 10.7 %collective-permute-start.28 = (f32[112,384]{1,0:T(8,128)S(1)}, f32[112,384]{1,0:T(8,128)S(1)}, u32[]{:S(2)}, u32[]{:S(2)}) collective-permute-start(f32[112,384]{1,0:T(8,128)S(1)} %pad_maximum_fusion.8), channel_id=1, source_target_pairs={{0,16},{1,17},{2,18},{3,19},{4,20},{5,21},{6,22},{7,23},{8,24},{9,... | collective-permute-start | bytes 516104 | tf_op jit(solution)/shard_map/attention_sum_z2/ppermute | solution.py:551
  216.4 9.6 %collective-permute-start.34 = (f32[2,96,384]{2,1,0:T(8,128)S(1)}, f32[2,96,384]{2,1,0:T(8,128)S(1)}, u32[]{:S(2)}, u32[]{:S(2)}) collective-permute-start(f32[2,96,384]{2,1,0:T(8,128)S(1)} %constant_dynamic-update-slice_fusion.10), channel_id=1, source_target_pairs={{0,8},{1,9},{2,10},{3,11},{4,12},{5,13},{6,14},{7,15},{8,0},{9,1},... | collective-permute-start | bytes 884744 | tf_op jit(solution)/shard_map/attention_rest_gather_z1/ppermute | solution.py:551
  224.9 7.6 %collective-permute-start.32 = (f32[1,96,384]{2,1,0:T(8,128)S(1)}, f32[1,96,384]{2,1,0:T(8,128)S(1)}, u32[]{:S(2)}, u32[]{:S(2)}) collective-permute-start(f32[1,96,384]{2,1,0:T(8,128)S(1)} %bitcast_add_fusion), channel_id=1, source_target_pairs={{0,16},{1,17},{2,18},{3,19},{4,20},{5,21},{6,22},{7,23},{8,24},{9,... | collective-permute-start | bytes 442376 | tf_op jit(solution)/shard_map/attention_gather_z2/ppermute | solution.py:551
  226.1 11.5 %collective-permute-start.36 = (f32[4,96,384]{2,1,0:T(8,128)S(1)}, f32[4,96,384]{2,1,0:T(8,128)S(1)}, u32[]{:S(2)}, u32[]{:S(2)}) collective-permute-start(f32[4,96,384]{2,1,0:T(8,128)S(1)} %constant_dynamic-update-slice_fusion.12), channel_id=1, source_target_pairs={{0,4},{1,3},{2,6},{3,1},{4,0},{5,7},{6,2},{7,5},{8,12},{9,11},{10,... | collective-permute-start | bytes 1769480 | tf_op jit(solution)/shard_map/attention_rest_gather_second/ppermute | solution.py:551
  232.5 6.8 %collective-permute-start.35 = (f32[2,96,384]{2,1,0:T(8,128)S(1)}, f32[2,96,384]{2,1,0:T(8,128)S(1)}, u32[]{:S(2)}, u32[]{:S(2)}) collective-permute-start(f32[2,96,384]{2,1,0:T(8,128)S(1)} %constant_dynamic-update-slice_fusion.16), channel_id=1, source_target_pairs={{0,8},{1,9},{2,10},{3,11},{4,12},{5,13},{6,14},{7,15},{8,0},{9,1},... | collective-permute-start | bytes 884744 | tf_op jit(solution)/shard_map/attention_gather_z1/ppermute | solution.py:551
  233.2 57.4 %collective-permute-start.40 = (f32[2,4,192,384]{3,2,1,0:T(8,128)S(1)}, f32[2,4,192,384]{3,2,1,0:T(8,128)}, u32[]{:S(2)}, u32[]{:S(2)}) collective-permute-start(f32[2,4,192,384]{3,2,1,0:T(8,128)S(1)} %pad_maximum_fusion.own_ref), channel_id=1, source_target_pairs={{0,2},{1,5},{2,0},{3,7},{4,6},{5,1},{6,4},{7,3},{8,10},{9,13},{10,... | collective-permute-start | bytes 7077896 | tf_op jit(solution)/shard_map/up_gather_first/ppermute | solution.py:551
  239.4 18.7 %collective-permute-start.37 = (f32[4,96,384]{2,1,0:T(8,128)S(1)}, f32[4,96,384]{2,1,0:T(8,128)S(1)}, u32[]{:S(2)}, u32[]{:S(2)}) collective-permute-start(f32[4,96,384]{2,1,0:T(8,128)S(1)} %constant_dynamic-update-slice_fusion.18), channel_id=1, source_target_pairs={{0,4},{1,3},{2,6},{3,1},{4,0},{5,7},{6,2},{7,5},{8,12},{9,11},{10,... | collective-permute-start | bytes 1769480 | tf_op jit(solution)/shard_map/attention_gather_second/ppermute | solution.py:551
  243.8 41.6 %collective-permute-start.41 = (f32[2,4,96,512]{3,2,1,0:T(8,128)}, f32[2,4,96,512]{3,2,1,0:T(8,128)}, u32[]{:S(2)}, u32[]{:S(2)}) collective-permute-start(f32[2,4,96,512]{3,2,1,0:T(8,128)} %pad_maximum_fusion.1.own_ref), channel_id=1, source_target_pairs={{0,2},{1,5},{2,0},{3,7},{4,6},{5,1},{6,4},{7,3},{8,10},{9,13},{10,... | collective-permute-start | bytes 4718600 | tf_op jit(solution)/shard_map/down_gather_first/ppermute | solution.py:551
  244.9 19.1 %collective-permute-start.42 = (f32[4,96,256]{2,1,0:T(8,128)S(1)}, f32[4,96,256]{2,1,0:T(8,128)S(1)}, u32[]{:S(2)}, u32[]{:S(2)}) collective-permute-start(f32[4,96,256]{2,1,0:T(8,128)S(1)} %constant_dynamic-update-slice_fusion.14), channel_id=1, source_target_pairs={{0,16},{1,17},{2,18},{3,19},{4,20},{5,21},{6,22},{7,23},{8,24},{9,... | collective-permute-start | bytes 1179656 | tf_op jit(solution)/shard_map/down_stack_gather_z2/ppermute | solution.py:551
  245.5 52.5 %collective-permute-start.39 = (f32[2,4,96,384]{3,2,1,0:T(8,128)S(1)}, f32[2,4,96,384]{3,2,1,0:T(8,128)}, u32[]{:S(2)}, u32[]{:S(2)}) collective-permute-start(f32[2,4,96,384]{3,2,1,0:T(8,128)S(1)} %pad_maximum_fusion.3.own_b), channel_id=1, source_target_pairs={{0,2},{1,5},{2,0},{3,7},{4,6},{5,1},{6,4},{7,3},{8,10},{9,13},{10,... | collective-permute-start | bytes 3538952 | tf_op jit(solution)/shard_map/attention_rest_gather_first/ppermute | solution.py:551
  259.2 51.4 %collective-permute-start.38 = (f32[2,4,96,384]{3,2,1,0:T(8,128)}, f32[2,4,96,384]{3,2,1,0:T(8,128)}, u32[]{:S(2)}, u32[]{:S(2)}) collective-permute-start(f32[2,4,96,384]{3,2,1,0:T(8,128)} %pad_maximum_fusion.4.own_a), channel_id=1, source_target_pairs={{0,2},{1,5},{2,0},{3,7},{4,6},{5,1},{6,4},{7,3},{8,10},{9,13},{10,... | collective-permute-start | bytes 3538952 | tf_op jit(solution)/shard_map/attention_gather_first/ppermute | solution.py:551
  260.3 5.4 %copy-start.17 = (f32[16,384]{1,0:T(8,128)}, f32[16,384]{1,0:T(8,128)S(1)}, u32[]{:S(2)}) copy-start(f32[16,384]{1,0:T(8,128)S(1)} %slice_add_fusion.19) | copy-start | bytes 73732
  264.0 1.2 collective-permute-start.31
  265.8 20.0 %collective-permute-start.43 = (f32[2,4,96,256]{3,2,1,0:T(8,128)}, f32[2,4,96,256]{3,2,1,0:T(8,128)}, u32[]{:S(2)}, u32[]{:S(2)}) collective-permute-start(f32[2,4,96,256]{3,2,1,0:T(8,128)} %pad_maximum_fusion.5.z_own_ref), channel_id=1, source_target_pairs={{0,8},{1,9},{2,10},{3,11},{4,12},{5,13},{6,14},{7,15},{8,0},{9,1},... | collective-permute-start | bytes 2359304 | tf_op jit(solution)/shard_map/down_stack_gather_z1/ppermute | solution.py:551
  (3 other events, 3.4 us)

commit v4 on v3

--- a/solution.py
+++ b/solution.py
@@ -28,9 +28,9 @@
 
 X, Y, Z1, Z2 = 1, 2, 4, 8
 FIRST, SECOND = (X, Y), (Y, X)
-Z_SLOTS = (0, 2, 1, 3)
-
-ORDER = "dcudcKcdudIuacbdudabudbudbcacbuabuabcabacdacuba"
+Z_FIRST, Z_SECOND = (Z1, Z2), (Z2, Z1)
+
+ORDER = "cduKdcubdIucdabcudbaucdbaucdbaudbacabuabca"
 
 CASES = ((0, 0, 256, 0), (128, 256, 384, 128), (256, 640, 128, 128), (384, 768, 256, 128))
 TILES = (
@@ -236,34 +236,39 @@
     return pl.ds(pl.multiple_of(start * part, 8), part)
 
 
-def z_place(me, block):
-    relative = (me // PLANE) ^ block
-    return (relative % 2) * 2 + relative // 2
+def slot_at(place):
+    core = lax.axis_index("mp") % 2
+    return (place // 2) * (1 + core) + (place % 2) * (2 - core)
 
 
 def quarter_at(place):
-    core = lax.axis_index("mp") % 2
-    slot = (place // 2) * (X + core) + (place % 2) * (Y - core)
-    return lax.axis_index("dp") % PLANE ^ slot
+    return lax.axis_index("dp") % PLANE ^ slot_at(place)
+
+
+def fourth_at(place):
+    return lax.axis_index("dp") % GROUP // PLANE ^ slot_at(place)
+
+
+def z_place(block):
+    slot = lax.axis_index("dp") % GROUP // PLANE ^ block
+    return jnp.where(lax.axis_index("mp") % 2 == 0, (slot % 2) * 2 + slot // 2, slot)
 
 
 def place_quarter(outs, place, value):
-    me = lax.axis_index("dp") % GROUP
     part = value.shape[0] // STACK
     for block in range(STACK):
-        outs[place // 2][place % 2, z_place(me, block)] = value[block * part : (block + 1) * part]
-
-
-def place_quarter_z_first(outs, place, value):
-    me = lax.axis_index("dp") % GROUP
+        outs[place // 2][place % 2, z_place(block)] = value[block * part : (block + 1) * part]
+
+
+def place_quarter_z_first(outs, place, first_row, value):
     part = value.shape[0] // STACK
     for block in range(STACK):
-        z = z_place(me, block)
+        z = z_place(block)
         for sent in range(2):
 
             @pl.when(z // 2 == sent)
             def _(out=outs[sent], z=z, piece=value[block * part : (block + 1) * part]):
-                out[z % 2, place] = piece
+                out[z % 2, place, first_row : first_row + part, :] = piece
 
 
 def mlp_kernel(
@@ -319,23 +324,29 @@
             gbu_ref[:, cols] += jnp.sum(low.astype(f32), axis=0, keepdims=True)
 
     quarter = units // PLANE
+    fourth = units // GROUP
     cut = cot_ref.shape[1] * 2 // 3
+    up_cut = quarter * 2 // 3
     quarters = {}
     for place in range(PLANE):
         quarters[place] = pl.ds(pl.multiple_of(quarter_at(place) * quarter, LANES), quarter)
     for place in (2, 3, 0, 1):
         grad = tn(act_ref[:, quarters[place]], cot_ref[...])
         place_quarter((d_kept_ref, d_sent_ref), place, grad[:, :cut])
-        place_quarter_z_first((c_kept_ref, c_sent_ref), place, grad[:, cut:])
+        place_quarter_z_first((c_kept_ref, c_sent_ref), place, 0, grad[:, cut:])
         if place == 3:
             sender.send(d_sent_ref, d_sent)
-    for source, target in ((c_sent_ref, c_sent), (d_kept_ref, d_kept), (c_kept_ref, c_kept)):
-        sender.send(source, target)
+    sender.send(d_kept_ref, d_kept)
     for place in (2, 3, 0, 1):
-        place_quarter((u_kept_ref, u_sent_ref), place, tn(normed_ref[...], du_ref[:, quarters[place]]))
+        grad = tn(normed_ref[...], du_ref[:, quarters[place]])
+        place_quarter((u_kept_ref, u_sent_ref), place, grad[:, :up_cut])
+        rest = grad[:, up_cut:].reshape(STACK, 2, fourth, -1)
+        rest = jnp.concatenate([rest[:, 0], rest[:, 1]], 2).reshape(STACK * fourth, -1)
+        place_quarter_z_first((c_kept_ref, c_sent_ref), place, fourth, rest)
         if place == 3:
             sender.send(u_sent_ref, u_sent)
-    sender.send(u_kept_ref, u_kept)
+    for source, target in ((c_sent_ref, c_sent), (u_kept_ref, u_kept), (c_kept_ref, c_kept)):
+        sender.send(source, target)
     for share in range(2):
         for rows in halves:
             if share == 0:
@@ -458,31 +469,41 @@
 
 
 def each_block(own_ref, got_ref, put, z_first=False):
-    me = lax.axis_index("dp") % GROUP
     for place in range(PLANE):
         for z in range(STACK):
             first, second = (z, place) if z_first else (place, z)
             value = (got_ref if first // 2 else own_ref)[first % 2, second]
-            put(quarter_at(place), me // PLANE ^ Z_SLOTS[z], value)
+            put(quarter_at(place), fourth_at(z), value)
 
 
 def unpack_down(own_ref, got_ref, z_own_ref, z_got_ref, out_ref):
-    cut = own_ref.shape[-1]
+    cut, part = own_ref.shape[-1], own_ref.shape[-2]
 
     def put(quarter, fourth, value):
-        cols = slice(0, cut) if value.shape[1] == cut else slice(cut, None)
-        out_ref[fourths(quarter * STACK + fourth, value.shape[0]), cols] = value
+        out_ref[fourths(quarter * STACK + fourth, part), :cut] = value
+
+    def put_z(quarter, fourth, value):
+        out_ref[fourths(quarter * STACK + fourth, part), cut:] = value[:part]
 
     each_block(own_ref, got_ref, put)
-    each_block(z_own_ref, z_got_ref, put, True)
-
-
-def unpack_up(own_ref, got_ref, out_ref):
+    each_block(z_own_ref, z_got_ref, put_z, True)
+
+
+def unpack_up(own_ref, got_ref, z_own_ref, z_got_ref, out_ref):
+    cut, part = own_ref.shape[-1], own_ref.shape[-2]
+    rest = z_own_ref.shape[-1] // 2
+
     def put(quarter, fourth, value):
-        part, cols = value.shape
-        out_ref[fourths(fourth, part), pl.ds(pl.multiple_of(quarter * cols, LANES), cols)] = value
+        cols = pl.ds(pl.multiple_of(quarter * (cut + rest), LANES), cut)
+        out_ref[fourths(fourth, part), cols] = value
+
+    def put_z(quarter, fourth, value):
+        cols = pl.ds(pl.multiple_of(quarter * (cut + rest) + cut, LANES), rest)
+        for half in range(2):
+            out_ref[fourths(fourth * 2 + half, part // 2), cols] = value[part // 2 :, half * rest : (half + 1) * rest]
 
     each_block(own_ref, got_ref, put)
+    each_block(z_own_ref, z_got_ref, put_z, True)
 
 
 def unpack_attention(own_a, got_a, own_b, got_b, *outs):
@@ -578,7 +599,7 @@
 
     def chain(name, parts, result, z_first=False, vec=None):
         keep, send = parts
-        plane, stack = [(FIRST, "first"), (SECOND, "second")], [((Z1, Z1), "z1"), ((Z2, Z2), "z2")]
+        plane, stack = [(FIRST, "first"), (SECOND, "second")], [(Z_FIRST, "z_first"), (Z_SECOND, "z_second")]
         steps = stack + plane if z_first else plane + stack
 
         def join(values):
@@ -593,26 +614,29 @@
             if step:
                 keep, got, vec = turn(keep, got, vec)
                 got, vec = part_of(got, keep, vec)
-                cut = keep.shape[0] // 2
-                send, keep = keep[cut:] + got[cut:], keep[:cut] + got[:cut]
-                if step == 1:
-                    keep, send = keep[0], send[0]
-                send = did(join(send))
+            if step == 0:
+                send = join(send)
+            elif step == 1:
+                send, keep = did(join(keep[1] + got[1])), keep[0] + got[0]
+            elif step == 2:
+                send, keep = did(join(keep[2:] + got[2:])), keep[:2] + got[:2]
             else:
-                send = join(send)
+                keep = keep + got
+                send = did(join(keep))
             got = flip(send, bits, f"{name}_sum_{label}")
             yield
         keep, got, vec = turn(keep, got, vec)
         got, vec = part_of(got, keep, vec)
-        own = over_groups(did(keep + got))
+        own = over_groups(did(keep + got[::-1]))
         if vec is not None:
             result.append(over_groups(vec))
-        for step, (bits, label) in enumerate(reversed(steps)):
+        for step, (bits, label) in enumerate(reversed(steps[:3])):
             got = flip(own, bits, f"{name}_gather_{label}")
             yield
             own, got = turn(own, got)
-            if step < 3:
-                own = did(jnp.stack([own, got]) if step == 2 else jnp.concatenate([own, got], 0))
+            if step < 2:
+                own = did(jnp.stack([own, got]) if step == 1 else jnp.concatenate([own, got], 0))
+        did(got)
         result.extend((own, got))
         yield
 
@@ -645,8 +669,8 @@
 
     big = [
         *portions(units // GROUP, width * 2 // 3),
-        *portions(units // GROUP, width // 3),
-        *portions(width // STACK, units // PLANE),
+        *portions(units // GROUP + width // STACK // 2, width // 3),
+        *portions(width // STACK, units // PLANE * 2 // 3),
         ((2, rows, width), f32),
     ]
     residual, grad_bu, grad_bd, *parts, shares = call(
@@ -723,8 +747,8 @@
         if "down" not in grads and len(made["d"]) == len(made["c"]) == 2:
             grads["down"] = call(unpack_down, [((units, width), f32)], held=made["d"] + made["c"])
             did(grads["down"][0])
-        if "up" not in grads and len(made["u"]) == 2:
-            grads["up"] = call(unpack_up, [((width, units), f32)], held=made["u"])
+        if "up" not in grads and len(made["u"]) == len(made["c"]) == 2:
+            grads["up"] = call(unpack_up, [((width, units), f32)], held=made["u"] + made["c"])
             did(grads["up"][0])
         if "attention" not in grads and len(made["a"]) == 3 and len(made["b"]) == 2:
             grads["attention"] = call(

time: 316 us -> 286 us (0.905)
  starting transfers between devices: 78.7 us -> 53.7 us
  waiting for transfers between devices: 154 us -> 139 us
  local copies, waits for them, and re-layouts: 7.8 us -> 21.2 us
  other arithmetic: 9.3 us -> 4.84 us
    ppermute x40 -> x35, starting transfers between devices: 77.7 us -> 52.3 us  [flip(): return lax.ppermute(values, ('dp', 'mp'), pairs)]
    ppermute x40 -> x35, waiting for transfers between devices: 151 us -> 134 us  [flip(): return lax.ppermute(values, ('dp', 'mp'), pairs)]
    unnamed x57 -> x62, local copies, waits for them, and re-layouts: 5.04 us -> 18.5 us
    squeeze x4 -> x0, other arithmetic: 3.74 us -> none  [chain(): keep, send = (keep[0], send[0])]
  transfers between devices with their start and end apart: 44 -> 39, of which waited for: 29 -> 18; matrix products, arithmetic and copies ran while one was open for 4% -> 3% of each run, Pallas kernels for 10% -> 10%
where the time goes in v4:
time: 286 us; the launch traced here: 284 us
  waiting for transfers between devices  139 us (49%)
  Pallas kernels  64.5 us (23%)
  starting transfers between devices  53.7 us (19%)
  local copies, waits for them, and re-layouts  21.2 us (7%)
  other arithmetic  4.84 us (2%)
    ppermute x35, waiting for transfers between devices, flip(): return lax.ppermute(values, ('dp', 'mp'), pairs)  134 us
    pallas_call x7, Pallas kernels, call(): pl.pallas_call(kernel, name=kernel.__name__, out_shape=shapes, in_specs=[...  64.5 us
    ppermute x35, starting transfers between devices, flip(): return lax.ppermute(values, ('dp', 'mp'), pairs)  52.3 us
    unnamed x62, local copies, waits for them, and re-layouts  18.5 us
  transfers between devices with their start and end apart: 39, of which 18 were waited for; matrix products, arithmetic and copies ran while one was open for 3% of the time, Pallas kernels for 10%

profile of v4, /device:TPU:0, one launch (start us, length us, event | category | flops | bytes accessed | tf_op | source)
XLA Modules:
  0.0 284.4 jit_solution(17143147352837552109)
XLA Ops:
  0.6 1.4 copy.28.lengths_in
  2.0 11.3 %attention_forward.1 = (bf16[512,768]{1,0:T(8,128)(2,1)}, bf16[512,384]{1,0:T(8,128)(2,1)}, bf16[512,384]{1,0:T(8,128)(2,1)}, bf16[512,384]{1,0:T(8,128)(2,1)}, ...) custom-call(s32[16,8]{1,0:T(8,128)} %copy.28.lengths_in, s32[16]{0:T(128)} %pads_in.1, ...), custom_call_target="tpu_custom_call" | custom-call | flops 1207959552 | bytes 8916544 | tf_op jit(solution)/shard_map/attention_forward/pallas_call | solution.py:542
  13.8 3.4 %collective-permute-done.theirs_in = f32[512,768]{1,0:T(8,128)} collective-permute-done((f32[512,768]{1,0:T(8,128)}, f32[512,768]{1,0:T(8,128)}, u32[]{:S(2)}, u32[]{:S(2)}) %collective-permute-start) | collective-permute-done | bytes 1572896 | tf_op jit(solution)/shard_map/ppermute | solution.py:567
  17.2 18.5 %mlp_kernel.1 = (f32[512,768]{1,0:T(8,128)}, f32[1,1536]{1,0:T(1,128)}, f32[1,768]{1,0:T(1,128)}, f32[2,4,96,512]{3,2,1,0:T(8,128)}, f32[2,4,96,512]{3,2,1,0:T(8...) custom-call(f32[768]{0:T(1024)} %gain_in.3, ...), custom_call_target="tpu_custom_call" | custom-call | flops 7247757312 | bytes 23611392 | tf_op jit(solution)/shard_map/mlp_kernel/pallas_call | solution.py:542
  36.2 2.6 collective-permute-start.3
  38.8 1.6 collective-permute-start.6
  40.9 0.7 collective-permute-done.1.theirs_ref
  41.7 1.7 copy-done.21
  43.4 1.1 copy-done.8
  44.5 1.1 copy-done.9
  45.6 1.1 copy-done.10
  46.6 1.1 copy-done.11
  47.7 1.1 copy-done.12
  48.8 1.0 copy-done.14
  49.8 1.0 copy-done.15
  50.7 1.0 copy-done.16
  51.7 0.9 copy-done.17
  52.6 0.9 copy-done.18
  53.6 0.7 copy-done.19
  54.2 0.7 copy-done.20
  54.9 18.3 %attention_backward.1 = (bf16[512,768]{1,0:T(8,128)(2,1)}, f32[512,768]{1,0:T(8,128)S(1)}, f32[16,384]{1,0:T(8,128)S(1)}, f32[512,768]{1,0:T(8,128)S(1)}, f32[2,...) custom-call(f32[2,512,768]{2,1,0:T(8,128)} %get-tuple-element.118.mi, ...), custom_call_target="tpu_custom_call" | custom-call | flops 3019898880 | bytes 24681472 | tf_op jit(solution)/shard_map/attention_backward/pallas_call | solution.py:542
  73.9 2.7 collective-permute-start.4
  76.9 1.2 copy-done.22
  78.3 0.9 collective-permute-start.11
  79.2 1.5 collective-permute-start.8
  80.7 2.6 collective-permute-start.10
  83.3 8.2 %collective-permute-done.4 = f32[4,96,512]{2,1,0:T(8,128)S(1)} collective-permute-done((f32[4,96,512]{2,1,0:T(8,128)S(1)}, f32[4,96,512]{2,1,0:T(8,128)S(1)}, u32[]{:S(2)}, u32[]{:S(2)}) %collective-permute-start.4) | collective-permute-done | bytes 786464 | tf_op jit(solution)/shard_map/down_sum_second/ppermute | solution.py:572
  91.6 2.8 collective-permute-start.7
  94.5 1.7 collective-permute-start.9
  96.2 3.5 %input_kernel.1 = bf16[512,768]{1,0:T(8,128)(2,1)} custom-call(f32[512,768]{1,0:T(8,128)S(1)} %get-tuple-element.130.mine_ref, f32[512,768]{1,0:T(8,128)S(1)} %collective-permute-done.2.theirs_ref, bf16[512,768]{1,0:T(8,128)(2,1)S(1)} %copy-done.2, f32[1,768]{1,0:T(1,128)S(1)} %reshape.77.gain_ref, f32[512,768]{1,0:T(8,128)S(1)} %get-tuple-element.147.delta_ref), custom_call_target="tpu_custom_call" | custom-call | bytes 6294528 | tf_op jit(solution)/shard_map/input_kernel/pallas_call | solution.py:542
  99.7 8.8 %collective-permute-done.11 = f32[4,192,256]{2,1,0:T(8,128)S(1)} collective-permute-done((f32[4,192,256]{2,1,0:T(8,128)S(1)}, f32[4,192,256]{2,1,0:T(8,128)S(1)}, u32[]{:S(2)}, u32[]{:S(2)}) %collective-permute-start.11) | collective-permute-done | bytes 786464 | tf_op jit(solution)/shard_map/up_sum_second/ppermute | solution.py:572
  108.5 2.6 collective-permute-start.14
  111.2 2.0 collective-permute-start.15
  113.2 2.6 collective-permute-start.13
  116.0 1.6 collective-permute-start.12
  117.5 13.2 %collective-permute-done.15 = f32[2,192,256]{2,1,0:T(8,128)S(1)} collective-permute-done((f32[2,192,256]{2,1,0:T(8,128)S(1)}, f32[2,192,256]{2,1,0:T(8,128)S(1)}, u32[]{:S(2)}, u32[]{:S(2)}) %collective-permute-start.15) | collective-permute-done | bytes 393248 | tf_op jit(solution)/shard_map/down_stack_sum_first/ppermute | solution.py:572
  130.8 1.8 collective-permute-start.19
  132.7 2.7 collective-permute-start.20
  135.4 1.6 collective-permute-start.18
  138.6 15.1 %collective-permute-done.20 = f32[2,192,256]{2,1,0:T(8,128)S(1)} collective-permute-done((f32[2,192,256]{2,1,0:T(8,128)S(1)}, f32[2,192,256]{2,1,0:T(8,128)S(1)}, u32[]{:S(2)}, u32[]{:S(2)}) %collective-permute-start.20) | collective-permute-done | bytes 393248 | tf_op jit(solution)/shard_map/up_sum_z_second/ppermute | solution.py:572
  153.7 4.5 %collective-permute-start.25 = (f32[2,192,256]{2,1,0:T(8,128)S(1)}, f32[2,192,256]{2,1,0:T(8,128)S(1)}, u32[]{:S(2)}, u32[]{:S(2)}) collective-permute-start(f32[2,192,256]{2,1,0:T(8,128)S(1)} %reverse_add_fusion.1), channel_id=1, source_target_pairs={{0,8},{1,17},{2,10},{3,19},{4,12},{5,21},{6,14},{7,23},{8,0},{9,25... | collective-permute-start | bytes 1179656 | tf_op jit(solution)/shard_map/up_gather_z_first/ppermute | solution.py:572
  158.3 3.7 %collective-permute-start.24 = (f32[2,192,256]{2,1,0:T(8,128)S(1)}, f32[2,192,256]{2,1,0:T(8,128)S(1)}, u32[]{:S(2)}, u32[]{:S(2)}) collective-permute-start(f32[2,192,256]{2,1,0:T(8,128)S(1)} %reverse_add_fusion), channel_id=1, source_target_pairs={{0,2},{1,5},{2,0},{3,7},{4,6},{5,1},{6,4},{7,3},{8,10},{9,13},{10,... | collective-permute-start | bytes 1179656 | tf_op jit(solution)/shard_map/down_stack_gather_first/ppermute | solution.py:572
  162.4 4.0 %collective-permute-done.25 = f32[2,192,256]{2,1,0:T(8,128)S(1)} collective-permute-done((f32[2,192,256]{2,1,0:T(8,128)S(1)}, f32[2,192,256]{2,1,0:T(8,128)S(1)}, u32[]{:S(2)}, u32[]{:S(2)}) %collective-permute-start.25) | collective-permute-done | bytes 393248 | tf_op jit(solution)/shard_map/up_gather_z_first/ppermute | solution.py:572
  166.5 3.9 %collective-permute-done.24 = f32[2,192,256]{2,1,0:T(8,128)S(1)} collective-permute-done((f32[2,192,256]{2,1,0:T(8,128)S(1)}, f32[2,192,256]{2,1,0:T(8,128)S(1)}, u32[]{:S(2)}, u32[]{:S(2)}) %collective-permute-start.24) | collective-permute-done | bytes 393248 | tf_op jit(solution)/shard_map/down_stack_gather_first/ppermute | solution.py:572
  170.5 6.1 %collective-permute-done.23 = f32[4,96,512]{2,1,0:T(8,128)S(1)} collective-permute-done((f32[4,96,512]{2,1,0:T(8,128)S(1)}, f32[4,96,512]{2,1,0:T(8,128)S(1)}, u32[]{:S(2)}, u32[]{:S(2)}) %collective-permute-start.23) | collective-permute-done | bytes 786464 | tf_op jit(solution)/shard_map/down_gather_second/ppermute | solution.py:572
  176.7 8.0 %collective-permute-start.22 = (f32[2,96,384]{2,1,0:T(8,128)S(1)}, f32[2,96,384]{2,1,0:T(8,128)S(1)}, u32[]{:S(2)}, u32[]{:S(2)}) collective-permute-start(f32[2,96,384]{2,1,0:T(8,128)S(1)} %add.163), channel_id=1, source_target_pairs={{0,16},{1,9},{2,18},{3,11},{4,20},{5,13},{6,22},{7,15},{8,24},{9,1... | collective-permute-start | bytes 884744 | tf_op jit(solution)/shard_map/attention_rest_sum_z_second/ppermute | solution.py:572
  184.9 7.8 %collective-permute-done.22 = f32[2,96,384]{2,1,0:T(8,128)S(1)} collective-permute-done((f32[2,96,384]{2,1,0:T(8,128)S(1)}, f32[2,96,384]{2,1,0:T(8,128)S(1)}, u32[]{:S(2)}, u32[]{:S(2)}) %collective-permute-start.22) | collective-permute-done | bytes 294944 | tf_op jit(solution)/shard_map/attention_rest_sum_z_second/ppermute | solution.py:572
  192.8 12.1 %collective-permute-done.21 = f32[208,384]{1,0:T(8,128)S(1)} collective-permute-done((f32[208,384]{1,0:T(8,128)S(1)}, f32[208,384]{1,0:T(8,128)S(1)}, u32[]{:S(2)}, u32[]{:S(2)}) %collective-permute-start.21) | collective-permute-done | bytes 319520 | tf_op jit(solution)/shard_map/attention_sum_z_first/ppermute | solution.py:572
  205.3 1.8 collective-permute-start.34
  207.1 9.4 %collective-permute-done.27 = f32[2,96,384]{2,1,0:T(8,128)S(1)} collective-permute-done((f32[2,96,384]{2,1,0:T(8,128)S(1)}, f32[2,96,384]{2,1,0:T(8,128)S(1)}, u32[]{:S(2)}, u32[]{:S(2)}) %collective-permute-start.27) | collective-permute-done | bytes 294944 | tf_op jit(solution)/shard_map/attention_rest_gather_z_first/ppermute | solution.py:572
  216.5 9.5 %collective-permute-done.26 = f32[208,384]{1,0:T(8,128)S(1)} collective-permute-done((f32[208,384]{1,0:T(8,128)S(1)}, f32[208,384]{1,0:T(8,128)S(1)}, u32[]{:S(2)}, u32[]{:S(2)}) %collective-permute-start.26) | collective-permute-done | bytes 319520 | tf_op jit(solution)/shard_map/attention_sum_z_second/ppermute | solution.py:572
  226.4 8.2 %collective-permute-done.31 = f32[2,96,384]{2,1,0:T(8,128)S(1)} collective-permute-done((f32[2,96,384]{2,1,0:T(8,128)S(1)}, f32[2,96,384]{2,1,0:T(8,128)S(1)}, u32[]{:S(2)}, u32[]{:S(2)}) %collective-permute-start.31) | collective-permute-done | bytes 294944 | tf_op jit(solution)/shard_map/attention_gather_z_first/ppermute | solution.py:572
  234.7 0.7 collective-permute-start.37
  235.5 0.6 collective-permute-done.35
  236.1 1.1 pad_maximum_fusion.4.own_b
  237.2 1.2 copy-done.5
  238.4 12.6 %collective-permute-done.33 = f32[4,96,384]{2,1,0:T(8,128)S(1)} collective-permute-done((f32[4,96,384]{2,1,0:T(8,128)S(1)}, f32[4,96,384]{2,1,0:T(8,128)S(1)}, u32[]{:S(2)}, u32[]{:S(2)}) %collective-permute-start.33) | collective-permute-done | bytes 589856 | tf_op jit(solution)/shard_map/attention_gather_second/ppermute | solution.py:572
  251.0 1.1 pad_maximum_fusion.5.own_a
  252.2 0.6 slice.228
  255.2 14.6 %collective-permute-done.37.z_got_ref = f32[2,4,192,256]{3,2,1,0:T(8,128)} collective-permute-done((f32[2,4,192,256]{3,2,1,0:T(8,128)S(1)}, f32[2,4,192,256]{3,2,1,0:T(8,128)}, u32[]{:S(2)}, u32[]{:S(2)}) %collective-permute-start.37) | collective-permute-done | bytes 1572896 | tf_op jit(solution)/shard_map/down_stack_gather_z_first/ppermute | solution.py:572
  269.8 1.4 copy-done.4
  271.2 4.0 %unpack_down.1 = f32[1536,768]{1,0:T(8,128)} custom-call(f32[2,4,96,512]{3,2,1,0:T(8,128)S(1)} %pad_maximum_fusion.own_ref, f32[2,4,96,512]{3,2,1,0:T(8,128)S(1)} %copy-done.4, f32[2,4,192,256]{3,2,1,0:T(8,128)S(1)} %pad_maximum_fusion.2.z_own_ref, f32[2,4,192,256]{3,2,1,0:T(8,128)} %collective-permute-done.37.z_got_ref), custom_call_target="tpu_custom_call" | custom-call | bytes 11010048 | tf_op jit(solution)/shard_map/unpack_down/pallas_call | solution.py:542
  275.2 4.1 %unpack_up.1 = f32[768,1536]{1,0:T(8,128)} custom-call(f32[2,4,192,256]{3,2,1,0:T(8,128)S(1)} %copy-done.1, f32[2,4,192,256]{3,2,1,0:T(8,128)S(1)} %copy-done.6, f32[2,4,192,256]{3,2,1,0:T(8,128)S(1)} %pad_maximum_fusion.2.z_own_ref, f32[2,4,192,256]{3,2,1,0:T(8,128)} %collective-permute-done.37.z_got_ref), custom_call_target="tpu_custom_call" | custom-call | bytes 11010048 | tf_op jit(solution)/shard_map/unpack_up/pallas_call | solution.py:542
  279.3 4.9 %unpack_attention.1 = (f32[384,768]{1,0:T(8,128)}, f32[768,384]{1,0:T(8,128)}, f32[768,384]{1,0:T(8,128)}, f32[768,384]{1,0:T(8,128)}) custom-call(f32[2,4,96,384]{3,2,1,0:T(8,128)} %pad_maximum_fusion.5.own_a, f32[2,4,96,384]{3,2,1,0:T(8,128)} %collective-permute-done.36.got_a, f32[2,4,96,384]{3,2,1,0:T(8,128)} %pad_maximum_fusion.4.own_b, ...), custom_call_target="tpu_custom_call" | custom-call | bytes 9437184 | tf_op jit(solution)/shard_map/unpack_attention/pallas_call | solution.py:542
  (137 shorter events, 9.4 us)
Async XLA Ops:
  13.3 27.7 %copy-start.25 = (f32[768]{0:T(1024)S(1)}, f32[768]{0:T(1024)}, u32[]{:S(2)}) copy-start(f32[768]{0:T(1024)} %gain_in.3) | copy-start | bytes 9220
  13.3 27.6 %copy-start.26 = (f32[768]{0:T(1024)S(1)}, f32[768]{0:T(1024)}, u32[]{:S(2)}) copy-start(f32[768]{0:T(1024)} %param.26) | copy-start | bytes 9220
  13.3 30.1 %copy-start.2 = (bf16[512,768]{1,0:T(8,128)(2,1)S(1)}, bf16[512,768]{1,0:T(8,128)(2,1)}, u32[]{:S(2)}) copy-start(bf16[512,768]{1,0:T(8,128)(2,1)} %x_ref.3) | copy-start | bytes 2359300
  13.3 30.1 %copy-start.7 = (bf16[512,768]{1,0:T(8,128)(2,1)S(1)}, bf16[512,768]{1,0:T(8,128)(2,1)}, u32[]{:S(2)}) copy-start(bf16[512,768]{1,0:T(8,128)(2,1)} %cot_ref.1) | copy-start | bytes 2359300
  13.3 30.0 %copy-start.13 = (bf16[512,384]{1,0:T(8,128)(2,1)S(1)}, bf16[512,384]{1,0:T(8,128)(2,1)}, u32[]{:S(2)}) copy-start(bf16[512,384]{1,0:T(8,128)(2,1)} %get-tuple-element.123.q_ref) | copy-start | bytes 1179652
  13.3 3.9 %collective-permute-start = (f32[512,768]{1,0:T(8,128)}, f32[512,768]{1,0:T(8,128)}, u32[]{:S(2)}, u32[]{:S(2)}) collective-permute-start(f32[512,768]{1,0:T(8,128)} %get-tuple-element.117.mine_in), channel_id=1, source_target_pairs={{0,1},{1,0},{2,3},{3,2},{4,5},{5,4},{6,7},{7,6},{8,9},{9,8},{10,11... | collective-permute-start | bytes 4718600 | tf_op jit(solution)/shard_map/ppermute | solution.py:567
  35.7 5.9 %collective-permute-start.1 = (f32[2,512,768]{2,1,0:T(8,128)}, f32[2,512,768]{2,1,0:T(8,128)S(1)}, u32[]{:S(2)}, u32[]{:S(2)}) collective-permute-start(f32[2,512,768]{2,1,0:T(8,128)} %get-tuple-element.118.mine_ref), channel_id=1, source_target_pairs={{0,1},{1,0},{2,3},{3,2},{4,5},{5,4},{6,7},{7,6},{8,9},{9,8},{10,11... | collective-permute-start | bytes 9437192 | tf_op jit(solution)/shard_map/ppermute | solution.py:567
  36.2 37.0 %collective-permute-start.3 = (f32[2,4,96,512]{3,2,1,0:T(8,128)}, f32[2,4,96,512]{3,2,1,0:T(8,128)S(1)}, u32[]{:S(2)}, u32[]{:S(2)}) collective-permute-start(f32[2,4,96,512]{3,2,1,0:T(8,128)} %get-tuple-element.132), channel_id=1, source_target_pairs={{0,2},{1,5},{2,0},{3,7},{4,6},{5,1},{6,4},{7,3},{8,10},{9,13},{10,... | collective-permute-start | bytes 4718600 | tf_op jit(solution)/shard_map/down_sum_first/ppermute | solution.py:572
  38.8 37.8 %collective-permute-start.6 = (f32[2,4,192,256]{3,2,1,0:T(8,128)}, f32[2,4,192,256]{3,2,1,0:T(8,128)S(1)}, u32[]{:S(2)}, u32[]{:S(2)}) collective-permute-start(f32[2,4,192,256]{3,2,1,0:T(8,128)} %get-tuple-element.139), channel_id=1, source_target_pairs={{0,8},{1,17},{2,10},{3,19},{4,12},{5,21},{6,14},{7,23},{8,0},{9,25... | collective-permute-start | bytes 4718600 | tf_op jit(solution)/shard_map/down_stack_sum_z_first/ppermute | solution.py:572
  40.4 36.5 %collective-permute-start.5 = (f32[2,4,192,256]{3,2,1,0:T(8,128)}, f32[2,4,192,256]{3,2,1,0:T(8,128)S(1)}, u32[]{:S(2)}, u32[]{:S(2)}) collective-permute-start(f32[2,4,192,256]{3,2,1,0:T(8,128)} %get-tuple-element.137), channel_id=1, source_target_pairs={{0,2},{1,5},{2,0},{3,7},{4,6},{5,1},{6,4},{7,3},{8,10},{9,13},{10,... | collective-permute-start | bytes 4718600 | tf_op jit(solution)/shard_map/up_sum_first/ppermute | solution.py:572
  41.7 1.7 copy-start.21
  43.4 1.1 copy-start.8
  44.5 1.1 copy-start.9
  45.6 1.1 copy-start.10
  46.6 1.1 copy-start.11
  47.7 1.1 copy-start.12
  48.8 1.0 copy-start.14
  49.7 1.0 copy-start.15
  50.7 1.0 copy-start.16
  51.7 0.9 copy-start.17
  54.9 18.6 %copy-start.24 = (f32[2,4,96,512]{3,2,1,0:T(8,128)S(1)}, f32[2,4,96,512]{3,2,1,0:T(8,128)}, u32[]{:S(2)}) copy-start(f32[2,4,96,512]{3,2,1,0:T(8,128)} %get-tuple-element.134) | copy-start | bytes 4718596
  73.2 3.4 %copy-start.23 = (f32[2,4,192,256]{3,2,1,0:T(8,128)S(1)}, f32[2,4,192,256]{3,2,1,0:T(8,128)}, u32[]{:S(2)}) copy-start(f32[2,4,192,256]{3,2,1,0:T(8,128)} %get-tuple-element.140) | copy-start | bytes 4718596
  73.2 21.3 %collective-permute-start.2 = (f32[512,768]{1,0:T(8,128)S(1)}, f32[512,768]{1,0:T(8,128)S(1)}, u32[]{:S(2)}, u32[]{:S(2)}) collective-permute-start(f32[512,768]{1,0:T(8,128)S(1)} %get-tuple-element.130.mine_ref), channel_id=1, source_target_pairs={{0,1},{1,0},{2,3},{3,2},{4,5},{5,4},{6,7},{7,6},{8,9},{9,8},{10,11... | collective-permute-start | bytes 4718600 | tf_op jit(solution)/shard_map/ppermute | solution.py:567
  73.9 17.7 %collective-permute-start.4 = (f32[4,96,512]{2,1,0:T(8,128)S(1)}, f32[4,96,512]{2,1,0:T(8,128)S(1)}, u32[]{:S(2)}, u32[]{:S(2)}) collective-permute-start(f32[4,96,512]{2,1,0:T(8,128)S(1)} %get-tuple-element.226), channel_id=1, source_target_pairs={{0,4},{1,3},{2,6},{3,1},{4,0},{5,7},{6,2},{7,5},{8,12},{9,11},{10,... | collective-permute-start | bytes 2359304 | tf_op jit(solution)/shard_map/down_sum_second/ppermute | solution.py:572
  76.6 1.4 copy-start.22
  78.0 5.2 %copy-start.27 = (f32[768]{0:T(1024)S(1)}, f32[768]{0:T(1024)}, u32[]{:S(2)}) copy-start(f32[768]{0:T(1024)} %gain_in.2) | copy-start | bytes 9220
  78.3 30.2 %collective-permute-start.11 = (f32[4,192,256]{2,1,0:T(8,128)S(1)}, f32[4,192,256]{2,1,0:T(8,128)S(1)}, u32[]{:S(2)}, u32[]{:S(2)}) collective-permute-start(f32[4,192,256]{2,1,0:T(8,128)S(1)} %get-tuple-element.223), channel_id=1, source_target_pairs={{0,4},{1,3},{2,6},{3,1},{4,0},{5,7},{6,2},{7,5},{8,12},{9,11},{10,... | collective-permute-start | bytes 2359304 | tf_op jit(solution)/shard_map/up_sum_second/ppermute | solution.py:572
  79.2 36.7 %collective-permute-start.8 = (f32[2,4,96,384]{3,2,1,0:T(8,128)S(1)}, f32[2,4,96,384]{3,2,1,0:T(8,128)S(1)}, u32[]{:S(2)}, u32[]{:S(2)}) collective-permute-start(f32[2,4,96,384]{3,2,1,0:T(8,128)S(1)} %get-tuple-element.151), channel_id=1, source_target_pairs={{0,2},{1,5},{2,0},{3,7},{4,6},{5,1},{6,4},{7,3},{8,10},{9,13},{10,... | collective-permute-start | bytes 3538952 | tf_op jit(solution)/shard_map/attention_rest_sum_first/ppermute | solution.py:572
  80.7 30.5 %collective-permute-start.10 = (f32[4,192,256]{2,1,0:T(8,128)S(1)}, f32[4,192,256]{2,1,0:T(8,128)S(1)}, u32[]{:S(2)}, u32[]{:S(2)}) collective-permute-start(f32[4,192,256]{2,1,0:T(8,128)S(1)} %get-tuple-element.225), channel_id=1, source_target_pairs={{0,16},{1,9},{2,18},{3,11},{4,20},{5,13},{6,22},{7,15},{8,24},{9,1... | collective-permute-start | bytes 2359304 | tf_op jit(solution)/shard_map/down_stack_sum_z_second/ppermute | solution.py:572
  91.6 46.1 %collective-permute-start.7 = (f32[784,384]{1,0:T(8,128)S(1)}, f32[784,384]{1,0:T(8,128)S(1)}, u32[]{:S(2)}, u32[]{:S(2)}) collective-permute-start(f32[784,384]{1,0:T(8,128)S(1)} %pad_maximum_fusion.3), channel_id=1, source_target_pairs={{0,2},{1,5},{2,0},{3,7},{4,6},{5,1},{6,4},{7,3},{8,10},{9,13},{10,... | collective-permute-start | bytes 3612680 | tf_op jit(solution)/shard_map/attention_sum_first/ppermute | solution.py:572
  94.5 18.6 %collective-permute-start.9 = (f32[2,96,512]{2,1,0:T(8,128)S(1)}, f32[2,96,512]{2,1,0:T(8,128)S(1)}, u32[]{:S(2)}, u32[]{:S(2)}) collective-permute-start(f32[2,96,512]{2,1,0:T(8,128)S(1)} %get-tuple-element.235), channel_id=1, source_target_pairs={{0,8},{1,17},{2,10},{3,19},{4,12},{5,21},{6,14},{7,23},{8,0},{9,25... | collective-permute-start | bytes 1179656 | tf_op jit(solution)/shard_map/down_sum_z_first/ppermute | solution.py:572
  108.5 24.1 %collective-permute-start.14 = (f32[2,192,256]{2,1,0:T(8,128)S(1)}, f32[2,192,256]{2,1,0:T(8,128)S(1)}, u32[]{:S(2)}, u32[]{:S(2)}) collective-permute-start(f32[2,192,256]{2,1,0:T(8,128)S(1)} %get-tuple-element.233), channel_id=1, source_target_pairs={{0,8},{1,17},{2,10},{3,19},{4,12},{5,21},{6,14},{7,23},{8,0},{9,25... | collective-permute-start | bytes 1179656 | tf_op jit(solution)/shard_map/up_sum_z_first/ppermute | solution.py:572
  111.2 19.6 %collective-permute-start.15 = (f32[2,192,256]{2,1,0:T(8,128)S(1)}, f32[2,192,256]{2,1,0:T(8,128)S(1)}, u32[]{:S(2)}, u32[]{:S(2)}) collective-permute-start(f32[2,192,256]{2,1,0:T(8,128)S(1)} %get-tuple-element.231), channel_id=1, source_target_pairs={{0,2},{1,5},{2,0},{3,7},{4,6},{5,1},{6,4},{7,3},{8,10},{9,13},{10,... | collective-permute-start | bytes 1179656 | tf_op jit(solution)/shard_map/down_stack_sum_first/ppermute | solution.py:572
  113.2 22.1 %collective-permute-start.13 = (f32[2,96,512]{2,1,0:T(8,128)S(1)}, f32[2,96,512]{2,1,0:T(8,128)S(1)}, u32[]{:S(2)}, u32[]{:S(2)}) collective-permute-start(f32[2,96,512]{2,1,0:T(8,128)S(1)} %add.146), channel_id=1, source_target_pairs={{0,16},{1,9},{2,18},{3,11},{4,20},{5,13},{6,22},{7,15},{8,24},{9,1... | collective-permute-start | bytes 1179656 | tf_op jit(solution)/shard_map/down_sum_z_second/ppermute | solution.py:572
  116.0 21.1 %collective-permute-start.12 = (f32[4,96,384]{2,1,0:T(8,128)S(1)}, f32[4,96,384]{2,1,0:T(8,128)S(1)}, u32[]{:S(2)}, u32[]{:S(2)}) collective-permute-start(f32[4,96,384]{2,1,0:T(8,128)S(1)} %get-tuple-element.228), channel_id=1, source_target_pairs={{0,4},{1,3},{2,6},{3,1},{4,0},{5,7},{6,2},{7,5},{8,12},{9,11},{10,... | collective-permute-start | bytes 1769480 | tf_op jit(solution)/shard_map/attention_rest_sum_second/ppermute | solution.py:572
  130.8 27.4 %collective-permute-start.19 = (f32[2,192,256]{2,1,0:T(8,128)S(1)}, f32[2,192,256]{2,1,0:T(8,128)S(1)}, u32[]{:S(2)}, u32[]{:S(2)}) collective-permute-start(f32[2,192,256]{2,1,0:T(8,128)S(1)} %add.153), channel_id=1, source_target_pairs={{0,4},{1,3},{2,6},{3,1},{4,0},{5,7},{6,2},{7,5},{8,12},{9,11},{10,... | collective-permute-start | bytes 1179656 | tf_op jit(solution)/shard_map/down_stack_sum_second/ppermute | solution.py:572
  132.7 20.9 %collective-permute-start.20 = (f32[2,192,256]{2,1,0:T(8,128)S(1)}, f32[2,192,256]{2,1,0:T(8,128)S(1)}, u32[]{:S(2)}, u32[]{:S(2)}) collective-permute-start(f32[2,192,256]{2,1,0:T(8,128)S(1)} %add.154), channel_id=1, source_target_pairs={{0,16},{1,9},{2,18},{3,11},{4,20},{5,13},{6,22},{7,15},{8,24},{9,1... | collective-permute-start | bytes 1179656 | tf_op jit(solution)/shard_map/up_sum_z_second/ppermute | solution.py:572
  135.4 26.5 %collective-permute-start.18 = (f32[2,96,512]{2,1,0:T(8,128)S(1)}, f32[2,96,512]{2,1,0:T(8,128)S(1)}, u32[]{:S(2)}, u32[]{:S(2)}) collective-permute-start(f32[2,96,512]{2,1,0:T(8,128)S(1)} %reverse_add_fusion.2), channel_id=1, source_target_pairs={{0,8},{1,17},{2,10},{3,19},{4,12},{5,21},{6,14},{7,23},{8,0},{9,25... | collective-permute-start | bytes 1179656 | tf_op jit(solution)/shard_map/down_gather_z_first/ppermute | solution.py:572
  137.1 25.0 %collective-permute-start.17 = (f32[2,96,384]{2,1,0:T(8,128)S(1)}, f32[2,96,384]{2,1,0:T(8,128)S(1)}, u32[]{:S(2)}, u32[]{:S(2)}) collective-permute-start(f32[2,96,384]{2,1,0:T(8,128)S(1)} %get-tuple-element.239), channel_id=1, source_target_pairs={{0,8},{1,17},{2,10},{3,19},{4,12},{5,21},{6,14},{7,23},{8,0},{9,25... | collective-permute-start | bytes 884744 | tf_op jit(solution)/shard_map/attention_rest_sum_z_first/ppermute | solution.py:572
  137.9 24.3 %collective-permute-start.16 = (f32[400,384]{1,0:T(8,128)S(1)}, f32[400,384]{1,0:T(8,128)S(1)}, u32[]{:S(2)}, u32[]{:S(2)}) collective-permute-start(f32[400,384]{1,0:T(8,128)S(1)} %pad_maximum_fusion.6), channel_id=1, source_target_pairs={{0,4},{1,3},{2,6},{3,1},{4,0},{5,7},{6,2},{7,5},{8,12},{9,11},{10,... | collective-permute-start | bytes 1843208 | tf_op jit(solution)/shard_map/attention_sum_second/ppermute | solution.py:572
  153.7 12.7 %collective-permute-start.25 = (f32[2,192,256]{2,1,0:T(8,128)S(1)}, f32[2,192,256]{2,1,0:T(8,128)S(1)}, u32[]{:S(2)}, u32[]{:S(2)}) collective-permute-start(f32[2,192,256]{2,1,0:T(8,128)S(1)} %reverse_add_fusion.1), channel_id=1, source_target_pairs={{0,8},{1,17},{2,10},{3,19},{4,12},{5,21},{6,14},{7,23},{8,0},{9,25... | collective-permute-start | bytes 1179656 | tf_op jit(solution)/shard_map/up_gather_z_first/ppermute | solution.py:572
  158.3 12.1 %collective-permute-start.24 = (f32[2,192,256]{2,1,0:T(8,128)S(1)}, f32[2,192,256]{2,1,0:T(8,128)S(1)}, u32[]{:S(2)}, u32[]{:S(2)}) collective-permute-start(f32[2,192,256]{2,1,0:T(8,128)S(1)} %reverse_add_fusion), channel_id=1, source_target_pairs={{0,2},{1,5},{2,0},{3,7},{4,6},{5,1},{6,4},{7,3},{8,10},{9,13},{10,... | collective-permute-start | bytes 1179656 | tf_op jit(solution)/shard_map/down_stack_gather_first/ppermute | solution.py:572
  162.1 14.5 %collective-permute-start.23 = (f32[4,96,512]{2,1,0:T(8,128)S(1)}, f32[4,96,512]{2,1,0:T(8,128)S(1)}, u32[]{:S(2)}, u32[]{:S(2)}) collective-permute-start(f32[4,96,512]{2,1,0:T(8,128)S(1)} %constant_dynamic-update-slice_fusion), channel_id=1, source_target_pairs={{0,4},{1,3},{2,6},{3,1},{4,0},{5,7},{6,2},{7,5},{8,12},{9,11},{10,... | collective-permute-start | bytes 2359304 | tf_op jit(solution)/shard_map/down_gather_second/ppermute | solution.py:572
  176.6 30.4 %collective-permute-start.28 = (f32[2,4,96,512]{3,2,1,0:T(8,128)S(1)}, f32[2,4,96,512]{3,2,1,0:T(8,128)S(1)}, u32[]{:S(2)}, u32[]{:S(2)}) collective-permute-start(f32[2,4,96,512]{3,2,1,0:T(8,128)S(1)} %pad_maximum_fusion.own_ref), channel_id=1, source_target_pairs={{0,2},{1,5},{2,0},{3,7},{4,6},{5,1},{6,4},{7,3},{8,10},{9,13},{10,... | collective-permute-start | bytes 4718600 | tf_op jit(solution)/shard_map/down_gather_first/ppermute | solution.py:572
  176.7 16.0 %collective-permute-start.22 = (f32[2,96,384]{2,1,0:T(8,128)S(1)}, f32[2,96,384]{2,1,0:T(8,128)S(1)}, u32[]{:S(2)}, u32[]{:S(2)}) collective-permute-start(f32[2,96,384]{2,1,0:T(8,128)S(1)} %add.163), channel_id=1, source_target_pairs={{0,16},{1,9},{2,18},{3,11},{4,20},{5,13},{6,22},{7,15},{8,24},{9,1... | collective-permute-start | bytes 884744 | tf_op jit(solution)/shard_map/attention_rest_sum_z_second/ppermute | solution.py:572
  184.7 20.5 %collective-permute-start.29 = (f32[4,192,256]{2,1,0:T(8,128)S(1)}, f32[4,192,256]{2,1,0:T(8,128)S(1)}, u32[]{:S(2)}, u32[]{:S(2)}) collective-permute-start(f32[4,192,256]{2,1,0:T(8,128)S(1)} %constant_dynamic-update-slice_fusion.2), channel_id=1, source_target_pairs={{0,4},{1,3},{2,6},{3,1},{4,0},{5,7},{6,2},{7,5},{8,12},{9,11},{10,... | collective-permute-start | bytes 2359304 | tf_op jit(solution)/shard_map/up_gather_second/ppermute | solution.py:572
  184.7 20.3 %collective-permute-start.21 = (f32[208,384]{1,0:T(8,128)S(1)}, f32[208,384]{1,0:T(8,128)S(1)}, u32[]{:S(2)}, u32[]{:S(2)}) collective-permute-start(f32[208,384]{1,0:T(8,128)S(1)} %pad_maximum_fusion.7), channel_id=1, source_target_pairs={{0,8},{1,17},{2,10},{3,19},{4,12},{5,21},{6,14},{7,23},{8,0},{9,25... | collective-permute-start | bytes 958472 | tf_op jit(solution)/shard_map/attention_sum_z_first/ppermute | solution.py:572
  184.7 41.5 %collective-permute-start.32 = (f32[4,192,256]{2,1,0:T(8,128)S(1)}, f32[4,192,256]{2,1,0:T(8,128)S(1)}, u32[]{:S(2)}, u32[]{:S(2)}) collective-permute-start(f32[4,192,256]{2,1,0:T(8,128)S(1)} %constant_dynamic-update-slice_fusion.4), channel_id=1, source_target_pairs={{0,16},{1,9},{2,18},{3,11},{4,20},{5,13},{6,22},{7,15},{8,24},{9,1... | collective-permute-start | bytes 2359304 | tf_op jit(solution)/shard_map/down_stack_gather_z_second/ppermute | solution.py:572
  192.8 23.7 %collective-permute-start.27 = (f32[2,96,384]{2,1,0:T(8,128)S(1)}, f32[2,96,384]{2,1,0:T(8,128)S(1)}, u32[]{:S(2)}, u32[]{:S(2)}) collective-permute-start(f32[2,96,384]{2,1,0:T(8,128)S(1)} %reverse_add_fusion.4), channel_id=1, source_target_pairs={{0,8},{1,17},{2,10},{3,19},{4,12},{5,21},{6,14},{7,23},{8,0},{9,25... | collective-permute-start | bytes 884744 | tf_op jit(solution)/shard_map/attention_rest_gather_z_first/ppermute | solution.py:572
  205.1 21.0 %collective-permute-start.26 = (f32[208,384]{1,0:T(8,128)S(1)}, f32[208,384]{1,0:T(8,128)S(1)}, u32[]{:S(2)}, u32[]{:S(2)}) collective-permute-start(f32[208,384]{1,0:T(8,128)S(1)} %pad_maximum_fusion.8), channel_id=1, source_target_pairs={{0,16},{1,9},{2,18},{3,11},{4,20},{5,13},{6,22},{7,15},{8,24},{9,1... | collective-permute-start | bytes 958472 | tf_op jit(solution)/shard_map/attention_sum_z_second/ppermute | solution.py:572
  205.3 21.1 %copy-start = (f32[2,4,192,256]{3,2,1,0:T(8,128)}, f32[2,4,192,256]{3,2,1,0:T(8,128)S(1)}, u32[]{:S(2)}) copy-start(f32[2,4,192,256]{3,2,1,0:T(8,128)S(1)} %pad_maximum_fusion.1.own_ref) | copy-start | bytes 4718596
  205.3 31.9 %collective-permute-start.34 = (f32[2,4,192,256]{3,2,1,0:T(8,128)S(1)}, f32[2,4,192,256]{3,2,1,0:T(8,128)S(1)}, u32[]{:S(2)}, u32[]{:S(2)}) collective-permute-start(f32[2,4,192,256]{3,2,1,0:T(8,128)S(1)} %pad_maximum_fusion.1.own_ref), channel_id=1, source_target_pairs={{0,2},{1,5},{2,0},{3,7},{4,6},{5,1},{6,4},{7,3},{8,10},{9,13},{10,... | collective-permute-start | bytes 4718600 | tf_op jit(solution)/shard_map/up_gather_first/ppermute | solution.py:572
  207.1 19.4 %copy-start.3 = (f32[2,4,96,512]{3,2,1,0:T(8,128)}, f32[2,4,96,512]{3,2,1,0:T(8,128)S(1)}, u32[]{:S(2)}) copy-start(f32[2,4,96,512]{3,2,1,0:T(8,128)S(1)} %collective-permute-done.28.got_ref) | copy-start | bytes 4718596
  226.1 8.5 %collective-permute-start.31 = (f32[2,96,384]{2,1,0:T(8,128)S(1)}, f32[2,96,384]{2,1,0:T(8,128)S(1)}, u32[]{:S(2)}, u32[]{:S(2)}) collective-permute-start(f32[2,96,384]{2,1,0:T(8,128)S(1)} %reverse_add_fusion.3), channel_id=1, source_target_pairs={{0,8},{1,17},{2,10},{3,19},{4,12},{5,21},{6,14},{7,23},{8,0},{9,25... | collective-permute-start | bytes 884744 | tf_op jit(solution)/shard_map/attention_gather_z_first/ppermute | solution.py:572
  226.2 9.9 %collective-permute-start.35 = (f32[4,96,384]{2,1,0:T(8,128)S(1)}, f32[4,96,384]{2,1,0:T(8,128)S(1)}, u32[]{:S(2)}, u32[]{:S(2)}) collective-permute-start(f32[4,96,384]{2,1,0:T(8,128)S(1)} %constant_dynamic-update-slice_fusion.6), channel_id=1, source_target_pairs={{0,4},{1,3},{2,6},{3,1},{4,0},{5,7},{6,2},{7,5},{8,12},{9,11},{10,... | collective-permute-start | bytes 1769480 | tf_op jit(solution)/shard_map/attention_rest_gather_second/ppermute | solution.py:572
  234.7 16.3 %collective-permute-start.33 = (f32[4,96,384]{2,1,0:T(8,128)S(1)}, f32[4,96,384]{2,1,0:T(8,128)S(1)}, u32[]{:S(2)}, u32[]{:S(2)}) collective-permute-start(f32[4,96,384]{2,1,0:T(8,128)S(1)} %constant_dynamic-update-slice_fusion.8), channel_id=1, source_target_pairs={{0,4},{1,3},{2,6},{3,1},{4,0},{5,7},{6,2},{7,5},{8,12},{9,11},{10,... | collective-permute-start | bytes 1769480 | tf_op jit(solution)/shard_map/attention_gather_second/ppermute | solution.py:572
  234.7 35.0 %collective-permute-start.37 = (f32[2,4,192,256]{3,2,1,0:T(8,128)S(1)}, f32[2,4,192,256]{3,2,1,0:T(8,128)}, u32[]{:S(2)}, u32[]{:S(2)}) collective-permute-start(f32[2,4,192,256]{3,2,1,0:T(8,128)S(1)} %pad_maximum_fusion.2.z_own_ref), channel_id=1, source_target_pairs={{0,8},{1,17},{2,10},{3,19},{4,12},{5,21},{6,14},{7,23},{8,0},{9,25... | collective-permute-start | bytes 4718600 | tf_op jit(solution)/shard_map/down_stack_gather_z_first/ppermute | solution.py:572
  237.2 17.9 %collective-permute-start.38 = (f32[2,4,96,384]{3,2,1,0:T(8,128)}, f32[2,4,96,384]{3,2,1,0:T(8,128)}, u32[]{:S(2)}, u32[]{:S(2)}) collective-permute-start(f32[2,4,96,384]{3,2,1,0:T(8,128)} %pad_maximum_fusion.4.own_b), channel_id=1, source_target_pairs={{0,2},{1,5},{2,0},{3,7},{4,6},{5,1},{6,4},{7,3},{8,10},{9,13},{10,... | collective-permute-start | bytes 3538952 | tf_op jit(solution)/shard_map/attention_rest_gather_first/ppermute | solution.py:572
  237.2 1.2 copy-start.5
  252.1 27.2 %collective-permute-start.36 = (f32[2,4,96,384]{3,2,1,0:T(8,128)}, f32[2,4,96,384]{3,2,1,0:T(8,128)}, u32[]{:S(2)}, u32[]{:S(2)}) collective-permute-start(f32[2,4,96,384]{3,2,1,0:T(8,128)} %pad_maximum_fusion.5.own_a), channel_id=1, source_target_pairs={{0,2},{1,5},{2,0},{3,7},{4,6},{5,1},{6,4},{7,3},{8,10},{9,13},{10,... | collective-permute-start | bytes 3538952 | tf_op jit(solution)/shard_map/attention_gather_first/ppermute | solution.py:572
  252.1 1.2 collective-permute-start.30
  255.2 20.0 %copy-start.1 = (f32[2,4,192,256]{3,2,1,0:T(8,128)S(1)}, f32[2,4,192,256]{3,2,1,0:T(8,128)}, u32[]{:S(2)}) copy-start(f32[2,4,192,256]{3,2,1,0:T(8,128)} %copy-done) | copy-start | bytes 4718596
  269.8 1.4 copy-start.4
  271.2 4.0 %copy-start.6 = (f32[2,4,192,256]{3,2,1,0:T(8,128)S(1)}, f32[2,4,192,256]{3,2,1,0:T(8,128)}, u32[]{:S(2)}) copy-start(f32[2,4,192,256]{3,2,1,0:T(8,128)} %copy-done.5) | copy-start | bytes 4718596
  (3 other events, 2.3 us)

commit v5 on v4

--- a/solution.py
+++ b/solution.py
@@ -30,7 +30,7 @@
 FIRST, SECOND = (X, Y), (Y, X)
 Z_FIRST, Z_SECOND = (Z1, Z2), (Z2, Z1)
 
-ORDER = "cduKdcubdIucdabcudbaucdbaucdbaudbacabuabca"
+ORDER = "cduKdcudbuIbdcuabdcaucbdaucdabuabcdaubabac"
 
 CASES = ((0, 0, 256, 0), (128, 256, 384, 128), (256, 640, 128, 128), (384, 768, 256, 128))
 TILES = (
@@ -468,66 +468,54 @@
         grad_ref[rows, :] = (delta_ref[rows, :] + back).astype(bf16)
 
 
-def each_block(own_ref, got_ref, put, z_first=False):
-    for place in range(PLANE):
-        for z in range(STACK):
-            first, second = (z, place) if z_first else (place, z)
-            value = (got_ref if first // 2 else own_ref)[first % 2, second]
-            put(quarter_at(place), fourth_at(z), value)
-
-
-def unpack_down(own_ref, got_ref, z_own_ref, z_got_ref, out_ref):
-    cut, part = own_ref.shape[-1], own_ref.shape[-2]
-
-    def put(quarter, fourth, value):
-        out_ref[fourths(quarter * STACK + fourth, part), :cut] = value
-
-    def put_z(quarter, fourth, value):
-        out_ref[fourths(quarter * STACK + fourth, part), cut:] = value[:part]
-
-    each_block(own_ref, got_ref, put)
-    each_block(z_own_ref, z_got_ref, put_z, True)
-
-
-def unpack_up(own_ref, got_ref, z_own_ref, z_got_ref, out_ref):
-    cut, part = own_ref.shape[-1], own_ref.shape[-2]
-    rest = z_own_ref.shape[-1] // 2
-
-    def put(quarter, fourth, value):
-        cols = pl.ds(pl.multiple_of(quarter * (cut + rest), LANES), cut)
-        out_ref[fourths(fourth, part), cols] = value
-
-    def put_z(quarter, fourth, value):
-        cols = pl.ds(pl.multiple_of(quarter * (cut + rest) + cut, LANES), rest)
-        for half in range(2):
-            out_ref[fourths(fourth * 2 + half, part // 2), cols] = value[part // 2 :, half * rest : (half + 1) * rest]
-
-    each_block(own_ref, got_ref, put)
-    each_block(z_own_ref, z_got_ref, put_z, True)
-
-
-def unpack_attention(own_a, got_a, own_b, got_b, *outs):
-    grads_ref = outs[4]
-    for portion, (own_ref, got_ref) in enumerate(((own_a, got_a), (own_b, got_b))):
-
-        def put(quarter, fourth, value, portion=portion):
-            grads_ref[quarter, portion, fourths(fourth, value.shape[0])] = value
-
-        each_block(own_ref, got_ref, put)
-    finish_att(outs)
-
-
-def finish_att(outs):
-    *outs, grads_ref, sems = outs
-    half = grads_ref.shape[-1]
-    copies = []
+def put_in_place(views, z_first, sent, olds, piece_ref, *refs):
+    *refs, sems = refs
+    outs = refs[olds:]
+    for start in (True, False):
+        count = 0
+        for i in range(2):
+            for j in range(STACK):
+                z, place = (2 * sent + i, j) if z_first else (j, 2 * sent + i)
+                for wanted, source, target in views(outs, quarter_at(place), fourth_at(z), piece_ref.at[i, j]):
+                    copy = pltpu.make_async_copy(source, target, sems.at[count])
+                    count += 1
+                    act = copy.start if start else copy.wait
+                    if wanted is None:
+                        act()
+                    else:
+                        pl.when(wanted)(act)
+
+
+def down_views(outs, quarter, fourth, block):
+    part, cols = block.shape
+    yield None, block, outs[0].at[fourths(quarter * STACK + fourth, part), pl.ds(0, cols)]
+
+
+def up_views(outs, quarter, fourth, block):
+    part, cols = block.shape
+    whole = outs[0].shape[1] // PLANE
+    yield None, block, outs[0].at[fourths(fourth, part), pl.ds(pl.multiple_of(quarter * whole, LANES), cols)]
+
+
+def stack_views(outs, quarter, fourth, block):
+    part, cols = block.shape[0] // 2, block.shape[1]
+    whole, rest = outs[1].shape[1] // PLANE, cols // 2
+    down_rows, down_cols = fourths(quarter * STACK + fourth, part), pl.ds(outs[0].shape[1] - cols, cols)
+    yield None, block.at[pl.ds(0, part), :], outs[0].at[down_rows, down_cols]
+    up_cols = pl.ds(pl.multiple_of((quarter + 1) * whole - rest, LANES), rest)
+    for half in range(2):
+        source = block.at[pl.ds(part, part), pl.ds(half * rest, rest)]
+        yield None, source, outs[1].at[fourths(fourth * 2 + half, part), up_cols]
+
+
+def attention_views(portion, outs, quarter, fourth, block):
+    part, half = block.shape[0], block.shape[1]
     for matrix, out in enumerate(outs):
-        for portion in range(2):
-            place = pl.ds(portion * half, half)
-            target = out.at[place, :] if matrix else out.at[:, place]
-            copies.append((grads_ref.at[matrix, portion], target))
-    for copy in fetch(copies, sems):
-        copy.wait()
+        if matrix:
+            target = out.at[pl.ds(pl.multiple_of(portion * half + fourth * part, 8), part), :]
+        else:
+            target = out.at[fourths(fourth, part), pl.ds(portion * half, half)]
+        yield quarter == matrix, block, target
 
 
 VMEM = pl.BlockSpec(memory_space=pltpu.VMEM)
@@ -629,15 +617,17 @@
         got, vec = part_of(got, keep, vec)
         own = over_groups(did(keep + got[::-1]))
         if vec is not None:
-            result.append(over_groups(vec))
+            sums.append(over_groups(vec))
         for step, (bits, label) in enumerate(reversed(steps[:3])):
             got = flip(own, bits, f"{name}_gather_{label}")
+            if step == 2:
+                result.append(own)
             yield
             own, got = turn(own, got)
             if step < 2:
                 own = did(jnp.stack([own, got]) if step == 1 else jnp.concatenate([own, got], 0))
         did(got)
-        result.extend((own, got))
+        result.append(got)
         yield
 
     scores = (heads, HALF, 8 * LANES)
@@ -698,7 +688,7 @@
         limit=62,
         loose_outs=(0, *range(3, 10)),
     )
-    made, grads = {key: [] for key in "dcuab"}, {}
+    made, grads, sums = {key: [] for key in "dcuab"}, {}, []
     chains = {
         "d": chain("down", parts[:2], made["d"]),
         "c": chain("down_stack", parts[2:4], made["c"], True),
@@ -743,38 +733,68 @@
         )
         did(state["grad_inputs"])
 
-    def unpack():
-        if "down" not in grads and len(made["d"]) == len(made["c"]) == 2:
-            grads["down"] = call(unpack_down, [((units, width), f32)], held=made["d"] + made["c"])
-            did(grads["down"][0])
-        if "up" not in grads and len(made["u"]) == len(made["c"]) == 2:
-            grads["up"] = call(unpack_up, [((width, units), f32)], held=made["u"] + made["c"])
-            did(grads["up"][0])
-        if "attention" not in grads and len(made["a"]) == 3 and len(made["b"]) == 2:
-            grads["attention"] = call(
-                unpack_attention,
-                [((heads_cols, width), f32)] + [((width, heads_cols), f32)] * 3,
-                held=made["a"][1:] + made["b"],
-                scratch=[((PLANE, 2, half, half), f32), sems(8)],
-                loose_outs=range(4),
-            )
+    shapes = {
+        "down": ((units, width), f32),
+        "up": ((width, units), f32),
+        "out": ((heads_cols, width), f32),
+        "query": ((width, heads_cols), f32),
+        "key": ((width, heads_cols), f32),
+        "value": ((width, heads_cols), f32),
+    }
+    attention = ("out", "query", "key", "value")
+    targets = {
+        "d": (down_views, ("down",)),
+        "u": (up_views, ("up",)),
+        "c": (stack_views, ("down", "up")),
+        "a": (partial(attention_views, 0), attention),
+        "b": (partial(attention_views, 1), attention),
+    }
+
+    def put(key, sent):
+        views, names = targets[key]
+        olds = [name for name in names if name in grads]
+        assert len(olds) in (0, len(names))
+        (piece,) = turn(made[key][sent])
+        results = pl.pallas_call(
+            partial(put_in_place, views, key == "c", sent, len(olds)),
+            name=f"put_{key}",
+            out_shape=[jax.ShapeDtypeStruct(*shapes[name]) for name in names],
+            in_specs=[VMEM] + [HBM] * len(olds),
+            out_specs=[HBM] * len(names),
+            scratch_shapes=[sems(32)],
+            input_output_aliases={1 + i: i for i in range(len(olds))},
+            compiler_params=pltpu.CompilerParams(vmem_limit_bytes=8 * 1024 * 1024),
+            cost_estimate=pl.CostEstimate(flops=0, bytes_accessed=2 * piece.size * 4, transcendentals=0),
+        )(piece, *[grads[name] for name in olds])
+        grads.update(zip(names, results))
+        did(results[0])
 
     did(grad_bd)
     pieces = {"K": backward, "I": input_back}
+    waiting = []
     for key in ORDER:
+        if key in waiting:
+            waiting.remove(key)
+            put(key, 0)
         if key in pieces:
             pieces[key]()
         else:
             next(chains[key])
-            unpack()
-    assert len(grads) == 3
-
-    vec = made["a"][0]
+        for other in list(waiting):
+            if other != "c" or ("down" in grads and "up" in grads):
+                waiting.remove(other)
+                put(other, 0)
+        if len(made.get(key, ())) == 1:
+            waiting.append(key)
+        elif len(made.get(key, ())) == 2:
+            put(key, 1)
+
+    vec = sums[0]
     n = width // half
     shared = (vec[: 3 * n] + swap(vec[: 3 * n])).reshape(3, width)
     grad_bu = vec[3 * n :].reshape(-1)[:units]
-    (grad_down,), (grad_up,) = grads["down"], grads["up"]
-    grad_out, grad_query, grad_key, grad_value = grads["attention"]
+    grad_down, grad_up = grads["down"], grads["up"]
+    grad_out, grad_query, grad_key, grad_value = (grads[name] for name in attention)
     output, grad_inputs = state["output"], state["grad_inputs"]
     return (
         output,

time: 286 us -> 278 us (0.972)
  waiting for transfers between devices: 139 us -> 115 us
  starting transfers between devices: 53.7 us -> 67 us
  Pallas kernels: 64.5 us -> 70.4 us
  local copies, waits for them, and re-layouts: 21.2 us -> 17.4 us
    ppermute x35, waiting for transfers between devices: 134 us -> 110 us  [flip(): return lax.ppermute(values, ('dp', 'mp'), pairs)]
    pallas_call x0 -> x10, Pallas kernels: none -> 18.9 us  [put(): pl.pallas_call(partial(put_in_place, views, key == 'c', sent, len(olds)),...]
    ppermute x35, starting transfers between devices: 52.3 us -> 66 us  [flip(): return lax.ppermute(values, ('dp', 'mp'), pairs)]
    pallas_call x7 -> x4, Pallas kernels: 64.5 us -> 51.5 us  [call(): pl.pallas_call(kernel, name=kernel.__name__, out_shape=shapes, in_specs=[...]
    unnamed x62 -> x50, local copies, waits for them, and re-layouts: 18.5 us -> 14.7 us
  transfers between devices with their start and end apart: 39 -> 39, of which waited for: 18 -> 17; matrix products, arithmetic and copies ran while one was open for 3% -> 2% of each run, Pallas kernels for 10% -> 14%
where the time goes in v5:
time: 278 us; the launch traced here: 275 us
  waiting for transfers between devices  115 us (41%)
  Pallas kernels  70.4 us (25%)
  starting transfers between devices  67 us (24%)
  local copies, waits for them, and re-layouts  17.4 us (6%)
  other arithmetic  3.78 us (1%)
    ppermute x35, waiting for transfers between devices, flip(): return lax.ppermute(values, ('dp', 'mp'), pairs)  110 us
    ppermute x35, starting transfers between devices, flip(): return lax.ppermute(values, ('dp', 'mp'), pairs)  66 us
    pallas_call x4, Pallas kernels, call(): pl.pallas_call(kernel, name=kernel.__name__, out_shape=shapes, in_specs=[...  51.5 us
    pallas_call x10, Pallas kernels, put(): pl.pallas_call(partial(put_in_place, views, key == 'c', sent, len(olds)),...  18.9 us
    unnamed x50, local copies, waits for them, and re-layouts  14.7 us
  transfers between devices with their start and end apart: 39, of which 17 were waited for; matrix products, arithmetic and copies ran while one was open for 2% of the time, Pallas kernels for 14%

profile of v5, /device:TPU:0, one launch (start us, length us, event | category | flops | bytes accessed | tf_op | source)
XLA Modules:
  0.0 275.1 jit_solution(1132926464788404860)
XLA Ops:
  0.6 1.4 copy.46.lengths_in
  2.0 11.3 %attention_forward.1 = (bf16[512,768]{1,0:T(8,128)(2,1)}, bf16[512,384]{1,0:T(8,128)(2,1)}, bf16[512,384]{1,0:T(8,128)(2,1)}, bf16[512,384]{1,0:T(8,128)(2,1)}, ...) custom-call(s32[16,8]{1,0:T(8,128)} %copy.46.lengths_in, s32[16]{0:T(128)} %pads_in.1, ...), custom_call_target="tpu_custom_call" | custom-call | flops 1207959552 | bytes 8916544 | tf_op jit(solution)/shard_map/attention_forward/pallas_call | solution.py:530
  13.8 3.4 %collective-permute-done.theirs_in = f32[512,768]{1,0:T(8,128)} collective-permute-done((f32[512,768]{1,0:T(8,128)}, f32[512,768]{1,0:T(8,128)}, u32[]{:S(2)}, u32[]{:S(2)}) %collective-permute-start) | collective-permute-done | bytes 1572896 | tf_op jit(solution)/shard_map/ppermute | solution.py:555
  17.2 18.5 %mlp_kernel.1 = (f32[512,768]{1,0:T(8,128)}, f32[1,1536]{1,0:T(1,128)}, f32[1,768]{1,0:T(1,128)}, f32[2,4,96,512]{3,2,1,0:T(8,128)}, f32[2,4,96,512]{3,2,1,0:T(8...) custom-call(f32[768]{0:T(1024)} %gain_in.3, ...), custom_call_target="tpu_custom_call" | custom-call | flops 7247757312 | bytes 23611392 | tf_op jit(solution)/shard_map/mlp_kernel/pallas_call | solution.py:530
  36.2 2.6 collective-permute-start.5
  38.8 1.6 collective-permute-start.4
  41.7 1.7 copy-done.15
  43.4 1.1 copy-done.2
  44.5 1.1 copy-done.3
  45.6 1.1 copy-done.4
  46.6 1.1 copy-done.5
  47.7 1.1 copy-done.6
  48.8 1.0 copy-done.8
  49.8 1.0 copy-done.9
  50.7 1.0 copy-done.10
  51.7 0.9 copy-done.11
  52.6 0.9 copy-done.12
  54.9 18.3 %attention_backward.1 = (bf16[512,768]{1,0:T(8,128)(2,1)}, f32[512,768]{1,0:T(8,128)S(1)}, f32[16,384]{1,0:T(8,128)S(1)}, f32[512,768]{1,0:T(8,128)S(1)}, f32[2,...) custom-call(f32[2,512,768]{2,1,0:T(8,128)} %get-tuple-element.136.mi, ...), custom_call_target="tpu_custom_call" | custom-call | flops 3019898880 | bytes 24681472 | tf_op jit(solution)/shard_map/attention_backward/pallas_call | solution.py:530
  73.6 2.9 %collective-permute-start.7 = (f32[4,96,512]{2,1,0:T(8,128)S(1)}, f32[4,96,512]{2,1,0:T(8,128)S(1)}, u32[]{:S(2)}, u32[]{:S(2)}) collective-permute-start(f32[4,96,512]{2,1,0:T(8,128)S(1)} %get-tuple-element.261), channel_id=1, source_target_pairs={{0,4},{1,3},{2,6},{3,1},{4,0},{5,7},{6,2},{7,5},{8,12},{9,11},{10,... | collective-permute-start | bytes 2359304 | tf_op jit(solution)/shard_map/down_sum_second/ppermute | solution.py:560
  76.8 1.6 collective-permute-start.11
  78.5 1.0 collective-permute-start.6
  79.6 2.6 collective-permute-start.9
  82.2 11.5 %collective-permute-done.7 = f32[4,96,512]{2,1,0:T(8,128)S(1)} collective-permute-done((f32[4,96,512]{2,1,0:T(8,128)S(1)}, f32[4,96,512]{2,1,0:T(8,128)S(1)}, u32[]{:S(2)}, u32[]{:S(2)}) %collective-permute-start.7) | collective-permute-done | bytes 786464 | tf_op jit(solution)/shard_map/down_sum_second/ppermute | solution.py:560
  93.8 1.8 collective-permute-start.8
  95.7 14.9 %collective-permute-done.6 = f32[4,192,256]{2,1,0:T(8,128)S(1)} collective-permute-done((f32[4,192,256]{2,1,0:T(8,128)S(1)}, f32[4,192,256]{2,1,0:T(8,128)S(1)}, u32[]{:S(2)}, u32[]{:S(2)}) %collective-permute-start.6) | collective-permute-done | bytes 786464 | tf_op jit(solution)/shard_map/up_sum_second/ppermute | solution.py:560
  110.6 1.7 collective-permute-start.10
  112.5 3.5 %input_kernel.1 = bf16[512,768]{1,0:T(8,128)(2,1)} custom-call(f32[512,768]{1,0:T(8,128)S(1)} %get-tuple-element.148.mine_ref, f32[512,768]{1,0:T(8,128)S(1)} %collective-permute-done.2.theirs_ref, bf16[512,768]{1,0:T(8,128)(2,1)S(1)} %copy-done, f32[1,768]{1,0:T(1,128)S(1)} %reshape.77.gain_ref, f32[512,768]{1,0:T(8,128)S(1)} %get-tuple-element.167.delta_ref), custom_call_target="tpu_custom_call" | custom-call | bytes 6294528 | tf_op jit(solution)/shard_map/input_kernel/pallas_call | solution.py:530
  116.1 2.3 collective-permute-start.14
  118.9 3.2 %collective-permute-done.10 = f32[2,96,512]{2,1,0:T(8,128)S(1)} collective-permute-done((f32[2,96,512]{2,1,0:T(8,128)S(1)}, f32[2,96,512]{2,1,0:T(8,128)S(1)}, u32[]{:S(2)}, u32[]{:S(2)}) %collective-permute-start.10) | collective-permute-done | bytes 393248 | tf_op jit(solution)/shard_map/down_sum_z_first/ppermute | solution.py:560
  122.1 2.3 collective-permute-start.13
  124.6 1.7 collective-permute-start.12
  126.3 11.5 %collective-permute-done.15 = f32[2,192,256]{2,1,0:T(8,128)S(1)} collective-permute-done((f32[2,192,256]{2,1,0:T(8,128)S(1)}, f32[2,192,256]{2,1,0:T(8,128)S(1)}, u32[]{:S(2)}, u32[]{:S(2)}) %collective-permute-start.15) | collective-permute-done | bytes 393248 | tf_op jit(solution)/shard_map/up_sum_z_first/ppermute | solution.py:560
  137.8 5.3 %collective-permute-start.20 = (f32[2,192,256]{2,1,0:T(8,128)S(1)}, f32[2,192,256]{2,1,0:T(8,128)S(1)}, u32[]{:S(2)}, u32[]{:S(2)}) collective-permute-start(f32[2,192,256]{2,1,0:T(8,128)S(1)} %add.153), channel_id=1, source_target_pairs={{0,16},{1,9},{2,18},{3,11},{4,20},{5,13},{6,22},{7,15},{8,24},{9,1... | collective-permute-start | bytes 1179656 | tf_op jit(solution)/shard_map/up_sum_z_second/ppermute | solution.py:560
  143.2 2.7 collective-permute-start.18
  146.1 1.7 collective-permute-start.19
  148.5 18.5 %collective-permute-done.20 = f32[2,192,256]{2,1,0:T(8,128)S(1)} collective-permute-done((f32[2,192,256]{2,1,0:T(8,128)S(1)}, f32[2,192,256]{2,1,0:T(8,128)S(1)}, u32[]{:S(2)}, u32[]{:S(2)}) %collective-permute-start.20) | collective-permute-done | bytes 393248 | tf_op jit(solution)/shard_map/up_sum_z_second/ppermute | solution.py:560
  167.3 1.6 collective-permute-start.23
  168.9 3.4 %collective-permute-start.27 = (f32[2,96,384]{2,1,0:T(8,128)S(1)}, f32[2,96,384]{2,1,0:T(8,128)S(1)}, u32[]{:S(2)}, u32[]{:S(2)}) collective-permute-start(f32[2,96,384]{2,1,0:T(8,128)S(1)} %add.163), channel_id=1, source_target_pairs={{0,16},{1,9},{2,18},{3,11},{4,20},{5,13},{6,22},{7,15},{8,24},{9,1... | collective-permute-start | bytes 884744 | tf_op jit(solution)/shard_map/attention_rest_sum_z_second/ppermute | solution.py:560
  172.3 2.5 collective-permute-start.22
  175.1 6.5 %collective-permute-done.24 = f32[2,192,256]{2,1,0:T(8,128)S(1)} collective-permute-done((f32[2,192,256]{2,1,0:T(8,128)S(1)}, f32[2,192,256]{2,1,0:T(8,128)S(1)}, u32[]{:S(2)}, u32[]{:S(2)}) %collective-permute-start.24) | collective-permute-done | bytes 393248 | tf_op jit(solution)/shard_map/up_gather_z_first/ppermute | solution.py:560
  182.6 2.2 collective-permute-done.22
  185.0 1.5 collective-permute-start.30
  186.5 13.0 %collective-permute-done.21 = f32[208,384]{1,0:T(8,128)S(1)} collective-permute-done((f32[208,384]{1,0:T(8,128)S(1)}, f32[208,384]{1,0:T(8,128)S(1)}, u32[]{:S(2)}, u32[]{:S(2)}) %collective-permute-start.21) | collective-permute-done | bytes 319520 | tf_op jit(solution)/shard_map/attention_sum_z_first/ppermute | solution.py:560
  199.7 1.4 put_d.2.refs_0_
  202.1 4.6 %collective-permute-start.35 = (f32[2,4,192,256]{3,2,1,0:T(8,128)S(1)}, f32[2,4,192,256]{3,2,1,0:T(8,128)S(1)}, u32[]{:S(2)}, u32[]{:S(2)}) collective-permute-start(f32[2,4,192,256]{3,2,1,0:T(8,128)S(1)} %pad_maximum_fusion.1.piece_ref), channel_id=1, source_target_pairs={{0,2},{1,5},{2,0},{3,7},{4,6},{5,1},{6,4},{7,3},{8,10},{9,13},{10,... | collective-permute-start | bytes 4718600 | tf_op jit(solution)/shard_map/up_gather_first/ppermute | solution.py:560
  206.7 15.8 %collective-permute-done.25 = f32[208,384]{1,0:T(8,128)S(1)} collective-permute-done((f32[208,384]{1,0:T(8,128)S(1)}, f32[208,384]{1,0:T(8,128)S(1)}, u32[]{:S(2)}, u32[]{:S(2)}) %collective-permute-start.25) | collective-permute-done | bytes 319520 | tf_op jit(solution)/shard_map/attention_sum_z_second/ppermute | solution.py:560
  222.7 1.4 put_u.2.refs_1_
  224.2 1.2 collective-permute-start.34
  225.6 1.4 put_c.2
  227.0 1.4 put_d.3.refs_0_
  228.5 0.9 collective-permute-done.29
  229.4 1.2 collective-permute-start.33
  231.5 1.4 put_u.3.refs_1_
  232.9 1.2 collective-permute-done.34
  234.2 7.3 %collective-permute-start.37 = (f32[2,4,96,384]{3,2,1,0:T(8,128)S(1)}, f32[2,4,96,384]{3,2,1,0:T(8,128)}, u32[]{:S(2)}, u32[]{:S(2)}) collective-permute-start(f32[2,4,96,384]{3,2,1,0:T(8,128)S(1)} %pad_maximum_fusion.4.piece_ref), channel_id=1, source_target_pairs={{0,2},{1,5},{2,0},{3,7},{4,6},{5,1},{6,4},{7,3},{8,10},{9,13},{10,... | collective-permute-start | bytes 3538952 | tf_op jit(solution)/shard_map/attention_rest_gather_first/ppermute | solution.py:560
  241.5 5.1 %collective-permute-done.33 = f32[4,96,384]{2,1,0:T(8,128)S(1)} collective-permute-done((f32[4,96,384]{2,1,0:T(8,128)S(1)}, f32[4,96,384]{2,1,0:T(8,128)S(1)}, u32[]{:S(2)}, u32[]{:S(2)}) %collective-permute-start.33) | collective-permute-done | bytes 589856 | tf_op jit(solution)/shard_map/attention_gather_second/ppermute | solution.py:560
  246.6 1.1 pad_maximum_fusion.5.piece_ref
  247.7 7.4 %collective-permute-start.36 = (f32[2,4,96,384]{3,2,1,0:T(8,128)}, f32[2,4,96,384]{3,2,1,0:T(8,128)}, u32[]{:S(2)}, u32[]{:S(2)}) collective-permute-start(f32[2,4,96,384]{3,2,1,0:T(8,128)} %pad_maximum_fusion.5.piece_ref), channel_id=1, source_target_pairs={{0,2},{1,5},{2,0},{3,7},{4,6},{5,1},{6,4},{7,3},{8,10},{9,13},{10,... | collective-permute-start | bytes 3538952 | tf_op jit(solution)/shard_map/attention_gather_first/ppermute | solution.py:560
  258.1 1.3 put_b.2
  259.5 2.6 put_a.2
  262.0 2.6 put_b.3
  264.6 5.0 %collective-permute-done.36.piece_ref = f32[2,4,96,384]{3,2,1,0:T(8,128)} collective-permute-done((f32[2,4,96,384]{3,2,1,0:T(8,128)}, f32[2,4,96,384]{3,2,1,0:T(8,128)}, u32[]{:S(2)}, u32[]{:S(2)}) %collective-permute-start.36) | collective-permute-done | bytes 1179680 | tf_op jit(solution)/shard_map/attention_gather_first/ppermute | solution.py:560
  269.6 2.6 put_a.3
  272.2 2.8 %put_c.3 = (f32[1536,768]{1,0:T(8,128)}, f32[768,1536]{1,0:T(8,128)}) custom-call(f32[2,4,192,256]{3,2,1,0:T(8,128)} %collective-permute-done.38.piece_ref, f32[1536,768]{1,0:T(8,128)} %put_d.3.refs_0_, f32[768,1536]{1,0:T(8,128)} %put_u.3.refs_1_), custom_call_target="tpu_custom_call", output_to_operand_aliasing={{0}: (1, {}), {1}: (2, {})} | custom-call | bytes 3145728 | tf_op jit(solution)/shard_map/put_c/pallas_call | solution.py:758
  (132 shorter events, 13.7 us)
Async XLA Ops:
  13.3 27.7 %copy-start.19 = (f32[768]{0:T(1024)S(1)}, f32[768]{0:T(1024)}, u32[]{:S(2)}) copy-start(f32[768]{0:T(1024)} %gain_in.3) | copy-start | bytes 9220
  13.3 27.6 %copy-start.20 = (f32[768]{0:T(1024)S(1)}, f32[768]{0:T(1024)}, u32[]{:S(2)}) copy-start(f32[768]{0:T(1024)} %param.26) | copy-start | bytes 9220
  13.3 30.1 %copy-start = (bf16[512,768]{1,0:T(8,128)(2,1)S(1)}, bf16[512,768]{1,0:T(8,128)(2,1)}, u32[]{:S(2)}) copy-start(bf16[512,768]{1,0:T(8,128)(2,1)} %x_ref.3) | copy-start | bytes 2359300
  13.3 30.1 %copy-start.1 = (bf16[512,768]{1,0:T(8,128)(2,1)S(1)}, bf16[512,768]{1,0:T(8,128)(2,1)}, u32[]{:S(2)}) copy-start(bf16[512,768]{1,0:T(8,128)(2,1)} %cot_ref.1) | copy-start | bytes 2359300
  13.3 30.0 %copy-start.7 = (bf16[512,384]{1,0:T(8,128)(2,1)S(1)}, bf16[512,384]{1,0:T(8,128)(2,1)}, u32[]{:S(2)}) copy-start(bf16[512,384]{1,0:T(8,128)(2,1)} %get-tuple-element.141.q_ref) | copy-start | bytes 1179652
  13.3 3.9 %collective-permute-start = (f32[512,768]{1,0:T(8,128)}, f32[512,768]{1,0:T(8,128)}, u32[]{:S(2)}, u32[]{:S(2)}) collective-permute-start(f32[512,768]{1,0:T(8,128)} %get-tuple-element.135.mine_in), channel_id=1, source_target_pairs={{0,1},{1,0},{2,3},{3,2},{4,5},{5,4},{6,7},{7,6},{8,9},{9,8},{10,11... | collective-permute-start | bytes 4718600 | tf_op jit(solution)/shard_map/ppermute | solution.py:555
  35.7 5.9 %collective-permute-start.1 = (f32[2,512,768]{2,1,0:T(8,128)}, f32[2,512,768]{2,1,0:T(8,128)S(1)}, u32[]{:S(2)}, u32[]{:S(2)}) collective-permute-start(f32[2,512,768]{2,1,0:T(8,128)} %get-tuple-element.136.mine_ref), channel_id=1, source_target_pairs={{0,1},{1,0},{2,3},{3,2},{4,5},{5,4},{6,7},{7,6},{8,9},{9,8},{10,11... | collective-permute-start | bytes 9437192 | tf_op jit(solution)/shard_map/ppermute | solution.py:555
  36.2 37.0 %collective-permute-start.5 = (f32[2,4,96,512]{3,2,1,0:T(8,128)}, f32[2,4,96,512]{3,2,1,0:T(8,128)S(1)}, u32[]{:S(2)}, u32[]{:S(2)}) collective-permute-start(f32[2,4,96,512]{3,2,1,0:T(8,128)} %get-tuple-element.154), channel_id=1, source_target_pairs={{0,2},{1,5},{2,0},{3,7},{4,6},{5,1},{6,4},{7,3},{8,10},{9,13},{10,... | collective-permute-start | bytes 4718600 | tf_op jit(solution)/shard_map/down_sum_first/ppermute | solution.py:560
  38.8 37.7 %collective-permute-start.4 = (f32[2,4,192,256]{3,2,1,0:T(8,128)}, f32[2,4,192,256]{3,2,1,0:T(8,128)S(1)}, u32[]{:S(2)}, u32[]{:S(2)}) collective-permute-start(f32[2,4,192,256]{3,2,1,0:T(8,128)} %get-tuple-element.152), channel_id=1, source_target_pairs={{0,8},{1,17},{2,10},{3,19},{4,12},{5,21},{6,14},{7,23},{8,0},{9,25... | collective-permute-start | bytes 4718600 | tf_op jit(solution)/shard_map/down_stack_sum_z_first/ppermute | solution.py:560
  40.4 36.4 %collective-permute-start.3 = (f32[2,4,192,256]{3,2,1,0:T(8,128)}, f32[2,4,192,256]{3,2,1,0:T(8,128)S(1)}, u32[]{:S(2)}, u32[]{:S(2)}) collective-permute-start(f32[2,4,192,256]{3,2,1,0:T(8,128)} %get-tuple-element.150), channel_id=1, source_target_pairs={{0,2},{1,5},{2,0},{3,7},{4,6},{5,1},{6,4},{7,3},{8,10},{9,13},{10,... | collective-permute-start | bytes 4718600 | tf_op jit(solution)/shard_map/up_sum_first/ppermute | solution.py:560
  41.7 1.7 copy-start.15
  43.4 1.1 copy-start.2
  44.5 1.1 copy-start.3
  45.6 1.1 copy-start.4
  46.6 1.1 copy-start.5
  47.7 1.1 copy-start.6
  48.8 1.0 copy-start.8
  49.7 1.0 copy-start.9
  50.7 1.0 copy-start.10
  51.7 0.9 copy-start.11
  52.6 0.9 copy-start.12
  53.6 0.7 copy-start.13
  54.2 0.7 copy-start.14
  54.9 18.3 %copy-start.18 = (f32[2,4,96,512]{3,2,1,0:T(8,128)S(1)}, f32[2,4,96,512]{3,2,1,0:T(8,128)}, u32[]{:S(2)}) copy-start(f32[2,4,96,512]{3,2,1,0:T(8,128)} %get-tuple-element.156) | copy-start | bytes 4718596
  73.2 3.3 %copy-start.17 = (f32[2,4,192,256]{3,2,1,0:T(8,128)S(1)}, f32[2,4,192,256]{3,2,1,0:T(8,128)}, u32[]{:S(2)}) copy-start(f32[2,4,192,256]{3,2,1,0:T(8,128)} %get-tuple-element.158) | copy-start | bytes 4718596
  73.6 20.2 %collective-permute-start.7 = (f32[4,96,512]{2,1,0:T(8,128)S(1)}, f32[4,96,512]{2,1,0:T(8,128)S(1)}, u32[]{:S(2)}, u32[]{:S(2)}) collective-permute-start(f32[4,96,512]{2,1,0:T(8,128)S(1)} %get-tuple-element.261), channel_id=1, source_target_pairs={{0,4},{1,3},{2,6},{3,1},{4,0},{5,7},{6,2},{7,5},{8,12},{9,11},{10,... | collective-permute-start | bytes 2359304 | tf_op jit(solution)/shard_map/down_sum_second/ppermute | solution.py:560
  76.5 1.8 copy-start.16
  76.5 36.0 %collective-permute-start.2 = (f32[512,768]{1,0:T(8,128)S(1)}, f32[512,768]{1,0:T(8,128)S(1)}, u32[]{:S(2)}, u32[]{:S(2)}) collective-permute-start(f32[512,768]{1,0:T(8,128)S(1)} %get-tuple-element.148.mine_ref), channel_id=1, source_target_pairs={{0,1},{1,0},{2,3},{3,2},{4,5},{5,4},{6,7},{7,6},{8,9},{9,8},{10,11... | collective-permute-start | bytes 4718600 | tf_op jit(solution)/shard_map/ppermute | solution.py:555
  76.7 2.8 %copy-start.21 = (f32[768]{0:T(1024)S(1)}, f32[768]{0:T(1024)}, u32[]{:S(2)}) copy-start(f32[768]{0:T(1024)} %gain_in.2) | copy-start | bytes 9220
  76.8 39.2 %collective-permute-start.11 = (f32[2,4,96,384]{3,2,1,0:T(8,128)S(1)}, f32[2,4,96,384]{3,2,1,0:T(8,128)S(1)}, u32[]{:S(2)}, u32[]{:S(2)}) collective-permute-start(f32[2,4,96,384]{3,2,1,0:T(8,128)S(1)} %get-tuple-element.171), channel_id=1, source_target_pairs={{0,2},{1,5},{2,0},{3,7},{4,6},{5,1},{6,4},{7,3},{8,10},{9,13},{10,... | collective-permute-start | bytes 3538952 | tf_op jit(solution)/shard_map/attention_rest_sum_first/ppermute | solution.py:560
  78.5 32.1 %collective-permute-start.6 = (f32[4,192,256]{2,1,0:T(8,128)S(1)}, f32[4,192,256]{2,1,0:T(8,128)S(1)}, u32[]{:S(2)}, u32[]{:S(2)}) collective-permute-start(f32[4,192,256]{2,1,0:T(8,128)S(1)} %get-tuple-element.262), channel_id=1, source_target_pairs={{0,4},{1,3},{2,6},{3,1},{4,0},{5,7},{6,2},{7,5},{8,12},{9,11},{10,... | collective-permute-start | bytes 2359304 | tf_op jit(solution)/shard_map/up_sum_second/ppermute | solution.py:560
  79.6 44.9 %collective-permute-start.9 = (f32[4,192,256]{2,1,0:T(8,128)S(1)}, f32[4,192,256]{2,1,0:T(8,128)S(1)}, u32[]{:S(2)}, u32[]{:S(2)}) collective-permute-start(f32[4,192,256]{2,1,0:T(8,128)S(1)} %get-tuple-element.259), channel_id=1, source_target_pairs={{0,16},{1,9},{2,18},{3,11},{4,20},{5,13},{6,22},{7,15},{8,24},{9,1... | collective-permute-start | bytes 2359304 | tf_op jit(solution)/shard_map/down_stack_sum_z_second/ppermute | solution.py:560
  93.8 54.0 %collective-permute-start.8 = (f32[784,384]{1,0:T(8,128)S(1)}, f32[784,384]{1,0:T(8,128)S(1)}, u32[]{:S(2)}, u32[]{:S(2)}) collective-permute-start(f32[784,384]{1,0:T(8,128)S(1)} %pad_maximum_fusion.3), channel_id=1, source_target_pairs={{0,2},{1,5},{2,0},{3,7},{4,6},{5,1},{6,4},{7,3},{8,10},{9,13},{10,... | collective-permute-start | bytes 3612680 | tf_op jit(solution)/shard_map/attention_sum_first/ppermute | solution.py:560
  110.6 11.4 %collective-permute-start.10 = (f32[2,96,512]{2,1,0:T(8,128)S(1)}, f32[2,96,512]{2,1,0:T(8,128)S(1)}, u32[]{:S(2)}, u32[]{:S(2)}) collective-permute-start(f32[2,96,512]{2,1,0:T(8,128)S(1)} %get-tuple-element.271), channel_id=1, source_target_pairs={{0,8},{1,17},{2,10},{3,19},{4,12},{5,21},{6,14},{7,23},{8,0},{9,25... | collective-permute-start | bytes 1179656 | tf_op jit(solution)/shard_map/down_sum_z_first/ppermute | solution.py:560
  116.1 27.0 %collective-permute-start.14 = (f32[4,96,384]{2,1,0:T(8,128)S(1)}, f32[4,96,384]{2,1,0:T(8,128)S(1)}, u32[]{:S(2)}, u32[]{:S(2)}) collective-permute-start(f32[4,96,384]{2,1,0:T(8,128)S(1)} %get-tuple-element.265), channel_id=1, source_target_pairs={{0,4},{1,3},{2,6},{3,1},{4,0},{5,7},{6,2},{7,5},{8,12},{9,11},{10,... | collective-permute-start | bytes 1769480 | tf_op jit(solution)/shard_map/attention_rest_sum_second/ppermute | solution.py:560
  118.4 19.4 %collective-permute-start.15 = (f32[2,192,256]{2,1,0:T(8,128)S(1)}, f32[2,192,256]{2,1,0:T(8,128)S(1)}, u32[]{:S(2)}, u32[]{:S(2)}) collective-permute-start(f32[2,192,256]{2,1,0:T(8,128)S(1)} %get-tuple-element.267), channel_id=1, source_target_pairs={{0,8},{1,17},{2,10},{3,19},{4,12},{5,21},{6,14},{7,23},{8,0},{9,25... | collective-permute-start | bytes 1179656 | tf_op jit(solution)/shard_map/up_sum_z_first/ppermute | solution.py:560
  122.1 23.7 %collective-permute-start.13 = (f32[2,96,512]{2,1,0:T(8,128)S(1)}, f32[2,96,512]{2,1,0:T(8,128)S(1)}, u32[]{:S(2)}, u32[]{:S(2)}) collective-permute-start(f32[2,96,512]{2,1,0:T(8,128)S(1)} %add.147), channel_id=1, source_target_pairs={{0,16},{1,9},{2,18},{3,11},{4,20},{5,13},{6,22},{7,15},{8,24},{9,1... | collective-permute-start | bytes 1179656 | tf_op jit(solution)/shard_map/down_sum_z_second/ppermute | solution.py:560
  124.6 21.5 %collective-permute-start.12 = (f32[2,192,256]{2,1,0:T(8,128)S(1)}, f32[2,192,256]{2,1,0:T(8,128)S(1)}, u32[]{:S(2)}, u32[]{:S(2)}) collective-permute-start(f32[2,192,256]{2,1,0:T(8,128)S(1)} %get-tuple-element.268), channel_id=1, source_target_pairs={{0,2},{1,5},{2,0},{3,7},{4,6},{5,1},{6,4},{7,3},{8,10},{9,13},{10,... | collective-permute-start | bytes 1179656 | tf_op jit(solution)/shard_map/down_stack_sum_first/ppermute | solution.py:560
  137.8 29.2 %collective-permute-start.20 = (f32[2,192,256]{2,1,0:T(8,128)S(1)}, f32[2,192,256]{2,1,0:T(8,128)S(1)}, u32[]{:S(2)}, u32[]{:S(2)}) collective-permute-start(f32[2,192,256]{2,1,0:T(8,128)S(1)} %add.153), channel_id=1, source_target_pairs={{0,16},{1,9},{2,18},{3,11},{4,20},{5,13},{6,22},{7,15},{8,24},{9,1... | collective-permute-start | bytes 1179656 | tf_op jit(solution)/shard_map/up_sum_z_second/ppermute | solution.py:560
  143.2 25.7 %collective-permute-start.18 = (f32[2,96,384]{2,1,0:T(8,128)S(1)}, f32[2,96,384]{2,1,0:T(8,128)S(1)}, u32[]{:S(2)}, u32[]{:S(2)}) collective-permute-start(f32[2,96,384]{2,1,0:T(8,128)S(1)} %get-tuple-element.275), channel_id=1, source_target_pairs={{0,8},{1,17},{2,10},{3,19},{4,12},{5,21},{6,14},{7,23},{8,0},{9,25... | collective-permute-start | bytes 884744 | tf_op jit(solution)/shard_map/attention_rest_sum_z_first/ppermute | solution.py:560
  145.9 26.3 %collective-permute-start.17 = (f32[2,96,512]{2,1,0:T(8,128)S(1)}, f32[2,96,512]{2,1,0:T(8,128)S(1)}, u32[]{:S(2)}, u32[]{:S(2)}) collective-permute-start(f32[2,96,512]{2,1,0:T(8,128)S(1)} %reverse_add_fusion.2), channel_id=1, source_target_pairs={{0,8},{1,17},{2,10},{3,19},{4,12},{5,21},{6,14},{7,23},{8,0},{9,25... | collective-permute-start | bytes 1179656 | tf_op jit(solution)/shard_map/down_gather_z_first/ppermute | solution.py:560
  146.1 21.1 %collective-permute-start.19 = (f32[2,192,256]{2,1,0:T(8,128)S(1)}, f32[2,192,256]{2,1,0:T(8,128)S(1)}, u32[]{:S(2)}, u32[]{:S(2)}) collective-permute-start(f32[2,192,256]{2,1,0:T(8,128)S(1)} %add.156), channel_id=1, source_target_pairs={{0,4},{1,3},{2,6},{3,1},{4,0},{5,7},{6,2},{7,5},{8,12},{9,11},{10,... | collective-permute-start | bytes 1179656 | tf_op jit(solution)/shard_map/down_stack_sum_second/ppermute | solution.py:560
  148.0 26.9 %collective-permute-start.16 = (f32[400,384]{1,0:T(8,128)S(1)}, f32[400,384]{1,0:T(8,128)S(1)}, u32[]{:S(2)}, u32[]{:S(2)}) collective-permute-start(f32[400,384]{1,0:T(8,128)S(1)} %pad_maximum_fusion.6), channel_id=1, source_target_pairs={{0,4},{1,3},{2,6},{3,1},{4,0},{5,7},{6,2},{7,5},{8,12},{9,11},{10,... | collective-permute-start | bytes 1843208 | tf_op jit(solution)/shard_map/attention_sum_second/ppermute | solution.py:560
  167.1 14.5 %collective-permute-start.24 = (f32[2,192,256]{2,1,0:T(8,128)S(1)}, f32[2,192,256]{2,1,0:T(8,128)S(1)}, u32[]{:S(2)}, u32[]{:S(2)}) collective-permute-start(f32[2,192,256]{2,1,0:T(8,128)S(1)} %reverse_add_fusion.1), channel_id=1, source_target_pairs={{0,8},{1,17},{2,10},{3,19},{4,12},{5,21},{6,14},{7,23},{8,0},{9,25... | collective-permute-start | bytes 1179656 | tf_op jit(solution)/shard_map/up_gather_z_first/ppermute | solution.py:560
  167.3 14.5 %collective-permute-start.23 = (f32[2,192,256]{2,1,0:T(8,128)S(1)}, f32[2,192,256]{2,1,0:T(8,128)S(1)}, u32[]{:S(2)}, u32[]{:S(2)}) collective-permute-start(f32[2,192,256]{2,1,0:T(8,128)S(1)} %reverse_add_fusion), channel_id=1, source_target_pairs={{0,2},{1,5},{2,0},{3,7},{4,6},{5,1},{6,4},{7,3},{8,10},{9,13},{10,... | collective-permute-start | bytes 1179656 | tf_op jit(solution)/shard_map/down_stack_gather_first/ppermute | solution.py:560
  168.9 32.2 %collective-permute-start.27 = (f32[2,96,384]{2,1,0:T(8,128)S(1)}, f32[2,96,384]{2,1,0:T(8,128)S(1)}, u32[]{:S(2)}, u32[]{:S(2)}) collective-permute-start(f32[2,96,384]{2,1,0:T(8,128)S(1)} %add.163), channel_id=1, source_target_pairs={{0,16},{1,9},{2,18},{3,11},{4,20},{5,13},{6,22},{7,15},{8,24},{9,1... | collective-permute-start | bytes 884744 | tf_op jit(solution)/shard_map/attention_rest_sum_z_second/ppermute | solution.py:560
  172.3 12.5 %collective-permute-start.22 = (f32[4,96,512]{2,1,0:T(8,128)S(1)}, f32[4,96,512]{2,1,0:T(8,128)S(1)}, u32[]{:S(2)}, u32[]{:S(2)}) collective-permute-start(f32[4,96,512]{2,1,0:T(8,128)S(1)} %constant_dynamic-update-slice_fusion), channel_id=1, source_target_pairs={{0,4},{1,3},{2,6},{3,1},{4,0},{5,7},{6,2},{7,5},{8,12},{9,11},{10,... | collective-permute-start | bytes 2359304 | tf_op jit(solution)/shard_map/down_gather_second/ppermute | solution.py:560
  175.0 24.5 %collective-permute-start.21 = (f32[208,384]{1,0:T(8,128)S(1)}, f32[208,384]{1,0:T(8,128)S(1)}, u32[]{:S(2)}, u32[]{:S(2)}) collective-permute-start(f32[208,384]{1,0:T(8,128)S(1)} %pad_maximum_fusion.7), channel_id=1, source_target_pairs={{0,8},{1,17},{2,10},{3,19},{4,12},{5,21},{6,14},{7,23},{8,0},{9,25... | collective-permute-start | bytes 958472 | tf_op jit(solution)/shard_map/attention_sum_z_first/ppermute | solution.py:560
  181.7 20.3 %collective-permute-start.26 = (f32[4,192,256]{2,1,0:T(8,128)S(1)}, f32[4,192,256]{2,1,0:T(8,128)S(1)}, u32[]{:S(2)}, u32[]{:S(2)}) collective-permute-start(f32[4,192,256]{2,1,0:T(8,128)S(1)} %constant_dynamic-update-slice_fusion.2), channel_id=1, source_target_pairs={{0,4},{1,3},{2,6},{3,1},{4,0},{5,7},{6,2},{7,5},{8,12},{9,11},{10,... | collective-permute-start | bytes 2359304 | tf_op jit(solution)/shard_map/up_gather_second/ppermute | solution.py:560
  181.9 43.5 %collective-permute-start.31 = (f32[4,192,256]{2,1,0:T(8,128)S(1)}, f32[4,192,256]{2,1,0:T(8,128)S(1)}, u32[]{:S(2)}, u32[]{:S(2)}) collective-permute-start(f32[4,192,256]{2,1,0:T(8,128)S(1)} %constant_dynamic-update-slice_fusion.4), channel_id=1, source_target_pairs={{0,16},{1,9},{2,18},{3,11},{4,20},{5,13},{6,22},{7,15},{8,24},{9,1... | collective-permute-start | bytes 2359304 | tf_op jit(solution)/shard_map/down_stack_gather_z_second/ppermute | solution.py:560
  185.0 40.6 %collective-permute-start.30 = (f32[2,4,96,512]{3,2,1,0:T(8,128)S(1)}, f32[2,4,96,512]{3,2,1,0:T(8,128)S(1)}, u32[]{:S(2)}, u32[]{:S(2)}) collective-permute-start(f32[2,4,96,512]{3,2,1,0:T(8,128)S(1)} %pad_maximum_fusion.piece_ref), channel_id=1, source_target_pairs={{0,2},{1,5},{2,0},{3,7},{4,6},{5,1},{6,4},{7,3},{8,10},{9,13},{10,... | collective-permute-start | bytes 4718600 | tf_op jit(solution)/shard_map/down_gather_first/ppermute | solution.py:560
  199.6 22.9 %collective-permute-start.25 = (f32[208,384]{1,0:T(8,128)S(1)}, f32[208,384]{1,0:T(8,128)S(1)}, u32[]{:S(2)}, u32[]{:S(2)}) collective-permute-start(f32[208,384]{1,0:T(8,128)S(1)} %pad_maximum_fusion.8), channel_id=1, source_target_pairs={{0,16},{1,9},{2,18},{3,11},{4,20},{5,13},{6,22},{7,15},{8,24},{9,1... | collective-permute-start | bytes 958472 | tf_op jit(solution)/shard_map/attention_sum_z_second/ppermute | solution.py:560
  202.1 29.4 %collective-permute-start.35 = (f32[2,4,192,256]{3,2,1,0:T(8,128)S(1)}, f32[2,4,192,256]{3,2,1,0:T(8,128)S(1)}, u32[]{:S(2)}, u32[]{:S(2)}) collective-permute-start(f32[2,4,192,256]{3,2,1,0:T(8,128)S(1)} %pad_maximum_fusion.1.piece_ref), channel_id=1, source_target_pairs={{0,2},{1,5},{2,0},{3,7},{4,6},{5,1},{6,4},{7,3},{8,10},{9,13},{10,... | collective-permute-start | bytes 4718600 | tf_op jit(solution)/shard_map/up_gather_first/ppermute | solution.py:560
  206.7 17.4 %collective-permute-start.32 = (f32[2,96,384]{2,1,0:T(8,128)S(1)}, f32[2,96,384]{2,1,0:T(8,128)S(1)}, u32[]{:S(2)}, u32[]{:S(2)}) collective-permute-start(f32[2,96,384]{2,1,0:T(8,128)S(1)} %reverse_add_fusion.4), channel_id=1, source_target_pairs={{0,8},{1,17},{2,10},{3,19},{4,12},{5,21},{6,14},{7,23},{8,0},{9,25... | collective-permute-start | bytes 884744 | tf_op jit(solution)/shard_map/attention_rest_gather_z_first/ppermute | solution.py:560
  222.6 6.8 %collective-permute-start.29 = (f32[2,96,384]{2,1,0:T(8,128)S(1)}, f32[2,96,384]{2,1,0:T(8,128)S(1)}, u32[]{:S(2)}, u32[]{:S(2)}) collective-permute-start(f32[2,96,384]{2,1,0:T(8,128)S(1)} %reverse_add_fusion.3), channel_id=1, source_target_pairs={{0,8},{1,17},{2,10},{3,19},{4,12},{5,21},{6,14},{7,23},{8,0},{9,25... | collective-permute-start | bytes 884744 | tf_op jit(solution)/shard_map/attention_gather_z_first/ppermute | solution.py:560
  224.2 9.9 %collective-permute-start.34 = (f32[4,96,384]{2,1,0:T(8,128)S(1)}, f32[4,96,384]{2,1,0:T(8,128)S(1)}, u32[]{:S(2)}, u32[]{:S(2)}) collective-permute-start(f32[4,96,384]{2,1,0:T(8,128)S(1)} %constant_dynamic-update-slice_fusion.6), channel_id=1, source_target_pairs={{0,4},{1,3},{2,6},{3,1},{4,0},{5,7},{6,2},{7,5},{8,12},{9,11},{10,... | collective-permute-start | bytes 1769480 | tf_op jit(solution)/shard_map/attention_rest_gather_second/ppermute | solution.py:560
  229.4 17.2 %collective-permute-start.33 = (f32[4,96,384]{2,1,0:T(8,128)S(1)}, f32[4,96,384]{2,1,0:T(8,128)S(1)}, u32[]{:S(2)}, u32[]{:S(2)}) collective-permute-start(f32[4,96,384]{2,1,0:T(8,128)S(1)} %constant_dynamic-update-slice_fusion.8), channel_id=1, source_target_pairs={{0,4},{1,3},{2,6},{3,1},{4,0},{5,7},{6,2},{7,5},{8,12},{9,11},{10,... | collective-permute-start | bytes 1769480 | tf_op jit(solution)/shard_map/attention_gather_second/ppermute | solution.py:560
  230.6 41.5 %collective-permute-start.38 = (f32[2,4,192,256]{3,2,1,0:T(8,128)S(1)}, f32[2,4,192,256]{3,2,1,0:T(8,128)}, u32[]{:S(2)}, u32[]{:S(2)}) collective-permute-start(f32[2,4,192,256]{3,2,1,0:T(8,128)S(1)} %pad_maximum_fusion.2.piece_ref), channel_id=1, source_target_pairs={{0,8},{1,17},{2,10},{3,19},{4,12},{5,21},{6,14},{7,23},{8,0},{9,25... | collective-permute-start | bytes 4718600 | tf_op jit(solution)/shard_map/down_stack_gather_z_first/ppermute | solution.py:560
  234.2 25.2 %collective-permute-start.37 = (f32[2,4,96,384]{3,2,1,0:T(8,128)S(1)}, f32[2,4,96,384]{3,2,1,0:T(8,128)}, u32[]{:S(2)}, u32[]{:S(2)}) collective-permute-start(f32[2,4,96,384]{3,2,1,0:T(8,128)S(1)} %pad_maximum_fusion.4.piece_ref), channel_id=1, source_target_pairs={{0,2},{1,5},{2,0},{3,7},{4,6},{5,1},{6,4},{7,3},{8,10},{9,13},{10,... | collective-permute-start | bytes 3538952 | tf_op jit(solution)/shard_map/attention_rest_gather_first/ppermute | solution.py:560
  247.7 21.9 %collective-permute-start.36 = (f32[2,4,96,384]{3,2,1,0:T(8,128)}, f32[2,4,96,384]{3,2,1,0:T(8,128)}, u32[]{:S(2)}, u32[]{:S(2)}) collective-permute-start(f32[2,4,96,384]{3,2,1,0:T(8,128)} %pad_maximum_fusion.5.piece_ref), channel_id=1, source_target_pairs={{0,2},{1,5},{2,0},{3,7},{4,6},{5,1},{6,4},{7,3},{8,10},{9,13},{10,... | collective-permute-start | bytes 3538952 | tf_op jit(solution)/shard_map/attention_gather_first/ppermute | solution.py:560
  255.1 1.2 collective-permute-start.28

commit v6 on v5

--- a/solution.py
+++ b/solution.py
@@ -30,7 +30,7 @@
 FIRST, SECOND = (X, Y), (Y, X)
 Z_FIRST, Z_SECOND = (Z1, Z2), (Z2, Z1)
 
-ORDER = "cduKdcudbuIbdcuabdcaucbdaucdabuabcdaubabac"
+ORDER = "cudKubcdIudabucdbuacdcaucbdauduabbcadbabac"
 
 CASES = ((0, 0, 256, 0), (128, 256, 384, 128), (256, 640, 128, 128), (384, 768, 256, 128))
 TILES = (
@@ -363,29 +363,48 @@
     sender.finish()
 
 
-def attention_backward(
-    mine_ref, theirs_ref, residual_ref, gain_ref, cot_ref, att_ref, wo_ref, q_ref, k_ref, v_ref, prob_ref,
-    normed_ref, wq_ref, wk_ref, wv_ref, cos_ref, sin_ref, x_ref, bd_ref, gbd_ref, gbu_ref,
-    output_ref, delta_ref, vec_ref, part_ref, *outs_and_scratch,
-):
-    *outs, branch_ref, datt_ref, dq_ref, dk_ref, dv_ref, dk_acc, dv_acc, grads_ref, gnorm_ref = outs_and_scratch
+def attention_backward(*refs):
+    ins, refs = refs[:21], refs[21:]
+    (output_out, delta_out, part_out, vec_ref), outs_at, refs = refs[:4], refs[4:8], refs[8:]
+    held, refs = refs[:21], refs[21:]
+    (output_ref, delta_ref, part_ref), outs, refs = refs[:3], refs[3:7], refs[7:]
+    branch_ref, datt_ref, dq_ref, dk_ref, dv_ref, dk_acc, dv_acc, grads_ref, gnorm_ref, sems, out_sems = refs
+    mine_ref, theirs_ref, residual_ref, cot_ref, gain_ref, bd_ref, att_ref, wo_ref, q_ref, k_ref, v_ref = held[:11]
+    prob_ref, cos_ref, sin_ref, wq_ref, wk_ref, wv_ref, x_ref, normed_ref, gbd_ref, gbu_ref = held[11:]
     row_count = residual_ref.shape[0]
     heads_cols = wq_ref.shape[1]
     pairs = heads_cols // LANES
+    halves = (slice(0, row_count // 2), slice(row_count // 2, row_count))
+    first = []
+    for rows in halves:
+        first += [(a.at[:, rows, :], b.at[:, rows, :]) for a, b in zip(ins[:2], held[:2])]
+        first += [(a.at[rows, :], b.at[rows, :]) for a, b in zip(ins[2:4], held[2:4])]
+    copies = fetch(first + list(zip(ins[4:], held[4:])), sems)
+    sender = Sender(out_sems)
     gnorm_ref[...] = jnp.zeros_like(gnorm_ref)
-
-    @pl.loop(0, row_count // 64)
-    def _(i):
-        rows = pl.ds(pl.multiple_of(i * 64, 64), 64)
-        delta = mine_ref[0, rows, :] + theirs_ref[0, rows, :]
-        residual = residual_ref[rows, :]
-        output_ref[rows, :] = (residual + (mine_ref[1, rows, :] + theirs_ref[1, rows, :]) + bd_ref[...]).astype(bf16)
-        back, gain_part = norm_back_rows(residual, gain_ref[...], delta)
-        back = back + cot_ref[rows, :].astype(f32)
-        delta_ref[rows, :] = back
-        branch_ref[rows, :] = back.astype(bf16)
-        gnorm_ref[0:1, :] += gain_part
-
+    copies[8].wait()
+    copies[9].wait()
+    gain, bias_down = gain_ref[...].reshape(1, -1), bd_ref[...].reshape(1, -1)
+    for half in range(2):
+        for copy in copies[4 * half : 4 * half + 4]:
+            copy.wait()
+
+        @pl.loop(0, row_count // 128)
+        def _(i, half=half):
+            rows = pl.ds(pl.multiple_of(half * (row_count // 2) + i * 64, 64), 64)
+            delta = mine_ref[0, rows, :] + theirs_ref[0, rows, :]
+            residual = residual_ref[rows, :]
+            output_ref[rows, :] = (residual + (mine_ref[1, rows, :] + theirs_ref[1, rows, :]) + bias_down).astype(bf16)
+            back, gain_part = norm_back_rows(residual, gain, delta)
+            back = back + cot_ref[rows, :].astype(f32)
+            delta_ref[rows, :] = back
+            branch_ref[rows, :] = back.astype(bf16)
+            gnorm_ref[0:1, :] += gain_part
+
+    sender.send(output_ref, output_out)
+    sender.send(delta_ref, delta_out)
+    for copy in copies[10:]:
+        copy.wait()
     for block in range(2):
         rows = slice(block * 256, block * 256 + 256)
         datt_ref[rows, :] = nt(branch_ref[rows, :], wo_ref[...]).astype(bf16)
@@ -436,6 +455,7 @@
         part_ref[rows, :] = (
             nt(dq_ref[rows, :], wq_ref[...]) + nt(dk_ref[rows, :], wk_ref[...]) + nt(dv_ref[rows, :], wv_ref[...])
         )
+    sender.send(part_ref, part_out)
 
     @pl.loop(0, row_count // 64)
     def _(i):
@@ -453,10 +473,15 @@
     for matrix, grad_rows in ((1, dq_ref), (2, dk_ref), (3, dv_ref)):
         grad = tn(normed_ref[...], grad_rows[...])
         grads_ref[matrix, 0], grads_ref[matrix, 1] = grad[:half], grad[half:]
-    for place in range(PLANE):
-        quarter = quarter_at(place)
-        place_quarter(outs[:2], place, grads_ref[quarter, 0])
-        place_quarter(outs[2:], place, grads_ref[quarter, 1])
+    for places in ((2, 3), (0, 1)):
+        for place in places:
+            quarter = quarter_at(place)
+            place_quarter(outs[:2], place, grads_ref[quarter, 0])
+            place_quarter(outs[2:], place, grads_ref[quarter, 1])
+        for portion in range(2):
+            which = 2 * portion + places[0] // 2
+            sender.send(outs[which], outs_at[which])
+    sender.finish()
 
 
 def input_kernel(mine_ref, theirs_ref, x_ref, gain_ref, delta_ref, grad_ref):
@@ -549,7 +574,7 @@
     units = w_up.shape[1]
     heads = heads_cols // HEAD
     cosine, sine = (jnp.asarray(t) for t in rope_tables())
-    gain_attn, gain_mlp = norm_attn.reshape(1, -1), norm_mlp.reshape(1, -1)
+    gain_attn = norm_attn.reshape(1, -1)
 
     def swap(values):
         return lax.ppermute(values, "mp", [(0, 1), (1, 0)])
@@ -698,26 +723,32 @@
 
     def backward():
         (shares_other,) = turn(state["shares_other"])
-        state["output"], state["delta_residual"], vec, state["normed_part"], *parts = call(
+        ins = [
+            shares, shares_other, residual, cotangent, norm_mlp, b_down, attended, w_out, q, k, v,
+            probs, cosine, sine, w_query, w_key, w_value, inputs, normed, grad_bd, grad_bu,
+        ]
+        outs = [rows_of["width"], rows_of["sum"], rows_of["sum"]]
+        pieces = portions(half // STACK, half) * 2
+        state["output"], state["delta_residual"], state["normed_part"], vec, *parts = call(
             attention_backward,
-            [((rows, width), bf16), ((rows, width), f32), ((16, half), f32), ((rows, width), f32)]
-            + portions(half // STACK, half) * 2,
-            held=[
-                shares, shares_other, residual, gain_mlp, cotangent, attended, w_out, q, k, v, probs,
-                normed, w_query, w_key, w_value, cosine, sine, inputs, b_down.reshape(1, -1), grad_bd, grad_bu,
-            ],
+            [*outs, ((16, half), f32), *pieces],
+            loose=ins,
             scratch=[
-                ((rows, width), bf16),
-                ((rows, heads_cols), bf16),
-                ((rows, heads_cols), bf16),
-                ((rows, heads_cols), bf16),
-                ((rows, heads_cols), bf16),
+                *[(a.shape, a.dtype) for a in ins],
+                *outs,
+                *pieces,
+                rows_of["width"],
+                *[rows_of["heads"]] * 4,
                 ((rows, LANES), f32),
                 ((rows, LANES), f32),
                 ((PLANE, 2, half, half), f32),
                 ((8, width), f32),
+                sems(25),
+                sems(7),
             ],
             flops=2 * rows * width * heads_cols * 10,
+            limit=62,
+            loose_outs=(0, 1, 2, 4, 5, 6, 7),
         )
         did(vec)
         state["normed_other"] = swap(state["normed_part"])

time: 278 us -> 262 us (0.942); the launches traced: 275 us -> 262 us
  local copies, waits for them, and re-layouts: 17.4 us -> 5.34 us
  other arithmetic: 3.78 us -> 7.47 us
  waiting for transfers between devices: 115 us -> 112 us
    unnamed x50 -> x30, local copies, waits for them, and re-layouts: 14.7 us -> 2.67 us
    add x6, other arithmetic: 1.08 us -> 4.65 us  [chain(): send, keep = (did(join(keep[1] + got[1])), keep[0] + got[0])]
    ppermute x35, waiting for transfers between devices: 110 us -> 107 us  [flip(): return lax.ppermute(values, ('dp', 'mp'), pairs)]
    ppermute x35, starting transfers between devices: 66 us -> 63.1 us  [flip(): return lax.ppermute(values, ('dp', 'mp'), pairs)]
  transfers between devices with their start and end apart: 39 -> 39, of which waited for: 17 -> 24; matrix products, arithmetic and copies ran while one was open for 2% -> 4% of each run, Pallas kernels for 14% -> 15%
where the time goes in v6:
time: 262 us
  waiting for transfers between devices  112 us (43%)
  Pallas kernels  71.8 us (27%)
  starting transfers between devices  64.5 us (25%)
  other arithmetic  7.47 us (3%)
  local copies, waits for them, and re-layouts  5.34 us (2%)
    ppermute x35, waiting for transfers between devices, flip(): return lax.ppermute(values, ('dp', 'mp'), pairs)  107 us
    ppermute x35, starting transfers between devices, flip(): return lax.ppermute(values, ('dp', 'mp'), pairs)  63.1 us
    pallas_call x4, Pallas kernels, call(): pl.pallas_call(kernel, name=kernel.__name__, out_shape=shapes, in_specs=[...  52.9 us
    pallas_call x10, Pallas kernels, put(): pl.pallas_call(partial(put_in_place, views, key == 'c', sent, len(olds)),...  18.9 us
  transfers between devices with their start and end apart: 39, of which 24 were waited for; matrix products, arithmetic and copies ran while one was open for 4% of the time, Pallas kernels for 15%

profile of v6, /device:TPU:0, one launch (start us, length us, event | category | flops | bytes accessed | tf_op | source)
XLA Modules:
  0.0 262.0 jit_solution(3943578461219695399)
XLA Ops:
  0.6 1.4 copy.46.lengths_in
  2.0 11.3 %attention_forward.1 = (bf16[512,768]{1,0:T(8,128)(2,1)}, bf16[512,384]{1,0:T(8,128)(2,1)}, bf16[512,384]{1,0:T(8,128)(2,1)}, bf16[512,384]{1,0:T(8,128)(2,1)}, ...) custom-call(s32[16,8]{1,0:T(8,128)} %copy.46.lengths_in, s32[16]{0:T(128)} %pads_in.1, ...), custom_call_target="tpu_custom_call" | custom-call | flops 1207959552 | bytes 8916544 | tf_op jit(solution)/shard_map/attention_forward/pallas_call | solution.py:555
  13.8 3.2 %collective-permute-done.theirs_in = f32[512,768]{1,0:T(8,128)S(1)} collective-permute-done((f32[512,768]{1,0:T(8,128)}, f32[512,768]{1,0:T(8,128)S(1)}, u32[]{:S(2)}, u32[]{:S(2)}) %collective-permute-start) | collective-permute-done | bytes 1572896 | tf_op jit(solution)/shard_map/ppermute | solution.py:580
  17.0 1.1 copy-done.10
  18.2 18.5 %mlp_kernel.1 = (f32[512,768]{1,0:T(8,128)}, f32[1,1536]{1,0:T(1,128)}, f32[1,768]{1,0:T(1,128)}, f32[2,4,96,512]{3,2,1,0:T(8,128)}, f32[2,4,96,512]{3,2,1,0:T(8...) custom-call(f32[768]{0:T(1024)} %refs_4_.1, ...), custom_call_target="tpu_custom_call" | custom-call | flops 7247757312 | bytes 23611392 | tf_op jit(solution)/shard_map/mlp_kernel/pallas_call | solution.py:555
  37.1 2.6 %collective-permute-start.5 = (f32[2,4,192,256]{3,2,1,0:T(8,128)}, f32[2,4,192,256]{3,2,1,0:T(8,128)}, u32[]{:S(2)}, u32[]{:S(2)}) collective-permute-start(f32[2,4,192,256]{3,2,1,0:T(8,128)} %get-tuple-element.154), channel_id=1, source_target_pairs={{0,2},{1,5},{2,0},{3,7},{4,6},{5,1},{6,4},{7,3},{8,10},{9,13},{10,... | collective-permute-start | bytes 4718600 | tf_op jit(solution)/shard_map/up_sum_first/ppermute | solution.py:585
  39.8 1.6 collective-permute-start.4
  42.8 19.6 %attention_backward.1 = (bf16[512,768]{1,0:T(8,128)(2,1)}, f32[512,768]{1,0:T(8,128)}, f32[512,768]{1,0:T(8,128)}, f32[16,384]{1,0:T(8,128)}, f32[2,4,96,384]{3,...) custom-call(f32[2,512,768]{2,1,0:T(8,128)} %get-tuple-element.136.refs_0_, ...), custom_call_target="tpu_custom_call" | custom-call | flops 3019898880 | bytes 24681472 | tf_op jit(solution)/shard_map/attention_backward/pallas_call | solution.py:555
  62.9 2.2 add_bitcast_fusion.2
  65.1 2.7 %collective-permute-start.7 = (f32[4,192,256]{2,1,0:T(8,128)S(1)}, f32[4,192,256]{2,1,0:T(8,128)S(1)}, u32[]{:S(2)}, u32[]{:S(2)}) collective-permute-start(f32[4,192,256]{2,1,0:T(8,128)S(1)} %get-tuple-element.263), channel_id=1, source_target_pairs={{0,4},{1,3},{2,6},{3,1},{4,0},{5,7},{6,2},{7,5},{8,12},{9,11},{10,... | collective-permute-start | bytes 2359304 | tf_op jit(solution)/shard_map/up_sum_second/ppermute | solution.py:585
  67.8 9.5 %collective-permute-done.4 = f32[2,4,192,256]{3,2,1,0:T(8,128)} collective-permute-done((f32[2,4,192,256]{3,2,1,0:T(8,128)}, f32[2,4,192,256]{3,2,1,0:T(8,128)}, u32[]{:S(2)}, u32[]{:S(2)}) %collective-permute-start.4) | collective-permute-done | bytes 1572896 | tf_op jit(solution)/shard_map/down_stack_sum_z_first/ppermute | solution.py:585
  77.3 1.7 add_bitcast_fusion
  79.1 2.3 collective-permute-done.3
  81.4 2.4 collective-permute-start.9
  84.1 1.6 collective-permute-start.10
  85.7 2.5 collective-permute-start.14
  89.0 3.5 %input_kernel.1 = bf16[512,768]{1,0:T(8,128)(2,1)} custom-call(f32[512,768]{1,0:T(8,128)S(1)} %copy-done.2, f32[512,768]{1,0:T(8,128)S(1)} %collective-permute-done.2.theirs_ref, bf16[512,768]{1,0:T(8,128)(2,1)S(1)} %copy-done, f32[1,768]{1,0:T(1,128)S(1)} %reshape.69.gain_ref, f32[512,768]{1,0:T(8,128)S(1)} %copy-done.1), custom_call_target="tpu_custom_call" | custom-call | bytes 6294528 | tf_op jit(solution)/shard_map/input_kernel/pallas_call | solution.py:555
  92.5 1.7 collective-permute-start.8
  94.2 10.5 %collective-permute-done.10 = f32[4,96,512]{2,1,0:T(8,128)S(1)} collective-permute-done((f32[4,96,512]{2,1,0:T(8,128)S(1)}, f32[4,96,512]{2,1,0:T(8,128)S(1)}, u32[]{:S(2)}, u32[]{:S(2)}) %collective-permute-start.10) | collective-permute-done | bytes 786464 | tf_op jit(solution)/shard_map/down_sum_second/ppermute | solution.py:585
  104.8 1.1 collective-permute-done.9
  107.0 1.6 collective-permute-start.13
  108.6 3.3 %collective-permute-done.8 = f32[2,192,256]{2,1,0:T(8,128)S(1)} collective-permute-done((f32[2,192,256]{2,1,0:T(8,128)S(1)}, f32[2,192,256]{2,1,0:T(8,128)S(1)}, u32[]{:S(2)}, u32[]{:S(2)}) %collective-permute-start.8) | collective-permute-done | bytes 393248 | tf_op jit(solution)/shard_map/up_sum_z_first/ppermute | solution.py:585
  111.9 4.8 %collective-permute-start.11 = (f32[2,192,256]{2,1,0:T(8,128)S(1)}, f32[2,192,256]{2,1,0:T(8,128)S(1)}, u32[]{:S(2)}, u32[]{:S(2)}) collective-permute-start(f32[2,192,256]{2,1,0:T(8,128)S(1)} %add.145), channel_id=1, source_target_pairs={{0,16},{1,9},{2,18},{3,11},{4,20},{5,13},{6,22},{7,15},{8,24},{9,1... | collective-permute-start | bytes 1179656 | tf_op jit(solution)/shard_map/up_sum_z_second/ppermute | solution.py:585
  116.8 5.6 %collective-permute-done.14 = f32[4,192,256]{2,1,0:T(8,128)S(1)} collective-permute-done((f32[4,192,256]{2,1,0:T(8,128)S(1)}, f32[4,192,256]{2,1,0:T(8,128)S(1)}, u32[]{:S(2)}, u32[]{:S(2)}) %collective-permute-start.14) | collective-permute-done | bytes 786464 | tf_op jit(solution)/shard_map/down_stack_sum_z_second/ppermute | solution.py:585
  123.1 2.5 collective-permute-done.13
  125.9 4.4 %collective-permute-start.21 = (f32[2,96,384]{2,1,0:T(8,128)S(1)}, f32[2,96,384]{2,1,0:T(8,128)S(1)}, u32[]{:S(2)}, u32[]{:S(2)}) collective-permute-start(f32[2,96,384]{2,1,0:T(8,128)S(1)} %get-tuple-element.275), channel_id=1, source_target_pairs={{0,8},{1,17},{2,10},{3,19},{4,12},{5,21},{6,14},{7,23},{8,0},{9,25... | collective-permute-start | bytes 884744 | tf_op jit(solution)/shard_map/attention_rest_sum_z_first/ppermute | solution.py:585
  130.3 6.3 %collective-permute-done.11 = f32[2,192,256]{2,1,0:T(8,128)S(1)} collective-permute-done((f32[2,192,256]{2,1,0:T(8,128)S(1)}, f32[2,192,256]{2,1,0:T(8,128)S(1)}, u32[]{:S(2)}, u32[]{:S(2)}) %collective-permute-start.11) | collective-permute-done | bytes 393248 | tf_op jit(solution)/shard_map/up_sum_z_second/ppermute | solution.py:585
  138.3 1.6 collective-permute-start.17
  139.9 3.8 %collective-permute-done.18 = f32[2,96,512]{2,1,0:T(8,128)S(1)} collective-permute-done((f32[2,96,512]{2,1,0:T(8,128)S(1)}, f32[2,96,512]{2,1,0:T(8,128)S(1)}, u32[]{:S(2)}, u32[]{:S(2)}) %collective-permute-start.18) | collective-permute-done | bytes 393248 | tf_op jit(solution)/shard_map/down_sum_z_second/ppermute | solution.py:585
  143.8 9.2 %collective-permute-start.20 = (f32[2,96,512]{2,1,0:T(8,128)S(1)}, f32[2,96,512]{2,1,0:T(8,128)S(1)}, u32[]{:S(2)}, u32[]{:S(2)}) collective-permute-start(f32[2,96,512]{2,1,0:T(8,128)S(1)} %reverse_add_fusion.1), channel_id=1, source_target_pairs={{0,8},{1,17},{2,10},{3,19},{4,12},{5,21},{6,14},{7,23},{8,0},{9,25... | collective-permute-start | bytes 1179656 | tf_op jit(solution)/shard_map/down_gather_z_first/ppermute | solution.py:585
  153.2 1.8 collective-permute-start.22
  155.2 0.9 collective-permute-done.23
  157.0 4.0 %collective-permute-done.22 = f32[2,192,256]{2,1,0:T(8,128)S(1)} collective-permute-done((f32[2,192,256]{2,1,0:T(8,128)S(1)}, f32[2,192,256]{2,1,0:T(8,128)S(1)}, u32[]{:S(2)}, u32[]{:S(2)}) %collective-permute-start.22) | collective-permute-done | bytes 393248 | tf_op jit(solution)/shard_map/down_stack_gather_first/ppermute | solution.py:585
  161.1 2.0 collective-permute-done.20
  163.2 6.3 %collective-permute-done.19 = f32[208,384]{1,0:T(8,128)S(1)} collective-permute-done((f32[208,384]{1,0:T(8,128)S(1)}, f32[208,384]{1,0:T(8,128)S(1)}, u32[]{:S(2)}, u32[]{:S(2)}) %collective-permute-start.19) | collective-permute-done | bytes 319520 | tf_op jit(solution)/shard_map/attention_sum_z_first/ppermute | solution.py:585
  169.6 2.9 %collective-permute-done.25 = f32[4,192,256]{2,1,0:T(8,128)S(1)} collective-permute-done((f32[4,192,256]{2,1,0:T(8,128)S(1)}, f32[4,192,256]{2,1,0:T(8,128)S(1)}, u32[]{:S(2)}, u32[]{:S(2)}) %collective-permute-start.25) | collective-permute-done | bytes 786464 | tf_op jit(solution)/shard_map/up_gather_second/ppermute | solution.py:585
  173.6 1.8 collective-permute-start.24
  175.3 1.1 collective-permute-start.31
  176.5 1.8 collective-permute-start.30
  178.3 14.3 %collective-permute-done.27 = f32[4,96,512]{2,1,0:T(8,128)S(1)} collective-permute-done((f32[4,96,512]{2,1,0:T(8,128)S(1)}, f32[4,96,512]{2,1,0:T(8,128)S(1)}, u32[]{:S(2)}, u32[]{:S(2)}) %collective-permute-start.27) | collective-permute-done | bytes 786464 | tf_op jit(solution)/shard_map/down_gather_second/ppermute | solution.py:585
  192.7 2.6 collective-permute-start.35
  195.3 1.4 put_u.2.refs_0_
  196.7 4.8 %collective-permute-done.26.piece_ref = f32[2,4,192,256]{3,2,1,0:T(8,128)S(1)} collective-permute-done((f32[2,4,192,256]{3,2,1,0:T(8,128)S(1)}, f32[2,4,192,256]{3,2,1,0:T(8,128)S(1)}, u32[]{:S(2)}, u32[]{:S(2)}) %collective-permute-start.26) | collective-permute-done | bytes 1572896 | tf_op jit(solution)/shard_map/up_gather_first/ppermute | solution.py:585
  201.6 1.4 put_d.2.refs_0_
  203.0 1.4 put_u.3.refs_1_
  204.6 1.1 collective-permute-start.32
  205.7 1.0 collective-permute-start.29
  206.7 7.8 %collective-permute-done.32 = f32[2,96,384]{2,1,0:T(8,128)S(1)} collective-permute-done((f32[2,96,384]{2,1,0:T(8,128)S(1)}, f32[2,96,384]{2,1,0:T(8,128)S(1)}, u32[]{:S(2)}, u32[]{:S(2)}) %collective-permute-start.32) | collective-permute-done | bytes 294944 | tf_op jit(solution)/shard_map/attention_rest_gather_z_first/ppermute | solution.py:585
  214.5 2.1 collective-permute-start.34
  216.8 4.0 %collective-permute-done.29 = f32[2,96,384]{2,1,0:T(8,128)S(1)} collective-permute-done((f32[2,96,384]{2,1,0:T(8,128)S(1)}, f32[2,96,384]{2,1,0:T(8,128)S(1)}, u32[]{:S(2)}, u32[]{:S(2)}) %collective-permute-start.29) | collective-permute-done | bytes 294944 | tf_op jit(solution)/shard_map/attention_gather_z_first/ppermute | solution.py:585
  220.8 1.6 collective-permute-start.33
  222.3 1.4 put_c.2
  223.8 1.4 put_d.3.refs_0_
  225.3 1.9 collective-permute-start.37
  227.2 6.1 %collective-permute-done.33 = f32[4,96,384]{2,1,0:T(8,128)S(1)} collective-permute-done((f32[4,96,384]{2,1,0:T(8,128)S(1)}, f32[4,96,384]{2,1,0:T(8,128)S(1)}, u32[]{:S(2)}, u32[]{:S(2)}) %collective-permute-start.33) | collective-permute-done | bytes 589856 | tf_op jit(solution)/shard_map/attention_gather_second/ppermute | solution.py:585
  233.3 1.1 pad_maximum_fusion.5.piece_ref
  234.4 3.7 %collective-permute-start.36 = (f32[2,4,96,384]{3,2,1,0:T(8,128)}, f32[2,4,96,384]{3,2,1,0:T(8,128)}, u32[]{:S(2)}, u32[]{:S(2)}) collective-permute-start(f32[2,4,96,384]{3,2,1,0:T(8,128)} %pad_maximum_fusion.5.piece_ref), channel_id=1, source_target_pairs={{0,2},{1,5},{2,0},{3,7},{4,6},{5,1},{6,4},{7,3},{8,10},{9,13},{10,... | collective-permute-start | bytes 3538952 | tf_op jit(solution)/shard_map/attention_gather_first/ppermute | solution.py:585
  241.2 1.3 put_b.2
  242.4 1.3 collective-permute-done.37.piece_ref
  243.8 2.6 put_a.2
  246.4 2.6 put_b.3
  248.9 7.5 %collective-permute-done.36.piece_ref = f32[2,4,96,384]{3,2,1,0:T(8,128)} collective-permute-done((f32[2,4,96,384]{3,2,1,0:T(8,128)}, f32[2,4,96,384]{3,2,1,0:T(8,128)}, u32[]{:S(2)}, u32[]{:S(2)}) %collective-permute-start.36) | collective-permute-done | bytes 1179680 | tf_op jit(solution)/shard_map/attention_gather_first/ppermute | solution.py:585
  256.4 2.6 put_a.3
  259.0 2.8 %put_c.3 = (f32[1536,768]{1,0:T(8,128)}, f32[768,1536]{1,0:T(8,128)}) custom-call(f32[2,4,192,256]{3,2,1,0:T(8,128)} %collective-permute-done.38.piece_ref, f32[1536,768]{1,0:T(8,128)} %put_d.3.refs_0_, f32[768,1536]{1,0:T(8,128)} %get-tuple-element.255.refs_1_), custom_call_target="tpu_custom_call", output_to_operand_aliasing={{0}: (1, {}), {1}: (2, {})} | custom-call | bytes 3145728 | tf_op jit(solution)/shard_map/put_c/pallas_call | solution.py:789
  (110 shorter events, 14.0 us)
Async XLA Ops:
  13.3 3.8 %collective-permute-start = (f32[512,768]{1,0:T(8,128)}, f32[512,768]{1,0:T(8,128)S(1)}, u32[]{:S(2)}, u32[]{:S(2)}) collective-permute-start(f32[512,768]{1,0:T(8,128)} %get-tuple-element.135.mine_in), channel_id=1, source_target_pairs={{0,1},{1,0},{2,3},{3,2},{4,5},{5,4},{6,7},{7,6},{8,9},{9,8},{10,11... | collective-permute-start | bytes 4718600 | tf_op jit(solution)/shard_map/ppermute | solution.py:580
  17.0 1.1 copy-start.10
  36.7 6.1 %collective-permute-start.1 = (f32[2,512,768]{2,1,0:T(8,128)}, f32[2,512,768]{2,1,0:T(8,128)}, u32[]{:S(2)}, u32[]{:S(2)}) collective-permute-start(f32[2,512,768]{2,1,0:T(8,128)} %get-tuple-element.136.refs_0_), channel_id=1, source_target_pairs={{0,1},{1,0},{2,3},{3,2},{4,5},{5,4},{6,7},{7,6},{8,9},{9,8},{10,11... | collective-permute-start | bytes 9437192 | tf_op jit(solution)/shard_map/ppermute | solution.py:580
  37.1 25.7 %collective-permute-start.5 = (f32[2,4,192,256]{3,2,1,0:T(8,128)}, f32[2,4,192,256]{3,2,1,0:T(8,128)}, u32[]{:S(2)}, u32[]{:S(2)}) collective-permute-start(f32[2,4,192,256]{3,2,1,0:T(8,128)} %get-tuple-element.154), channel_id=1, source_target_pairs={{0,2},{1,5},{2,0},{3,7},{4,6},{5,1},{6,4},{7,3},{8,10},{9,13},{10,... | collective-permute-start | bytes 4718600 | tf_op jit(solution)/shard_map/up_sum_first/ppermute | solution.py:585
  39.8 37.5 %collective-permute-start.4 = (f32[2,4,192,256]{3,2,1,0:T(8,128)}, f32[2,4,192,256]{3,2,1,0:T(8,128)}, u32[]{:S(2)}, u32[]{:S(2)}) collective-permute-start(f32[2,4,192,256]{3,2,1,0:T(8,128)} %get-tuple-element.152), channel_id=1, source_target_pairs={{0,8},{1,17},{2,10},{3,19},{4,12},{5,21},{6,14},{7,23},{8,0},{9,25... | collective-permute-start | bytes 4718600 | tf_op jit(solution)/shard_map/down_stack_sum_z_first/ppermute | solution.py:585
  41.3 40.0 %collective-permute-start.3 = (f32[2,4,96,512]{3,2,1,0:T(8,128)}, f32[2,4,96,512]{3,2,1,0:T(8,128)S(1)}, u32[]{:S(2)}, u32[]{:S(2)}) collective-permute-start(f32[2,4,96,512]{3,2,1,0:T(8,128)} %get-tuple-element.150), channel_id=1, source_target_pairs={{0,2},{1,5},{2,0},{3,7},{4,6},{5,1},{6,4},{7,3},{8,10},{9,13},{10,... | collective-permute-start | bytes 4718600 | tf_op jit(solution)/shard_map/down_sum_first/ppermute | solution.py:585
  62.4 25.9 %collective-permute-start.2 = (f32[512,768]{1,0:T(8,128)}, f32[512,768]{1,0:T(8,128)S(1)}, u32[]{:S(2)}, u32[]{:S(2)}) collective-permute-start(f32[512,768]{1,0:T(8,128)} %get-tuple-element.148.mine_ref), channel_id=1, source_target_pairs={{0,1},{1,0},{2,3},{3,2},{4,5},{5,4},{6,7},{7,6},{8,9},{9,8},{10,11... | collective-permute-start | bytes 4718600 | tf_op jit(solution)/shard_map/ppermute | solution.py:580
  62.9 14.5 %copy-start.4 = (f32[2,4,192,256]{3,2,1,0:T(8,128)S(1)}, f32[2,4,192,256]{3,2,1,0:T(8,128)}, u32[]{:S(2)}) copy-start(f32[2,4,192,256]{3,2,1,0:T(8,128)} %get-tuple-element.158) | copy-start | bytes 4718596
  65.1 27.3 %collective-permute-start.7 = (f32[4,192,256]{2,1,0:T(8,128)S(1)}, f32[4,192,256]{2,1,0:T(8,128)S(1)}, u32[]{:S(2)}, u32[]{:S(2)}) collective-permute-start(f32[4,192,256]{2,1,0:T(8,128)S(1)} %get-tuple-element.263), channel_id=1, source_target_pairs={{0,4},{1,3},{2,6},{3,1},{4,0},{5,7},{6,2},{7,5},{8,12},{9,11},{10,... | collective-permute-start | bytes 2359304 | tf_op jit(solution)/shard_map/up_sum_second/ppermute | solution.py:585
  77.3 4.1 %copy-start.11 = (f32[2,4,96,384]{3,2,1,0:T(8,128)S(1)}, f32[2,4,96,384]{3,2,1,0:T(8,128)}, u32[]{:S(2)}) copy-start(f32[2,4,96,384]{3,2,1,0:T(8,128)} %get-tuple-element.169) | copy-start | bytes 3538948
  77.3 6.4 %copy-start.3 = (f32[2,4,96,512]{3,2,1,0:T(8,128)S(1)}, f32[2,4,96,512]{3,2,1,0:T(8,128)}, u32[]{:S(2)}) copy-start(f32[2,4,96,512]{3,2,1,0:T(8,128)} %get-tuple-element.160) | copy-start | bytes 4718596
  81.4 4.3 %copy-start.9 = (f32[768]{0:T(1024)S(1)}, f32[768]{0:T(1024)}, u32[]{:S(2)}) copy-start(f32[768]{0:T(1024)} %gain_in.2) | copy-start | bytes 9220
  81.4 6.9 %copy-start.7 = (f32[2,4,96,384]{3,2,1,0:T(8,128)S(1)}, f32[2,4,96,384]{3,2,1,0:T(8,128)}, u32[]{:S(2)}) copy-start(f32[2,4,96,384]{3,2,1,0:T(8,128)} %get-tuple-element.165) | copy-start | bytes 3538948
  81.4 6.9 %copy-start.8 = (f32[16,384]{1,0:T(8,128)S(1)}, f32[16,384]{1,0:T(8,128)}, u32[]{:S(2)}) copy-start(f32[16,384]{1,0:T(8,128)} %get-tuple-element.186) | copy-start | bytes 73732
  81.4 24.5 %collective-permute-start.9 = (f32[2,4,96,384]{3,2,1,0:T(8,128)S(1)}, f32[2,4,96,384]{3,2,1,0:T(8,128)S(1)}, u32[]{:S(2)}, u32[]{:S(2)}) collective-permute-start(f32[2,4,96,384]{3,2,1,0:T(8,128)S(1)} %copy-done.11), channel_id=1, source_target_pairs={{0,2},{1,5},{2,0},{3,7},{4,6},{5,1},{6,4},{7,3},{8,10},{9,13},{10,... | collective-permute-start | bytes 3538952 | tf_op jit(solution)/shard_map/attention_rest_sum_first/ppermute | solution.py:585
  83.8 5.2 %copy-start.2 = (f32[512,768]{1,0:T(8,128)S(1)}, f32[512,768]{1,0:T(8,128)}, u32[]{:S(2)}) copy-start(f32[512,768]{1,0:T(8,128)} %get-tuple-element.148.mine_ref) | copy-start | bytes 4718596
  84.1 4.8 %copy-start = (bf16[512,768]{1,0:T(8,128)(2,1)S(1)}, bf16[512,768]{1,0:T(8,128)(2,1)}, u32[]{:S(2)}) copy-start(bf16[512,768]{1,0:T(8,128)(2,1)} %x_ref.1) | copy-start | bytes 2359300
  84.1 4.8 %copy-start.1 = (f32[512,768]{1,0:T(8,128)S(1)}, f32[512,768]{1,0:T(8,128)}, u32[]{:S(2)}) copy-start(f32[512,768]{1,0:T(8,128)} %get-tuple-element.163.delta_ref) | copy-start | bytes 4718596
  84.1 20.5 %collective-permute-start.10 = (f32[4,96,512]{2,1,0:T(8,128)S(1)}, f32[4,96,512]{2,1,0:T(8,128)S(1)}, u32[]{:S(2)}, u32[]{:S(2)}) collective-permute-start(f32[4,96,512]{2,1,0:T(8,128)S(1)} %get-tuple-element.261), channel_id=1, source_target_pairs={{0,4},{1,3},{2,6},{3,1},{4,0},{5,7},{6,2},{7,5},{8,12},{9,11},{10,... | collective-permute-start | bytes 2359304 | tf_op jit(solution)/shard_map/down_sum_second/ppermute | solution.py:585
  85.7 36.7 %collective-permute-start.14 = (f32[4,192,256]{2,1,0:T(8,128)S(1)}, f32[4,192,256]{2,1,0:T(8,128)S(1)}, u32[]{:S(2)}, u32[]{:S(2)}) collective-permute-start(f32[4,192,256]{2,1,0:T(8,128)S(1)} %get-tuple-element.259), channel_id=1, source_target_pairs={{0,16},{1,9},{2,18},{3,11},{4,20},{5,13},{6,22},{7,15},{8,24},{9,1... | collective-permute-start | bytes 2359304 | tf_op jit(solution)/shard_map/down_stack_sum_z_second/ppermute | solution.py:585
  88.3 49.1 %collective-permute-start.6 = (f32[784,384]{1,0:T(8,128)S(1)}, f32[784,384]{1,0:T(8,128)S(1)}, u32[]{:S(2)}, u32[]{:S(2)}) collective-permute-start(f32[784,384]{1,0:T(8,128)S(1)} %pad_maximum_fusion.3), channel_id=1, source_target_pairs={{0,2},{1,5},{2,0},{3,7},{4,6},{5,1},{6,4},{7,3},{8,10},{9,13},{10,... | collective-permute-start | bytes 3612680 | tf_op jit(solution)/shard_map/attention_sum_first/ppermute | solution.py:585
  92.5 13.4 %copy-start.5 = (f32[2,4,96,384]{3,2,1,0:T(8,128)S(1)}, f32[2,4,96,384]{3,2,1,0:T(8,128)}, u32[]{:S(2)}) copy-start(f32[2,4,96,384]{3,2,1,0:T(8,128)} %get-tuple-element.172) | copy-start | bytes 3538948
  92.5 19.3 %collective-permute-start.8 = (f32[2,192,256]{2,1,0:T(8,128)S(1)}, f32[2,192,256]{2,1,0:T(8,128)S(1)}, u32[]{:S(2)}, u32[]{:S(2)}) collective-permute-start(f32[2,192,256]{2,1,0:T(8,128)S(1)} %get-tuple-element.270), channel_id=1, source_target_pairs={{0,8},{1,17},{2,10},{3,19},{4,12},{5,21},{6,14},{7,23},{8,0},{9,25... | collective-permute-start | bytes 1179656 | tf_op jit(solution)/shard_map/up_sum_z_first/ppermute | solution.py:585
  106.1 19.7 %collective-permute-start.12 = (f32[4,96,384]{2,1,0:T(8,128)S(1)}, f32[4,96,384]{2,1,0:T(8,128)S(1)}, u32[]{:S(2)}, u32[]{:S(2)}) collective-permute-start(f32[4,96,384]{2,1,0:T(8,128)S(1)} %get-tuple-element.265), channel_id=1, source_target_pairs={{0,4},{1,3},{2,6},{3,1},{4,0},{5,7},{6,2},{7,5},{8,12},{9,11},{10,... | collective-permute-start | bytes 1769480 | tf_op jit(solution)/shard_map/attention_rest_sum_second/ppermute | solution.py:585
  107.0 18.7 %collective-permute-start.13 = (f32[2,96,512]{2,1,0:T(8,128)S(1)}, f32[2,96,512]{2,1,0:T(8,128)S(1)}, u32[]{:S(2)}, u32[]{:S(2)}) collective-permute-start(f32[2,96,512]{2,1,0:T(8,128)S(1)} %get-tuple-element.269), channel_id=1, source_target_pairs={{0,8},{1,17},{2,10},{3,19},{4,12},{5,21},{6,14},{7,23},{8,0},{9,25... | collective-permute-start | bytes 1179656 | tf_op jit(solution)/shard_map/down_sum_z_first/ppermute | solution.py:585
  111.9 24.7 %collective-permute-start.11 = (f32[2,192,256]{2,1,0:T(8,128)S(1)}, f32[2,192,256]{2,1,0:T(8,128)S(1)}, u32[]{:S(2)}, u32[]{:S(2)}) collective-permute-start(f32[2,192,256]{2,1,0:T(8,128)S(1)} %add.145), channel_id=1, source_target_pairs={{0,16},{1,9},{2,18},{3,11},{4,20},{5,13},{6,22},{7,15},{8,24},{9,1... | collective-permute-start | bytes 1179656 | tf_op jit(solution)/shard_map/up_sum_z_second/ppermute | solution.py:585
  122.5 15.7 %collective-permute-start.16 = (f32[2,192,256]{2,1,0:T(8,128)S(1)}, f32[2,192,256]{2,1,0:T(8,128)S(1)}, u32[]{:S(2)}, u32[]{:S(2)}) collective-permute-start(f32[2,192,256]{2,1,0:T(8,128)S(1)} %get-tuple-element.267), channel_id=1, source_target_pairs={{0,2},{1,5},{2,0},{3,7},{4,6},{5,1},{6,4},{7,3},{8,10},{9,13},{10,... | collective-permute-start | bytes 1179656 | tf_op jit(solution)/shard_map/down_stack_sum_first/ppermute | solution.py:585
  125.7 11.7 %copy-start.6 = (f32[2,4,96,384]{3,2,1,0:T(8,128)S(1)}, f32[2,4,96,384]{3,2,1,0:T(8,128)}, u32[]{:S(2)}) copy-start(f32[2,4,96,384]{3,2,1,0:T(8,128)} %get-tuple-element.184) | copy-start | bytes 3538948
  125.7 18.0 %collective-permute-start.18 = (f32[2,96,512]{2,1,0:T(8,128)S(1)}, f32[2,96,512]{2,1,0:T(8,128)S(1)}, u32[]{:S(2)}, u32[]{:S(2)}) collective-permute-start(f32[2,96,512]{2,1,0:T(8,128)S(1)} %add.152), channel_id=1, source_target_pairs={{0,16},{1,9},{2,18},{3,11},{4,20},{5,13},{6,22},{7,15},{8,24},{9,1... | collective-permute-start | bytes 1179656 | tf_op jit(solution)/shard_map/down_sum_z_second/ppermute | solution.py:585
  125.9 35.2 %collective-permute-start.21 = (f32[2,96,384]{2,1,0:T(8,128)S(1)}, f32[2,96,384]{2,1,0:T(8,128)S(1)}, u32[]{:S(2)}, u32[]{:S(2)}) collective-permute-start(f32[2,96,384]{2,1,0:T(8,128)S(1)} %get-tuple-element.275), channel_id=1, source_target_pairs={{0,8},{1,17},{2,10},{3,19},{4,12},{5,21},{6,14},{7,23},{8,0},{9,25... | collective-permute-start | bytes 884744 | tf_op jit(solution)/shard_map/attention_rest_sum_z_first/ppermute | solution.py:585
  136.7 19.4 %collective-permute-start.23 = (f32[2,192,256]{2,1,0:T(8,128)S(1)}, f32[2,192,256]{2,1,0:T(8,128)S(1)}, u32[]{:S(2)}, u32[]{:S(2)}) collective-permute-start(f32[2,192,256]{2,1,0:T(8,128)S(1)} %reverse_add_fusion.2), channel_id=1, source_target_pairs={{0,8},{1,17},{2,10},{3,19},{4,12},{5,21},{6,14},{7,23},{8,0},{9,25... | collective-permute-start | bytes 1179656 | tf_op jit(solution)/shard_map/up_gather_z_first/ppermute | solution.py:585
  137.7 17.3 %collective-permute-start.15 = (f32[400,384]{1,0:T(8,128)S(1)}, f32[400,384]{1,0:T(8,128)S(1)}, u32[]{:S(2)}, u32[]{:S(2)}) collective-permute-start(f32[400,384]{1,0:T(8,128)S(1)} %pad_maximum_fusion.6), channel_id=1, source_target_pairs={{0,4},{1,3},{2,6},{3,1},{4,0},{5,7},{6,2},{7,5},{8,12},{9,11},{10,... | collective-permute-start | bytes 1843208 | tf_op jit(solution)/shard_map/attention_sum_second/ppermute | solution.py:585
  138.3 14.8 %collective-permute-start.17 = (f32[2,192,256]{2,1,0:T(8,128)S(1)}, f32[2,192,256]{2,1,0:T(8,128)S(1)}, u32[]{:S(2)}, u32[]{:S(2)}) collective-permute-start(f32[2,192,256]{2,1,0:T(8,128)S(1)} %add.159), channel_id=1, source_target_pairs={{0,4},{1,3},{2,6},{3,1},{4,0},{5,7},{6,2},{7,5},{8,12},{9,11},{10,... | collective-permute-start | bytes 1179656 | tf_op jit(solution)/shard_map/down_stack_sum_second/ppermute | solution.py:585
  143.8 19.4 %collective-permute-start.20 = (f32[2,96,512]{2,1,0:T(8,128)S(1)}, f32[2,96,512]{2,1,0:T(8,128)S(1)}, u32[]{:S(2)}, u32[]{:S(2)}) collective-permute-start(f32[2,96,512]{2,1,0:T(8,128)S(1)} %reverse_add_fusion.1), channel_id=1, source_target_pairs={{0,8},{1,17},{2,10},{3,19},{4,12},{5,21},{6,14},{7,23},{8,0},{9,25... | collective-permute-start | bytes 1179656 | tf_op jit(solution)/shard_map/down_gather_z_first/ppermute | solution.py:585
  153.2 7.8 %collective-permute-start.22 = (f32[2,192,256]{2,1,0:T(8,128)S(1)}, f32[2,192,256]{2,1,0:T(8,128)S(1)}, u32[]{:S(2)}, u32[]{:S(2)}) collective-permute-start(f32[2,192,256]{2,1,0:T(8,128)S(1)} %reverse_add_fusion), channel_id=1, source_target_pairs={{0,2},{1,5},{2,0},{3,7},{4,6},{5,1},{6,4},{7,3},{8,10},{9,13},{10,... | collective-permute-start | bytes 1179656 | tf_op jit(solution)/shard_map/down_stack_gather_first/ppermute | solution.py:585
  155.1 14.4 %collective-permute-start.19 = (f32[208,384]{1,0:T(8,128)S(1)}, f32[208,384]{1,0:T(8,128)S(1)}, u32[]{:S(2)}, u32[]{:S(2)}) collective-permute-start(f32[208,384]{1,0:T(8,128)S(1)} %pad_maximum_fusion.7), channel_id=1, source_target_pairs={{0,8},{1,17},{2,10},{3,19},{4,12},{5,21},{6,14},{7,23},{8,0},{9,25... | collective-permute-start | bytes 958472 | tf_op jit(solution)/shard_map/attention_sum_z_first/ppermute | solution.py:585
  156.2 16.3 %collective-permute-start.25 = (f32[4,192,256]{2,1,0:T(8,128)S(1)}, f32[4,192,256]{2,1,0:T(8,128)S(1)}, u32[]{:S(2)}, u32[]{:S(2)}) collective-permute-start(f32[4,192,256]{2,1,0:T(8,128)S(1)} %constant_dynamic-update-slice_fusion), channel_id=1, source_target_pairs={{0,4},{1,3},{2,6},{3,1},{4,0},{5,7},{6,2},{7,5},{8,12},{9,11},{10,... | collective-permute-start | bytes 2359304 | tf_op jit(solution)/shard_map/up_gather_second/ppermute | solution.py:585
  172.6 28.9 %collective-permute-start.26 = (f32[2,4,192,256]{3,2,1,0:T(8,128)S(1)}, f32[2,4,192,256]{3,2,1,0:T(8,128)S(1)}, u32[]{:S(2)}, u32[]{:S(2)}) collective-permute-start(f32[2,4,192,256]{3,2,1,0:T(8,128)S(1)} %pad_maximum_fusion.piece_ref), channel_id=1, source_target_pairs={{0,2},{1,5},{2,0},{3,7},{4,6},{5,1},{6,4},{7,3},{8,10},{9,13},{10,... | collective-permute-start | bytes 4718600 | tf_op jit(solution)/shard_map/up_gather_first/ppermute | solution.py:585
  173.1 19.5 %collective-permute-start.27 = (f32[4,96,512]{2,1,0:T(8,128)S(1)}, f32[4,96,512]{2,1,0:T(8,128)S(1)}, u32[]{:S(2)}, u32[]{:S(2)}) collective-permute-start(f32[4,96,512]{2,1,0:T(8,128)S(1)} %constant_dynamic-update-slice_fusion.4), channel_id=1, source_target_pairs={{0,4},{1,3},{2,6},{3,1},{4,0},{5,7},{6,2},{7,5},{8,12},{9,11},{10,... | collective-permute-start | bytes 2359304 | tf_op jit(solution)/shard_map/down_gather_second/ppermute | solution.py:585
  173.6 30.9 %collective-permute-start.24 = (f32[208,384]{1,0:T(8,128)S(1)}, f32[208,384]{1,0:T(8,128)S(1)}, u32[]{:S(2)}, u32[]{:S(2)}) collective-permute-start(f32[208,384]{1,0:T(8,128)S(1)} %pad_maximum_fusion.8), channel_id=1, source_target_pairs={{0,16},{1,9},{2,18},{3,11},{4,20},{5,13},{6,22},{7,15},{8,24},{9,1... | collective-permute-start | bytes 958472 | tf_op jit(solution)/shard_map/attention_sum_z_second/ppermute | solution.py:585
  175.3 29.2 %collective-permute-start.31 = (f32[2,96,384]{2,1,0:T(8,128)S(1)}, f32[2,96,384]{2,1,0:T(8,128)S(1)}, u32[]{:S(2)}, u32[]{:S(2)}) collective-permute-start(f32[2,96,384]{2,1,0:T(8,128)S(1)} %add.166), channel_id=1, source_target_pairs={{0,16},{1,9},{2,18},{3,11},{4,20},{5,13},{6,22},{7,15},{8,24},{9,1... | collective-permute-start | bytes 884744 | tf_op jit(solution)/shard_map/attention_rest_sum_z_second/ppermute | solution.py:585
  176.5 40.1 %collective-permute-start.30 = (f32[4,192,256]{2,1,0:T(8,128)S(1)}, f32[4,192,256]{2,1,0:T(8,128)S(1)}, u32[]{:S(2)}, u32[]{:S(2)}) collective-permute-start(f32[4,192,256]{2,1,0:T(8,128)S(1)} %constant_dynamic-update-slice_fusion.2), channel_id=1, source_target_pairs={{0,16},{1,9},{2,18},{3,11},{4,20},{5,13},{6,22},{7,15},{8,24},{9,1... | collective-permute-start | bytes 2359304 | tf_op jit(solution)/shard_map/down_stack_gather_z_second/ppermute | solution.py:585
  192.7 31.0 %collective-permute-start.35 = (f32[2,4,96,512]{3,2,1,0:T(8,128)S(1)}, f32[2,4,96,512]{3,2,1,0:T(8,128)S(1)}, u32[]{:S(2)}, u32[]{:S(2)}) collective-permute-start(f32[2,4,96,512]{3,2,1,0:T(8,128)S(1)} %pad_maximum_fusion.1.piece_ref), channel_id=1, source_target_pairs={{0,2},{1,5},{2,0},{3,7},{4,6},{5,1},{6,4},{7,3},{8,10},{9,13},{10,... | collective-permute-start | bytes 4718600 | tf_op jit(solution)/shard_map/down_gather_first/ppermute | solution.py:585
  204.6 9.8 %collective-permute-start.32 = (f32[2,96,384]{2,1,0:T(8,128)S(1)}, f32[2,96,384]{2,1,0:T(8,128)S(1)}, u32[]{:S(2)}, u32[]{:S(2)}) collective-permute-start(f32[2,96,384]{2,1,0:T(8,128)S(1)} %reverse_add_fusion.3), channel_id=1, source_target_pairs={{0,8},{1,17},{2,10},{3,19},{4,12},{5,21},{6,14},{7,23},{8,0},{9,25... | collective-permute-start | bytes 884744 | tf_op jit(solution)/shard_map/attention_rest_gather_z_first/ppermute | solution.py:585
  205.7 15.0 %collective-permute-start.29 = (f32[2,96,384]{2,1,0:T(8,128)S(1)}, f32[2,96,384]{2,1,0:T(8,128)S(1)}, u32[]{:S(2)}, u32[]{:S(2)}) collective-permute-start(f32[2,96,384]{2,1,0:T(8,128)S(1)} %reverse_add_fusion.4), channel_id=1, source_target_pairs={{0,8},{1,17},{2,10},{3,19},{4,12},{5,21},{6,14},{7,23},{8,0},{9,25... | collective-permute-start | bytes 884744 | tf_op jit(solution)/shard_map/attention_gather_z_first/ppermute | solution.py:585
  214.5 10.7 %collective-permute-start.34 = (f32[4,96,384]{2,1,0:T(8,128)S(1)}, f32[4,96,384]{2,1,0:T(8,128)S(1)}, u32[]{:S(2)}, u32[]{:S(2)}) collective-permute-start(f32[4,96,384]{2,1,0:T(8,128)S(1)} %constant_dynamic-update-slice_fusion.6), channel_id=1, source_target_pairs={{0,4},{1,3},{2,6},{3,1},{4,0},{5,7},{6,2},{7,5},{8,12},{9,11},{10,... | collective-permute-start | bytes 1769480 | tf_op jit(solution)/shard_map/attention_rest_gather_second/ppermute | solution.py:585
  220.8 12.5 %collective-permute-start.33 = (f32[4,96,384]{2,1,0:T(8,128)S(1)}, f32[4,96,384]{2,1,0:T(8,128)S(1)}, u32[]{:S(2)}, u32[]{:S(2)}) collective-permute-start(f32[4,96,384]{2,1,0:T(8,128)S(1)} %constant_dynamic-update-slice_fusion.8), channel_id=1, source_target_pairs={{0,4},{1,3},{2,6},{3,1},{4,0},{5,7},{6,2},{7,5},{8,12},{9,11},{10,... | collective-permute-start | bytes 1769480 | tf_op jit(solution)/shard_map/attention_gather_second/ppermute | solution.py:585
  222.3 36.7 %collective-permute-start.38 = (f32[2,4,192,256]{3,2,1,0:T(8,128)S(1)}, f32[2,4,192,256]{3,2,1,0:T(8,128)}, u32[]{:S(2)}, u32[]{:S(2)}) collective-permute-start(f32[2,4,192,256]{3,2,1,0:T(8,128)S(1)} %pad_maximum_fusion.2.piece_ref), channel_id=1, source_target_pairs={{0,8},{1,17},{2,10},{3,19},{4,12},{5,21},{6,14},{7,23},{8,0},{9,25... | collective-permute-start | bytes 4718600 | tf_op jit(solution)/shard_map/down_stack_gather_z_first/ppermute | solution.py:585
  225.3 18.5 %collective-permute-start.37 = (f32[2,4,96,384]{3,2,1,0:T(8,128)S(1)}, f32[2,4,96,384]{3,2,1,0:T(8,128)}, u32[]{:S(2)}, u32[]{:S(2)}) collective-permute-start(f32[2,4,96,384]{3,2,1,0:T(8,128)S(1)} %pad_maximum_fusion.4.piece_ref), channel_id=1, source_target_pairs={{0,2},{1,5},{2,0},{3,7},{4,6},{5,1},{6,4},{7,3},{8,10},{9,13},{10,... | collective-permute-start | bytes 3538952 | tf_op jit(solution)/shard_map/attention_rest_gather_first/ppermute | solution.py:585
  234.4 22.0 %collective-permute-start.36 = (f32[2,4,96,384]{3,2,1,0:T(8,128)}, f32[2,4,96,384]{3,2,1,0:T(8,128)}, u32[]{:S(2)}, u32[]{:S(2)}) collective-permute-start(f32[2,4,96,384]{3,2,1,0:T(8,128)} %pad_maximum_fusion.5.piece_ref), channel_id=1, source_target_pairs={{0,2},{1,5},{2,0},{3,7},{4,6},{5,1},{6,4},{7,3},{8,10},{9,13},{10,... | collective-permute-start | bytes 3538952 | tf_op jit(solution)/shard_map/attention_gather_first/ppermute | solution.py:585
  238.1 1.2 collective-permute-start.28

commit v7 on v6

--- a/solution.py
+++ b/solution.py
@@ -30,7 +30,7 @@
 FIRST, SECOND = (X, Y), (Y, X)
 Z_FIRST, Z_SECOND = (Z1, Z2), (Z2, Z1)
 
-ORDER = "cudKubcdIudabucdbuacdcaucbdauduabbcadbabac"
+ORDER = "cudKucbdIudabucdbuacdcaucbdaudabubcadbabac"
 
 CASES = ((0, 0, 256, 0), (128, 256, 384, 128), (256, 640, 128, 128), (384, 768, 256, 128))
 TILES = (
@@ -103,10 +103,10 @@
 
 def fill_bias(lengths_ref, pads_ref, bias_ref):
     sequence = lax.axis_index("dp")
-    docs = lengths_ref.shape[1]
+    docs = lengths_ref.shape[0]
     ends, total = [], jnp.int32(0)
     for j in range(docs):
-        total = total + lengths_ref[sequence, j]
+        total = total + lengths_ref[j, sequence]
         ends.append(total)
     first_pad = LEN - pads_ref[sequence]
 
@@ -207,18 +207,23 @@
         cols = slice(t * LANES, (t + 1) * LANES)
         key_pair, value_pair = k_ref[:, cols], v_ref[:, cols]
         mixed = [None] * 4
+        jobs, scores, values = [(which, case) for which in range(2) for case in range(4)], [], []
         for which in range(2):
             mask = head_mask(key_pair.shape[0], which)
             key_head = jnp.where(mask, key_pair, jnp.zeros_like(key_pair))
-            value_head = jnp.where(mask, value_pair, jnp.zeros_like(value_pair))
-            for case, (query_row, first, width, key_row) in enumerate(CASES):
-                scores = nt(q_ref[query_row : query_row + HALF, cols], key_head[key_row : key_row + width])
-                scores = scores + bias_ref[:, first : first + width]
-                weights = jnp.exp(scores - jnp.max(scores, axis=1, keepdims=True))
-                low = (weights * (1.0 / jnp.sum(weights, axis=1, keepdims=True))).astype(bf16)
-                prob_ref[2 * t + which, :, first : first + width] = low
-                part = mm(low, value_head[key_row : key_row + width])
-                mixed[case] = part if mixed[case] is None else mixed[case] + part
+            values.append(jnp.where(mask, value_pair, jnp.zeros_like(value_pair)))
+            for query_row, first, width, key_row in CASES:
+                found = nt(q_ref[query_row : query_row + HALF, cols], key_head[key_row : key_row + width])
+                scores.append(found + bias_ref[:, first : first + width])
+        tops = [jnp.max(a, axis=1, keepdims=True) for a in scores]
+        weights = [jnp.exp(a - top) for a, top in zip(scores, tops)]
+        shares = [1.0 / jnp.sum(a, axis=1, keepdims=True) for a in weights]
+        lows = [(a * share).astype(bf16) for a, share in zip(weights, shares)]
+        for (which, case), low in zip(jobs, lows):
+            _, first, width, key_row = CASES[case]
+            prob_ref[2 * t + which, :, first : first + width] = low
+            part = mm(low, values[which][key_row : key_row + width])
+            mixed[case] = part if mixed[case] is None else mixed[case] + part
         for case, (query_row, _, _, _) in enumerate(CASES):
             att_ref[query_row : query_row + HALF, cols] = mixed[case].astype(bf16)
         sender.send(prob_ref.at[2 * t : 2 * t + 2], prob_out.at[2 * t : 2 * t + 2])
@@ -273,7 +278,7 @@
 
 def mlp_kernel(
     gain_in, bu_in, x_in, mine_in, theirs_in, cot_in, wu_in, wd_in,
-    residual_out, gbu_ref, gbd_ref, d_kept, d_sent, c_kept, c_sent, u_kept, u_sent, shares_out,
+    residual_out, gbu_ref, d_kept, d_sent, c_kept, c_sent, u_kept, u_sent, shares_out,
     gain_ref, bu_ref, x_ref, mine_ref, theirs_ref, cot_ref, wu_ref, wd_ref,
     residual_ref, normed_ref, act_ref, du_ref, d_kept_ref, d_sent_ref, c_kept_ref, c_sent_ref, u_kept_ref, u_sent_ref, shares_ref,
     sems, out_sems,
@@ -287,7 +292,6 @@
     copies = fetch(pairs + [(cot_in, cot_ref), (wu_in, wu_ref), (wd_in, wd_ref)], sems)
     sender = Sender(out_sems)
     gbu_ref[...] = jnp.zeros_like(gbu_ref)
-    gbd_ref[...] = jnp.zeros_like(gbd_ref)
     copies[0].wait()
     gain = gain_ref[...].reshape(1, -1)
     for half in range(2):
@@ -307,18 +311,19 @@
     c0 = math.sqrt(2.0 / math.pi)
     c1 = c0 * 0.044715
 
-    @pl.loop(0, units // 256)
+    @pl.loop(0, units // 512)
     def _(j):
-        cols = pl.ds(pl.multiple_of(j * 256, 256), 256)
-        for block in range(row_count // 256):
-            rows = slice(block * 256, block * 256 + 256)
-            u = mm(normed_ref[rows, :], wu_ref[:, cols]) + bu_ref[cols].reshape(1, -1)
-            delta = nt(cot_ref[rows, :], wd_ref[cols, :])
+        cols = pl.ds(pl.multiple_of(j * 512, 512), 512)
+        blocks = [slice(block * 256, block * 256 + 256) for block in range(row_count // 256)]
+        ups = [mm(normed_ref[rows, :], wu_ref[:, cols]) + bu_ref[cols].reshape(1, -1) for rows in blocks]
+        deltas = [nt(cot_ref[rows, :], wd_ref[cols, :]) for rows in blocks]
+        for rows, u, delta in zip(blocks, ups, deltas):
             square = u * u
             t = jnp.tanh(u * (c0 + c1 * square))
-            half_up = 0.5 * (1.0 + t)
-            act_ref[rows, cols] = (u * half_up).astype(bf16)
-            slope = half_up + (0.5 * u) * (1.0 - t * t) * (c0 + (3.0 * c1) * square)
+            half_up = 0.5 + 0.5 * t
+            act = u * half_up
+            act_ref[rows, cols] = act.astype(bf16)
+            slope = half_up + act * ((1.0 - t) * (c0 + (3.0 * c1) * square))
             low = (delta * slope).astype(bf16)
             du_ref[rows, cols] = low
             gbu_ref[:, cols] += jnp.sum(low.astype(f32), axis=0, keepdims=True)
@@ -330,23 +335,6 @@
     quarters = {}
     for place in range(PLANE):
         quarters[place] = pl.ds(pl.multiple_of(quarter_at(place) * quarter, LANES), quarter)
-    for place in (2, 3, 0, 1):
-        grad = tn(act_ref[:, quarters[place]], cot_ref[...])
-        place_quarter((d_kept_ref, d_sent_ref), place, grad[:, :cut])
-        place_quarter_z_first((c_kept_ref, c_sent_ref), place, 0, grad[:, cut:])
-        if place == 3:
-            sender.send(d_sent_ref, d_sent)
-    sender.send(d_kept_ref, d_kept)
-    for place in (2, 3, 0, 1):
-        grad = tn(normed_ref[...], du_ref[:, quarters[place]])
-        place_quarter((u_kept_ref, u_sent_ref), place, grad[:, :up_cut])
-        rest = grad[:, up_cut:].reshape(STACK, 2, fourth, -1)
-        rest = jnp.concatenate([rest[:, 0], rest[:, 1]], 2).reshape(STACK * fourth, -1)
-        place_quarter_z_first((c_kept_ref, c_sent_ref), place, fourth, rest)
-        if place == 3:
-            sender.send(u_sent_ref, u_sent)
-    for source, target in ((c_sent_ref, c_sent), (u_kept_ref, u_kept), (c_kept_ref, c_kept)):
-        sender.send(source, target)
     for share in range(2):
         for rows in halves:
             if share == 0:
@@ -354,23 +342,38 @@
             else:
                 shares_ref[share, rows, :] = mm(act_ref[rows, :], wd_ref[...])
         sender.send(shares_ref.at[share], shares_out.at[share])
-
-    @pl.loop(0, row_count // 64)
-    def _(i):
-        rows = pl.ds(pl.multiple_of(i * 64, 64), 64)
-        gbd_ref[...] += jnp.sum(cot_ref[rows, :].astype(f32), axis=0, keepdims=True)
-
+    c_pairs = ((c_kept_ref, c_kept), (c_sent_ref, c_sent))
+    for place in (2, 3, 0, 1):
+        grad = tn(act_ref[:, quarters[place]], cot_ref[...])
+        place_quarter((d_kept_ref, d_sent_ref), place, grad[:, :cut])
+        place_quarter_z_first((c_kept_ref, c_sent_ref), place, 0, grad[:, cut:])
+        source, target = ((d_kept_ref, d_kept), (d_sent_ref, d_sent))[place // 2]
+        sender.send(source.at[place % 2], target.at[place % 2])
+        for source, target in c_pairs:
+            rows = pl.ds(0, fourth)
+            sender.send(source.at[:, place, rows, :], target.at[:, place, rows, :])
+    for place in (2, 3, 0, 1):
+        grad = tn(normed_ref[...], du_ref[:, quarters[place]])
+        place_quarter((u_kept_ref, u_sent_ref), place, grad[:, :up_cut])
+        rest = grad[:, up_cut:].reshape(STACK, 2, fourth, -1)
+        rest = jnp.concatenate([rest[:, 0], rest[:, 1]], 2).reshape(STACK * fourth, -1)
+        place_quarter_z_first((c_kept_ref, c_sent_ref), place, fourth, rest)
+        source, target = ((u_kept_ref, u_kept), (u_sent_ref, u_sent))[place // 2]
+        sender.send(source.at[place % 2], target.at[place % 2])
+        for source, target in c_pairs:
+            rows = pl.ds(fourth, fourth)
+            sender.send(source.at[:, place, rows, :], target.at[:, place, rows, :])
     sender.finish()
 
 
 def attention_backward(*refs):
-    ins, refs = refs[:21], refs[21:]
+    ins, refs = refs[:20], refs[20:]
     (output_out, delta_out, part_out, vec_ref), outs_at, refs = refs[:4], refs[4:8], refs[8:]
-    held, refs = refs[:21], refs[21:]
+    held, refs = refs[:20], refs[20:]
     (output_ref, delta_ref, part_ref), outs, refs = refs[:3], refs[3:7], refs[7:]
     branch_ref, datt_ref, dq_ref, dk_ref, dv_ref, dk_acc, dv_acc, grads_ref, gnorm_ref, sems, out_sems = refs
     mine_ref, theirs_ref, residual_ref, cot_ref, gain_ref, bd_ref, att_ref, wo_ref, q_ref, k_ref, v_ref = held[:11]
-    prob_ref, cos_ref, sin_ref, wq_ref, wk_ref, wv_ref, x_ref, normed_ref, gbd_ref, gbu_ref = held[11:]
+    prob_ref, cos_ref, sin_ref, wq_ref, wk_ref, wv_ref, x_ref, normed_ref, gbu_ref = held[11:]
     row_count = residual_ref.shape[0]
     heads_cols = wq_ref.shape[1]
     pairs = heads_cols // LANES
@@ -396,10 +399,12 @@
             residual = residual_ref[rows, :]
             output_ref[rows, :] = (residual + (mine_ref[1, rows, :] + theirs_ref[1, rows, :]) + bias_down).astype(bf16)
             back, gain_part = norm_back_rows(residual, gain, delta)
-            back = back + cot_ref[rows, :].astype(f32)
+            cotangent = cot_ref[rows, :].astype(f32)
+            back = back + cotangent
             delta_ref[rows, :] = back
             branch_ref[rows, :] = back.astype(bf16)
             gnorm_ref[0:1, :] += gain_part
+            gnorm_ref[2:3, :] += jnp.sum(cotangent, axis=0, keepdims=True)
 
     sender.send(output_ref, output_out)
     sender.send(delta_ref, delta_out)
@@ -418,27 +423,29 @@
         dk_acc[...] = jnp.zeros_like(dk_acc)
         dv_acc[...] = jnp.zeros_like(dv_acc)
         query_grads = [None] * 4
+        jobs, deltas, lows, keys_of = [], [], [], []
         for which in range(2):
             mask = head_mask(key_pair.shape[0], which)
-            key_head = jnp.where(mask, key_pair, jnp.zeros_like(key_pair))
+            keys_of.append(jnp.where(mask, key_pair, jnp.zeros_like(key_pair)))
             value_head = jnp.where(mask, value_pair, jnp.zeros_like(value_pair))
+            for case, (query_row, first, width, key_row) in enumerate(CASES):
+                jobs.append((which, case))
+                lows.append(prob_ref[2 * t + which, :, first : first + width])
+                rows = slice(query_row, query_row + HALF)
+                deltas.append(nt(datt_ref[rows, cols], value_head[key_row : key_row + width]))
+        wides = [low.astype(f32) for low in lows]
+        weighted = [wide * g for wide, g in zip(wides, deltas)]
+        totals = [jnp.sum(a, axis=1, keepdims=True) for a in weighted]
+        backs = [(a - wide * total).astype(bf16) for a, wide, total in zip(weighted, wides, totals)]
+        for (which, case), low, back in zip(jobs, lows, backs):
+            query_row, _, width, key_row = CASES[case]
+            rows, keys = slice(query_row, query_row + HALF), slice(key_row, key_row + width)
             small = head_mask(HALF, which)
-            for case, (query_row, first, width, key_row) in enumerate(CASES):
-                rows = slice(query_row, query_row + HALF)
-                keys = slice(key_row, key_row + width)
-                low = prob_ref[2 * t + which, :, first : first + width]
-                wide = low.astype(f32)
-                delta_head = datt_ref[rows, cols]
-                g = nt(delta_head, value_head[keys])
-                weighted = wide * g
-                scores_back = (weighted - wide * jnp.sum(weighted, axis=1, keepdims=True)).astype(bf16)
-                part = mm(scores_back, key_head[keys])
-                query_grads[case] = part if query_grads[case] is None else query_grads[case] + part
-                query = q_ref[rows, cols]
-                query = jnp.where(small, query, jnp.zeros_like(query))
-                delta_head = jnp.where(small, delta_head, jnp.zeros_like(delta_head))
-                dk_acc[keys, :] += tn(scores_back, query)
-                dv_acc[keys, :] += tn(low, delta_head)
+            part = mm(back, keys_of[which][keys])
+            query_grads[case] = part if query_grads[case] is None else query_grads[case] + part
+            query, delta_head = q_ref[rows, cols], datt_ref[rows, cols]
+            dk_acc[keys, :] += tn(back, jnp.where(small, query, jnp.zeros_like(query)))
+            dv_acc[keys, :] += tn(low, jnp.where(small, delta_head, jnp.zeros_like(delta_head)))
         for block in range(4):
             rows = slice(block * HALF, block * HALF + HALF)
             places = slice((block % 2) * HALF, (block % 2) * HALF + HALF)
@@ -465,7 +472,7 @@
     vec_ref[...] = jnp.zeros_like(vec_ref)
     row = 0
     once = jnp.where(lax.axis_index("mp") == 0, 1.0, 0.0)
-    for values in (gnorm_ref[1:2, :], gnorm_ref[0:1, :] * once, gbd_ref[...] * once, gbu_ref[...]):
+    for values in (gnorm_ref[1:2, :], gnorm_ref[0:1, :] * once, gnorm_ref[2:3, :] * once, gbu_ref[...]):
         for first in range(0, values.shape[1], half):
             vec_ref[row : row + 1, :] = values[:, first : first + half]
             row += 1
@@ -661,10 +668,10 @@
     normed, q, k, v, attended, probs, branch = call(
         attention_forward,
         outs,
-        loose=[doc_lengths, pad_counts, norm_attn, inputs, w_query, w_key, w_value, cosine, sine, w_out],
+        loose=[doc_lengths.T, pad_counts, norm_attn, inputs, w_query, w_key, w_value, cosine, sine, w_out],
         scratch=[
             (scores[1:], f32),
-            pltpu.SMEM(doc_lengths.shape, jnp.int32),
+            pltpu.SMEM(doc_lengths.shape[::-1], jnp.int32),
             pltpu.SMEM(pad_counts.shape, jnp.int32),
             (norm_attn.shape, f32),
             rows_of["width"],
@@ -688,9 +695,9 @@
         *portions(width // STACK, units // PLANE * 2 // 3),
         ((2, rows, width), f32),
     ]
-    residual, grad_bu, grad_bd, *parts, shares = call(
+    residual, grad_bu, *parts, shares = call(
         mlp_kernel,
-        [rows_of["sum"], ((1, units), f32), ((1, width), f32), *big],
+        [rows_of["sum"], ((1, units), f32), *big],
         loose=[norm_mlp, b_up, inputs, branch, branch_other, cotangent, w_up, w_down],
         scratch=[
             (norm_mlp.shape, f32),
@@ -707,11 +714,11 @@
             ((rows, units), bf16),
             *big,
             sems(11),
-            sems(9),
+            sems(27),
         ],
         flops=2 * rows * width * units * 6,
         limit=62,
-        loose_outs=(0, *range(3, 10)),
+        loose_outs=(0, *range(2, 9)),
     )
     made, grads, sums = {key: [] for key in "dcuab"}, {}, []
     chains = {
@@ -725,7 +732,7 @@
         (shares_other,) = turn(state["shares_other"])
         ins = [
             shares, shares_other, residual, cotangent, norm_mlp, b_down, attended, w_out, q, k, v,
-            probs, cosine, sine, w_query, w_key, w_value, inputs, normed, grad_bd, grad_bu,
+            probs, cosine, sine, w_query, w_key, w_value, inputs, normed, grad_bu,
         ]
         outs = [rows_of["width"], rows_of["sum"], rows_of["sum"]]
         pieces = portions(half // STACK, half) * 2
@@ -743,7 +750,7 @@
                 ((rows, LANES), f32),
                 ((PLANE, 2, half, half), f32),
                 ((8, width), f32),
-                sems(25),
+                sems(24),
                 sems(7),
             ],
             flops=2 * rows * width * heads_cols * 10,
@@ -800,7 +807,7 @@
         grads.update(zip(names, results))
         did(results[0])
 
-    did(grad_bd)
+    did(grad_bu)
     pieces = {"K": backward, "I": input_back}
     waiting = []
     for key in ORDER:

time: 262 us -> 260 us (level)
  waiting for transfers between devices: 112 us -> 130 us
  starting transfers between devices: 64.5 us -> 52.2 us
  Pallas kernels: 71.8 us -> 64.4 us
    ppermute x35, waiting for transfers between devices: 107 us -> 125 us  [flip(): return lax.ppermute(values, ('dp', 'mp'), pairs)]
    ppermute x35, starting transfers between devices: 63.1 us -> 50.8 us  [flip(): return lax.ppermute(values, ('dp', 'mp'), pairs)]
    pallas_call x4, Pallas kernels: 52.9 us -> 45.5 us  [call(): pl.pallas_call(kernel, name=kernel.__name__, out_shape=shapes, in_specs=[...]
  transfers between devices with their start and end apart: 39 -> 39, of which waited for: 24 -> 22; matrix products, arithmetic and copies ran while one was open for 4% -> 4% of each run, Pallas kernels for 15% -> 14%
where the time goes in v7:
time: 260 us; the launch traced here: 259 us
  waiting for transfers between devices  130 us (50%)
  Pallas kernels  64.4 us (25%)
  starting transfers between devices  52.2 us (20%)
  other arithmetic  7.41 us (3%)
  local copies, waits for them, and re-layouts  3.99 us (2%)
    ppermute x35, waiting for transfers between devices, flip(): return lax.ppermute(values, ('dp', 'mp'), pairs)  125 us
    ppermute x35, starting transfers between devices, flip(): return lax.ppermute(values, ('dp', 'mp'), pairs)  50.8 us
    pallas_call x4, Pallas kernels, call(): pl.pallas_call(kernel, name=kernel.__name__, out_shape=shapes, in_specs=[...  45.5 us
    pallas_call x10, Pallas kernels, put(): pl.pallas_call(partial(put_in_place, views, key == 'c', sent, len(olds)),...  18.9 us
  transfers between devices with their start and end apart: 39, of which 22 were waited for; matrix products, arithmetic and copies ran while one was open for 4% of the time, Pallas kernels for 14%

profile of v7, /device:TPU:0, one launch (start us, length us, event | category | flops | bytes accessed | tf_op | source)
XLA Modules:
  0.0 259.3 jit_solution(5043863899563304369)
XLA Ops:
  0.6 8.1 %attention_forward.1 = (bf16[512,768]{1,0:T(8,128)(2,1)}, bf16[512,384]{1,0:T(8,128)(2,1)}, bf16[512,384]{1,0:T(8,128)(2,1)}, bf16[512,384]{1,0:T(8,128)(2,1)}, ...) custom-call(s32[8,16]{1,0:T(8,128)} %bitcast.57, s32[16]{0:T(128)} %pads_in.1, ...), custom_call_target="tpu_custom_call" | custom-call | flops 1207959552 | bytes 8916544 | tf_op jit(solution)/shard_map/attention_forward/pallas_call | solution.py:562
  9.2 3.2 %collective-permute-done.theirs_in = f32[512,768]{1,0:T(8,128)S(1)} collective-permute-done((f32[512,768]{1,0:T(8,128)}, f32[512,768]{1,0:T(8,128)S(1)}, u32[]{:S(2)}, u32[]{:S(2)}) %collective-permute-start) | collective-permute-done | bytes 1572896 | tf_op jit(solution)/shard_map/ppermute | solution.py:587
  12.5 1.1 copy-done.10
  13.6 17.0 %mlp_kernel.1 = (f32[512,768]{1,0:T(8,128)}, f32[1,1536]{1,0:T(1,128)}, f32[2,4,96,512]{3,2,1,0:T(8,128)}, f32[2,4,96,512]{3,2,1,0:T(8,128)}, f32[2,4,192,256]{3...) custom-call(f32[768]{0:T(1024)} %refs_4_.1, ...), custom_call_target="tpu_custom_call" | custom-call | flops 7247757312 | bytes 23608320 | tf_op jit(solution)/shard_map/mlp_kernel/pallas_call | solution.py:562
  31.1 2.6 %collective-permute-start.5 = (f32[2,4,192,256]{3,2,1,0:T(8,128)}, f32[2,4,192,256]{3,2,1,0:T(8,128)}, u32[]{:S(2)}, u32[]{:S(2)}) collective-permute-start(f32[2,4,192,256]{3,2,1,0:T(8,128)} %get-tuple-element.151), channel_id=1, source_target_pairs={{0,2},{1,5},{2,0},{3,7},{4,6},{5,1},{6,4},{7,3},{8,10},{9,13},{10,... | collective-permute-start | bytes 4718600 | tf_op jit(solution)/shard_map/up_sum_first/ppermute | solution.py:592
  33.7 1.6 collective-permute-start.4
  35.8 0.9 collective-permute-done.1.refs_1_
  36.7 16.9 %attention_backward.1 = (bf16[512,768]{1,0:T(8,128)(2,1)}, f32[512,768]{1,0:T(8,128)}, f32[512,768]{1,0:T(8,128)}, f32[16,384]{1,0:T(8,128)}, f32[2,4,96,384]{3,...) custom-call(f32[2,512,768]{2,1,0:T(8,128)} %get-tuple-element.134.refs_0_, ...), custom_call_target="tpu_custom_call" | custom-call | flops 3019898880 | bytes 24678400 | tf_op jit(solution)/shard_map/attention_backward/pallas_call | solution.py:562
  54.1 2.2 add_bitcast_fusion.2
  56.3 2.7 %collective-permute-start.7 = (f32[4,192,256]{2,1,0:T(8,128)S(1)}, f32[4,192,256]{2,1,0:T(8,128)S(1)}, u32[]{:S(2)}, u32[]{:S(2)}) collective-permute-start(f32[4,192,256]{2,1,0:T(8,128)S(1)} %get-tuple-element.259), channel_id=1, source_target_pairs={{0,4},{1,3},{2,6},{3,1},{4,0},{5,7},{6,2},{7,5},{8,12},{9,11},{10,... | collective-permute-start | bytes 2359304 | tf_op jit(solution)/shard_map/up_sum_second/ppermute | solution.py:592
  59.0 12.2 %collective-permute-done.4 = f32[2,4,192,256]{3,2,1,0:T(8,128)} collective-permute-done((f32[2,4,192,256]{3,2,1,0:T(8,128)}, f32[2,4,192,256]{3,2,1,0:T(8,128)}, u32[]{:S(2)}, u32[]{:S(2)}) %collective-permute-start.4) | collective-permute-done | bytes 1572896 | tf_op jit(solution)/shard_map/down_stack_sum_z_first/ppermute | solution.py:592
  71.3 1.7 add_bitcast_fusion
  73.0 4.6 %collective-permute-done.3 = f32[2,4,96,512]{3,2,1,0:T(8,128)S(1)} collective-permute-done((f32[2,4,96,512]{3,2,1,0:T(8,128)}, f32[2,4,96,512]{3,2,1,0:T(8,128)S(1)}, u32[]{:S(2)}, u32[]{:S(2)}) %collective-permute-start.3) | collective-permute-done | bytes 1572896 | tf_op jit(solution)/shard_map/down_sum_first/ppermute | solution.py:592
  77.6 2.1 collective-permute-start.9
  80.1 1.6 collective-permute-start.10
  81.7 2.6 collective-permute-start.14
  84.3 0.6 collective-permute-start.6
  84.9 3.5 %input_kernel.1 = bf16[512,768]{1,0:T(8,128)(2,1)} custom-call(f32[512,768]{1,0:T(8,128)S(1)} %copy-done.2, f32[512,768]{1,0:T(8,128)S(1)} %collective-permute-done.2.theirs_ref, bf16[512,768]{1,0:T(8,128)(2,1)S(1)} %copy-done, f32[1,768]{1,0:T(1,128)S(1)} %reshape.69.gain_ref, f32[512,768]{1,0:T(8,128)S(1)} %copy-done.1), custom_call_target="tpu_custom_call" | custom-call | bytes 6294528 | tf_op jit(solution)/shard_map/input_kernel/pallas_call | solution.py:562
  88.5 1.6 collective-permute-start.8
  90.2 10.4 %collective-permute-done.10 = f32[4,96,512]{2,1,0:T(8,128)S(1)} collective-permute-done((f32[4,96,512]{2,1,0:T(8,128)S(1)}, f32[4,96,512]{2,1,0:T(8,128)S(1)}, u32[]{:S(2)}, u32[]{:S(2)}) %collective-permute-start.10) | collective-permute-done | bytes 786464 | tf_op jit(solution)/shard_map/down_sum_second/ppermute | solution.py:592
  100.8 1.5 collective-permute-done.9
  102.5 0.9 collective-permute-start.12
  103.4 1.5 collective-permute-start.13
  104.9 4.1 %collective-permute-done.8 = f32[2,192,256]{2,1,0:T(8,128)S(1)} collective-permute-done((f32[2,192,256]{2,1,0:T(8,128)S(1)}, f32[2,192,256]{2,1,0:T(8,128)S(1)}, u32[]{:S(2)}, u32[]{:S(2)}) %collective-permute-start.8) | collective-permute-done | bytes 393248 | tf_op jit(solution)/shard_map/up_sum_z_first/ppermute | solution.py:592
  109.0 4.2 %collective-permute-start.11 = (f32[2,192,256]{2,1,0:T(8,128)S(1)}, f32[2,192,256]{2,1,0:T(8,128)S(1)}, u32[]{:S(2)}, u32[]{:S(2)}) collective-permute-start(f32[2,192,256]{2,1,0:T(8,128)S(1)} %add.145), channel_id=1, source_target_pairs={{0,16},{1,9},{2,18},{3,11},{4,20},{5,13},{6,22},{7,15},{8,24},{9,1... | collective-permute-start | bytes 1179656 | tf_op jit(solution)/shard_map/up_sum_z_second/ppermute | solution.py:592
  113.2 4.8 %collective-permute-done.14 = f32[4,192,256]{2,1,0:T(8,128)S(1)} collective-permute-done((f32[4,192,256]{2,1,0:T(8,128)S(1)}, f32[4,192,256]{2,1,0:T(8,128)S(1)}, u32[]{:S(2)}, u32[]{:S(2)}) %collective-permute-start.14) | collective-permute-done | bytes 786464 | tf_op jit(solution)/shard_map/down_stack_sum_z_second/ppermute | solution.py:592
  118.1 0.6 collective-permute-start.16
  118.7 3.1 %collective-permute-done.13 = f32[2,96,512]{2,1,0:T(8,128)S(1)} collective-permute-done((f32[2,96,512]{2,1,0:T(8,128)S(1)}, f32[2,96,512]{2,1,0:T(8,128)S(1)}, u32[]{:S(2)}, u32[]{:S(2)}) %collective-permute-start.13) | collective-permute-done | bytes 393248 | tf_op jit(solution)/shard_map/down_sum_z_first/ppermute | solution.py:592
  122.4 3.0 %collective-permute-start.21 = (f32[2,96,384]{2,1,0:T(8,128)S(1)}, f32[2,96,384]{2,1,0:T(8,128)S(1)}, u32[]{:S(2)}, u32[]{:S(2)}) collective-permute-start(f32[2,96,384]{2,1,0:T(8,128)S(1)} %get-tuple-element.271), channel_id=1, source_target_pairs={{0,8},{1,17},{2,10},{3,19},{4,12},{5,21},{6,14},{7,23},{8,0},{9,25... | collective-permute-start | bytes 884744 | tf_op jit(solution)/shard_map/attention_rest_sum_z_first/ppermute | solution.py:592
  125.5 8.3 %collective-permute-done.11 = f32[2,192,256]{2,1,0:T(8,128)S(1)} collective-permute-done((f32[2,192,256]{2,1,0:T(8,128)S(1)}, f32[2,192,256]{2,1,0:T(8,128)S(1)}, u32[]{:S(2)}, u32[]{:S(2)}) %collective-permute-start.11) | collective-permute-done | bytes 393248 | tf_op jit(solution)/shard_map/up_sum_z_second/ppermute | solution.py:592
  133.8 0.7 collective-permute-start.23
  134.9 2.1 collective-permute-start.17
  137.0 9.6 %collective-permute-done.18 = f32[2,96,512]{2,1,0:T(8,128)S(1)} collective-permute-done((f32[2,96,512]{2,1,0:T(8,128)S(1)}, f32[2,96,512]{2,1,0:T(8,128)S(1)}, u32[]{:S(2)}, u32[]{:S(2)}) %collective-permute-start.18) | collective-permute-done | bytes 393248 | tf_op jit(solution)/shard_map/down_sum_z_second/ppermute | solution.py:592
  146.6 8.0 %collective-permute-start.20 = (f32[2,96,512]{2,1,0:T(8,128)S(1)}, f32[2,96,512]{2,1,0:T(8,128)S(1)}, u32[]{:S(2)}, u32[]{:S(2)}) collective-permute-start(f32[2,96,512]{2,1,0:T(8,128)S(1)} %reverse_add_fusion.1), channel_id=1, source_target_pairs={{0,8},{1,17},{2,10},{3,19},{4,12},{5,21},{6,14},{7,23},{8,0},{9,25... | collective-permute-start | bytes 1179656 | tf_op jit(solution)/shard_map/down_gather_z_first/ppermute | solution.py:592
  155.3 11.5 %collective-permute-done.22 = f32[2,192,256]{2,1,0:T(8,128)S(1)} collective-permute-done((f32[2,192,256]{2,1,0:T(8,128)S(1)}, f32[2,192,256]{2,1,0:T(8,128)S(1)}, u32[]{:S(2)}, u32[]{:S(2)}) %collective-permute-start.22) | collective-permute-done | bytes 393248 | tf_op jit(solution)/shard_map/down_stack_gather_first/ppermute | solution.py:592
  166.9 0.7 collective-permute-done.20
  167.8 3.3 %collective-permute-done.19 = f32[208,384]{1,0:T(8,128)S(1)} collective-permute-done((f32[208,384]{1,0:T(8,128)S(1)}, f32[208,384]{1,0:T(8,128)S(1)}, u32[]{:S(2)}, u32[]{:S(2)}) %collective-permute-start.19) | collective-permute-done | bytes 319520 | tf_op jit(solution)/shard_map/attention_sum_z_first/ppermute | solution.py:592
  171.4 2.0 collective-permute-start.24
  173.3 1.0 collective-permute-start.30
  174.4 1.9 collective-permute-start.29
  176.3 9.3 %collective-permute-done.26 = f32[4,96,512]{2,1,0:T(8,128)S(1)} collective-permute-done((f32[4,96,512]{2,1,0:T(8,128)S(1)}, f32[4,96,512]{2,1,0:T(8,128)S(1)}, u32[]{:S(2)}, u32[]{:S(2)}) %collective-permute-start.26) | collective-permute-done | bytes 786464 | tf_op jit(solution)/shard_map/down_gather_second/ppermute | solution.py:592
  185.7 1.4 put_u.2.refs_0_
  187.3 1.4 put_d.2.refs_0_
  188.8 1.9 collective-permute-start.31
  190.8 5.5 %collective-permute-done.32.piece_ref = f32[2,4,192,256]{3,2,1,0:T(8,128)S(1)} collective-permute-done((f32[2,4,192,256]{3,2,1,0:T(8,128)S(1)}, f32[2,4,192,256]{3,2,1,0:T(8,128)S(1)}, u32[]{:S(2)}, u32[]{:S(2)}) %collective-permute-start.32) | collective-permute-done | bytes 1572896 | tf_op jit(solution)/shard_map/up_gather_first/ppermute | solution.py:592
  196.3 1.4 put_u.3.refs_1_
  197.8 13.1 %collective-permute-done.31 = f32[2,96,384]{2,1,0:T(8,128)S(1)} collective-permute-done((f32[2,96,384]{2,1,0:T(8,128)S(1)}, f32[2,96,384]{2,1,0:T(8,128)S(1)}, u32[]{:S(2)}, u32[]{:S(2)}) %collective-permute-start.31) | collective-permute-done | bytes 294944 | tf_op jit(solution)/shard_map/attention_rest_gather_z_first/ppermute | solution.py:592
  211.0 7.6 %collective-permute-done.29 = f32[4,192,256]{2,1,0:T(8,128)S(1)} collective-permute-done((f32[4,192,256]{2,1,0:T(8,128)S(1)}, f32[4,192,256]{2,1,0:T(8,128)S(1)}, u32[]{:S(2)}, u32[]{:S(2)}) %collective-permute-start.29) | collective-permute-done | bytes 786464 | tf_op jit(solution)/shard_map/down_stack_gather_z_second/ppermute | solution.py:592
  219.5 1.4 put_c.2
  220.9 1.4 put_d.3.refs_0_
  222.4 2.0 collective-permute-start.37
  224.4 7.8 %collective-permute-done.33 = f32[4,96,384]{2,1,0:T(8,128)S(1)} collective-permute-done((f32[4,96,384]{2,1,0:T(8,128)S(1)}, f32[4,96,384]{2,1,0:T(8,128)S(1)}, u32[]{:S(2)}, u32[]{:S(2)}) %collective-permute-start.33) | collective-permute-done | bytes 589856 | tf_op jit(solution)/shard_map/attention_gather_second/ppermute | solution.py:592
  232.2 1.1 pad_maximum_fusion.5.piece_ref
  233.4 3.2 %collective-permute-start.36 = (f32[2,4,96,384]{3,2,1,0:T(8,128)}, f32[2,4,96,384]{3,2,1,0:T(8,128)}, u32[]{:S(2)}, u32[]{:S(2)}) collective-permute-start(f32[2,4,96,384]{3,2,1,0:T(8,128)} %pad_maximum_fusion.5.piece_ref), channel_id=1, source_target_pairs={{0,2},{1,5},{2,0},{3,7},{4,6},{5,1},{6,4},{7,3},{8,10},{9,13},{10,... | collective-permute-start | bytes 3538952 | tf_op jit(solution)/shard_map/attention_gather_first/ppermute | solution.py:592
  236.6 0.6 slice.228
  237.8 0.6 squeeze.15
  238.4 0.6 squeeze.16
  239.6 1.3 put_b.2
  240.9 2.6 put_a.2
  243.5 2.6 put_b.3
  246.0 6.8 %collective-permute-done.36.piece_ref = f32[2,4,96,384]{3,2,1,0:T(8,128)} collective-permute-done((f32[2,4,96,384]{3,2,1,0:T(8,128)}, f32[2,4,96,384]{3,2,1,0:T(8,128)}, u32[]{:S(2)}, u32[]{:S(2)}) %collective-permute-start.36) | collective-permute-done | bytes 1179680 | tf_op jit(solution)/shard_map/attention_gather_first/ppermute | solution.py:592
  252.9 2.6 put_a.3
  255.4 0.9 collective-permute-done.38.piece_ref
  256.3 2.8 %put_c.3 = (f32[1536,768]{1,0:T(8,128)}, f32[768,1536]{1,0:T(8,128)}) custom-call(f32[2,4,192,256]{3,2,1,0:T(8,128)} %collective-permute-done.38.piece_ref, f32[1536,768]{1,0:T(8,128)} %put_d.3.refs_0_, f32[768,1536]{1,0:T(8,128)} %get-tuple-element.251.refs_1_), custom_call_target="tpu_custom_call", output_to_operand_aliasing={{0}: (1, {}), {1}: (2, {})} | custom-call | bytes 3145728 | tf_op jit(solution)/shard_map/put_c/pallas_call | solution.py:796
  (109 shorter events, 7.9 us)
Async XLA Ops:
  8.7 3.8 %collective-permute-start = (f32[512,768]{1,0:T(8,128)}, f32[512,768]{1,0:T(8,128)S(1)}, u32[]{:S(2)}, u32[]{:S(2)}) collective-permute-start(f32[512,768]{1,0:T(8,128)} %get-tuple-element.133.mine_in), channel_id=1, source_target_pairs={{0,1},{1,0},{2,3},{3,2},{4,5},{5,4},{6,7},{7,6},{8,9},{9,8},{10,11... | collective-permute-start | bytes 4718600 | tf_op jit(solution)/shard_map/ppermute | solution.py:587
  12.5 1.1 copy-start.10
  30.7 6.1 %collective-permute-start.1 = (f32[2,512,768]{2,1,0:T(8,128)}, f32[2,512,768]{2,1,0:T(8,128)}, u32[]{:S(2)}, u32[]{:S(2)}) collective-permute-start(f32[2,512,768]{2,1,0:T(8,128)} %get-tuple-element.134.refs_0_), channel_id=1, source_target_pairs={{0,1},{1,0},{2,3},{3,2},{4,5},{5,4},{6,7},{7,6},{8,9},{9,8},{10,11... | collective-permute-start | bytes 9437192 | tf_op jit(solution)/shard_map/ppermute | solution.py:587
  31.1 23.0 %collective-permute-start.5 = (f32[2,4,192,256]{3,2,1,0:T(8,128)}, f32[2,4,192,256]{3,2,1,0:T(8,128)}, u32[]{:S(2)}, u32[]{:S(2)}) collective-permute-start(f32[2,4,192,256]{3,2,1,0:T(8,128)} %get-tuple-element.151), channel_id=1, source_target_pairs={{0,2},{1,5},{2,0},{3,7},{4,6},{5,1},{6,4},{7,3},{8,10},{9,13},{10,... | collective-permute-start | bytes 4718600 | tf_op jit(solution)/shard_map/up_sum_first/ppermute | solution.py:592
  33.7 37.5 %collective-permute-start.4 = (f32[2,4,192,256]{3,2,1,0:T(8,128)}, f32[2,4,192,256]{3,2,1,0:T(8,128)}, u32[]{:S(2)}, u32[]{:S(2)}) collective-permute-start(f32[2,4,192,256]{3,2,1,0:T(8,128)} %get-tuple-element.149), channel_id=1, source_target_pairs={{0,8},{1,17},{2,10},{3,19},{4,12},{5,21},{6,14},{7,23},{8,0},{9,25... | collective-permute-start | bytes 4718600 | tf_op jit(solution)/shard_map/down_stack_sum_z_first/ppermute | solution.py:592
  35.3 42.3 %collective-permute-start.3 = (f32[2,4,96,512]{3,2,1,0:T(8,128)}, f32[2,4,96,512]{3,2,1,0:T(8,128)S(1)}, u32[]{:S(2)}, u32[]{:S(2)}) collective-permute-start(f32[2,4,96,512]{3,2,1,0:T(8,128)} %get-tuple-element.147), channel_id=1, source_target_pairs={{0,2},{1,5},{2,0},{3,7},{4,6},{5,1},{6,4},{7,3},{8,10},{9,13},{10,... | collective-permute-start | bytes 4718600 | tf_op jit(solution)/shard_map/down_sum_first/ppermute | solution.py:592
  53.7 30.7 %collective-permute-start.2 = (f32[512,768]{1,0:T(8,128)}, f32[512,768]{1,0:T(8,128)S(1)}, u32[]{:S(2)}, u32[]{:S(2)}) collective-permute-start(f32[512,768]{1,0:T(8,128)} %get-tuple-element.145.mine_ref), channel_id=1, source_target_pairs={{0,1},{1,0},{2,3},{3,2},{4,5},{5,4},{6,7},{7,6},{8,9},{9,8},{10,11... | collective-permute-start | bytes 4718600 | tf_op jit(solution)/shard_map/ppermute | solution.py:587
  54.1 17.2 %copy-start.4 = (f32[2,4,192,256]{3,2,1,0:T(8,128)S(1)}, f32[2,4,192,256]{3,2,1,0:T(8,128)}, u32[]{:S(2)}) copy-start(f32[2,4,192,256]{3,2,1,0:T(8,128)} %get-tuple-element.155) | copy-start | bytes 4718596
  56.3 32.1 %collective-permute-start.7 = (f32[4,192,256]{2,1,0:T(8,128)S(1)}, f32[4,192,256]{2,1,0:T(8,128)S(1)}, u32[]{:S(2)}, u32[]{:S(2)}) collective-permute-start(f32[4,192,256]{2,1,0:T(8,128)S(1)} %get-tuple-element.259), channel_id=1, source_target_pairs={{0,4},{1,3},{2,6},{3,1},{4,0},{5,7},{6,2},{7,5},{8,12},{9,11},{10,... | collective-permute-start | bytes 2359304 | tf_op jit(solution)/shard_map/up_sum_second/ppermute | solution.py:592
  71.3 6.3 %copy-start.11 = (f32[2,4,96,384]{3,2,1,0:T(8,128)S(1)}, f32[2,4,96,384]{3,2,1,0:T(8,128)}, u32[]{:S(2)}) copy-start(f32[2,4,96,384]{3,2,1,0:T(8,128)} %get-tuple-element.166) | copy-start | bytes 3538948
  71.3 8.4 %copy-start.3 = (f32[2,4,96,512]{3,2,1,0:T(8,128)S(1)}, f32[2,4,96,512]{3,2,1,0:T(8,128)}, u32[]{:S(2)}) copy-start(f32[2,4,96,512]{3,2,1,0:T(8,128)} %get-tuple-element.157) | copy-start | bytes 4718596
  77.6 4.1 %copy-start.9 = (f32[768]{0:T(1024)S(1)}, f32[768]{0:T(1024)}, u32[]{:S(2)}) copy-start(f32[768]{0:T(1024)} %gain_in.2) | copy-start | bytes 9220
  77.6 6.6 %copy-start.7 = (f32[2,4,96,384]{3,2,1,0:T(8,128)S(1)}, f32[2,4,96,384]{3,2,1,0:T(8,128)}, u32[]{:S(2)}) copy-start(f32[2,4,96,384]{3,2,1,0:T(8,128)} %get-tuple-element.162) | copy-start | bytes 3538948
  77.6 6.6 %copy-start.8 = (f32[16,384]{1,0:T(8,128)S(1)}, f32[16,384]{1,0:T(8,128)}, u32[]{:S(2)}) copy-start(f32[16,384]{1,0:T(8,128)} %get-tuple-element.183) | copy-start | bytes 73732
  77.6 24.7 %collective-permute-start.9 = (f32[2,4,96,384]{3,2,1,0:T(8,128)S(1)}, f32[2,4,96,384]{3,2,1,0:T(8,128)S(1)}, u32[]{:S(2)}, u32[]{:S(2)}) collective-permute-start(f32[2,4,96,384]{3,2,1,0:T(8,128)S(1)} %copy-done.11), channel_id=1, source_target_pairs={{0,2},{1,5},{2,0},{3,7},{4,6},{5,1},{6,4},{7,3},{8,10},{9,13},{10,... | collective-permute-start | bytes 3538952 | tf_op jit(solution)/shard_map/attention_rest_sum_first/ppermute | solution.py:592
  79.7 5.2 %copy-start.2 = (f32[512,768]{1,0:T(8,128)S(1)}, f32[512,768]{1,0:T(8,128)}, u32[]{:S(2)}) copy-start(f32[512,768]{1,0:T(8,128)} %get-tuple-element.145.mine_ref) | copy-start | bytes 4718596
  80.1 4.9 %copy-start = (bf16[512,768]{1,0:T(8,128)(2,1)S(1)}, bf16[512,768]{1,0:T(8,128)(2,1)}, u32[]{:S(2)}) copy-start(bf16[512,768]{1,0:T(8,128)(2,1)} %x_ref.1) | copy-start | bytes 2359300
  80.1 4.9 %copy-start.1 = (f32[512,768]{1,0:T(8,128)S(1)}, f32[512,768]{1,0:T(8,128)}, u32[]{:S(2)}) copy-start(f32[512,768]{1,0:T(8,128)} %get-tuple-element.160.delta_ref) | copy-start | bytes 4718596
  80.1 20.5 %collective-permute-start.10 = (f32[4,96,512]{2,1,0:T(8,128)S(1)}, f32[4,96,512]{2,1,0:T(8,128)S(1)}, u32[]{:S(2)}, u32[]{:S(2)}) collective-permute-start(f32[4,96,512]{2,1,0:T(8,128)S(1)} %get-tuple-element.257), channel_id=1, source_target_pairs={{0,4},{1,3},{2,6},{3,1},{4,0},{5,7},{6,2},{7,5},{8,12},{9,11},{10,... | collective-permute-start | bytes 2359304 | tf_op jit(solution)/shard_map/down_sum_second/ppermute | solution.py:592
  81.7 36.3 %collective-permute-start.14 = (f32[4,192,256]{2,1,0:T(8,128)S(1)}, f32[4,192,256]{2,1,0:T(8,128)S(1)}, u32[]{:S(2)}, u32[]{:S(2)}) collective-permute-start(f32[4,192,256]{2,1,0:T(8,128)S(1)} %get-tuple-element.255), channel_id=1, source_target_pairs={{0,16},{1,9},{2,18},{3,11},{4,20},{5,13},{6,22},{7,15},{8,24},{9,1... | collective-permute-start | bytes 2359304 | tf_op jit(solution)/shard_map/down_stack_sum_z_second/ppermute | solution.py:592
  84.3 50.2 %collective-permute-start.6 = (f32[784,384]{1,0:T(8,128)S(1)}, f32[784,384]{1,0:T(8,128)S(1)}, u32[]{:S(2)}, u32[]{:S(2)}) collective-permute-start(f32[784,384]{1,0:T(8,128)S(1)} %pad_maximum_fusion.3), channel_id=1, source_target_pairs={{0,2},{1,5},{2,0},{3,7},{4,6},{5,1},{6,4},{7,3},{8,10},{9,13},{10,... | collective-permute-start | bytes 3612680 | tf_op jit(solution)/shard_map/attention_sum_first/ppermute | solution.py:592
  88.5 13.8 %copy-start.5 = (f32[2,4,96,384]{3,2,1,0:T(8,128)S(1)}, f32[2,4,96,384]{3,2,1,0:T(8,128)}, u32[]{:S(2)}) copy-start(f32[2,4,96,384]{3,2,1,0:T(8,128)} %get-tuple-element.169) | copy-start | bytes 3538948
  88.5 20.4 %collective-permute-start.8 = (f32[2,192,256]{2,1,0:T(8,128)S(1)}, f32[2,192,256]{2,1,0:T(8,128)S(1)}, u32[]{:S(2)}, u32[]{:S(2)}) collective-permute-start(f32[2,192,256]{2,1,0:T(8,128)S(1)} %get-tuple-element.266), channel_id=1, source_target_pairs={{0,8},{1,17},{2,10},{3,19},{4,12},{5,21},{6,14},{7,23},{8,0},{9,25... | collective-permute-start | bytes 1179656 | tf_op jit(solution)/shard_map/up_sum_z_first/ppermute | solution.py:592
  102.5 19.9 %collective-permute-start.12 = (f32[4,96,384]{2,1,0:T(8,128)S(1)}, f32[4,96,384]{2,1,0:T(8,128)S(1)}, u32[]{:S(2)}, u32[]{:S(2)}) collective-permute-start(f32[4,96,384]{2,1,0:T(8,128)S(1)} %get-tuple-element.261), channel_id=1, source_target_pairs={{0,4},{1,3},{2,6},{3,1},{4,0},{5,7},{6,2},{7,5},{8,12},{9,11},{10,... | collective-permute-start | bytes 1769480 | tf_op jit(solution)/shard_map/attention_rest_sum_second/ppermute | solution.py:592
  103.4 18.4 %collective-permute-start.13 = (f32[2,96,512]{2,1,0:T(8,128)S(1)}, f32[2,96,512]{2,1,0:T(8,128)S(1)}, u32[]{:S(2)}, u32[]{:S(2)}) collective-permute-start(f32[2,96,512]{2,1,0:T(8,128)S(1)} %get-tuple-element.265), channel_id=1, source_target_pairs={{0,8},{1,17},{2,10},{3,19},{4,12},{5,21},{6,14},{7,23},{8,0},{9,25... | collective-permute-start | bytes 1179656 | tf_op jit(solution)/shard_map/down_sum_z_first/ppermute | solution.py:592
  109.0 24.8 %collective-permute-start.11 = (f32[2,192,256]{2,1,0:T(8,128)S(1)}, f32[2,192,256]{2,1,0:T(8,128)S(1)}, u32[]{:S(2)}, u32[]{:S(2)}) collective-permute-start(f32[2,192,256]{2,1,0:T(8,128)S(1)} %add.145), channel_id=1, source_target_pairs={{0,16},{1,9},{2,18},{3,11},{4,20},{5,13},{6,22},{7,15},{8,24},{9,1... | collective-permute-start | bytes 1179656 | tf_op jit(solution)/shard_map/up_sum_z_second/ppermute | solution.py:592
  118.1 16.7 %collective-permute-start.16 = (f32[2,192,256]{2,1,0:T(8,128)S(1)}, f32[2,192,256]{2,1,0:T(8,128)S(1)}, u32[]{:S(2)}, u32[]{:S(2)}) collective-permute-start(f32[2,192,256]{2,1,0:T(8,128)S(1)} %get-tuple-element.263), channel_id=1, source_target_pairs={{0,2},{1,5},{2,0},{3,7},{4,6},{5,1},{6,4},{7,3},{8,10},{9,13},{10,... | collective-permute-start | bytes 1179656 | tf_op jit(solution)/shard_map/down_stack_sum_first/ppermute | solution.py:592
  121.9 12.6 %copy-start.6 = (f32[2,4,96,384]{3,2,1,0:T(8,128)S(1)}, f32[2,4,96,384]{3,2,1,0:T(8,128)}, u32[]{:S(2)}) copy-start(f32[2,4,96,384]{3,2,1,0:T(8,128)} %get-tuple-element.181) | copy-start | bytes 3538948
  121.9 24.6 %collective-permute-start.18 = (f32[2,96,512]{2,1,0:T(8,128)S(1)}, f32[2,96,512]{2,1,0:T(8,128)S(1)}, u32[]{:S(2)}, u32[]{:S(2)}) collective-permute-start(f32[2,96,512]{2,1,0:T(8,128)S(1)} %add.152), channel_id=1, source_target_pairs={{0,16},{1,9},{2,18},{3,11},{4,20},{5,13},{6,22},{7,15},{8,24},{9,1... | collective-permute-start | bytes 1179656 | tf_op jit(solution)/shard_map/down_sum_z_second/ppermute | solution.py:592
  122.4 44.4 %collective-permute-start.21 = (f32[2,96,384]{2,1,0:T(8,128)S(1)}, f32[2,96,384]{2,1,0:T(8,128)S(1)}, u32[]{:S(2)}, u32[]{:S(2)}) collective-permute-start(f32[2,96,384]{2,1,0:T(8,128)S(1)} %get-tuple-element.271), channel_id=1, source_target_pairs={{0,8},{1,17},{2,10},{3,19},{4,12},{5,21},{6,14},{7,23},{8,0},{9,25... | collective-permute-start | bytes 884744 | tf_op jit(solution)/shard_map/attention_rest_sum_z_first/ppermute | solution.py:592
  133.8 21.3 %collective-permute-start.23 = (f32[2,192,256]{2,1,0:T(8,128)S(1)}, f32[2,192,256]{2,1,0:T(8,128)S(1)}, u32[]{:S(2)}, u32[]{:S(2)}) collective-permute-start(f32[2,192,256]{2,1,0:T(8,128)S(1)} %reverse_add_fusion.2), channel_id=1, source_target_pairs={{0,8},{1,17},{2,10},{3,19},{4,12},{5,21},{6,14},{7,23},{8,0},{9,25... | collective-permute-start | bytes 1179656 | tf_op jit(solution)/shard_map/up_gather_z_first/ppermute | solution.py:592
  134.7 20.1 %collective-permute-start.15 = (f32[400,384]{1,0:T(8,128)S(1)}, f32[400,384]{1,0:T(8,128)S(1)}, u32[]{:S(2)}, u32[]{:S(2)}) collective-permute-start(f32[400,384]{1,0:T(8,128)S(1)} %pad_maximum_fusion.6), channel_id=1, source_target_pairs={{0,4},{1,3},{2,6},{3,1},{4,0},{5,7},{6,2},{7,5},{8,12},{9,11},{10,... | collective-permute-start | bytes 1843208 | tf_op jit(solution)/shard_map/attention_sum_second/ppermute | solution.py:592
  134.9 19.8 %collective-permute-start.17 = (f32[2,192,256]{2,1,0:T(8,128)S(1)}, f32[2,192,256]{2,1,0:T(8,128)S(1)}, u32[]{:S(2)}, u32[]{:S(2)}) collective-permute-start(f32[2,192,256]{2,1,0:T(8,128)S(1)} %add.159), channel_id=1, source_target_pairs={{0,4},{1,3},{2,6},{3,1},{4,0},{5,7},{6,2},{7,5},{8,12},{9,11},{10,... | collective-permute-start | bytes 1179656 | tf_op jit(solution)/shard_map/down_stack_sum_second/ppermute | solution.py:592
  146.6 21.0 %collective-permute-start.20 = (f32[2,96,512]{2,1,0:T(8,128)S(1)}, f32[2,96,512]{2,1,0:T(8,128)S(1)}, u32[]{:S(2)}, u32[]{:S(2)}) collective-permute-start(f32[2,96,512]{2,1,0:T(8,128)S(1)} %reverse_add_fusion.1), channel_id=1, source_target_pairs={{0,8},{1,17},{2,10},{3,19},{4,12},{5,21},{6,14},{7,23},{8,0},{9,25... | collective-permute-start | bytes 1179656 | tf_op jit(solution)/shard_map/down_gather_z_first/ppermute | solution.py:592
  154.8 12.0 %collective-permute-start.22 = (f32[2,192,256]{2,1,0:T(8,128)S(1)}, f32[2,192,256]{2,1,0:T(8,128)S(1)}, u32[]{:S(2)}, u32[]{:S(2)}) collective-permute-start(f32[2,192,256]{2,1,0:T(8,128)S(1)} %reverse_add_fusion), channel_id=1, source_target_pairs={{0,2},{1,5},{2,0},{3,7},{4,6},{5,1},{6,4},{7,3},{8,10},{9,13},{10,... | collective-permute-start | bytes 1179656 | tf_op jit(solution)/shard_map/down_stack_gather_first/ppermute | solution.py:592
  155.1 16.0 %collective-permute-start.19 = (f32[208,384]{1,0:T(8,128)S(1)}, f32[208,384]{1,0:T(8,128)S(1)}, u32[]{:S(2)}, u32[]{:S(2)}) collective-permute-start(f32[208,384]{1,0:T(8,128)S(1)} %pad_maximum_fusion.7), channel_id=1, source_target_pairs={{0,8},{1,17},{2,10},{3,19},{4,12},{5,21},{6,14},{7,23},{8,0},{9,25... | collective-permute-start | bytes 958472 | tf_op jit(solution)/shard_map/attention_sum_z_first/ppermute | solution.py:592
  155.2 16.0 %collective-permute-start.25 = (f32[4,192,256]{2,1,0:T(8,128)S(1)}, f32[4,192,256]{2,1,0:T(8,128)S(1)}, u32[]{:S(2)}, u32[]{:S(2)}) collective-permute-start(f32[4,192,256]{2,1,0:T(8,128)S(1)} %constant_dynamic-update-slice_fusion), channel_id=1, source_target_pairs={{0,4},{1,3},{2,6},{3,1},{4,0},{5,7},{6,2},{7,5},{8,12},{9,11},{10,... | collective-permute-start | bytes 2359304 | tf_op jit(solution)/shard_map/up_gather_second/ppermute | solution.py:592
  167.7 17.8 %collective-permute-start.26 = (f32[4,96,512]{2,1,0:T(8,128)S(1)}, f32[4,96,512]{2,1,0:T(8,128)S(1)}, u32[]{:S(2)}, u32[]{:S(2)}) collective-permute-start(f32[4,96,512]{2,1,0:T(8,128)S(1)} %constant_dynamic-update-slice_fusion.4), channel_id=1, source_target_pairs={{0,4},{1,3},{2,6},{3,1},{4,0},{5,7},{6,2},{7,5},{8,12},{9,11},{10,... | collective-permute-start | bytes 2359304 | tf_op jit(solution)/shard_map/down_gather_second/ppermute | solution.py:592
  171.3 25.0 %collective-permute-start.32 = (f32[2,4,192,256]{3,2,1,0:T(8,128)S(1)}, f32[2,4,192,256]{3,2,1,0:T(8,128)S(1)}, u32[]{:S(2)}, u32[]{:S(2)}) collective-permute-start(f32[2,4,192,256]{3,2,1,0:T(8,128)S(1)} %pad_maximum_fusion.piece_ref), channel_id=1, source_target_pairs={{0,2},{1,5},{2,0},{3,7},{4,6},{5,1},{6,4},{7,3},{8,10},{9,13},{10,... | collective-permute-start | bytes 4718600 | tf_op jit(solution)/shard_map/up_gather_first/ppermute | solution.py:592
  171.4 15.8 %collective-permute-start.24 = (f32[208,384]{1,0:T(8,128)S(1)}, f32[208,384]{1,0:T(8,128)S(1)}, u32[]{:S(2)}, u32[]{:S(2)}) collective-permute-start(f32[208,384]{1,0:T(8,128)S(1)} %pad_maximum_fusion.8), channel_id=1, source_target_pairs={{0,16},{1,9},{2,18},{3,11},{4,20},{5,13},{6,22},{7,15},{8,24},{9,1... | collective-permute-start | bytes 958472 | tf_op jit(solution)/shard_map/attention_sum_z_second/ppermute | solution.py:592
  173.3 15.4 %collective-permute-start.30 = (f32[2,96,384]{2,1,0:T(8,128)S(1)}, f32[2,96,384]{2,1,0:T(8,128)S(1)}, u32[]{:S(2)}, u32[]{:S(2)}) collective-permute-start(f32[2,96,384]{2,1,0:T(8,128)S(1)} %add.166), channel_id=1, source_target_pairs={{0,16},{1,9},{2,18},{3,11},{4,20},{5,13},{6,22},{7,15},{8,24},{9,1... | collective-permute-start | bytes 884744 | tf_op jit(solution)/shard_map/attention_rest_sum_z_second/ppermute | solution.py:592
  174.4 44.2 %collective-permute-start.29 = (f32[4,192,256]{2,1,0:T(8,128)S(1)}, f32[4,192,256]{2,1,0:T(8,128)S(1)}, u32[]{:S(2)}, u32[]{:S(2)}) collective-permute-start(f32[4,192,256]{2,1,0:T(8,128)S(1)} %constant_dynamic-update-slice_fusion.2), channel_id=1, source_target_pairs={{0,16},{1,9},{2,18},{3,11},{4,20},{5,13},{6,22},{7,15},{8,24},{9,1... | collective-permute-start | bytes 2359304 | tf_op jit(solution)/shard_map/down_stack_gather_z_second/ppermute | solution.py:592
  185.6 35.2 %collective-permute-start.35 = (f32[2,4,96,512]{3,2,1,0:T(8,128)S(1)}, f32[2,4,96,512]{3,2,1,0:T(8,128)S(1)}, u32[]{:S(2)}, u32[]{:S(2)}) collective-permute-start(f32[2,4,96,512]{3,2,1,0:T(8,128)S(1)} %pad_maximum_fusion.1.piece_ref), channel_id=1, source_target_pairs={{0,2},{1,5},{2,0},{3,7},{4,6},{5,1},{6,4},{7,3},{8,10},{9,13},{10,... | collective-permute-start | bytes 4718600 | tf_op jit(solution)/shard_map/down_gather_first/ppermute | solution.py:592
  188.8 22.1 %collective-permute-start.31 = (f32[2,96,384]{2,1,0:T(8,128)S(1)}, f32[2,96,384]{2,1,0:T(8,128)S(1)}, u32[]{:S(2)}, u32[]{:S(2)}) collective-permute-start(f32[2,96,384]{2,1,0:T(8,128)S(1)} %reverse_add_fusion.3), channel_id=1, source_target_pairs={{0,8},{1,17},{2,10},{3,19},{4,12},{5,21},{6,14},{7,23},{8,0},{9,25... | collective-permute-start | bytes 884744 | tf_op jit(solution)/shard_map/attention_rest_gather_z_first/ppermute | solution.py:592
  190.7 28.1 %collective-permute-start.28 = (f32[2,96,384]{2,1,0:T(8,128)S(1)}, f32[2,96,384]{2,1,0:T(8,128)S(1)}, u32[]{:S(2)}, u32[]{:S(2)}) collective-permute-start(f32[2,96,384]{2,1,0:T(8,128)S(1)} %reverse_add_fusion.4), channel_id=1, source_target_pairs={{0,8},{1,17},{2,10},{3,19},{4,12},{5,21},{6,14},{7,23},{8,0},{9,25... | collective-permute-start | bytes 884744 | tf_op jit(solution)/shard_map/attention_gather_z_first/ppermute | solution.py:592
  210.9 11.4 %collective-permute-start.34 = (f32[4,96,384]{2,1,0:T(8,128)S(1)}, f32[4,96,384]{2,1,0:T(8,128)S(1)}, u32[]{:S(2)}, u32[]{:S(2)}) collective-permute-start(f32[4,96,384]{2,1,0:T(8,128)S(1)} %constant_dynamic-update-slice_fusion.6), channel_id=1, source_target_pairs={{0,4},{1,3},{2,6},{3,1},{4,0},{5,7},{6,2},{7,5},{8,12},{9,11},{10,... | collective-permute-start | bytes 1769480 | tf_op jit(solution)/shard_map/attention_rest_gather_second/ppermute | solution.py:592
  218.8 13.4 %collective-permute-start.33 = (f32[4,96,384]{2,1,0:T(8,128)S(1)}, f32[4,96,384]{2,1,0:T(8,128)S(1)}, u32[]{:S(2)}, u32[]{:S(2)}) collective-permute-start(f32[4,96,384]{2,1,0:T(8,128)S(1)} %constant_dynamic-update-slice_fusion.8), channel_id=1, source_target_pairs={{0,4},{1,3},{2,6},{3,1},{4,0},{5,7},{6,2},{7,5},{8,12},{9,11},{10,... | collective-permute-start | bytes 1769480 | tf_op jit(solution)/shard_map/attention_gather_second/ppermute | solution.py:592
  218.9 37.4 %collective-permute-start.38 = (f32[2,4,192,256]{3,2,1,0:T(8,128)S(1)}, f32[2,4,192,256]{3,2,1,0:T(8,128)}, u32[]{:S(2)}, u32[]{:S(2)}) collective-permute-start(f32[2,4,192,256]{3,2,1,0:T(8,128)S(1)} %pad_maximum_fusion.2.piece_ref), channel_id=1, source_target_pairs={{0,8},{1,17},{2,10},{3,19},{4,12},{5,21},{6,14},{7,23},{8,0},{9,25... | collective-permute-start | bytes 4718600 | tf_op jit(solution)/shard_map/down_stack_gather_z_first/ppermute | solution.py:592
  222.4 18.5 %collective-permute-start.37 = (f32[2,4,96,384]{3,2,1,0:T(8,128)S(1)}, f32[2,4,96,384]{3,2,1,0:T(8,128)}, u32[]{:S(2)}, u32[]{:S(2)}) collective-permute-start(f32[2,4,96,384]{3,2,1,0:T(8,128)S(1)} %pad_maximum_fusion.4.piece_ref), channel_id=1, source_target_pairs={{0,2},{1,5},{2,0},{3,7},{4,6},{5,1},{6,4},{7,3},{8,10},{9,13},{10,... | collective-permute-start | bytes 3538952 | tf_op jit(solution)/shard_map/attention_rest_gather_first/ppermute | solution.py:592
  233.4 19.5 %collective-permute-start.36 = (f32[2,4,96,384]{3,2,1,0:T(8,128)}, f32[2,4,96,384]{3,2,1,0:T(8,128)}, u32[]{:S(2)}, u32[]{:S(2)}) collective-permute-start(f32[2,4,96,384]{3,2,1,0:T(8,128)} %pad_maximum_fusion.5.piece_ref), channel_id=1, source_target_pairs={{0,2},{1,5},{2,0},{3,7},{4,6},{5,1},{6,4},{7,3},{8,10},{9,13},{10,... | collective-permute-start | bytes 3538952 | tf_op jit(solution)/shard_map/attention_gather_first/ppermute | solution.py:592
  236.6 1.2 collective-permute-start.27

commit v8 on v7

--- a/solution.py
+++ b/solution.py
@@ -30,7 +30,7 @@
 FIRST, SECOND = (X, Y), (Y, X)
 Z_FIRST, Z_SECOND = (Z1, Z2), (Z2, Z1)
 
-ORDER = "cudKucbdIudabucdbuacdcaucbdaudabubcadbabac"
+ORDER = "cudKubcdIuabducdbuacdcaucbdaudabubcadbabac"
 
 CASES = ((0, 0, 256, 0), (128, 256, 384, 128), (256, 640, 128, 128), (384, 768, 256, 128))
 TILES = (

time: 260 us -> 257 us (0.988)
  waiting for transfers between devices: 130 us -> 99.7 us
  starting transfers between devices: 52.2 us -> 80.2 us
    ppermute x35, waiting for transfers between devices: 125 us -> 95 us  [flip(): return lax.ppermute(values, ('dp', 'mp'), pairs)]
    ppermute x35, starting transfers between devices: 50.8 us -> 78.8 us  [flip(): return lax.ppermute(values, ('dp', 'mp'), pairs)]
  transfers between devices with their start and end apart: 39 -> 39, of which waited for: 22 -> 23; matrix products, arithmetic and copies ran while one was open for 4% -> 4% of each run, Pallas kernels for 14% -> 14%
where the time goes in v8:
time: 257 us
  waiting for transfers between devices  99.7 us (39%)
  starting transfers between devices  80.2 us (31%)
  Pallas kernels  64.4 us (25%)
  other arithmetic  7.23 us (3%)
  local copies, waits for them, and re-layouts  3.99 us (2%)
    ppermute x35, waiting for transfers between devices, flip(): return lax.ppermute(values, ('dp', 'mp'), pairs)  95 us
    ppermute x35, starting transfers between devices, flip(): return lax.ppermute(values, ('dp', 'mp'), pairs)  78.8 us
    pallas_call x4, Pallas kernels, call(): pl.pallas_call(kernel, name=kernel.__name__, out_shape=shapes, in_specs=[...  45.5 us
    pallas_call x10, Pallas kernels, put(): pl.pallas_call(partial(put_in_place, views, key == 'c', sent, len(olds)),...  18.9 us
  transfers between devices with their start and end apart: 39, of which 23 were waited for; matrix products, arithmetic and copies ran while one was open for 4% of the time, Pallas kernels for 14%

profile of v8, /device:TPU:0, one launch (start us, length us, event | category | flops | bytes accessed | tf_op | source)
XLA Modules:
  0.0 256.8 jit_solution(2816698327431883194)
XLA Ops:
  0.6 8.1 %attention_forward.1 = (bf16[512,768]{1,0:T(8,128)(2,1)}, bf16[512,384]{1,0:T(8,128)(2,1)}, bf16[512,384]{1,0:T(8,128)(2,1)}, bf16[512,384]{1,0:T(8,128)(2,1)}, ...) custom-call(s32[8,16]{1,0:T(8,128)} %bitcast.57, s32[16]{0:T(128)} %pads_in.1, ...), custom_call_target="tpu_custom_call" | custom-call | flops 1207959552 | bytes 8916544 | tf_op jit(solution)/shard_map/attention_forward/pallas_call | solution.py:562
  9.2 3.2 %collective-permute-done.theirs_in = f32[512,768]{1,0:T(8,128)S(1)} collective-permute-done((f32[512,768]{1,0:T(8,128)}, f32[512,768]{1,0:T(8,128)S(1)}, u32[]{:S(2)}, u32[]{:S(2)}) %collective-permute-start) | collective-permute-done | bytes 1572896 | tf_op jit(solution)/shard_map/ppermute | solution.py:587
  12.5 1.1 copy-done.10
  13.6 17.0 %mlp_kernel.1 = (f32[512,768]{1,0:T(8,128)}, f32[1,1536]{1,0:T(1,128)}, f32[2,4,96,512]{3,2,1,0:T(8,128)}, f32[2,4,96,512]{3,2,1,0:T(8,128)}, f32[2,4,192,256]{3...) custom-call(f32[768]{0:T(1024)} %refs_4_.1, ...), custom_call_target="tpu_custom_call" | custom-call | flops 7247757312 | bytes 23608320 | tf_op jit(solution)/shard_map/mlp_kernel/pallas_call | solution.py:562
  31.1 2.6 %collective-permute-start.5 = (f32[2,4,192,256]{3,2,1,0:T(8,128)}, f32[2,4,192,256]{3,2,1,0:T(8,128)}, u32[]{:S(2)}, u32[]{:S(2)}) collective-permute-start(f32[2,4,192,256]{3,2,1,0:T(8,128)} %get-tuple-element.151), channel_id=1, source_target_pairs={{0,2},{1,5},{2,0},{3,7},{4,6},{5,1},{6,4},{7,3},{8,10},{9,13},{10,... | collective-permute-start | bytes 4718600 | tf_op jit(solution)/shard_map/up_sum_first/ppermute | solution.py:592
  33.7 1.6 collective-permute-start.4
  35.9 0.9 collective-permute-done.1.refs_1_
  36.7 16.9 %attention_backward.1 = (bf16[512,768]{1,0:T(8,128)(2,1)}, f32[512,768]{1,0:T(8,128)}, f32[512,768]{1,0:T(8,128)}, f32[16,384]{1,0:T(8,128)}, f32[2,4,96,384]{3,...) custom-call(f32[2,512,768]{2,1,0:T(8,128)} %get-tuple-element.134.refs_0_, ...), custom_call_target="tpu_custom_call" | custom-call | flops 3019898880 | bytes 24678400 | tf_op jit(solution)/shard_map/attention_backward/pallas_call | solution.py:562
  54.1 2.6 %collective-permute-start.10 = (f32[2,4,96,384]{3,2,1,0:T(8,128)}, f32[2,4,96,384]{3,2,1,0:T(8,128)S(1)}, u32[]{:S(2)}, u32[]{:S(2)}) collective-permute-start(f32[2,4,96,384]{3,2,1,0:T(8,128)} %get-tuple-element.166), channel_id=1, source_target_pairs={{0,2},{1,5},{2,0},{3,7},{4,6},{5,1},{6,4},{7,3},{8,10},{9,13},{10,... | collective-permute-start | bytes 3538952 | tf_op jit(solution)/shard_map/attention_rest_sum_first/ppermute | solution.py:592
  56.8 2.1 add_bitcast_fusion.2
  58.9 1.6 collective-permute-start.7
  60.5 10.8 %collective-permute-done.4 = f32[2,4,192,256]{3,2,1,0:T(8,128)} collective-permute-done((f32[2,4,192,256]{3,2,1,0:T(8,128)}, f32[2,4,192,256]{3,2,1,0:T(8,128)}, u32[]{:S(2)}, u32[]{:S(2)}) %collective-permute-start.4) | collective-permute-done | bytes 1572896 | tf_op jit(solution)/shard_map/down_stack_sum_z_first/ppermute | solution.py:592
  71.3 1.7 add_bitcast_fusion
  73.0 3.9 %collective-permute-done.3 = f32[2,4,96,512]{3,2,1,0:T(8,128)S(1)} collective-permute-done((f32[2,4,96,512]{3,2,1,0:T(8,128)}, f32[2,4,96,512]{3,2,1,0:T(8,128)S(1)}, u32[]{:S(2)}, u32[]{:S(2)}) %collective-permute-start.3) | collective-permute-done | bytes 1572896 | tf_op jit(solution)/shard_map/down_sum_first/ppermute | solution.py:592
  77.3 2.9 %collective-permute-start.9 = (f32[4,96,512]{2,1,0:T(8,128)S(1)}, f32[4,96,512]{2,1,0:T(8,128)S(1)}, u32[]{:S(2)}, u32[]{:S(2)}) collective-permute-start(f32[4,96,512]{2,1,0:T(8,128)S(1)} %get-tuple-element.257), channel_id=1, source_target_pairs={{0,4},{1,3},{2,6},{3,1},{4,0},{5,7},{6,2},{7,5},{8,12},{9,11},{10,... | collective-permute-start | bytes 2359304 | tf_op jit(solution)/shard_map/down_sum_second/ppermute | solution.py:592
  80.1 2.6 collective-permute-start.14
  82.8 1.6 collective-permute-start.6
  84.4 3.5 %input_kernel.1 = bf16[512,768]{1,0:T(8,128)(2,1)} custom-call(f32[512,768]{1,0:T(8,128)S(1)} %copy-done.2, f32[512,768]{1,0:T(8,128)S(1)} %collective-permute-done.2.theirs_ref, bf16[512,768]{1,0:T(8,128)(2,1)S(1)} %copy-done, f32[1,768]{1,0:T(1,128)S(1)} %reshape.69.gain_ref, f32[512,768]{1,0:T(8,128)S(1)} %copy-done.1), custom_call_target="tpu_custom_call" | custom-call | bytes 6294528 | tf_op jit(solution)/shard_map/input_kernel/pallas_call | solution.py:562
  88.0 1.6 collective-permute-start.8
  89.6 9.1 %collective-permute-done.10 = f32[2,4,96,384]{3,2,1,0:T(8,128)S(1)} collective-permute-done((f32[2,4,96,384]{3,2,1,0:T(8,128)}, f32[2,4,96,384]{3,2,1,0:T(8,128)S(1)}, u32[]{:S(2)}, u32[]{:S(2)}) %collective-permute-start.10) | collective-permute-done | bytes 1179680 | tf_op jit(solution)/shard_map/attention_rest_sum_first/ppermute | solution.py:592
  98.9 2.1 collective-permute-start.12
  101.1 1.6 collective-permute-start.13
  102.8 4.8 %collective-permute-done.8 = f32[2,192,256]{2,1,0:T(8,128)S(1)} collective-permute-done((f32[2,192,256]{2,1,0:T(8,128)S(1)}, f32[2,192,256]{2,1,0:T(8,128)S(1)}, u32[]{:S(2)}, u32[]{:S(2)}) %collective-permute-start.8) | collective-permute-done | bytes 393248 | tf_op jit(solution)/shard_map/up_sum_z_first/ppermute | solution.py:592
  107.7 4.0 %collective-permute-start.11 = (f32[2,192,256]{2,1,0:T(8,128)S(1)}, f32[2,192,256]{2,1,0:T(8,128)S(1)}, u32[]{:S(2)}, u32[]{:S(2)}) collective-permute-start(f32[2,192,256]{2,1,0:T(8,128)S(1)} %add.145), channel_id=1, source_target_pairs={{0,16},{1,9},{2,18},{3,11},{4,20},{5,13},{6,22},{7,15},{8,24},{9,1... | collective-permute-start | bytes 1179656 | tf_op jit(solution)/shard_map/up_sum_z_second/ppermute | solution.py:592
  111.7 4.4 %collective-permute-done.14 = f32[4,192,256]{2,1,0:T(8,128)S(1)} collective-permute-done((f32[4,192,256]{2,1,0:T(8,128)S(1)}, f32[4,192,256]{2,1,0:T(8,128)S(1)}, u32[]{:S(2)}, u32[]{:S(2)}) %collective-permute-start.14) | collective-permute-done | bytes 786464 | tf_op jit(solution)/shard_map/down_stack_sum_z_second/ppermute | solution.py:592
  116.2 2.1 collective-permute-start.16
  118.3 1.2 collective-permute-start.18
  119.6 6.7 %collective-permute-start.21 = (f32[2,96,384]{2,1,0:T(8,128)S(1)}, f32[2,96,384]{2,1,0:T(8,128)S(1)}, u32[]{:S(2)}, u32[]{:S(2)}) collective-permute-start(f32[2,96,384]{2,1,0:T(8,128)S(1)} %get-tuple-element.271), channel_id=1, source_target_pairs={{0,8},{1,17},{2,10},{3,19},{4,12},{5,21},{6,14},{7,23},{8,0},{9,25... | collective-permute-start | bytes 884744 | tf_op jit(solution)/shard_map/attention_rest_sum_z_first/ppermute | solution.py:592
  126.9 5.0 %collective-permute-start.23 = (f32[2,192,256]{2,1,0:T(8,128)S(1)}, f32[2,192,256]{2,1,0:T(8,128)S(1)}, u32[]{:S(2)}, u32[]{:S(2)}) collective-permute-start(f32[2,192,256]{2,1,0:T(8,128)S(1)} %reverse_add_fusion.2), channel_id=1, source_target_pairs={{0,8},{1,17},{2,10},{3,19},{4,12},{5,21},{6,14},{7,23},{8,0},{9,25... | collective-permute-start | bytes 1179656 | tf_op jit(solution)/shard_map/up_gather_z_first/ppermute | solution.py:592
  133.0 1.3 collective-permute-start.17
  134.4 3.0 %collective-permute-done.18 = f32[2,96,512]{2,1,0:T(8,128)S(1)} collective-permute-done((f32[2,96,512]{2,1,0:T(8,128)S(1)}, f32[2,96,512]{2,1,0:T(8,128)S(1)}, u32[]{:S(2)}, u32[]{:S(2)}) %collective-permute-start.18) | collective-permute-done | bytes 393248 | tf_op jit(solution)/shard_map/down_sum_z_second/ppermute | solution.py:592
  137.4 2.7 %collective-permute-start.20 = (f32[2,96,512]{2,1,0:T(8,128)S(1)}, f32[2,96,512]{2,1,0:T(8,128)S(1)}, u32[]{:S(2)}, u32[]{:S(2)}) collective-permute-start(f32[2,96,512]{2,1,0:T(8,128)S(1)} %reverse_add_fusion.1), channel_id=1, source_target_pairs={{0,8},{1,17},{2,10},{3,19},{4,12},{5,21},{6,14},{7,23},{8,0},{9,25... | collective-permute-start | bytes 1179656 | tf_op jit(solution)/shard_map/down_gather_z_first/ppermute | solution.py:592
  140.2 6.4 %collective-permute-done.17 = f32[2,192,256]{2,1,0:T(8,128)S(1)} collective-permute-done((f32[2,192,256]{2,1,0:T(8,128)S(1)}, f32[2,192,256]{2,1,0:T(8,128)S(1)}, u32[]{:S(2)}, u32[]{:S(2)}) %collective-permute-start.17) | collective-permute-done | bytes 393248 | tf_op jit(solution)/shard_map/down_stack_sum_second/ppermute | solution.py:592
  146.6 1.5 collective-permute-start.22
  148.3 1.5 collective-permute-start.19
  150.7 3.7 %collective-permute-start.25 = (f32[4,192,256]{2,1,0:T(8,128)S(1)}, f32[4,192,256]{2,1,0:T(8,128)S(1)}, u32[]{:S(2)}, u32[]{:S(2)}) collective-permute-start(f32[4,192,256]{2,1,0:T(8,128)S(1)} %constant_dynamic-update-slice_fusion), channel_id=1, source_target_pairs={{0,4},{1,3},{2,6},{3,1},{4,0},{5,7},{6,2},{7,5},{8,12},{9,11},{10,... | collective-permute-start | bytes 2359304 | tf_op jit(solution)/shard_map/up_gather_second/ppermute | solution.py:592
  154.6 1.6 collective-permute-done.20
  156.3 10.2 %collective-permute-start.26 = (f32[4,96,512]{2,1,0:T(8,128)S(1)}, f32[4,96,512]{2,1,0:T(8,128)S(1)}, u32[]{:S(2)}, u32[]{:S(2)}) collective-permute-start(f32[4,96,512]{2,1,0:T(8,128)S(1)} %constant_dynamic-update-slice_fusion.4), channel_id=1, source_target_pairs={{0,4},{1,3},{2,6},{3,1},{4,0},{5,7},{6,2},{7,5},{8,12},{9,11},{10,... | collective-permute-start | bytes 2359304 | tf_op jit(solution)/shard_map/down_gather_second/ppermute | solution.py:592
  166.5 1.7 collective-permute-done.25
  168.3 1.5 collective-permute-start.32
  170.5 2.3 collective-permute-start.30
  173.5 7.8 %collective-permute-done.26 = f32[4,96,512]{2,1,0:T(8,128)S(1)} collective-permute-done((f32[4,96,512]{2,1,0:T(8,128)S(1)}, f32[4,96,512]{2,1,0:T(8,128)S(1)}, u32[]{:S(2)}, u32[]{:S(2)}) %collective-permute-start.26) | collective-permute-done | bytes 786464 | tf_op jit(solution)/shard_map/down_gather_second/ppermute | solution.py:592
  181.3 1.2 collective-permute-start.35
  182.6 1.4 put_u.2.refs_0_
  184.1 1.4 put_d.2.refs_0_
  185.7 4.5 %collective-permute-start.31 = (f32[2,96,384]{2,1,0:T(8,128)S(1)}, f32[2,96,384]{2,1,0:T(8,128)S(1)}, u32[]{:S(2)}, u32[]{:S(2)}) collective-permute-start(f32[2,96,384]{2,1,0:T(8,128)S(1)} %reverse_add_fusion.3), channel_id=1, source_target_pairs={{0,8},{1,17},{2,10},{3,19},{4,12},{5,21},{6,14},{7,23},{8,0},{9,25... | collective-permute-start | bytes 884744 | tf_op jit(solution)/shard_map/attention_rest_gather_z_first/ppermute | solution.py:592
  190.2 4.0 %collective-permute-done.32.piece_ref = f32[2,4,192,256]{3,2,1,0:T(8,128)S(1)} collective-permute-done((f32[2,4,192,256]{3,2,1,0:T(8,128)S(1)}, f32[2,4,192,256]{3,2,1,0:T(8,128)S(1)}, u32[]{:S(2)}, u32[]{:S(2)}) %collective-permute-start.32) | collective-permute-done | bytes 1572896 | tf_op jit(solution)/shard_map/up_gather_first/ppermute | solution.py:592
  194.3 1.4 put_u.3.refs_1_
  195.7 12.3 %collective-permute-done.31 = f32[2,96,384]{2,1,0:T(8,128)S(1)} collective-permute-done((f32[2,96,384]{2,1,0:T(8,128)S(1)}, f32[2,96,384]{2,1,0:T(8,128)S(1)}, u32[]{:S(2)}, u32[]{:S(2)}) %collective-permute-start.31) | collective-permute-done | bytes 294944 | tf_op jit(solution)/shard_map/attention_rest_gather_z_first/ppermute | solution.py:592
  208.0 1.5 collective-permute-start.34
  209.5 6.7 %collective-permute-done.29 = f32[4,192,256]{2,1,0:T(8,128)S(1)} collective-permute-done((f32[4,192,256]{2,1,0:T(8,128)S(1)}, f32[4,192,256]{2,1,0:T(8,128)S(1)}, u32[]{:S(2)}, u32[]{:S(2)}) %collective-permute-start.29) | collective-permute-done | bytes 786464 | tf_op jit(solution)/shard_map/down_stack_gather_z_second/ppermute | solution.py:592
  216.5 1.4 collective-permute-start.38
  218.0 1.4 put_c.2
  219.4 1.4 put_d.3.refs_0_
  220.9 2.0 collective-permute-start.37
  223.0 6.9 %collective-permute-done.33 = f32[4,96,384]{2,1,0:T(8,128)S(1)} collective-permute-done((f32[4,96,384]{2,1,0:T(8,128)S(1)}, f32[4,96,384]{2,1,0:T(8,128)S(1)}, u32[]{:S(2)}, u32[]{:S(2)}) %collective-permute-start.33) | collective-permute-done | bytes 589856 | tf_op jit(solution)/shard_map/attention_gather_second/ppermute | solution.py:592
  229.9 1.1 pad_maximum_fusion.5.piece_ref
  234.8 1.3 put_b.2
  236.1 2.6 %collective-permute-done.37.piece_ref = f32[2,4,96,384]{3,2,1,0:T(8,128)} collective-permute-done((f32[2,4,96,384]{3,2,1,0:T(8,128)S(1)}, f32[2,4,96,384]{3,2,1,0:T(8,128)}, u32[]{:S(2)}, u32[]{:S(2)}) %collective-permute-start.37) | collective-permute-done | bytes 1179680 | tf_op jit(solution)/shard_map/attention_rest_gather_first/ppermute | solution.py:592
  238.6 2.6 put_a.2
  241.2 2.6 put_b.3
  243.8 7.5 %collective-permute-done.36.piece_ref = f32[2,4,96,384]{3,2,1,0:T(8,128)} collective-permute-done((f32[2,4,96,384]{3,2,1,0:T(8,128)}, f32[2,4,96,384]{3,2,1,0:T(8,128)}, u32[]{:S(2)}, u32[]{:S(2)}) %collective-permute-start.36) | collective-permute-done | bytes 1179680 | tf_op jit(solution)/shard_map/attention_gather_first/ppermute | solution.py:592
  251.3 2.6 put_a.3
  253.9 2.8 %put_c.3 = (f32[1536,768]{1,0:T(8,128)}, f32[768,1536]{1,0:T(8,128)}) custom-call(f32[2,4,192,256]{3,2,1,0:T(8,128)} %collective-permute-done.38.piece_ref, f32[1536,768]{1,0:T(8,128)} %put_d.3.refs_0_, f32[768,1536]{1,0:T(8,128)} %get-tuple-element.251.refs_1_), custom_call_target="tpu_custom_call", output_to_operand_aliasing={{0}: (1, {}), {1}: (2, {})} | custom-call | bytes 3145728 | tf_op jit(solution)/shard_map/put_c/pallas_call | solution.py:796
  (107 shorter events, 12.2 us)
Async XLA Ops:
  8.7 3.8 %collective-permute-start = (f32[512,768]{1,0:T(8,128)}, f32[512,768]{1,0:T(8,128)S(1)}, u32[]{:S(2)}, u32[]{:S(2)}) collective-permute-start(f32[512,768]{1,0:T(8,128)} %get-tuple-element.133.mine_in), channel_id=1, source_target_pairs={{0,1},{1,0},{2,3},{3,2},{4,5},{5,4},{6,7},{7,6},{8,9},{9,8},{10,11... | collective-permute-start | bytes 4718600 | tf_op jit(solution)/shard_map/ppermute | solution.py:587
  12.5 1.1 copy-start.10
  30.7 6.1 %collective-permute-start.1 = (f32[2,512,768]{2,1,0:T(8,128)}, f32[2,512,768]{2,1,0:T(8,128)}, u32[]{:S(2)}, u32[]{:S(2)}) collective-permute-start(f32[2,512,768]{2,1,0:T(8,128)} %get-tuple-element.134.refs_0_), channel_id=1, source_target_pairs={{0,1},{1,0},{2,3},{3,2},{4,5},{5,4},{6,7},{7,6},{8,9},{9,8},{10,11... | collective-permute-start | bytes 9437192 | tf_op jit(solution)/shard_map/ppermute | solution.py:587
  31.1 23.0 %collective-permute-start.5 = (f32[2,4,192,256]{3,2,1,0:T(8,128)}, f32[2,4,192,256]{3,2,1,0:T(8,128)}, u32[]{:S(2)}, u32[]{:S(2)}) collective-permute-start(f32[2,4,192,256]{3,2,1,0:T(8,128)} %get-tuple-element.151), channel_id=1, source_target_pairs={{0,2},{1,5},{2,0},{3,7},{4,6},{5,1},{6,4},{7,3},{8,10},{9,13},{10,... | collective-permute-start | bytes 4718600 | tf_op jit(solution)/shard_map/up_sum_first/ppermute | solution.py:592
  33.7 37.5 %collective-permute-start.4 = (f32[2,4,192,256]{3,2,1,0:T(8,128)}, f32[2,4,192,256]{3,2,1,0:T(8,128)}, u32[]{:S(2)}, u32[]{:S(2)}) collective-permute-start(f32[2,4,192,256]{3,2,1,0:T(8,128)} %get-tuple-element.149), channel_id=1, source_target_pairs={{0,8},{1,17},{2,10},{3,19},{4,12},{5,21},{6,14},{7,23},{8,0},{9,25... | collective-permute-start | bytes 4718600 | tf_op jit(solution)/shard_map/down_stack_sum_z_first/ppermute | solution.py:592
  35.3 41.5 %collective-permute-start.3 = (f32[2,4,96,512]{3,2,1,0:T(8,128)}, f32[2,4,96,512]{3,2,1,0:T(8,128)S(1)}, u32[]{:S(2)}, u32[]{:S(2)}) collective-permute-start(f32[2,4,96,512]{3,2,1,0:T(8,128)} %get-tuple-element.147), channel_id=1, source_target_pairs={{0,2},{1,5},{2,0},{3,7},{4,6},{5,1},{6,4},{7,3},{8,10},{9,13},{10,... | collective-permute-start | bytes 4718600 | tf_op jit(solution)/shard_map/down_sum_first/ppermute | solution.py:592
  53.7 29.1 %collective-permute-start.2 = (f32[512,768]{1,0:T(8,128)}, f32[512,768]{1,0:T(8,128)S(1)}, u32[]{:S(2)}, u32[]{:S(2)}) collective-permute-start(f32[512,768]{1,0:T(8,128)} %get-tuple-element.145.mine_ref), channel_id=1, source_target_pairs={{0,1},{1,0},{2,3},{3,2},{4,5},{5,4},{6,7},{7,6},{8,9},{9,8},{10,11... | collective-permute-start | bytes 4718600 | tf_op jit(solution)/shard_map/ppermute | solution.py:587
  54.1 17.1 %copy-start.4 = (f32[2,4,192,256]{3,2,1,0:T(8,128)S(1)}, f32[2,4,192,256]{3,2,1,0:T(8,128)}, u32[]{:S(2)}) copy-start(f32[2,4,192,256]{3,2,1,0:T(8,128)} %get-tuple-element.155) | copy-start | bytes 4718596
  54.1 44.5 %collective-permute-start.10 = (f32[2,4,96,384]{3,2,1,0:T(8,128)}, f32[2,4,96,384]{3,2,1,0:T(8,128)S(1)}, u32[]{:S(2)}, u32[]{:S(2)}) collective-permute-start(f32[2,4,96,384]{3,2,1,0:T(8,128)} %get-tuple-element.166), channel_id=1, source_target_pairs={{0,2},{1,5},{2,0},{3,7},{4,6},{5,1},{6,4},{7,3},{8,10},{9,13},{10,... | collective-permute-start | bytes 3538952 | tf_op jit(solution)/shard_map/attention_rest_sum_first/ppermute | solution.py:592
  58.9 29.0 %collective-permute-start.7 = (f32[4,192,256]{2,1,0:T(8,128)S(1)}, f32[4,192,256]{2,1,0:T(8,128)S(1)}, u32[]{:S(2)}, u32[]{:S(2)}) collective-permute-start(f32[4,192,256]{2,1,0:T(8,128)S(1)} %get-tuple-element.259), channel_id=1, source_target_pairs={{0,4},{1,3},{2,6},{3,1},{4,0},{5,7},{6,2},{7,5},{8,12},{9,11},{10,... | collective-permute-start | bytes 2359304 | tf_op jit(solution)/shard_map/up_sum_second/ppermute | solution.py:592
  71.3 5.6 %copy-start.3 = (f32[2,4,96,512]{3,2,1,0:T(8,128)S(1)}, f32[2,4,96,512]{3,2,1,0:T(8,128)}, u32[]{:S(2)}) copy-start(f32[2,4,96,512]{3,2,1,0:T(8,128)} %get-tuple-element.157) | copy-start | bytes 4718596
  76.9 3.3 %copy-start.9 = (f32[768]{0:T(1024)S(1)}, f32[768]{0:T(1024)}, u32[]{:S(2)}) copy-start(f32[768]{0:T(1024)} %gain_in.2) | copy-start | bytes 9220
  76.9 5.8 %copy-start.7 = (f32[2,4,96,384]{3,2,1,0:T(8,128)S(1)}, f32[2,4,96,384]{3,2,1,0:T(8,128)}, u32[]{:S(2)}) copy-start(f32[2,4,96,384]{3,2,1,0:T(8,128)} %get-tuple-element.162) | copy-start | bytes 3538948
  76.9 5.8 %copy-start.8 = (f32[16,384]{1,0:T(8,128)S(1)}, f32[16,384]{1,0:T(8,128)}, u32[]{:S(2)}) copy-start(f32[16,384]{1,0:T(8,128)} %get-tuple-element.183) | copy-start | bytes 73732
  76.9 7.5 %copy-start.2 = (f32[512,768]{1,0:T(8,128)S(1)}, f32[512,768]{1,0:T(8,128)}, u32[]{:S(2)}) copy-start(f32[512,768]{1,0:T(8,128)} %get-tuple-element.145.mine_ref) | copy-start | bytes 4718596
  77.2 7.1 %copy-start = (bf16[512,768]{1,0:T(8,128)(2,1)S(1)}, bf16[512,768]{1,0:T(8,128)(2,1)}, u32[]{:S(2)}) copy-start(bf16[512,768]{1,0:T(8,128)(2,1)} %x_ref.1) | copy-start | bytes 2359300
  77.3 7.1 %copy-start.1 = (f32[512,768]{1,0:T(8,128)S(1)}, f32[512,768]{1,0:T(8,128)}, u32[]{:S(2)}) copy-start(f32[512,768]{1,0:T(8,128)} %get-tuple-element.160.delta_ref) | copy-start | bytes 4718596
  77.3 23.7 %collective-permute-start.9 = (f32[4,96,512]{2,1,0:T(8,128)S(1)}, f32[4,96,512]{2,1,0:T(8,128)S(1)}, u32[]{:S(2)}, u32[]{:S(2)}) collective-permute-start(f32[4,96,512]{2,1,0:T(8,128)S(1)} %get-tuple-element.257), channel_id=1, source_target_pairs={{0,4},{1,3},{2,6},{3,1},{4,0},{5,7},{6,2},{7,5},{8,12},{9,11},{10,... | collective-permute-start | bytes 2359304 | tf_op jit(solution)/shard_map/down_sum_second/ppermute | solution.py:592
  80.1 35.9 %collective-permute-start.14 = (f32[4,192,256]{2,1,0:T(8,128)S(1)}, f32[4,192,256]{2,1,0:T(8,128)S(1)}, u32[]{:S(2)}, u32[]{:S(2)}) collective-permute-start(f32[4,192,256]{2,1,0:T(8,128)S(1)} %get-tuple-element.255), channel_id=1, source_target_pairs={{0,16},{1,9},{2,18},{3,11},{4,20},{5,13},{6,22},{7,15},{8,24},{9,1... | collective-permute-start | bytes 2359304 | tf_op jit(solution)/shard_map/down_stack_sum_z_second/ppermute | solution.py:592
  82.8 49.1 %collective-permute-start.6 = (f32[784,384]{1,0:T(8,128)S(1)}, f32[784,384]{1,0:T(8,128)S(1)}, u32[]{:S(2)}, u32[]{:S(2)}) collective-permute-start(f32[784,384]{1,0:T(8,128)S(1)} %pad_maximum_fusion.3), channel_id=1, source_target_pairs={{0,2},{1,5},{2,0},{3,7},{4,6},{5,1},{6,4},{7,3},{8,10},{9,13},{10,... | collective-permute-start | bytes 3612680 | tf_op jit(solution)/shard_map/attention_sum_first/ppermute | solution.py:592
  87.8 10.9 %copy-start.5 = (f32[2,4,96,384]{3,2,1,0:T(8,128)S(1)}, f32[2,4,96,384]{3,2,1,0:T(8,128)}, u32[]{:S(2)}) copy-start(f32[2,4,96,384]{3,2,1,0:T(8,128)} %get-tuple-element.167) | copy-start | bytes 3538948
  88.0 19.7 %collective-permute-start.8 = (f32[2,192,256]{2,1,0:T(8,128)S(1)}, f32[2,192,256]{2,1,0:T(8,128)S(1)}, u32[]{:S(2)}, u32[]{:S(2)}) collective-permute-start(f32[2,192,256]{2,1,0:T(8,128)S(1)} %get-tuple-element.266), channel_id=1, source_target_pairs={{0,8},{1,17},{2,10},{3,19},{4,12},{5,21},{6,14},{7,23},{8,0},{9,25... | collective-permute-start | bytes 1179656 | tf_op jit(solution)/shard_map/up_sum_z_first/ppermute | solution.py:592
  98.9 20.6 %collective-permute-start.12 = (f32[4,96,384]{2,1,0:T(8,128)S(1)}, f32[4,96,384]{2,1,0:T(8,128)S(1)}, u32[]{:S(2)}, u32[]{:S(2)}) collective-permute-start(f32[4,96,384]{2,1,0:T(8,128)S(1)} %get-tuple-element.261), channel_id=1, source_target_pairs={{0,4},{1,3},{2,6},{3,1},{4,0},{5,7},{6,2},{7,5},{8,12},{9,11},{10,... | collective-permute-start | bytes 1769480 | tf_op jit(solution)/shard_map/attention_rest_sum_second/ppermute | solution.py:592
  101.1 17.1 %collective-permute-start.13 = (f32[2,96,512]{2,1,0:T(8,128)S(1)}, f32[2,96,512]{2,1,0:T(8,128)S(1)}, u32[]{:S(2)}, u32[]{:S(2)}) collective-permute-start(f32[2,96,512]{2,1,0:T(8,128)S(1)} %get-tuple-element.265), channel_id=1, source_target_pairs={{0,8},{1,17},{2,10},{3,19},{4,12},{5,21},{6,14},{7,23},{8,0},{9,25... | collective-permute-start | bytes 1179656 | tf_op jit(solution)/shard_map/down_sum_z_first/ppermute | solution.py:592
  107.7 19.1 %collective-permute-start.11 = (f32[2,192,256]{2,1,0:T(8,128)S(1)}, f32[2,192,256]{2,1,0:T(8,128)S(1)}, u32[]{:S(2)}, u32[]{:S(2)}) collective-permute-start(f32[2,192,256]{2,1,0:T(8,128)S(1)} %add.145), channel_id=1, source_target_pairs={{0,16},{1,9},{2,18},{3,11},{4,20},{5,13},{6,22},{7,15},{8,24},{9,1... | collective-permute-start | bytes 1179656 | tf_op jit(solution)/shard_map/up_sum_z_second/ppermute | solution.py:592
  116.2 16.8 %collective-permute-start.16 = (f32[2,192,256]{2,1,0:T(8,128)S(1)}, f32[2,192,256]{2,1,0:T(8,128)S(1)}, u32[]{:S(2)}, u32[]{:S(2)}) collective-permute-start(f32[2,192,256]{2,1,0:T(8,128)S(1)} %get-tuple-element.263), channel_id=1, source_target_pairs={{0,2},{1,5},{2,0},{3,7},{4,6},{5,1},{6,4},{7,3},{8,10},{9,13},{10,... | collective-permute-start | bytes 1179656 | tf_op jit(solution)/shard_map/down_stack_sum_first/ppermute | solution.py:592
  118.3 13.6 %copy-start.6 = (f32[2,4,96,384]{3,2,1,0:T(8,128)S(1)}, f32[2,4,96,384]{3,2,1,0:T(8,128)}, u32[]{:S(2)}) copy-start(f32[2,4,96,384]{3,2,1,0:T(8,128)} %get-tuple-element.181) | copy-start | bytes 3538948
  118.3 19.0 %collective-permute-start.18 = (f32[2,96,512]{2,1,0:T(8,128)S(1)}, f32[2,96,512]{2,1,0:T(8,128)S(1)}, u32[]{:S(2)}, u32[]{:S(2)}) collective-permute-start(f32[2,96,512]{2,1,0:T(8,128)S(1)} %add.152), channel_id=1, source_target_pairs={{0,16},{1,9},{2,18},{3,11},{4,20},{5,13},{6,22},{7,15},{8,24},{9,1... | collective-permute-start | bytes 1179656 | tf_op jit(solution)/shard_map/down_sum_z_second/ppermute | solution.py:592
  119.6 35.0 %collective-permute-start.21 = (f32[2,96,384]{2,1,0:T(8,128)S(1)}, f32[2,96,384]{2,1,0:T(8,128)S(1)}, u32[]{:S(2)}, u32[]{:S(2)}) collective-permute-start(f32[2,96,384]{2,1,0:T(8,128)S(1)} %get-tuple-element.271), channel_id=1, source_target_pairs={{0,8},{1,17},{2,10},{3,19},{4,12},{5,21},{6,14},{7,23},{8,0},{9,25... | collective-permute-start | bytes 884744 | tf_op jit(solution)/shard_map/attention_rest_sum_z_first/ppermute | solution.py:592
  126.9 23.7 %collective-permute-start.23 = (f32[2,192,256]{2,1,0:T(8,128)S(1)}, f32[2,192,256]{2,1,0:T(8,128)S(1)}, u32[]{:S(2)}, u32[]{:S(2)}) collective-permute-start(f32[2,192,256]{2,1,0:T(8,128)S(1)} %reverse_add_fusion.2), channel_id=1, source_target_pairs={{0,8},{1,17},{2,10},{3,19},{4,12},{5,21},{6,14},{7,23},{8,0},{9,25... | collective-permute-start | bytes 1179656 | tf_op jit(solution)/shard_map/up_gather_z_first/ppermute | solution.py:592
  132.1 16.0 %collective-permute-start.15 = (f32[400,384]{1,0:T(8,128)S(1)}, f32[400,384]{1,0:T(8,128)S(1)}, u32[]{:S(2)}, u32[]{:S(2)}) collective-permute-start(f32[400,384]{1,0:T(8,128)S(1)} %pad_maximum_fusion.6), channel_id=1, source_target_pairs={{0,4},{1,3},{2,6},{3,1},{4,0},{5,7},{6,2},{7,5},{8,12},{9,11},{10,... | collective-permute-start | bytes 1843208 | tf_op jit(solution)/shard_map/attention_sum_second/ppermute | solution.py:592
  133.0 13.5 %collective-permute-start.17 = (f32[2,192,256]{2,1,0:T(8,128)S(1)}, f32[2,192,256]{2,1,0:T(8,128)S(1)}, u32[]{:S(2)}, u32[]{:S(2)}) collective-permute-start(f32[2,192,256]{2,1,0:T(8,128)S(1)} %add.159), channel_id=1, source_target_pairs={{0,4},{1,3},{2,6},{3,1},{4,0},{5,7},{6,2},{7,5},{8,12},{9,11},{10,... | collective-permute-start | bytes 1179656 | tf_op jit(solution)/shard_map/down_stack_sum_second/ppermute | solution.py:592
  137.4 18.8 %collective-permute-start.20 = (f32[2,96,512]{2,1,0:T(8,128)S(1)}, f32[2,96,512]{2,1,0:T(8,128)S(1)}, u32[]{:S(2)}, u32[]{:S(2)}) collective-permute-start(f32[2,96,512]{2,1,0:T(8,128)S(1)} %reverse_add_fusion.1), channel_id=1, source_target_pairs={{0,8},{1,17},{2,10},{3,19},{4,12},{5,21},{6,14},{7,23},{8,0},{9,25... | collective-permute-start | bytes 1179656 | tf_op jit(solution)/shard_map/down_gather_z_first/ppermute | solution.py:592
  146.6 7.8 %collective-permute-start.22 = (f32[2,192,256]{2,1,0:T(8,128)S(1)}, f32[2,192,256]{2,1,0:T(8,128)S(1)}, u32[]{:S(2)}, u32[]{:S(2)}) collective-permute-start(f32[2,192,256]{2,1,0:T(8,128)S(1)} %reverse_add_fusion), channel_id=1, source_target_pairs={{0,2},{1,5},{2,0},{3,7},{4,6},{5,1},{6,4},{7,3},{8,10},{9,13},{10,... | collective-permute-start | bytes 1179656 | tf_op jit(solution)/shard_map/down_stack_gather_first/ppermute | solution.py:592
  148.3 18.1 %collective-permute-start.19 = (f32[208,384]{1,0:T(8,128)S(1)}, f32[208,384]{1,0:T(8,128)S(1)}, u32[]{:S(2)}, u32[]{:S(2)}) collective-permute-start(f32[208,384]{1,0:T(8,128)S(1)} %pad_maximum_fusion.7), channel_id=1, source_target_pairs={{0,8},{1,17},{2,10},{3,19},{4,12},{5,21},{6,14},{7,23},{8,0},{9,25... | collective-permute-start | bytes 958472 | tf_op jit(solution)/shard_map/attention_sum_z_first/ppermute | solution.py:592
  150.7 17.6 %collective-permute-start.25 = (f32[4,192,256]{2,1,0:T(8,128)S(1)}, f32[4,192,256]{2,1,0:T(8,128)S(1)}, u32[]{:S(2)}, u32[]{:S(2)}) collective-permute-start(f32[4,192,256]{2,1,0:T(8,128)S(1)} %constant_dynamic-update-slice_fusion), channel_id=1, source_target_pairs={{0,4},{1,3},{2,6},{3,1},{4,0},{5,7},{6,2},{7,5},{8,12},{9,11},{10,... | collective-permute-start | bytes 2359304 | tf_op jit(solution)/shard_map/up_gather_second/ppermute | solution.py:592
  156.3 25.0 %collective-permute-start.26 = (f32[4,96,512]{2,1,0:T(8,128)S(1)}, f32[4,96,512]{2,1,0:T(8,128)S(1)}, u32[]{:S(2)}, u32[]{:S(2)}) collective-permute-start(f32[4,96,512]{2,1,0:T(8,128)S(1)} %constant_dynamic-update-slice_fusion.4), channel_id=1, source_target_pairs={{0,4},{1,3},{2,6},{3,1},{4,0},{5,7},{6,2},{7,5},{8,12},{9,11},{10,... | collective-permute-start | bytes 2359304 | tf_op jit(solution)/shard_map/down_gather_second/ppermute | solution.py:592
  168.3 25.9 %collective-permute-start.32 = (f32[2,4,192,256]{3,2,1,0:T(8,128)S(1)}, f32[2,4,192,256]{3,2,1,0:T(8,128)S(1)}, u32[]{:S(2)}, u32[]{:S(2)}) collective-permute-start(f32[2,4,192,256]{3,2,1,0:T(8,128)S(1)} %pad_maximum_fusion.piece_ref), channel_id=1, source_target_pairs={{0,2},{1,5},{2,0},{3,7},{4,6},{5,1},{6,4},{7,3},{8,10},{9,13},{10,... | collective-permute-start | bytes 4718600 | tf_op jit(solution)/shard_map/up_gather_first/ppermute | solution.py:592
  169.9 14.1 %collective-permute-start.24 = (f32[208,384]{1,0:T(8,128)S(1)}, f32[208,384]{1,0:T(8,128)S(1)}, u32[]{:S(2)}, u32[]{:S(2)}) collective-permute-start(f32[208,384]{1,0:T(8,128)S(1)} %pad_maximum_fusion.8), channel_id=1, source_target_pairs={{0,16},{1,9},{2,18},{3,11},{4,20},{5,13},{6,22},{7,15},{8,24},{9,1... | collective-permute-start | bytes 958472 | tf_op jit(solution)/shard_map/attention_sum_z_second/ppermute | solution.py:592
  170.5 15.1 %collective-permute-start.30 = (f32[2,96,384]{2,1,0:T(8,128)S(1)}, f32[2,96,384]{2,1,0:T(8,128)S(1)}, u32[]{:S(2)}, u32[]{:S(2)}) collective-permute-start(f32[2,96,384]{2,1,0:T(8,128)S(1)} %add.166), channel_id=1, source_target_pairs={{0,16},{1,9},{2,18},{3,11},{4,20},{5,13},{6,22},{7,15},{8,24},{9,1... | collective-permute-start | bytes 884744 | tf_op jit(solution)/shard_map/attention_rest_sum_z_second/ppermute | solution.py:592
  172.8 43.4 %collective-permute-start.29 = (f32[4,192,256]{2,1,0:T(8,128)S(1)}, f32[4,192,256]{2,1,0:T(8,128)S(1)}, u32[]{:S(2)}, u32[]{:S(2)}) collective-permute-start(f32[4,192,256]{2,1,0:T(8,128)S(1)} %constant_dynamic-update-slice_fusion.2), channel_id=1, source_target_pairs={{0,16},{1,9},{2,18},{3,11},{4,20},{5,13},{6,22},{7,15},{8,24},{9,1... | collective-permute-start | bytes 2359304 | tf_op jit(solution)/shard_map/down_stack_gather_z_second/ppermute | solution.py:592
  181.3 38.0 %collective-permute-start.35 = (f32[2,4,96,512]{3,2,1,0:T(8,128)S(1)}, f32[2,4,96,512]{3,2,1,0:T(8,128)S(1)}, u32[]{:S(2)}, u32[]{:S(2)}) collective-permute-start(f32[2,4,96,512]{3,2,1,0:T(8,128)S(1)} %pad_maximum_fusion.1.piece_ref), channel_id=1, source_target_pairs={{0,2},{1,5},{2,0},{3,7},{4,6},{5,1},{6,4},{7,3},{8,10},{9,13},{10,... | collective-permute-start | bytes 4718600 | tf_op jit(solution)/shard_map/down_gather_first/ppermute | solution.py:592
  185.7 22.3 %collective-permute-start.31 = (f32[2,96,384]{2,1,0:T(8,128)S(1)}, f32[2,96,384]{2,1,0:T(8,128)S(1)}, u32[]{:S(2)}, u32[]{:S(2)}) collective-permute-start(f32[2,96,384]{2,1,0:T(8,128)S(1)} %reverse_add_fusion.3), channel_id=1, source_target_pairs={{0,8},{1,17},{2,10},{3,19},{4,12},{5,21},{6,14},{7,23},{8,0},{9,25... | collective-permute-start | bytes 884744 | tf_op jit(solution)/shard_map/attention_rest_gather_z_first/ppermute | solution.py:592
  190.2 26.3 %collective-permute-start.28 = (f32[2,96,384]{2,1,0:T(8,128)S(1)}, f32[2,96,384]{2,1,0:T(8,128)S(1)}, u32[]{:S(2)}, u32[]{:S(2)}) collective-permute-start(f32[2,96,384]{2,1,0:T(8,128)S(1)} %reverse_add_fusion.4), channel_id=1, source_target_pairs={{0,8},{1,17},{2,10},{3,19},{4,12},{5,21},{6,14},{7,23},{8,0},{9,25... | collective-permute-start | bytes 884744 | tf_op jit(solution)/shard_map/attention_gather_z_first/ppermute | solution.py:592
  208.0 12.9 %collective-permute-start.34 = (f32[4,96,384]{2,1,0:T(8,128)S(1)}, f32[4,96,384]{2,1,0:T(8,128)S(1)}, u32[]{:S(2)}, u32[]{:S(2)}) collective-permute-start(f32[4,96,384]{2,1,0:T(8,128)S(1)} %constant_dynamic-update-slice_fusion.6), channel_id=1, source_target_pairs={{0,4},{1,3},{2,6},{3,1},{4,0},{5,7},{6,2},{7,5},{8,12},{9,11},{10,... | collective-permute-start | bytes 1769480 | tf_op jit(solution)/shard_map/attention_rest_gather_second/ppermute | solution.py:592
  216.5 13.4 %collective-permute-start.33 = (f32[4,96,384]{2,1,0:T(8,128)S(1)}, f32[4,96,384]{2,1,0:T(8,128)S(1)}, u32[]{:S(2)}, u32[]{:S(2)}) collective-permute-start(f32[4,96,384]{2,1,0:T(8,128)S(1)} %constant_dynamic-update-slice_fusion.8), channel_id=1, source_target_pairs={{0,4},{1,3},{2,6},{3,1},{4,0},{5,7},{6,2},{7,5},{8,12},{9,11},{10,... | collective-permute-start | bytes 1769480 | tf_op jit(solution)/shard_map/attention_gather_second/ppermute | solution.py:592
  216.5 37.3 %collective-permute-start.38 = (f32[2,4,192,256]{3,2,1,0:T(8,128)S(1)}, f32[2,4,192,256]{3,2,1,0:T(8,128)}, u32[]{:S(2)}, u32[]{:S(2)}) collective-permute-start(f32[2,4,192,256]{3,2,1,0:T(8,128)S(1)} %pad_maximum_fusion.2.piece_ref), channel_id=1, source_target_pairs={{0,8},{1,17},{2,10},{3,19},{4,12},{5,21},{6,14},{7,23},{8,0},{9,25... | collective-permute-start | bytes 4718600 | tf_op jit(solution)/shard_map/down_stack_gather_z_first/ppermute | solution.py:592
  220.9 17.7 %collective-permute-start.37 = (f32[2,4,96,384]{3,2,1,0:T(8,128)S(1)}, f32[2,4,96,384]{3,2,1,0:T(8,128)}, u32[]{:S(2)}, u32[]{:S(2)}) collective-permute-start(f32[2,4,96,384]{3,2,1,0:T(8,128)S(1)} %pad_maximum_fusion.4.piece_ref), channel_id=1, source_target_pairs={{0,2},{1,5},{2,0},{3,7},{4,6},{5,1},{6,4},{7,3},{8,10},{9,13},{10,... | collective-permute-start | bytes 3538952 | tf_op jit(solution)/shard_map/attention_rest_gather_first/ppermute | solution.py:592
  231.0 20.3 %collective-permute-start.36 = (f32[2,4,96,384]{3,2,1,0:T(8,128)}, f32[2,4,96,384]{3,2,1,0:T(8,128)}, u32[]{:S(2)}, u32[]{:S(2)}) collective-permute-start(f32[2,4,96,384]{3,2,1,0:T(8,128)} %pad_maximum_fusion.5.piece_ref), channel_id=1, source_target_pairs={{0,2},{1,5},{2,0},{3,7},{4,6},{5,1},{6,4},{7,3},{8,10},{9,13},{10,... | collective-permute-start | bytes 3538952 | tf_op jit(solution)/shard_map/attention_gather_first/ppermute | solution.py:592
  231.7 1.2 collective-permute-start.27

commit v9 on v8

--- a/solution.py
+++ b/solution.py
@@ -501,14 +501,18 @@
 
 
 def put_in_place(views, z_first, sent, olds, piece_ref, *refs):
-    *refs, sems = refs
+    *refs, held_ref, in_sems, sems = refs
     outs = refs[olds:]
+    blocks = [(i, j) for i in range(2) for j in range(STACK)]
+    copies = fetch([(piece_ref.at[i, j], held_ref.at[i, j]) for i, j in blocks], in_sems)
     for start in (True, False):
         count = 0
         for i in range(2):
             for j in range(STACK):
+                if start:
+                    copies[STACK * i + j].wait()
                 z, place = (2 * sent + i, j) if z_first else (j, 2 * sent + i)
-                for wanted, source, target in views(outs, quarter_at(place), fourth_at(z), piece_ref.at[i, j]):
+                for wanted, source, target in views(outs, quarter_at(place), fourth_at(z), held_ref.at[i, j]):
                     copy = pltpu.make_async_copy(source, target, sems.at[count])
                     count += 1
                     act = copy.start if start else copy.wait
@@ -797,9 +801,9 @@
             partial(put_in_place, views, key == "c", sent, len(olds)),
             name=f"put_{key}",
             out_shape=[jax.ShapeDtypeStruct(*shapes[name]) for name in names],
-            in_specs=[VMEM] + [HBM] * len(olds),
+            in_specs=[pl.BlockSpec(memory_space=pl.ANY)] + [HBM] * len(olds),
             out_specs=[HBM] * len(names),
-            scratch_shapes=[sems(32)],
+            scratch_shapes=[pltpu.VMEM(piece.shape, f32), sems(8), sems(32)],
             input_output_aliases={1 + i: i for i in range(len(olds))},
             compiler_params=pltpu.CompilerParams(vmem_limit_bytes=8 * 1024 * 1024),
             cost_estimate=pl.CostEstimate(flops=0, bytes_accessed=2 * piece.size * 4, transcendentals=0),

time: 257 us -> 259 us (level)
  Pallas kernels: 64.4 us -> 75.4 us
  waiting for transfers between devices: 99.7 us -> 89.4 us
    pallas_call x10, Pallas kernels: 18.9 us -> 30.2 us  [put(): pl.pallas_call(partial(put_in_place, views, key == 'c', sent, len(olds)),...]
    ppermute x35, waiting for transfers between devices: 95 us -> 84.7 us  [flip(): return lax.ppermute(values, ('dp', 'mp'), pairs)]
  transfers between devices with their start and end apart: 39 -> 39, of which waited for: 23 -> 21; matrix products, arithmetic and copies ran while one was open for 4% -> 4% of each run, Pallas kernels for 14% -> 19%
where the time goes in v9:
time: 259 us
  waiting for transfers between devices  89.4 us (35%)
  starting transfers between devices  81.8 us (32%)
  Pallas kernels  75.4 us (29%)
  other arithmetic  7.23 us (3%)
  local copies, waits for them, and re-layouts  3.99 us (2%)
    ppermute x35, waiting for transfers between devices, flip(): return lax.ppermute(values, ('dp', 'mp'), pairs)  84.7 us
    ppermute x35, starting transfers between devices, flip(): return lax.ppermute(values, ('dp', 'mp'), pairs)  80.3 us
    pallas_call x4, Pallas kernels, call(): pl.pallas_call(kernel, name=kernel.__name__, out_shape=shapes, in_specs=[...  45.1 us
    pallas_call x10, Pallas kernels, put(): pl.pallas_call(partial(put_in_place, views, key == 'c', sent, len(olds)),...  30.2 us
  transfers between devices with their start and end apart: 39, of which 21 were waited for; matrix products, arithmetic and copies ran while one was open for 4% of the time, Pallas kernels for 19%

profile of v9, /device:TPU:0, one launch (start us, length us, event | category | flops | bytes accessed | tf_op | source)
XLA Modules:
  0.0 259.0 jit_solution(7419076637460725371)
XLA Ops:
  0.6 8.1 %attention_forward.1 = (bf16[512,768]{1,0:T(8,128)(2,1)}, bf16[512,384]{1,0:T(8,128)(2,1)}, bf16[512,384]{1,0:T(8,128)(2,1)}, bf16[512,384]{1,0:T(8,128)(2,1)}, ...) custom-call(s32[8,16]{1,0:T(8,128)} %bitcast.57, s32[16]{0:T(128)} %pads_in.1, ...), custom_call_target="tpu_custom_call" | custom-call | flops 1207959552 | bytes 8916544 | tf_op jit(solution)/shard_map/attention_forward/pallas_call | solution.py:566
  9.2 3.2 %collective-permute-done.theirs_in = f32[512,768]{1,0:T(8,128)S(1)} collective-permute-done((f32[512,768]{1,0:T(8,128)}, f32[512,768]{1,0:T(8,128)S(1)}, u32[]{:S(2)}, u32[]{:S(2)}) %collective-permute-start) | collective-permute-done | bytes 1572896 | tf_op jit(solution)/shard_map/ppermute | solution.py:591
  12.5 1.1 copy-done.10
  13.6 16.8 %mlp_kernel.1 = (f32[512,768]{1,0:T(8,128)}, f32[1,1536]{1,0:T(1,128)}, f32[2,4,96,512]{3,2,1,0:T(8,128)}, f32[2,4,96,512]{3,2,1,0:T(8,128)}, f32[2,4,192,256]{3...) custom-call(f32[768]{0:T(1024)} %refs_4_.1, ...), custom_call_target="tpu_custom_call" | custom-call | flops 7247757312 | bytes 23608320 | tf_op jit(solution)/shard_map/mlp_kernel/pallas_call | solution.py:566
  30.9 2.6 %collective-permute-start.5 = (f32[2,4,192,256]{3,2,1,0:T(8,128)}, f32[2,4,192,256]{3,2,1,0:T(8,128)}, u32[]{:S(2)}, u32[]{:S(2)}) collective-permute-start(f32[2,4,192,256]{3,2,1,0:T(8,128)} %get-tuple-element.151), channel_id=1, source_target_pairs={{0,2},{1,5},{2,0},{3,7},{4,6},{5,1},{6,4},{7,3},{8,10},{9,13},{10,... | collective-permute-start | bytes 4718600 | tf_op jit(solution)/shard_map/up_sum_first/ppermute | solution.py:596
  33.6 1.6 collective-permute-start.4
  35.7 0.9 collective-permute-done.1.refs_1_
  36.6 17.0 %attention_backward.1 = (bf16[512,768]{1,0:T(8,128)(2,1)}, f32[512,768]{1,0:T(8,128)}, f32[512,768]{1,0:T(8,128)}, f32[16,384]{1,0:T(8,128)}, f32[2,4,96,384]{3,...) custom-call(f32[2,512,768]{2,1,0:T(8,128)} %get-tuple-element.134.refs_0_, ...), custom_call_target="tpu_custom_call" | custom-call | flops 3019898880 | bytes 24678400 | tf_op jit(solution)/shard_map/attention_backward/pallas_call | solution.py:566
  54.0 2.6 %collective-permute-start.10 = (f32[2,4,96,384]{3,2,1,0:T(8,128)}, f32[2,4,96,384]{3,2,1,0:T(8,128)S(1)}, u32[]{:S(2)}, u32[]{:S(2)}) collective-permute-start(f32[2,4,96,384]{3,2,1,0:T(8,128)} %get-tuple-element.166), channel_id=1, source_target_pairs={{0,2},{1,5},{2,0},{3,7},{4,6},{5,1},{6,4},{7,3},{8,10},{9,13},{10,... | collective-permute-start | bytes 3538952 | tf_op jit(solution)/shard_map/attention_rest_sum_first/ppermute | solution.py:596
  56.6 2.1 add_bitcast_fusion.2
  58.7 1.6 collective-permute-start.7
  60.3 10.8 %collective-permute-done.4 = f32[2,4,192,256]{3,2,1,0:T(8,128)} collective-permute-done((f32[2,4,192,256]{3,2,1,0:T(8,128)}, f32[2,4,192,256]{3,2,1,0:T(8,128)}, u32[]{:S(2)}, u32[]{:S(2)}) %collective-permute-start.4) | collective-permute-done | bytes 1572896 | tf_op jit(solution)/shard_map/down_stack_sum_z_first/ppermute | solution.py:596
  71.1 1.7 add_bitcast_fusion
  72.8 3.9 %collective-permute-done.3 = f32[2,4,96,512]{3,2,1,0:T(8,128)S(1)} collective-permute-done((f32[2,4,96,512]{3,2,1,0:T(8,128)}, f32[2,4,96,512]{3,2,1,0:T(8,128)S(1)}, u32[]{:S(2)}, u32[]{:S(2)}) %collective-permute-start.3) | collective-permute-done | bytes 1572896 | tf_op jit(solution)/shard_map/down_sum_first/ppermute | solution.py:596
  77.1 2.9 %collective-permute-start.9 = (f32[4,96,512]{2,1,0:T(8,128)S(1)}, f32[4,96,512]{2,1,0:T(8,128)S(1)}, u32[]{:S(2)}, u32[]{:S(2)}) collective-permute-start(f32[4,96,512]{2,1,0:T(8,128)S(1)} %get-tuple-element.257), channel_id=1, source_target_pairs={{0,4},{1,3},{2,6},{3,1},{4,0},{5,7},{6,2},{7,5},{8,12},{9,11},{10,... | collective-permute-start | bytes 2359304 | tf_op jit(solution)/shard_map/down_sum_second/ppermute | solution.py:596
  80.0 2.6 collective-permute-start.14
  82.6 1.6 collective-permute-start.6
  84.2 3.3 %input_kernel.1 = bf16[512,768]{1,0:T(8,128)(2,1)} custom-call(f32[512,768]{1,0:T(8,128)S(1)} %copy-done.2, f32[512,768]{1,0:T(8,128)S(1)} %collective-permute-done.2.theirs_ref, bf16[512,768]{1,0:T(8,128)(2,1)S(1)} %copy-done, f32[1,768]{1,0:T(1,128)S(1)} %reshape.69.gain_ref, f32[512,768]{1,0:T(8,128)S(1)} %copy-done.1), custom_call_target="tpu_custom_call" | custom-call | bytes 6294528 | tf_op jit(solution)/shard_map/input_kernel/pallas_call | solution.py:566
  87.6 1.6 collective-permute-start.8
  89.2 9.3 %collective-permute-done.10 = f32[2,4,96,384]{3,2,1,0:T(8,128)S(1)} collective-permute-done((f32[2,4,96,384]{3,2,1,0:T(8,128)}, f32[2,4,96,384]{3,2,1,0:T(8,128)S(1)}, u32[]{:S(2)}, u32[]{:S(2)}) %collective-permute-start.10) | collective-permute-done | bytes 1179680 | tf_op jit(solution)/shard_map/attention_rest_sum_first/ppermute | solution.py:596
  98.7 2.1 collective-permute-start.12
  101.0 1.6 collective-permute-start.13
  102.6 4.8 %collective-permute-done.8 = f32[2,192,256]{2,1,0:T(8,128)S(1)} collective-permute-done((f32[2,192,256]{2,1,0:T(8,128)S(1)}, f32[2,192,256]{2,1,0:T(8,128)S(1)}, u32[]{:S(2)}, u32[]{:S(2)}) %collective-permute-start.8) | collective-permute-done | bytes 393248 | tf_op jit(solution)/shard_map/up_sum_z_first/ppermute | solution.py:596
  107.5 4.0 %collective-permute-start.11 = (f32[2,192,256]{2,1,0:T(8,128)S(1)}, f32[2,192,256]{2,1,0:T(8,128)S(1)}, u32[]{:S(2)}, u32[]{:S(2)}) collective-permute-start(f32[2,192,256]{2,1,0:T(8,128)S(1)} %add.145), channel_id=1, source_target_pairs={{0,16},{1,9},{2,18},{3,11},{4,20},{5,13},{6,22},{7,15},{8,24},{9,1... | collective-permute-start | bytes 1179656 | tf_op jit(solution)/shard_map/up_sum_z_second/ppermute | solution.py:596
  111.5 4.5 %collective-permute-done.14 = f32[4,192,256]{2,1,0:T(8,128)S(1)} collective-permute-done((f32[4,192,256]{2,1,0:T(8,128)S(1)}, f32[4,192,256]{2,1,0:T(8,128)S(1)}, u32[]{:S(2)}, u32[]{:S(2)}) %collective-permute-start.14) | collective-permute-done | bytes 786464 | tf_op jit(solution)/shard_map/down_stack_sum_z_second/ppermute | solution.py:596
  116.1 2.1 collective-permute-start.16
  118.2 1.3 collective-permute-start.18
  119.6 6.5 %collective-permute-start.21 = (f32[2,96,384]{2,1,0:T(8,128)S(1)}, f32[2,96,384]{2,1,0:T(8,128)S(1)}, u32[]{:S(2)}, u32[]{:S(2)}) collective-permute-start(f32[2,96,384]{2,1,0:T(8,128)S(1)} %get-tuple-element.271), channel_id=1, source_target_pairs={{0,8},{1,17},{2,10},{3,19},{4,12},{5,21},{6,14},{7,23},{8,0},{9,25... | collective-permute-start | bytes 884744 | tf_op jit(solution)/shard_map/attention_rest_sum_z_first/ppermute | solution.py:596
  126.7 5.0 %collective-permute-start.23 = (f32[2,192,256]{2,1,0:T(8,128)S(1)}, f32[2,192,256]{2,1,0:T(8,128)S(1)}, u32[]{:S(2)}, u32[]{:S(2)}) collective-permute-start(f32[2,192,256]{2,1,0:T(8,128)S(1)} %reverse_add_fusion.2), channel_id=1, source_target_pairs={{0,8},{1,17},{2,10},{3,19},{4,12},{5,21},{6,14},{7,23},{8,0},{9,25... | collective-permute-start | bytes 1179656 | tf_op jit(solution)/shard_map/up_gather_z_first/ppermute | solution.py:596
  132.7 1.5 collective-permute-start.17
  134.2 3.1 %collective-permute-done.18 = f32[2,96,512]{2,1,0:T(8,128)S(1)} collective-permute-done((f32[2,96,512]{2,1,0:T(8,128)S(1)}, f32[2,96,512]{2,1,0:T(8,128)S(1)}, u32[]{:S(2)}, u32[]{:S(2)}) %collective-permute-start.18) | collective-permute-done | bytes 393248 | tf_op jit(solution)/shard_map/down_sum_z_second/ppermute | solution.py:596
  137.3 2.8 %collective-permute-start.20 = (f32[2,96,512]{2,1,0:T(8,128)S(1)}, f32[2,96,512]{2,1,0:T(8,128)S(1)}, u32[]{:S(2)}, u32[]{:S(2)}) collective-permute-start(f32[2,96,512]{2,1,0:T(8,128)S(1)} %reverse_add_fusion.1), channel_id=1, source_target_pairs={{0,8},{1,17},{2,10},{3,19},{4,12},{5,21},{6,14},{7,23},{8,0},{9,25... | collective-permute-start | bytes 1179656 | tf_op jit(solution)/shard_map/down_gather_z_first/ppermute | solution.py:596
  140.2 6.2 %collective-permute-done.17 = f32[2,192,256]{2,1,0:T(8,128)S(1)} collective-permute-done((f32[2,192,256]{2,1,0:T(8,128)S(1)}, f32[2,192,256]{2,1,0:T(8,128)S(1)}, u32[]{:S(2)}, u32[]{:S(2)}) %collective-permute-start.17) | collective-permute-done | bytes 393248 | tf_op jit(solution)/shard_map/down_stack_sum_second/ppermute | solution.py:596
  146.4 1.9 collective-permute-start.22
  148.5 1.1 collective-permute-start.19
  150.5 3.7 %collective-permute-start.25 = (f32[4,192,256]{2,1,0:T(8,128)S(1)}, f32[4,192,256]{2,1,0:T(8,128)S(1)}, u32[]{:S(2)}, u32[]{:S(2)}) collective-permute-start(f32[4,192,256]{2,1,0:T(8,128)S(1)} %constant_dynamic-update-slice_fusion), channel_id=1, source_target_pairs={{0,4},{1,3},{2,6},{3,1},{4,0},{5,7},{6,2},{7,5},{8,12},{9,11},{10,... | collective-permute-start | bytes 2359304 | tf_op jit(solution)/shard_map/up_gather_second/ppermute | solution.py:596
  154.4 1.6 collective-permute-done.20
  156.1 10.2 %collective-permute-start.26 = (f32[4,96,512]{2,1,0:T(8,128)S(1)}, f32[4,96,512]{2,1,0:T(8,128)S(1)}, u32[]{:S(2)}, u32[]{:S(2)}) collective-permute-start(f32[4,96,512]{2,1,0:T(8,128)S(1)} %constant_dynamic-update-slice_fusion.4), channel_id=1, source_target_pairs={{0,4},{1,3},{2,6},{3,1},{4,0},{5,7},{6,2},{7,5},{8,12},{9,11},{10,... | collective-permute-start | bytes 2359304 | tf_op jit(solution)/shard_map/down_gather_second/ppermute | solution.py:596
  166.4 1.7 collective-permute-done.25
  168.2 1.5 collective-permute-start.32
  170.1 2.5 collective-permute-start.30
  173.0 8.0 %collective-permute-done.26 = f32[4,96,512]{2,1,0:T(8,128)S(1)} collective-permute-done((f32[4,96,512]{2,1,0:T(8,128)S(1)}, f32[4,96,512]{2,1,0:T(8,128)S(1)}, u32[]{:S(2)}, u32[]{:S(2)}) %collective-permute-start.26) | collective-permute-done | bytes 786464 | tf_op jit(solution)/shard_map/down_gather_second/ppermute | solution.py:596
  181.2 1.5 collective-permute-start.35
  182.7 3.5 %put_u.2.refs_0_ = f32[768,1536]{1,0:T(8,128)} custom-call(f32[2,4,192,256]{3,2,1,0:T(8,128)S(1)} %pad_maximum_fusion.piece_ref), custom_call_target="tpu_custom_call" | custom-call | bytes 3145728 | tf_op jit(solution)/shard_map/put_u/pallas_call | solution.py:800
  186.3 3.8 %put_d.2.refs_0_ = f32[1536,768]{1,0:T(8,128)} custom-call(f32[2,4,96,512]{3,2,1,0:T(8,128)S(1)} %pad_maximum_fusion.1.piece_ref), custom_call_target="tpu_custom_call" | custom-call | bytes 3145728 | tf_op jit(solution)/shard_map/put_d/pallas_call | solution.py:800
  190.1 3.6 %collective-permute-start.31 = (f32[2,96,384]{2,1,0:T(8,128)S(1)}, f32[2,96,384]{2,1,0:T(8,128)S(1)}, u32[]{:S(2)}, u32[]{:S(2)}) collective-permute-start(f32[2,96,384]{2,1,0:T(8,128)S(1)} %reverse_add_fusion.3), channel_id=1, source_target_pairs={{0,8},{1,17},{2,10},{3,19},{4,12},{5,21},{6,14},{7,23},{8,0},{9,25... | collective-permute-start | bytes 884744 | tf_op jit(solution)/shard_map/attention_rest_gather_z_first/ppermute | solution.py:596
  193.8 3.5 %put_u.3.refs_1_ = f32[768,1536]{1,0:T(8,128)} custom-call(f32[2,4,192,256]{3,2,1,0:T(8,128)S(1)} %collective-permute-done.32.piece_ref, f32[768,1536]{1,0:T(8,128)} %put_u.2.refs_0_), custom_call_target="tpu_custom_call", output_to_operand_aliasing={{}: (1, {})} | custom-call | bytes 3145728 | tf_op jit(solution)/shard_map/put_u/pallas_call | solution.py:800
  197.3 10.2 %collective-permute-done.31 = f32[2,96,384]{2,1,0:T(8,128)S(1)} collective-permute-done((f32[2,96,384]{2,1,0:T(8,128)S(1)}, f32[2,96,384]{2,1,0:T(8,128)S(1)}, u32[]{:S(2)}, u32[]{:S(2)}) %collective-permute-start.31) | collective-permute-done | bytes 294944 | tf_op jit(solution)/shard_map/attention_rest_gather_z_first/ppermute | solution.py:596
  207.5 1.8 collective-permute-start.34
  209.3 2.8 %collective-permute-done.29 = f32[4,192,256]{2,1,0:T(8,128)S(1)} collective-permute-done((f32[4,192,256]{2,1,0:T(8,128)S(1)}, f32[4,192,256]{2,1,0:T(8,128)S(1)}, u32[]{:S(2)}, u32[]{:S(2)}) %collective-permute-start.29) | collective-permute-done | bytes 786464 | tf_op jit(solution)/shard_map/down_stack_gather_z_second/ppermute | solution.py:596
  212.3 1.3 collective-permute-done.28
  213.6 3.3 %collective-permute-start.33 = (f32[4,96,384]{2,1,0:T(8,128)S(1)}, f32[4,96,384]{2,1,0:T(8,128)S(1)}, u32[]{:S(2)}, u32[]{:S(2)}) collective-permute-start(f32[4,96,384]{2,1,0:T(8,128)S(1)} %constant_dynamic-update-slice_fusion.8), channel_id=1, source_target_pairs={{0,4},{1,3},{2,6},{3,1},{4,0},{5,7},{6,2},{7,5},{8,12},{9,11},{10,... | collective-permute-start | bytes 1769480 | tf_op jit(solution)/shard_map/attention_gather_second/ppermute | solution.py:596
  216.9 0.9 collective-permute-start.38
  217.8 3.5 %put_c.2 = (f32[1536,768]{1,0:T(8,128)}, f32[768,1536]{1,0:T(8,128)}) custom-call(f32[2,4,192,256]{3,2,1,0:T(8,128)S(1)} %pad_maximum_fusion.2.piece_ref, f32[1536,768]{1,0:T(8,128)} %put_d.2.refs_0_, f32[768,1536]{1,0:T(8,128)} %put_u.3.refs_1_), custom_call_target="tpu_custom_call", output_to_operand_aliasing={{0}: (1, {}), {1}: (2, {})} | custom-call | bytes 3145728 | tf_op jit(solution)/shard_map/put_c/pallas_call | solution.py:800
  221.3 3.5 %put_d.3.refs_0_ = f32[1536,768]{1,0:T(8,128)} custom-call(f32[2,4,96,512]{3,2,1,0:T(8,128)S(1)} %collective-permute-done.35.piece_ref, f32[1536,768]{1,0:T(8,128)} %get-tuple-element.223.refs_0_), custom_call_target="tpu_custom_call", output_to_operand_aliasing={{}: (1, {})} | custom-call | bytes 3145728 | tf_op jit(solution)/shard_map/put_d/pallas_call | solution.py:800
  224.9 1.6 collective-permute-start.37
  226.5 1.1 pad_maximum_fusion.5.piece_ref
  231.2 2.9 %put_b.2 = (f32[384,768]{1,0:T(8,128)}, f32[768,384]{1,0:T(8,128)}, f32[768,384]{1,0:T(8,128)}, f32[768,384]{1,0:T(8,128)}) custom-call(f32[2,4,96,384]{3,2,1,0:T(8,128)S(1)} %pad_maximum_fusion.4.piece_ref), custom_call_target="tpu_custom_call" | custom-call | bytes 2359296 | tf_op jit(solution)/shard_map/put_b/pallas_call | solution.py:800
  234.1 7.2 %collective-permute-done.37.piece_ref = f32[2,4,96,384]{3,2,1,0:T(8,128)} collective-permute-done((f32[2,4,96,384]{3,2,1,0:T(8,128)S(1)}, f32[2,4,96,384]{3,2,1,0:T(8,128)}, u32[]{:S(2)}, u32[]{:S(2)}) %collective-permute-start.37) | collective-permute-done | bytes 1179680 | tf_op jit(solution)/shard_map/attention_rest_gather_first/ppermute | solution.py:596
  241.3 2.4 put_a.2
  243.7 2.4 put_b.3
  246.1 7.9 %collective-permute-done.36.piece_ref = f32[2,4,96,384]{3,2,1,0:T(8,128)} collective-permute-done((f32[2,4,96,384]{3,2,1,0:T(8,128)}, f32[2,4,96,384]{3,2,1,0:T(8,128)}, u32[]{:S(2)}, u32[]{:S(2)}) %collective-permute-start.36) | collective-permute-done | bytes 1179680 | tf_op jit(solution)/shard_map/attention_gather_first/ppermute | solution.py:596
  254.0 2.4 put_a.3
  256.3 2.5 put_c.3
  (107 shorter events, 11.1 us)
Async XLA Ops:
  8.7 3.8 %collective-permute-start = (f32[512,768]{1,0:T(8,128)}, f32[512,768]{1,0:T(8,128)S(1)}, u32[]{:S(2)}, u32[]{:S(2)}) collective-permute-start(f32[512,768]{1,0:T(8,128)} %get-tuple-element.133.mine_in), channel_id=1, source_target_pairs={{0,1},{1,0},{2,3},{3,2},{4,5},{5,4},{6,7},{7,6},{8,9},{9,8},{10,11... | collective-permute-start | bytes 4718600 | tf_op jit(solution)/shard_map/ppermute | solution.py:591
  12.5 1.1 copy-start.10
  30.5 6.1 %collective-permute-start.1 = (f32[2,512,768]{2,1,0:T(8,128)}, f32[2,512,768]{2,1,0:T(8,128)}, u32[]{:S(2)}, u32[]{:S(2)}) collective-permute-start(f32[2,512,768]{2,1,0:T(8,128)} %get-tuple-element.134.refs_0_), channel_id=1, source_target_pairs={{0,1},{1,0},{2,3},{3,2},{4,5},{5,4},{6,7},{7,6},{8,9},{9,8},{10,11... | collective-permute-start | bytes 9437192 | tf_op jit(solution)/shard_map/ppermute | solution.py:591
  30.9 23.0 %collective-permute-start.5 = (f32[2,4,192,256]{3,2,1,0:T(8,128)}, f32[2,4,192,256]{3,2,1,0:T(8,128)}, u32[]{:S(2)}, u32[]{:S(2)}) collective-permute-start(f32[2,4,192,256]{3,2,1,0:T(8,128)} %get-tuple-element.151), channel_id=1, source_target_pairs={{0,2},{1,5},{2,0},{3,7},{4,6},{5,1},{6,4},{7,3},{8,10},{9,13},{10,... | collective-permute-start | bytes 4718600 | tf_op jit(solution)/shard_map/up_sum_first/ppermute | solution.py:596
  33.6 37.5 %collective-permute-start.4 = (f32[2,4,192,256]{3,2,1,0:T(8,128)}, f32[2,4,192,256]{3,2,1,0:T(8,128)}, u32[]{:S(2)}, u32[]{:S(2)}) collective-permute-start(f32[2,4,192,256]{3,2,1,0:T(8,128)} %get-tuple-element.149), channel_id=1, source_target_pairs={{0,8},{1,17},{2,10},{3,19},{4,12},{5,21},{6,14},{7,23},{8,0},{9,25... | collective-permute-start | bytes 4718600 | tf_op jit(solution)/shard_map/down_stack_sum_z_first/ppermute | solution.py:596
  35.1 41.5 %collective-permute-start.3 = (f32[2,4,96,512]{3,2,1,0:T(8,128)}, f32[2,4,96,512]{3,2,1,0:T(8,128)S(1)}, u32[]{:S(2)}, u32[]{:S(2)}) collective-permute-start(f32[2,4,96,512]{3,2,1,0:T(8,128)} %get-tuple-element.147), channel_id=1, source_target_pairs={{0,2},{1,5},{2,0},{3,7},{4,6},{5,1},{6,4},{7,3},{8,10},{9,13},{10,... | collective-permute-start | bytes 4718600 | tf_op jit(solution)/shard_map/down_sum_first/ppermute | solution.py:596
  53.5 29.1 %collective-permute-start.2 = (f32[512,768]{1,0:T(8,128)}, f32[512,768]{1,0:T(8,128)S(1)}, u32[]{:S(2)}, u32[]{:S(2)}) collective-permute-start(f32[512,768]{1,0:T(8,128)} %get-tuple-element.145.mine_ref), channel_id=1, source_target_pairs={{0,1},{1,0},{2,3},{3,2},{4,5},{5,4},{6,7},{7,6},{8,9},{9,8},{10,11... | collective-permute-start | bytes 4718600 | tf_op jit(solution)/shard_map/ppermute | solution.py:591
  54.0 17.1 %copy-start.4 = (f32[2,4,192,256]{3,2,1,0:T(8,128)S(1)}, f32[2,4,192,256]{3,2,1,0:T(8,128)}, u32[]{:S(2)}) copy-start(f32[2,4,192,256]{3,2,1,0:T(8,128)} %get-tuple-element.155) | copy-start | bytes 4718596
  54.0 44.5 %collective-permute-start.10 = (f32[2,4,96,384]{3,2,1,0:T(8,128)}, f32[2,4,96,384]{3,2,1,0:T(8,128)S(1)}, u32[]{:S(2)}, u32[]{:S(2)}) collective-permute-start(f32[2,4,96,384]{3,2,1,0:T(8,128)} %get-tuple-element.166), channel_id=1, source_target_pairs={{0,2},{1,5},{2,0},{3,7},{4,6},{5,1},{6,4},{7,3},{8,10},{9,13},{10,... | collective-permute-start | bytes 3538952 | tf_op jit(solution)/shard_map/attention_rest_sum_first/ppermute | solution.py:596
  58.7 28.8 %collective-permute-start.7 = (f32[4,192,256]{2,1,0:T(8,128)S(1)}, f32[4,192,256]{2,1,0:T(8,128)S(1)}, u32[]{:S(2)}, u32[]{:S(2)}) collective-permute-start(f32[4,192,256]{2,1,0:T(8,128)S(1)} %get-tuple-element.259), channel_id=1, source_target_pairs={{0,4},{1,3},{2,6},{3,1},{4,0},{5,7},{6,2},{7,5},{8,12},{9,11},{10,... | collective-permute-start | bytes 2359304 | tf_op jit(solution)/shard_map/up_sum_second/ppermute | solution.py:596
  71.1 5.6 %copy-start.3 = (f32[2,4,96,512]{3,2,1,0:T(8,128)S(1)}, f32[2,4,96,512]{3,2,1,0:T(8,128)}, u32[]{:S(2)}) copy-start(f32[2,4,96,512]{3,2,1,0:T(8,128)} %get-tuple-element.157) | copy-start | bytes 4718596
  76.7 3.3 %copy-start.9 = (f32[768]{0:T(1024)S(1)}, f32[768]{0:T(1024)}, u32[]{:S(2)}) copy-start(f32[768]{0:T(1024)} %gain_in.2) | copy-start | bytes 9220
  76.7 5.8 %copy-start.7 = (f32[2,4,96,384]{3,2,1,0:T(8,128)S(1)}, f32[2,4,96,384]{3,2,1,0:T(8,128)}, u32[]{:S(2)}) copy-start(f32[2,4,96,384]{3,2,1,0:T(8,128)} %get-tuple-element.162) | copy-start | bytes 3538948
  76.7 5.8 %copy-start.8 = (f32[16,384]{1,0:T(8,128)S(1)}, f32[16,384]{1,0:T(8,128)}, u32[]{:S(2)}) copy-start(f32[16,384]{1,0:T(8,128)} %get-tuple-element.183) | copy-start | bytes 73732
  76.7 7.5 %copy-start.2 = (f32[512,768]{1,0:T(8,128)S(1)}, f32[512,768]{1,0:T(8,128)}, u32[]{:S(2)}) copy-start(f32[512,768]{1,0:T(8,128)} %get-tuple-element.145.mine_ref) | copy-start | bytes 4718596
  77.1 7.1 %copy-start = (bf16[512,768]{1,0:T(8,128)(2,1)S(1)}, bf16[512,768]{1,0:T(8,128)(2,1)}, u32[]{:S(2)}) copy-start(bf16[512,768]{1,0:T(8,128)(2,1)} %x_ref.1) | copy-start | bytes 2359300
  77.1 7.1 %copy-start.1 = (f32[512,768]{1,0:T(8,128)S(1)}, f32[512,768]{1,0:T(8,128)}, u32[]{:S(2)}) copy-start(f32[512,768]{1,0:T(8,128)} %get-tuple-element.160.delta_ref) | copy-start | bytes 4718596
  77.1 23.7 %collective-permute-start.9 = (f32[4,96,512]{2,1,0:T(8,128)S(1)}, f32[4,96,512]{2,1,0:T(8,128)S(1)}, u32[]{:S(2)}, u32[]{:S(2)}) collective-permute-start(f32[4,96,512]{2,1,0:T(8,128)S(1)} %get-tuple-element.257), channel_id=1, source_target_pairs={{0,4},{1,3},{2,6},{3,1},{4,0},{5,7},{6,2},{7,5},{8,12},{9,11},{10,... | collective-permute-start | bytes 2359304 | tf_op jit(solution)/shard_map/down_sum_second/ppermute | solution.py:596
  80.0 36.0 %collective-permute-start.14 = (f32[4,192,256]{2,1,0:T(8,128)S(1)}, f32[4,192,256]{2,1,0:T(8,128)S(1)}, u32[]{:S(2)}, u32[]{:S(2)}) collective-permute-start(f32[4,192,256]{2,1,0:T(8,128)S(1)} %get-tuple-element.255), channel_id=1, source_target_pairs={{0,16},{1,9},{2,18},{3,11},{4,20},{5,13},{6,22},{7,15},{8,24},{9,1... | collective-permute-start | bytes 2359304 | tf_op jit(solution)/shard_map/down_stack_sum_z_second/ppermute | solution.py:596
  82.6 49.1 %collective-permute-start.6 = (f32[784,384]{1,0:T(8,128)S(1)}, f32[784,384]{1,0:T(8,128)S(1)}, u32[]{:S(2)}, u32[]{:S(2)}) collective-permute-start(f32[784,384]{1,0:T(8,128)S(1)} %pad_maximum_fusion.3), channel_id=1, source_target_pairs={{0,2},{1,5},{2,0},{3,7},{4,6},{5,1},{6,4},{7,3},{8,10},{9,13},{10,... | collective-permute-start | bytes 3612680 | tf_op jit(solution)/shard_map/attention_sum_first/ppermute | solution.py:596
  87.4 11.1 %copy-start.5 = (f32[2,4,96,384]{3,2,1,0:T(8,128)S(1)}, f32[2,4,96,384]{3,2,1,0:T(8,128)}, u32[]{:S(2)}) copy-start(f32[2,4,96,384]{3,2,1,0:T(8,128)} %get-tuple-element.167) | copy-start | bytes 3538948
  87.6 19.9 %collective-permute-start.8 = (f32[2,192,256]{2,1,0:T(8,128)S(1)}, f32[2,192,256]{2,1,0:T(8,128)S(1)}, u32[]{:S(2)}, u32[]{:S(2)}) collective-permute-start(f32[2,192,256]{2,1,0:T(8,128)S(1)} %get-tuple-element.266), channel_id=1, source_target_pairs={{0,8},{1,17},{2,10},{3,19},{4,12},{5,21},{6,14},{7,23},{8,0},{9,25... | collective-permute-start | bytes 1179656 | tf_op jit(solution)/shard_map/up_sum_z_first/ppermute | solution.py:596
  98.7 20.8 %collective-permute-start.12 = (f32[4,96,384]{2,1,0:T(8,128)S(1)}, f32[4,96,384]{2,1,0:T(8,128)S(1)}, u32[]{:S(2)}, u32[]{:S(2)}) collective-permute-start(f32[4,96,384]{2,1,0:T(8,128)S(1)} %get-tuple-element.261), channel_id=1, source_target_pairs={{0,4},{1,3},{2,6},{3,1},{4,0},{5,7},{6,2},{7,5},{8,12},{9,11},{10,... | collective-permute-start | bytes 1769480 | tf_op jit(solution)/shard_map/attention_rest_sum_second/ppermute | solution.py:596
  101.0 17.2 %collective-permute-start.13 = (f32[2,96,512]{2,1,0:T(8,128)S(1)}, f32[2,96,512]{2,1,0:T(8,128)S(1)}, u32[]{:S(2)}, u32[]{:S(2)}) collective-permute-start(f32[2,96,512]{2,1,0:T(8,128)S(1)} %get-tuple-element.265), channel_id=1, source_target_pairs={{0,8},{1,17},{2,10},{3,19},{4,12},{5,21},{6,14},{7,23},{8,0},{9,25... | collective-permute-start | bytes 1179656 | tf_op jit(solution)/shard_map/down_sum_z_first/ppermute | solution.py:596
  107.5 19.1 %collective-permute-start.11 = (f32[2,192,256]{2,1,0:T(8,128)S(1)}, f32[2,192,256]{2,1,0:T(8,128)S(1)}, u32[]{:S(2)}, u32[]{:S(2)}) collective-permute-start(f32[2,192,256]{2,1,0:T(8,128)S(1)} %add.145), channel_id=1, source_target_pairs={{0,16},{1,9},{2,18},{3,11},{4,20},{5,13},{6,22},{7,15},{8,24},{9,1... | collective-permute-start | bytes 1179656 | tf_op jit(solution)/shard_map/up_sum_z_second/ppermute | solution.py:596
  116.1 16.5 %collective-permute-start.16 = (f32[2,192,256]{2,1,0:T(8,128)S(1)}, f32[2,192,256]{2,1,0:T(8,128)S(1)}, u32[]{:S(2)}, u32[]{:S(2)}) collective-permute-start(f32[2,192,256]{2,1,0:T(8,128)S(1)} %get-tuple-element.263), channel_id=1, source_target_pairs={{0,2},{1,5},{2,0},{3,7},{4,6},{5,1},{6,4},{7,3},{8,10},{9,13},{10,... | collective-permute-start | bytes 1179656 | tf_op jit(solution)/shard_map/down_stack_sum_first/ppermute | solution.py:596
  118.2 13.5 %copy-start.6 = (f32[2,4,96,384]{3,2,1,0:T(8,128)S(1)}, f32[2,4,96,384]{3,2,1,0:T(8,128)}, u32[]{:S(2)}) copy-start(f32[2,4,96,384]{3,2,1,0:T(8,128)} %get-tuple-element.181) | copy-start | bytes 3538948
  118.2 19.0 %collective-permute-start.18 = (f32[2,96,512]{2,1,0:T(8,128)S(1)}, f32[2,96,512]{2,1,0:T(8,128)S(1)}, u32[]{:S(2)}, u32[]{:S(2)}) collective-permute-start(f32[2,96,512]{2,1,0:T(8,128)S(1)} %add.152), channel_id=1, source_target_pairs={{0,16},{1,9},{2,18},{3,11},{4,20},{5,13},{6,22},{7,15},{8,24},{9,1... | collective-permute-start | bytes 1179656 | tf_op jit(solution)/shard_map/down_sum_z_second/ppermute | solution.py:596
  119.6 34.8 %collective-permute-start.21 = (f32[2,96,384]{2,1,0:T(8,128)S(1)}, f32[2,96,384]{2,1,0:T(8,128)S(1)}, u32[]{:S(2)}, u32[]{:S(2)}) collective-permute-start(f32[2,96,384]{2,1,0:T(8,128)S(1)} %get-tuple-element.271), channel_id=1, source_target_pairs={{0,8},{1,17},{2,10},{3,19},{4,12},{5,21},{6,14},{7,23},{8,0},{9,25... | collective-permute-start | bytes 884744 | tf_op jit(solution)/shard_map/attention_rest_sum_z_first/ppermute | solution.py:596
  126.7 23.7 %collective-permute-start.23 = (f32[2,192,256]{2,1,0:T(8,128)S(1)}, f32[2,192,256]{2,1,0:T(8,128)S(1)}, u32[]{:S(2)}, u32[]{:S(2)}) collective-permute-start(f32[2,192,256]{2,1,0:T(8,128)S(1)} %reverse_add_fusion.2), channel_id=1, source_target_pairs={{0,8},{1,17},{2,10},{3,19},{4,12},{5,21},{6,14},{7,23},{8,0},{9,25... | collective-permute-start | bytes 1179656 | tf_op jit(solution)/shard_map/up_gather_z_first/ppermute | solution.py:596
  132.0 16.4 %collective-permute-start.15 = (f32[400,384]{1,0:T(8,128)S(1)}, f32[400,384]{1,0:T(8,128)S(1)}, u32[]{:S(2)}, u32[]{:S(2)}) collective-permute-start(f32[400,384]{1,0:T(8,128)S(1)} %pad_maximum_fusion.6), channel_id=1, source_target_pairs={{0,4},{1,3},{2,6},{3,1},{4,0},{5,7},{6,2},{7,5},{8,12},{9,11},{10,... | collective-permute-start | bytes 1843208 | tf_op jit(solution)/shard_map/attention_sum_second/ppermute | solution.py:596
  132.7 13.7 %collective-permute-start.17 = (f32[2,192,256]{2,1,0:T(8,128)S(1)}, f32[2,192,256]{2,1,0:T(8,128)S(1)}, u32[]{:S(2)}, u32[]{:S(2)}) collective-permute-start(f32[2,192,256]{2,1,0:T(8,128)S(1)} %add.159), channel_id=1, source_target_pairs={{0,4},{1,3},{2,6},{3,1},{4,0},{5,7},{6,2},{7,5},{8,12},{9,11},{10,... | collective-permute-start | bytes 1179656 | tf_op jit(solution)/shard_map/down_stack_sum_second/ppermute | solution.py:596
  137.3 18.7 %collective-permute-start.20 = (f32[2,96,512]{2,1,0:T(8,128)S(1)}, f32[2,96,512]{2,1,0:T(8,128)S(1)}, u32[]{:S(2)}, u32[]{:S(2)}) collective-permute-start(f32[2,96,512]{2,1,0:T(8,128)S(1)} %reverse_add_fusion.1), channel_id=1, source_target_pairs={{0,8},{1,17},{2,10},{3,19},{4,12},{5,21},{6,14},{7,23},{8,0},{9,25... | collective-permute-start | bytes 1179656 | tf_op jit(solution)/shard_map/down_gather_z_first/ppermute | solution.py:596
  146.4 7.8 %collective-permute-start.22 = (f32[2,192,256]{2,1,0:T(8,128)S(1)}, f32[2,192,256]{2,1,0:T(8,128)S(1)}, u32[]{:S(2)}, u32[]{:S(2)}) collective-permute-start(f32[2,192,256]{2,1,0:T(8,128)S(1)} %reverse_add_fusion), channel_id=1, source_target_pairs={{0,2},{1,5},{2,0},{3,7},{4,6},{5,1},{6,4},{7,3},{8,10},{9,13},{10,... | collective-permute-start | bytes 1179656 | tf_op jit(solution)/shard_map/down_stack_gather_first/ppermute | solution.py:596
  148.5 17.7 %collective-permute-start.19 = (f32[208,384]{1,0:T(8,128)S(1)}, f32[208,384]{1,0:T(8,128)S(1)}, u32[]{:S(2)}, u32[]{:S(2)}) collective-permute-start(f32[208,384]{1,0:T(8,128)S(1)} %pad_maximum_fusion.7), channel_id=1, source_target_pairs={{0,8},{1,17},{2,10},{3,19},{4,12},{5,21},{6,14},{7,23},{8,0},{9,25... | collective-permute-start | bytes 958472 | tf_op jit(solution)/shard_map/attention_sum_z_first/ppermute | solution.py:596
  150.5 17.6 %collective-permute-start.25 = (f32[4,192,256]{2,1,0:T(8,128)S(1)}, f32[4,192,256]{2,1,0:T(8,128)S(1)}, u32[]{:S(2)}, u32[]{:S(2)}) collective-permute-start(f32[4,192,256]{2,1,0:T(8,128)S(1)} %constant_dynamic-update-slice_fusion), channel_id=1, source_target_pairs={{0,4},{1,3},{2,6},{3,1},{4,0},{5,7},{6,2},{7,5},{8,12},{9,11},{10,... | collective-permute-start | bytes 2359304 | tf_op jit(solution)/shard_map/up_gather_second/ppermute | solution.py:596
  156.1 25.0 %collective-permute-start.26 = (f32[4,96,512]{2,1,0:T(8,128)S(1)}, f32[4,96,512]{2,1,0:T(8,128)S(1)}, u32[]{:S(2)}, u32[]{:S(2)}) collective-permute-start(f32[4,96,512]{2,1,0:T(8,128)S(1)} %constant_dynamic-update-slice_fusion.4), channel_id=1, source_target_pairs={{0,4},{1,3},{2,6},{3,1},{4,0},{5,7},{6,2},{7,5},{8,12},{9,11},{10,... | collective-permute-start | bytes 2359304 | tf_op jit(solution)/shard_map/down_gather_second/ppermute | solution.py:596
  168.2 25.6 %collective-permute-start.32 = (f32[2,4,192,256]{3,2,1,0:T(8,128)S(1)}, f32[2,4,192,256]{3,2,1,0:T(8,128)S(1)}, u32[]{:S(2)}, u32[]{:S(2)}) collective-permute-start(f32[2,4,192,256]{3,2,1,0:T(8,128)S(1)} %pad_maximum_fusion.piece_ref), channel_id=1, source_target_pairs={{0,2},{1,5},{2,0},{3,7},{4,6},{5,1},{6,4},{7,3},{8,10},{9,13},{10,... | collective-permute-start | bytes 4718600 | tf_op jit(solution)/shard_map/up_gather_first/ppermute | solution.py:596
  169.7 16.5 %collective-permute-start.24 = (f32[208,384]{1,0:T(8,128)S(1)}, f32[208,384]{1,0:T(8,128)S(1)}, u32[]{:S(2)}, u32[]{:S(2)}) collective-permute-start(f32[208,384]{1,0:T(8,128)S(1)} %pad_maximum_fusion.8), channel_id=1, source_target_pairs={{0,16},{1,9},{2,18},{3,11},{4,20},{5,13},{6,22},{7,15},{8,24},{9,1... | collective-permute-start | bytes 958472 | tf_op jit(solution)/shard_map/attention_sum_z_second/ppermute | solution.py:596
  170.1 20.0 %collective-permute-start.30 = (f32[2,96,384]{2,1,0:T(8,128)S(1)}, f32[2,96,384]{2,1,0:T(8,128)S(1)}, u32[]{:S(2)}, u32[]{:S(2)}) collective-permute-start(f32[2,96,384]{2,1,0:T(8,128)S(1)} %add.166), channel_id=1, source_target_pairs={{0,16},{1,9},{2,18},{3,11},{4,20},{5,13},{6,22},{7,15},{8,24},{9,1... | collective-permute-start | bytes 884744 | tf_op jit(solution)/shard_map/attention_rest_sum_z_second/ppermute | solution.py:596
  172.6 39.5 %collective-permute-start.29 = (f32[4,192,256]{2,1,0:T(8,128)S(1)}, f32[4,192,256]{2,1,0:T(8,128)S(1)}, u32[]{:S(2)}, u32[]{:S(2)}) collective-permute-start(f32[4,192,256]{2,1,0:T(8,128)S(1)} %constant_dynamic-update-slice_fusion.2), channel_id=1, source_target_pairs={{0,16},{1,9},{2,18},{3,11},{4,20},{5,13},{6,22},{7,15},{8,24},{9,1... | collective-permute-start | bytes 2359304 | tf_op jit(solution)/shard_map/down_stack_gather_z_second/ppermute | solution.py:596
  181.2 40.1 %collective-permute-start.35 = (f32[2,4,96,512]{3,2,1,0:T(8,128)S(1)}, f32[2,4,96,512]{3,2,1,0:T(8,128)S(1)}, u32[]{:S(2)}, u32[]{:S(2)}) collective-permute-start(f32[2,4,96,512]{3,2,1,0:T(8,128)S(1)} %pad_maximum_fusion.1.piece_ref), channel_id=1, source_target_pairs={{0,2},{1,5},{2,0},{3,7},{4,6},{5,1},{6,4},{7,3},{8,10},{9,13},{10,... | collective-permute-start | bytes 4718600 | tf_op jit(solution)/shard_map/down_gather_first/ppermute | solution.py:596
  190.1 17.4 %collective-permute-start.31 = (f32[2,96,384]{2,1,0:T(8,128)S(1)}, f32[2,96,384]{2,1,0:T(8,128)S(1)}, u32[]{:S(2)}, u32[]{:S(2)}) collective-permute-start(f32[2,96,384]{2,1,0:T(8,128)S(1)} %reverse_add_fusion.3), channel_id=1, source_target_pairs={{0,8},{1,17},{2,10},{3,19},{4,12},{5,21},{6,14},{7,23},{8,0},{9,25... | collective-permute-start | bytes 884744 | tf_op jit(solution)/shard_map/attention_rest_gather_z_first/ppermute | solution.py:596
  193.7 19.8 %collective-permute-start.28 = (f32[2,96,384]{2,1,0:T(8,128)S(1)}, f32[2,96,384]{2,1,0:T(8,128)S(1)}, u32[]{:S(2)}, u32[]{:S(2)}) collective-permute-start(f32[2,96,384]{2,1,0:T(8,128)S(1)} %reverse_add_fusion.4), channel_id=1, source_target_pairs={{0,8},{1,17},{2,10},{3,19},{4,12},{5,21},{6,14},{7,23},{8,0},{9,25... | collective-permute-start | bytes 884744 | tf_op jit(solution)/shard_map/attention_gather_z_first/ppermute | solution.py:596
  207.5 17.3 %collective-permute-start.34 = (f32[4,96,384]{2,1,0:T(8,128)S(1)}, f32[4,96,384]{2,1,0:T(8,128)S(1)}, u32[]{:S(2)}, u32[]{:S(2)}) collective-permute-start(f32[4,96,384]{2,1,0:T(8,128)S(1)} %constant_dynamic-update-slice_fusion.6), channel_id=1, source_target_pairs={{0,4},{1,3},{2,6},{3,1},{4,0},{5,7},{6,2},{7,5},{8,12},{9,11},{10,... | collective-permute-start | bytes 1769480 | tf_op jit(solution)/shard_map/attention_rest_gather_second/ppermute | solution.py:596
  213.6 13.0 %collective-permute-start.33 = (f32[4,96,384]{2,1,0:T(8,128)S(1)}, f32[4,96,384]{2,1,0:T(8,128)S(1)}, u32[]{:S(2)}, u32[]{:S(2)}) collective-permute-start(f32[4,96,384]{2,1,0:T(8,128)S(1)} %constant_dynamic-update-slice_fusion.8), channel_id=1, source_target_pairs={{0,4},{1,3},{2,6},{3,1},{4,0},{5,7},{6,2},{7,5},{8,12},{9,11},{10,... | collective-permute-start | bytes 1769480 | tf_op jit(solution)/shard_map/attention_gather_second/ppermute | solution.py:596
  216.9 39.4 %collective-permute-start.38 = (f32[2,4,192,256]{3,2,1,0:T(8,128)S(1)}, f32[2,4,192,256]{3,2,1,0:T(8,128)}, u32[]{:S(2)}, u32[]{:S(2)}) collective-permute-start(f32[2,4,192,256]{3,2,1,0:T(8,128)S(1)} %pad_maximum_fusion.2.piece_ref), channel_id=1, source_target_pairs={{0,8},{1,17},{2,10},{3,19},{4,12},{5,21},{6,14},{7,23},{8,0},{9,25... | collective-permute-start | bytes 4718600 | tf_op jit(solution)/shard_map/down_stack_gather_z_first/ppermute | solution.py:596
  224.9 16.4 %collective-permute-start.37 = (f32[2,4,96,384]{3,2,1,0:T(8,128)S(1)}, f32[2,4,96,384]{3,2,1,0:T(8,128)}, u32[]{:S(2)}, u32[]{:S(2)}) collective-permute-start(f32[2,4,96,384]{3,2,1,0:T(8,128)S(1)} %pad_maximum_fusion.4.piece_ref), channel_id=1, source_target_pairs={{0,2},{1,5},{2,0},{3,7},{4,6},{5,1},{6,4},{7,3},{8,10},{9,13},{10,... | collective-permute-start | bytes 3538952 | tf_op jit(solution)/shard_map/attention_rest_gather_first/ppermute | solution.py:596
  227.7 26.3 %collective-permute-start.36 = (f32[2,4,96,384]{3,2,1,0:T(8,128)}, f32[2,4,96,384]{3,2,1,0:T(8,128)}, u32[]{:S(2)}, u32[]{:S(2)}) collective-permute-start(f32[2,4,96,384]{3,2,1,0:T(8,128)} %pad_maximum_fusion.5.piece_ref), channel_id=1, source_target_pairs={{0,2},{1,5},{2,0},{3,7},{4,6},{5,1},{6,4},{7,3},{8,10},{9,13},{10,... | collective-permute-start | bytes 3538952 | tf_op jit(solution)/shard_map/attention_gather_first/ppermute | solution.py:596
  228.2 1.2 collective-permute-start.27
